TPU v7x, 32 devices: a whole 2x2x4 slice. The times are simulated.
32 devices in a mesh: dp: 16 (over z, y, x), table: 2 (over core).
Axes of the slice: x: 2, y: 2, z: 4, core: 2. Of those that a mesh axis runs over, the one named last changes fastest.
Arguments:
- item_table: bfloat16 [131072, 512], P(('dp', 'table')), may hold values from -6 to 6
- token_request_slot: int32 [8192], P(('dp', 'table')), may hold values from 0 to 255
- request_rows: int32 [32, 32, 8], P(('dp', 'table')), may hold values from 0 to 4095, as said below
- lengths: int32 [2, 64], P('table'), may hold values from 0 to 256, as said below
- assignment: int32 [2, 64], P('table'), may hold values from 0 to 15
- timestamps: int32 [8192], P(('dp', 'table')), may hold values from 1 to 524288, as said below
- item_counts: int32 [131072], P(('dp', 'table')), may hold values from 0 to 3
- first_norm_gain: float32 [512], replicated, may hold values from 0.5 to 1.5
- w_uvqk: bfloat16 [512, 2048], replicated, may hold values from -0.25 to 0.25
- b_uvqk: float32 [2048], replicated, may hold values from -2 to 2
- norm2_gain: float32 [512], replicated, may hold values from 0.5 to 1.5
- w_out: bfloat16 [512, 512], replicated, may hold values from -0.25 to 0.25
- b_out: float32 [512], replicated, may hold values from -2 to 2
- pos_weight: float32 [8, 10], replicated, may hold values from -2 to 2
- time_weight: float32 [8, 10], replicated, may hold values from -2 to 2
- out_grad: bfloat16 [8192, 512], P(('dp', 'table')), may hold values from -6 to 6
Outputs:
- layer_out: bfloat16 [8192, 512], P(('dp', 'table'))
- table_grad: float32 [131072, 512], P(('dp', 'table'))
- norm1_gain_grad: float32 [512], replicated
- w_uvqk_grad: float32 [512, 2048], replicated
- b_uvqk_grad: float32 [2048], replicated
- norm2_gain_grad: float32 [512], replicated
- w_out_grad: float32 [512, 512], replicated
- b_out_grad: float32 [512], replicated
- pos_weight_grad: float32 [8, 10], replicated
- time_weight_grad: float32 [8, 10], replicated
- new_counts: int32 [131072], P(('dp', 'table'))
- log_q: float32 [131072], P(('dp', 'table'))
Inputs may be any that keep to these rules, and one draw needn't show every extreme that they name: `lengths`: in each table group the histories given to one dp index sum to at most 256 rows; each group has one history of 256 rows; 0 marks an unused entry. `request_rows`: the rows one device requests from one owner are distinct. `timestamps`: Non-decreasing within each device's 256 rows; both ends of the range are reached.
All inputs are finite; a program needn't handle non-finite values.
Results may differ from a plain program's by a relative error of at most 0.0079.
Values may be sent and summed in bfloat16 or wider, within the bound.
No kernel may reach another device: no remote copies, remote signals or barrier semaphores. Data moves between devices by JAX's collectives and lax.ppermute only.
A program may use at most 128 MiB of HBM per device.

v0:
```python
import jax
import jax.numpy as jnp
from jax import lax
from jax.sharding import PartitionSpec as P

EPSILON = 1e-05


def silu_slope(value):
    sig = jax.nn.sigmoid(value)
    return sig * (1.0 + value * (1.0 - sig))


def apply_rownorm(value):
    centered = value - jnp.mean(value, axis=-1, keepdims=True)
    scale = lax.rsqrt(jnp.mean(centered * centered, axis=-1, keepdims=True) + EPSILON)
    return (centered * scale, scale)


def norm_backward_pass(grad_hat, normed, scale):
    first = jnp.mean(grad_hat, axis=-1, keepdims=True)
    second = jnp.mean(grad_hat * normed, axis=-1, keepdims=True)
    return scale * (grad_hat - first - normed * second)


def pair_terms(
    segment, timestamps, pos_weight, time_weight, row_start, col_start, block, slot_rows
):
    rows = jnp.arange(block, dtype=jnp.int32) + row_start
    cols = jnp.arange(block, dtype=jnp.int32) + col_start
    dist = rows[:, None] - cols[None, :]
    delta = timestamps[:, None] - timestamps[None, :]
    mask = ((segment[:, None] == segment[None, :]) & (segment[:, None] >= 0) & (dist >= 0)).astype(
        jnp.float32
    )
    count = pos_weight.shape[1]
    near_list = []
    later_list = []
    bias = jnp.zeros((pos_weight.shape[0], block, block), jnp.float32)
    for m in range(count):
        near = (dist >= max(1, slot_rows // 2 ** (count - m))).astype(jnp.float32)
        later = (delta >= 4**m).astype(jnp.float32)
        near_list.append(near)
        later_list.append(later)
        bias = (
            bias
            + pos_weight[:, m, None, None] * near[None]
            + time_weight[:, m, None, None] * later[None]
        )
    return (mask, bias, near_list, later_list)


def on_device(
    item_table,
    token_request_slot,
    request_rows,
    lengths,
    assignment,
    timestamps,
    item_counts,
    first_norm_gain,
    w_uvqk,
    b_uvqk,
    norm2_gain,
    w_out,
    b_out,
    pos_weight,
    time_weight,
    out_grad,
):
    slot_rows = token_request_slot.shape[0]
    width = item_table.shape[1]
    rows_dev = item_table.shape[0]
    replica_count = lax.axis_size("dp")
    group_count = lax.axis_size("table")
    request_slots = request_rows.shape[2]
    piece = slot_rows // replica_count
    heads = pos_weight.shape[0]
    head_dim = width // heads
    wanted = request_rows[0].reshape(replica_count, group_count, request_slots)
    asked = lax.all_to_all(
        lax.all_to_all(wanted, "dp", split_axis=0, concat_axis=0, tiled=True),
        "table",
        split_axis=1,
        concat_axis=1,
        tiled=True,
    )
    served = jnp.take(item_table, asked.reshape(-1), axis=0).reshape(
        replica_count, group_count, request_slots, width
    )
    fetched = lax.all_to_all(
        lax.all_to_all(served, "dp", split_axis=0, concat_axis=0, tiled=True),
        "table",
        split_axis=1,
        concat_axis=1,
        tiled=True,
    ).reshape(replica_count * group_count * request_slots, width)
    home_rows = jnp.take(fetched, token_request_slot, axis=0)
    moved = lax.all_to_all(
        home_rows.reshape(replica_count, piece, width),
        "dp",
        split_axis=0,
        concat_axis=0,
        tiled=True,
    ).reshape(slot_rows, width)
    my_dp = lax.axis_index("dp")
    hist_len = lengths[0]
    hist_dest = assignment[0]
    nhist = hist_len.shape[0]
    mine_len = jnp.where(hist_dest == my_dp, hist_len, 0)
    ends = jnp.cumsum(mine_len)
    starts = ends - mine_len
    places = jnp.arange(slot_rows, dtype=jnp.int32)
    inside = (starts[None, :] <= places[:, None]) & (places[:, None] < ends[None, :])
    labels = jnp.arange(1, nhist + 1, dtype=jnp.int32)
    segment = jnp.sum(jnp.where(inside, labels[None, :], 0), axis=1) - 1
    valid = (segment >= 0).astype(jnp.float32)
    complete_input = moved.astype(jnp.float32)
    first_centered_scaled, first_inverse_deviation = apply_rownorm(complete_input)
    first_normed_batch = (first_centered_scaled * first_norm_gain).astype(jnp.bfloat16)
    pre = jnp.dot(first_normed_batch, w_uvqk, preferred_element_type=jnp.float32) + b_uvqk
    act = jax.nn.silu(pre)
    gate_u = act[:, :width]
    values = act[:, width : 2 * width].astype(jnp.bfloat16).reshape(slot_rows, heads, head_dim)
    queries = act[:, 2 * width : 3 * width].astype(jnp.bfloat16).reshape(slot_rows, heads, head_dim)
    keys = act[:, 3 * width :].astype(jnp.bfloat16).reshape(slot_rows, heads, head_dim)
    block = min(512, slot_rows)
    qi = 0
    kj = 0
    mask, bias, near_list, later_list = pair_terms(
        segment, timestamps, pos_weight, time_weight, qi * block, kj * block, block, slot_rows
    )
    scores = (
        jnp.einsum("qhd,khd->hqk", queries, keys, preferred_element_type=jnp.float32) * 0.125 + bias
    )
    weights = (jax.nn.silu(scores) * mask[None]).astype(jnp.bfloat16)
    acc = jnp.einsum("hqk,khd->qhd", weights, values, preferred_element_type=jnp.float32)
    attn = acc.reshape(slot_rows, width)
    ohat, rstd2 = apply_rownorm(attn)
    n2 = ohat * norm2_gain
    mixed_b = (n2 * gate_u).astype(jnp.bfloat16)
    branch = jnp.dot(mixed_b, w_out, preferred_element_type=jnp.float32) + b_out
    layer_out = (valid[:, None] * (complete_input + branch)).astype(jnp.bfloat16)
    output_gradient = out_grad.astype(jnp.float32) * valid[:, None]
    goutb = output_gradient.astype(jnp.bfloat16)
    w_out_grad = jnp.dot(mixed_b.T, goutb, preferred_element_type=jnp.float32)
    b_out_grad = jnp.sum(output_gradient, axis=0)
    dmixed = jnp.dot(goutb, w_out.T, preferred_element_type=jnp.float32)
    du = dmixed * n2
    dn2 = dmixed * gate_u
    gain2_grad = jnp.sum(dn2 * ohat, axis=0)
    dattn = norm_backward_pass(dn2 * norm2_gain, ohat, rstd2)
    dob = dattn.astype(jnp.bfloat16).reshape(slot_rows, heads, head_dim)
    dq_blocks = [jnp.zeros((block, heads, head_dim), jnp.float32)]
    dk_blocks = [jnp.zeros((block, heads, head_dim), jnp.float32)]
    dv_blocks = [jnp.zeros((block, heads, head_dim), jnp.float32)]
    qi = 0
    kj = 0
    mask, bias, near_list, later_list = pair_terms(
        segment, timestamps, pos_weight, time_weight, qi * block, kj * block, block, slot_rows
    )
    scores = (
        jnp.einsum("qhd,khd->hqk", queries, keys, preferred_element_type=jnp.float32) * 0.125 + bias
    )
    weights = (jax.nn.silu(scores) * mask[None]).astype(jnp.bfloat16)
    dweights = jnp.einsum("qhd,khd->hqk", dob, values, preferred_element_type=jnp.float32)
    dv_blocks[kj] = jnp.einsum("hqk,qhd->khd", weights, dob, preferred_element_type=jnp.float32)
    dscore = (dweights * mask[None] * silu_slope(scores)).astype(jnp.bfloat16)
    dq_blocks[qi] = (
        jnp.einsum("hqk,khd->qhd", dscore, keys, preferred_element_type=jnp.float32) * 0.125
    )
    dk_blocks[kj] = (
        jnp.einsum("hqk,qhd->khd", dscore, queries, preferred_element_type=jnp.float32) * 0.125
    )
    dscore_f = dscore.astype(jnp.float32)
    pos_grad = jnp.stack(
        [jnp.sum(dscore_f * near[None], axis=(1, 2)) for near in near_list], axis=1
    )
    time_grad = jnp.stack(
        [jnp.sum(dscore_f * later[None], axis=(1, 2)) for later in later_list], axis=1
    )
    dq_all = dq_blocks[0].reshape(slot_rows, width)
    dk_all = dk_blocks[0].reshape(slot_rows, width)
    dv_all = dv_blocks[0].reshape(slot_rows, width)
    dpre_b = (jnp.concatenate([du, dv_all, dq_all, dk_all], axis=1) * silu_slope(pre)).astype(
        jnp.bfloat16
    )
    w_uvqk_grad = jnp.dot(first_normed_batch.T, dpre_b, preferred_element_type=jnp.float32)
    b_uvqk_grad = jnp.sum(dpre_b.astype(jnp.float32), axis=0)
    first_norm_gradient = jnp.dot(dpre_b, w_uvqk.T, preferred_element_type=jnp.float32)
    first_gain_gradient = jnp.sum(first_norm_gradient * first_centered_scaled, axis=0)
    input_gradient_batch = (
        norm_backward_pass(
            first_norm_gradient * first_norm_gain, first_centered_scaled, first_inverse_deviation
        )
        + output_gradient
    ).astype(jnp.bfloat16)
    back = lax.all_to_all(
        input_gradient_batch.reshape(replica_count, piece, width),
        "dp",
        split_axis=0,
        concat_axis=0,
        tiled=True,
    ).reshape(slot_rows, width)
    dest_ids = jnp.arange(replica_count, dtype=jnp.int32)
    dest_totals = jnp.sum(
        jnp.where(hist_dest[None, :] == dest_ids[:, None], hist_len[None, :], 0), axis=1
    )
    home_pos = my_dp * piece + jnp.arange(piece, dtype=jnp.int32)
    home_valid = (home_pos[None, :] < dest_totals[:, None]).reshape(slot_rows).astype(jnp.bfloat16)
    request_slot_count = replica_count * group_count * request_slots
    indicator_matrix = (
        jnp.arange(request_slot_count, dtype=jnp.int32)[:, None] == token_request_slot[None, :]
    ).astype(jnp.bfloat16)
    slot_grad = jnp.dot(indicator_matrix, back, preferred_element_type=jnp.float32)
    slot_count = jnp.dot(indicator_matrix, home_valid, preferred_element_type=jnp.float32)
    got_grad, got_count = (
        lax.all_to_all(
            lax.all_to_all(
                slot_grad.reshape(replica_count, group_count, request_slots, width).astype(
                    jnp.bfloat16
                ),
                "dp",
                split_axis=0,
                concat_axis=0,
                tiled=True,
            ),
            "table",
            split_axis=1,
            concat_axis=1,
            tiled=True,
        ).astype(jnp.float32),
        lax.all_to_all(
            lax.all_to_all(
                slot_count.reshape(replica_count, group_count, request_slots).astype(jnp.bfloat16),
                "dp",
                split_axis=0,
                concat_axis=0,
                tiled=True,
            ),
            "table",
            split_axis=1,
            concat_axis=1,
            tiled=True,
        ).astype(jnp.float32),
    )
    owned_rows = asked.reshape(-1)
    table_grad = jax.ops.segment_sum(got_grad.reshape(-1, width), owned_rows, num_segments=rows_dev)
    added = jax.ops.segment_sum(got_count.reshape(-1), owned_rows, num_segments=rows_dev)
    new_counts = item_counts + added.astype(jnp.int32)
    local_total = (jnp.sum(item_counts) + jnp.sum(mine_len)).astype(jnp.float32)
    gain1_sum, w_uvqk_sum, b_uvqk_sum, gain2_sum, w_out_sum, b_out_sum, pos_sum, time_sum, total = (
        lax.psum(
            (
                first_gain_gradient,
                w_uvqk_grad,
                b_uvqk_grad,
                gain2_grad,
                w_out_grad,
                b_out_grad,
                pos_grad,
                time_grad,
                local_total,
            ),
            ("dp", "table"),
        )
    )
    item_total = float(rows_dev * replica_count * group_count)
    log_q = jnp.log(new_counts.astype(jnp.float32) + 1.0) - jnp.log(total + item_total)
    return (
        layer_out,
        table_grad,
        gain1_sum,
        w_uvqk_sum,
        b_uvqk_sum,
        gain2_sum,
        w_out_sum,
        b_out_sum,
        pos_sum,
        time_sum,
        new_counts,
        log_q,
    )


def solution(mesh):
    placed = (
        P(("dp", "table"), None),
        P(("dp", "table")),
        P(("dp", "table"), None, None),
        P("table", None),
        P("table", None),
        P(("dp", "table")),
        P(("dp", "table")),
        P(),
        P(),
        P(),
        P(),
        P(),
        P(),
        P(),
        P(),
        P(("dp", "table"), None),
    )
    return jax.shard_map(
        on_device,
        mesh=mesh,
        in_specs=placed,
        out_specs=(
            P(("dp", "table"), None),
            P(("dp", "table"), None),
            P(),
            P(),
            P(),
            P(),
            P(),
            P(),
            P(),
            P(),
            P(("dp", "table")),
            P(("dp", "table")),
        ),
        check_vma=False,
    )
```

profile of v0, /device:TPU:0, one launch (start us, length us, event | category | flops | bytes accessed | tf_op | source)
XLA Modules:
  0.0 274.0 jit_solution(3239298735418125460)
XLA Ops:
  7.2 1.5 copy.120
  8.7 8.3 %all-to-all-start = ((s32[16,2,8]{2,1,0:T(2,128)}), s32[16,2,8]{2,1,0:T(2,128)S(1)}, u32[]{:S(2)}, u32[]{:S(2)}) async-start(s32[16,2,8]{2,1,0:T(2,128)} %bitcast.2), calls=%async_computation | async-start | bytes 32768 | tf_op jit(solution)/shard_map/all_to_all | solution.py:82
  24.5 3.6 %all_to_all.50 = s32[2,1,128]{2,1,0:T(1,128)S(1)} all-to-all(s32[2,1,128]{2,1,0:T(1,128)S(1)} %reshape.786), channel_id=1, replica_groups=mesh['dp'=16,'table'=2] {'table'}, dimensions={0} | all-to-all | bytes 2048 | tf_op jit(solution)/shard_map/all_to_all | solution.py:81
  29.8 3.9 %gather_fusion = bf16[256,512]{1,0:T(8,128)(2,1)S(1)} fusion(bf16[4096,512]{1,0:T(8,128)(2,1)} %param.16, s32[1024]{0:T(1024)S(1)} %pad_clamp_fusion.1), kind=kCustom, calls=%fused_computation | custom fusion | bytes 525312 | tf_op jit(solution)/shard_map/jit(_take)/gather | solution.py:88
  34.5 5.5 %all-to-all-start.2 = ((bf16[16,2,8,512]{3,2,1,0:T(8,128)(2,1)}), bf16[16,2,8,512]{3,2,1,0:T(8,128)(2,1)S(1)}, u32[]{:S(2)}, u32[]{:S(2)}) async-start(bf16[16,2,8,512]{3,2,1,0:T(8,128)(2,1)} %broadcast_select_fusion), calls=%async_computation.2 | async-start | bytes 524288 | tf_op jit(solution)/shard_map/all_to_all | solution.py:92
  41.0 9.3 %all-to-all-done.2 = bf16[16,2,8,512]{3,2,1,0:T(8,128)(2,1)S(1)} async-done(((bf16[16,2,8,512]{3,2,1,0:T(8,128)(2,1)}), bf16[16,2,8,512]{3,2,1,0:T(8,128)(2,1)S(1)}, u32[]{:S(2)}, u32[]{:S(2)}) %all-to-all-start.2) | async-done | bytes 262176 | tf_op jit(solution)/shard_map/all_to_all | solution.py:92
  50.3 3.9 %all_to_all.51 = bf16[16,2,8,512]{3,2,0,1:T(8,128)(2,1)S(1)} all-to-all(bf16[16,2,8,512]{3,2,0,1:T(8,128)(2,1)S(1)} %copy.124), channel_id=1, replica_groups=mesh['dp'=16,'table'=2] {'table'}, dimensions={1} | all-to-all | bytes 524288 | tf_op jit(solution)/shard_map/all_to_all | solution.py:91
  56.3 3.7 %all-to-all-start.4 = ((bf16[16,16,512]{2,1,0:T(8,128)(2,1)}), bf16[16,16,512]{2,1,0:T(8,128)(2,1)S(1)}, u32[]{:S(2)}, u32[]{:S(2)}) async-start(bf16[16,16,512]{2,1,0:T(8,128)(2,1)} %broadcast_select_fusion.1), calls=%async_computation.4 | async-start | bytes 524288 | tf_op jit(solution)/shard_map/all_to_all | solution.py:99
  60.3 1.9 fusion.53
  62.1 8.2 %all-to-all-done.4 = bf16[16,16,512]{2,1,0:T(8,128)(2,1)S(1)} async-done(((bf16[16,16,512]{2,1,0:T(8,128)(2,1)}), bf16[16,16,512]{2,1,0:T(8,128)(2,1)S(1)}, u32[]{:S(2)}, u32[]{:S(2)}) %all-to-all-start.4) | async-done | bytes 262176 | tf_op jit(solution)/shard_map/all_to_all | solution.py:99
  71.1 2.9 %fusion.80 = (bf16[256,2048]{1,0:T(8,128)(2,1)S(1)}, f32[256,2048]{1,0:T(8,128)}, f32[256,2048]{1,0:T(8,128)}) fusion(f32[2048]{0:T(1024)S(1)} %copy-done.25, bf16[256,512]{1,0:T(8,128)(2,1)S(1)} %multiply_convert_fusion.4, bf16[512,2048]{1,0:T(8,128)(2,1)S(1)} %copy-done), kind=kOutput, calls=%fused_computation.193 | convolution fusion | flops 540016640 | bytes 7610368 | tf_op jit(solution)/shard_map/dot_general | solution.py:121
  75.2 7.6 %multiply_convert_fusion.1 = (bf16[8,256,256]{2,1,0:T(8,128)(2,1)S(1)}, f32[8,256,256]{2,1,0:T(8,128)}) fusion(f32[256,256]{1,0:T(8,128)} %fusion.52, f32[256,256]{1,0:T(8,128)} %get-tuple-element.162, f32[8]{0:T(128)S(1)} %get-tuple-element.126, f32[256,256]{1,0:T(8,128)} %get-tuple-element.177, f32[8]{0:T(128)S(1)} %get-tuple-element.116, ...), kind=kOutput, calls=%fused_computation.47 | convolution fusion | flops 91750400 | bytes 8651392 | tf_op jit(solution)/shard_map/qhd,khd->hqk/dot_general | solution.py:134
  84.0 2.6 multiply_reduce_fusion
  88.7 1.5 fusion.84
  90.2 7.4 %fusion.19 = (f32[8]{0:T(128)S(1)}, f32[8]{0:T(128)}, f32[8]{0:T(128)}, f32[8]{0:T(128)}, f32[8]{0:T(128)}, /*index=5*/f32[8]{0:T(128)}, f32[8]{0:T(128)}, f32[8...) fusion(f32[256,256]{1,0:T(8,128)} %get-tuple-element.162, ...), kind=kOutput, calls=%fused_computation.42 | convolution fusion | flops 91750256 | bytes 8651328 | tf_op jit(solution)/shard_map/qhd,khd->hqk/dot_general | solution.py:166
  101.2 2.0 copy.134
  103.2 3.0 %convert_reduce_fusion = (f32[2048]{0:T(1024)S(1)}, bf16[256,2048]{1,0:T(8,128)(2,1)S(1)}) fusion(f32[256,2048]{1,0:T(8,128)} %get-tuple-element.163, f32[256,512]{1,0:T(8,128)} %copy.134, f32[256,512]{1,0:T(8,128)} %copy.133, f32[256,512]{1,0:T(8,128)} %copy.132, f32[256,512]{1,0:T(8,128)} %get-tuple-element.147), kind=kLoop, calls=%fused_computation.45 | loop fusion | flops 7337984 | bytes 5251072 | tf_op jit(solution)/shard_map/reduce_sum | solution.py:189
  106.2 2.7 %fusion.85 = f32[512,2048]{1,0:T(8,128)} fusion(bf16[256,512]{1,0:T(8,128)(2,1)S(1)} %copy-done.5, bf16[256,2048]{1,0:T(8,128)(2,1)S(1)} %get-tuple-element.140), kind=kOutput, calls=%fused_computation.197 | convolution fusion | flops 536870912 | bytes 5505024 | tf_op jit(solution)/shard_map/dot_general | solution.py:188
  112.1 3.5 %all-to-all-start.8 = ((bf16[16,2,8]{2,1,0:T(2,128)(2,1)}), bf16[16,2,8]{2,1,0:T(2,128)(2,1)S(1)}, u32[]{:S(2)}, u32[]{:S(2)}) async-start(bf16[16,2,8]{2,1,0:T(2,128)(2,1)} %convert_element_type.288), calls=%async_computation.8 | async-start | bytes 16384 | tf_op jit(solution)/shard_map/all_to_all | solution.py:234
  117.6 5.3 %all-to-all-done.8 = bf16[16,2,8]{2,1,0:T(2,128)(2,1)S(1)} async-done(((bf16[16,2,8]{2,1,0:T(2,128)(2,1)}), bf16[16,2,8]{2,1,0:T(2,128)(2,1)S(1)}, u32[]{:S(2)}, u32[]{:S(2)}) %all-to-all-start.8) | async-done | bytes 544 | tf_op jit(solution)/shard_map/all_to_all | solution.py:234
  122.9 3.5 %all-to-all-start.5 = ((bf16[16,16,512]{2,1,0:T(8,128)(2,1)}), bf16[16,16,512]{2,1,0:T(8,128)(2,1)S(1)}, u32[]{:S(2)}, u32[]{:S(2)}) async-start(bf16[16,16,512]{2,1,0:T(8,128)(2,1)} %bitcast.20), calls=%async_computation.5 | async-start | bytes 524288 | tf_op jit(solution)/shard_map/all_to_all | solution.py:198
  127.1 13.1 %all-to-all-done.5 = bf16[16,16,512]{2,1,0:T(8,128)(2,1)S(1)} async-done(((bf16[16,16,512]{2,1,0:T(8,128)(2,1)}), bf16[16,16,512]{2,1,0:T(8,128)(2,1)S(1)}, u32[]{:S(2)}, u32[]{:S(2)}) %all-to-all-start.5) | async-done | bytes 262176 | tf_op jit(solution)/shard_map/all_to_all | solution.py:198
  140.2 3.2 %all-to-all-start.9 = ((bf16[16,2,8]{0,2,1:T(8,128)(2,1)}), bf16[16,2,8]{0,2,1:T(8,128)(2,1)S(1)}, u32[]{:S(2)}, u32[]{:S(2)}) async-start(bf16[16,2,8]{0,2,1:T(8,128)(2,1)} %copy.137), calls=%async_computation.9 | async-start | bytes 8192 | tf_op jit(solution)/shard_map/all_to_all | solution.py:233
  144.8 3.5 %all-to-all-start.6 = ((bf16[16,2,8,512]{3,2,1,0:T(8,128)(2,1)}), bf16[16,2,8,512]{3,2,1,0:T(8,128)(2,1)S(1)}, u32[]{:S(2)}, u32[]{:S(2)}) async-start(bf16[16,2,8,512]{3,2,1,0:T(8,128)(2,1)} %convolution_convert_fusion), calls=%async_computation.6 | async-start | bytes 524288 | tf_op jit(solution)/shard_map/all_to_all | solution.py:219
  151.2 1.9 scatter_custom_fusion.1
  153.1 1.4 stack.70
  155.8 41.7 %all-reduce = (f32[512]{0:T(512)}, f32[2048]{0:T(1024)}, f32[512]{0:T(512)}, f32[512]{0:T(512)}, f32[8,10]{0,1:T(8,128)S(1)}, /*index=5*/f32[8,10]{0,1:T(8,128)S(1)}, f32[]{:T(128)}) all-reduce(f32[512]{0:T(512)S(1)} %get-tuple-element.104, f32[2048]{0:T(1024)S(1)} %get-tuple-element.139, ...), channel_id=1, replica_groups=mesh['dp'=16,'table'=2] {'dp','table'}, use_global_device_ids=true, to_apply=%region_12.13 | all-reduce | flops 3745 | bytes 29960 | tf_op jit(solution)/shard_map/psum | solution.py:253
  200.1 1.7 fusion.24
  201.8 3.9 %all_to_all.52 = bf16[16,2,8,512]{3,2,0,1:T(8,128)(2,1)S(1)} all-to-all(bf16[16,2,8,512]{3,2,0,1:T(8,128)(2,1)S(1)} %copy.135), channel_id=1, replica_groups=mesh['dp'=16,'table'=2] {'table'}, dimensions={1} | all-to-all | bytes 524288 | tf_op jit(solution)/shard_map/all_to_all | solution.py:218
  205.8 6.0 %scatter_custom_fusion = f32[4096,512]{1,0:T(8,128)} fusion(s32[256]{0:T(256)S(1)} %reshape.739, f32[]{:T(128)} %constant.48.clone.1, bf16[256,512]{1,0:T(8,128)(2,1)S(1)} %bitcast.123), kind=kCustom, calls=%fused_computation.22 | custom fusion | flops 262144 | bytes 8650756 | tf_op jit(solution)/shard_map/scatter-add | solution.py:248
  211.8 49.5 %all-reduce.4.cloned.1.call-done = (f32[512,2048]{1,0:T(8,128)}, f32[512,512]{1,0:T(8,128)}) async-done(((f32[512,2048]{1,0:T(8,128)}, f32[512,512]{1,0:T(8,128)}), (f32[512,2048]{1,0:T(8,128)}, f32[512,512]{1,0:T(8,128)})) %all-reduce.4.cloned.1.call-update) | async-done | bytes 5242896 | tf_op jit(solution)/shard_map/psum | solution.py:253
  261.4 4.8 %copy.146 = f32[512,2048]{1,0:T(8,128)} copy(f32[512,2048]{1,0:T(8,128)} %get-tuple-element.181) | data formatting | bytes 8388608
  (143 shorter events, 34.4 us)
Async XLA Ops:
  7.2 63.9 %copy-start = (bf16[512,2048]{1,0:T(8,128)(2,1)S(1)}, bf16[512,2048]{1,0:T(8,128)(2,1)}, u32[]{:S(2)}) copy-start(bf16[512,2048]{1,0:T(8,128)(2,1)} %param.24) | copy-start | bytes 6291460
  7.2 14.6 %copy-start.21 = (s32[1,64]{1,0:T(1,128)S(1)}, s32[1,64]{1,0:T(1,128)}, u32[]{:S(2)}) copy-start(s32[1,64]{1,0:T(1,128)} %param.19) | copy-start | bytes 772
  7.2 14.6 %copy-start.22 = (s32[1,64]{1,0:T(1,128)S(1)}, s32[1,64]{1,0:T(1,128)}, u32[]{:S(2)}) copy-start(s32[1,64]{1,0:T(1,128)} %param.20) | copy-start | bytes 772
  7.2 15.0 %copy-start.16 = (f32[8,10]{1,0:T(8,128)S(1)}, f32[8,10]{1,0:T(8,128)}, u32[]{:S(2)}) copy-start(f32[8,10]{1,0:T(8,128)} %param.29) | copy-start | bytes 964
  7.2 15.3 %copy-start.17 = (f32[8,10]{1,0:T(8,128)S(1)}, f32[8,10]{1,0:T(8,128)}, u32[]{:S(2)}) copy-start(f32[8,10]{1,0:T(8,128)} %param.30) | copy-start | bytes 964
  8.7 15.7 %all-to-all-start = ((s32[16,2,8]{2,1,0:T(2,128)}), s32[16,2,8]{2,1,0:T(2,128)S(1)}, u32[]{:S(2)}, u32[]{:S(2)}) async-start(s32[16,2,8]{2,1,0:T(2,128)} %bitcast.2), calls=%async_computation | async-start | bytes 32768 | tf_op jit(solution)/shard_map/all_to_all | solution.py:82
  34.5 15.8 %all-to-all-start.2 = ((bf16[16,2,8,512]{3,2,1,0:T(8,128)(2,1)}), bf16[16,2,8,512]{3,2,1,0:T(8,128)(2,1)S(1)}, u32[]{:S(2)}, u32[]{:S(2)}) async-start(bf16[16,2,8,512]{3,2,1,0:T(8,128)(2,1)} %broadcast_select_fusion), calls=%async_computation.2 | async-start | bytes 524288 | tf_op jit(solution)/shard_map/all_to_all | solution.py:92
  54.3 6.0 %copy-start.23 = (s32[256]{0:T(256)S(1)}, s32[256]{0:T(256)}, u32[]{:S(2)}) copy-start(s32[256]{0:T(256)} %param.21) | copy-start | bytes 3076
  55.5 15.4 %copy-start.19 = (f32[512]{0:T(512)S(1)}, f32[512]{0:T(512)}, u32[]{:S(2)}) copy-start(f32[512]{0:T(512)} %param.23) | copy-start | bytes 6148
  56.3 14.8 %copy-start.25 = (f32[2048]{0:T(1024)S(1)}, f32[2048]{0:T(1024)}, u32[]{:S(2)}) copy-start(f32[2048]{0:T(1024)} %param.25) | copy-start | bytes 24580
  56.3 14.1 %all-to-all-start.4 = ((bf16[16,16,512]{2,1,0:T(8,128)(2,1)}), bf16[16,16,512]{2,1,0:T(8,128)(2,1)S(1)}, u32[]{:S(2)}, u32[]{:S(2)}) async-start(bf16[16,16,512]{2,1,0:T(8,128)(2,1)} %broadcast_select_fusion.1), calls=%async_computation.4 | async-start | bytes 524288 | tf_op jit(solution)/shard_map/all_to_all | solution.py:99
  60.0 201.4 %all-reduce.4.cloned.1.call-start = ((), (), s32[]{:S(2)}) async-start(), calls=%async_computation.10 | async-start | bytes 10485760 | tf_op jit(solution)/shard_map/psum | solution.py:253
  71.0 2.9 %copy-start.4 = (bf16[256,512]{1,0:T(8,128)(2,1)}, bf16[256,512]{1,0:T(8,128)(2,1)S(1)}, u32[]{:S(2)}) copy-start(bf16[256,512]{1,0:T(8,128)(2,1)S(1)} %multiply_convert_fusion.4) | copy-start | bytes 786436
  74.1 8.7 %copy-start.6 = (bf16[256,512]{0,1:T(8,128)(2,1)}, bf16[256,512]{0,1:T(8,128)(2,1)S(1)}, u32[]{:S(2)}) copy-start(bf16[256,512]{0,1:T(8,128)(2,1)S(1)} %copy.128) | copy-start | bytes 786436
  74.3 8.5 %copy-start.8 = (bf16[256,512]{0,1:T(8,128)(2,1)}, bf16[256,512]{0,1:T(8,128)(2,1)S(1)}, u32[]{:S(2)}) copy-start(bf16[256,512]{0,1:T(8,128)(2,1)S(1)} %copy.127) | copy-start | bytes 786436
  75.1 7.7 %copy-start.10 = (bf16[256,512]{0,1:T(8,128)(2,1)S(1)}, bf16[256,512]{0,1:T(8,128)(2,1)}, u32[]{:S(2)}) copy-start(bf16[256,512]{0,1:T(8,128)(2,1)} %copy.126) | copy-start | bytes 786436
  82.8 1.2 copy-start.20
  86.6 3.6 %copy-start.11 = (bf16[256,512]{0,1:T(8,128)(2,1)S(1)}, bf16[256,512]{0,1:T(8,128)(2,1)}, u32[]{:S(2)}) copy-start(bf16[256,512]{0,1:T(8,128)(2,1)} %copy.126) | copy-start | bytes 786436
  90.2 7.4 %copy-start.7 = (bf16[256,512]{0,1:T(8,128)(2,1)S(1)}, bf16[256,512]{0,1:T(8,128)(2,1)}, u32[]{:S(2)}) copy-start(bf16[256,512]{0,1:T(8,128)(2,1)} %copy-done.6) | copy-start | bytes 786436
  90.2 7.9 %copy-start.9 = (bf16[256,512]{0,1:T(8,128)(2,1)S(1)}, bf16[256,512]{0,1:T(8,128)(2,1)}, u32[]{:S(2)}) copy-start(bf16[256,512]{0,1:T(8,128)(2,1)} %copy-done.8) | copy-start | bytes 786436
  103.2 3.0 %copy-start.5 = (bf16[256,512]{1,0:T(8,128)(2,1)S(1)}, bf16[256,512]{1,0:T(8,128)(2,1)}, u32[]{:S(2)}) copy-start(bf16[256,512]{1,0:T(8,128)(2,1)} %copy-done.4) | copy-start | bytes 786436
  106.2 2.8 %copy-start.2 = (bf16[256,512]{1,0:T(8,128)(2,1)S(1)}, bf16[256,512]{1,0:T(8,128)(2,1)}, u32[]{:S(2)}) copy-start(bf16[256,512]{1,0:T(8,128)(2,1)} %param.31) | copy-start | bytes 786436
  106.2 2.8 %copy-start.13 = (bf16[256,512]{1,0:T(8,128)(2,1)S(1)}, bf16[256,512]{1,0:T(8,128)(2,1)}, u32[]{:S(2)}) copy-start(bf16[256,512]{1,0:T(8,128)(2,1)} %get-tuple-element.146) | copy-start | bytes 786436
  112.1 10.8 %all-to-all-start.8 = ((bf16[16,2,8]{2,1,0:T(2,128)(2,1)}), bf16[16,2,8]{2,1,0:T(2,128)(2,1)S(1)}, u32[]{:S(2)}, u32[]{:S(2)}) async-start(bf16[16,2,8]{2,1,0:T(2,128)(2,1)} %convert_element_type.288), calls=%async_computation.8 | async-start | bytes 16384 | tf_op jit(solution)/shard_map/all_to_all | solution.py:234
  115.6 1.0 copy-start.3
  116.5 32.4 %copy-start.18 = (s32[4096]{0:T(1024)S(1)}, s32[4096]{0:T(1024)}, u32[]{:S(2)}) copy-start(s32[4096]{0:T(1024)} %param.22) | copy-start | bytes 49156
  116.5 83.6 %copy-start.14 = (bf16[256,512]{1,0:T(8,128)(2,1)S(1)}, bf16[256,512]{1,0:T(8,128)(2,1)}, u32[]{:S(2)}) copy-start(bf16[256,512]{1,0:T(8,128)(2,1)} %get-tuple-element.146) | copy-start | bytes 786436
  116.5 83.6 %copy-start.15 = (bf16[512,512]{1,0:T(8,128)(2,1)S(1)}, bf16[512,512]{1,0:T(8,128)(2,1)}, u32[]{:S(2)}) copy-start(bf16[512,512]{1,0:T(8,128)(2,1)} %param.27) | copy-start | bytes 1572868
  122.9 17.3 %all-to-all-start.5 = ((bf16[16,16,512]{2,1,0:T(8,128)(2,1)}), bf16[16,16,512]{2,1,0:T(8,128)(2,1)S(1)}, u32[]{:S(2)}, u32[]{:S(2)}) async-start(bf16[16,16,512]{2,1,0:T(8,128)(2,1)} %bitcast.20), calls=%async_computation.5 | async-start | bytes 524288 | tf_op jit(solution)/shard_map/all_to_all | solution.py:198
  140.2 4.6 %all-to-all-start.9 = ((bf16[16,2,8]{0,2,1:T(8,128)(2,1)}), bf16[16,2,8]{0,2,1:T(8,128)(2,1)S(1)}, u32[]{:S(2)}, u32[]{:S(2)}) async-start(bf16[16,2,8]{0,2,1:T(8,128)(2,1)} %copy.137), calls=%async_computation.9 | async-start | bytes 8192 | tf_op jit(solution)/shard_map/all_to_all | solution.py:233
  144.8 57.1 %all-to-all-start.6 = ((bf16[16,2,8,512]{3,2,1,0:T(8,128)(2,1)}), bf16[16,2,8,512]{3,2,1,0:T(8,128)(2,1)S(1)}, u32[]{:S(2)}, u32[]{:S(2)}) async-start(bf16[16,2,8,512]{3,2,1,0:T(8,128)(2,1)} %convolution_convert_fusion), calls=%async_computation.6 | async-start | bytes 524288 | tf_op jit(solution)/shard_map/all_to_all | solution.py:219
  261.4 4.8 %copy-start.12 = (f32[512,512]{1,0:T(8,128)S(1)}, f32[512,512]{1,0:T(8,128)}, u32[]{:S(2)}) copy-start(f32[512,512]{1,0:T(8,128)} %get-tuple-element.184) | copy-start | bytes 3145732
  (2 other events, 1.7 us)
Sparse Core Ops, SparseCore 0:
  110.5 150.8 all-reduce.3
where the time goes:
time: 275 us; the launch traced here: 274 us
  waiting for transfers between devices  87.2 us (32%)
  blocking collectives  53.2 us (19%)
  matrix products  32.2 us (12%)
  starting transfers between devices  31.5 us (11%)
  local copies, waits for them, and re-layouts  26.9 us (10%)
  other arithmetic  26.2 us (10%)
  between operations  16.6 us (6%)
    psum x1, waiting for transfers between devices, on_device(): lax.psum((first_gain_gradient, w_uvqk_grad, b_uvqk_grad, gain2_grad, w_ou...  49.5 us
    psum x1, blocking collectives, on_device(): lax.psum((first_gain_gradient, w_uvqk_grad, b_uvqk_grad, gain2_grad, w_ou...  41.7 us
    all_to_all x1, waiting for transfers between devices, on_device(): lax.all_to_all(input_gradient_batch.reshape(replica_count, piece, width),...  13.1 us
    unnamed x59, local copies, waits for them, and re-layouts  9.78 us
    all_to_all x1, waiting for transfers between devices, on_device(): lax.all_to_all(served, 'dp', split_axis=0, concat_axis=0, tiled=True)  9.27 us
    all_to_all x1, starting transfers between devices, on_device(): lax.all_to_all(wanted, 'dp', split_axis=0, concat_axis=0, tiled=True)  8.31 us
    all_to_all x1, waiting for transfers between devices, on_device(): lax.all_to_all(home_rows.reshape(replica_count, piece, width), 'dp', spli...  8.23 us
    dot_general x1, matrix products, on_device(): jnp.einsum('qhd,khd->hqk', queries, keys, preferred_element_type=jnp.floa...  7.65 us
  transfers between devices with their start and end apart: 8, of which 7 were waited for; matrix products, arithmetic and copies ran while one was open for 11% of the time, Pallas kernels for 0%

commit v1 on v0

v1 whole, which is shorter than its diff:
```python
import functools

import jax
import jax.numpy as jnp
from jax import lax
from jax.experimental import pallas as pl
from jax.experimental.pallas import tpu as pltpu
from jax.sharding import PartitionSpec as P

EPSILON = 1e-05
MASKED = -1e30
F32 = jnp.float32
BF16 = jnp.bfloat16
I32 = jnp.int32
BOTH = ("dp", "table")
LANES = 128
VMEM = pl.BlockSpec(memory_space=pltpu.VMEM)
SMEM = pl.BlockSpec(memory_space=pltpu.SMEM)
PARAMS = pltpu.CompilerParams(vmem_limit_bytes=48 * 1024 * 1024)


def dot_nn(a, b):
    return lax.dot_general(a, b, (((1,), (0,)), ((), ())), preferred_element_type=F32)


def dot_nt(a, b):
    return lax.dot_general(a, b, (((1,), (1,)), ((), ())), preferred_element_type=F32)


def dot_tn(a, b):
    return lax.dot_general(a, b, (((0,), (0,)), ((), ())), preferred_element_type=F32)


def dot_exact(a, b):
    return lax.dot_general(
        a, b, (((1,), (0,)), ((), ())), precision=lax.Precision.HIGHEST, preferred_element_type=F32
    )


def iota(shape, dim):
    return lax.broadcasted_iota(I32, shape, dim)


def shape_of(shape, dtype):
    return jax.ShapeDtypeStruct(shape, dtype)


def cost(flops, moved):
    return pl.CostEstimate(flops=int(flops), bytes_accessed=int(moved), transcendentals=0)


def call(body, outs, specs, flops, moved, scratch=()):
    many = isinstance(outs, tuple)
    return pl.pallas_call(
        body,
        out_shape=outs,
        in_specs=specs,
        out_specs=tuple(VMEM for _ in outs) if many else VMEM,
        scratch_shapes=list(scratch),
        compiler_params=PARAMS,
        cost_estimate=cost(flops, moved),
    )


def request_kernel(piece, cap, rows_ref, slot_ref, len_ref, dest_ref, counts_ref, msg_ref):
    owners = rows_ref.shape[0]
    tokens = slot_ref.shape[1]
    replicas = tokens // piece
    my_dp = lax.axis_index("dp")
    lens = len_ref[...].astype(F32)
    takes = dest_ref[...] == iota((replicas, dest_ref.shape[1]), 0)
    totals = jnp.sum(jnp.where(takes, lens, 0.0), axis=1, keepdims=True)
    token = iota((replicas, tokens), 1)
    target = iota((replicas, tokens), 0)
    place = (my_dp * piece + token - target * piece).astype(F32)
    here = (token >= target * piece) & (token < (target + 1) * piece) & (place < totals)
    valid = jnp.sum(jnp.where(here, 1.0, 0.0), axis=0, keepdims=True)
    slot = slot_ref[...]
    by_owner = jnp.where(slot // cap == iota((owners, tokens), 0), valid, 0.0).astype(BF16)
    by_slot = jnp.where(slot % cap + cap == iota((LANES, tokens), 0), 1.0, 0.0).astype(BF16)
    counts = dot_nt(by_owner, by_slot)
    old = jnp.sum(counts_ref[...].astype(F32), axis=0, keepdims=True)
    total = jnp.sum(old, axis=1, keepdims=True) + jnp.sum(valid, axis=1, keepdims=True)
    lane = iota((owners, LANES), 1)
    msg_ref[...] = jnp.where(lane == 2 * cap, total, counts).astype(I32)
    msg_ref[:, 0:cap] = rows_ref[...]


def asked_column(cap, asked_ref, first):
    askers = asked_ref.shape[0]
    total = askers * cap
    spread = jnp.where(iota((total, askers), 0) // cap == iota((total, askers), 1), 1.0, 0.0)
    each = dot_exact(spread, asked_ref[...].astype(F32))
    pick = iota((total, LANES), 1) == iota((total, LANES), 0) % cap + first
    return jnp.sum(jnp.where(pick, each, 0.0), axis=1, keepdims=True)


def serve_kernel(cap, asked_ref, table_ref, served_ref):
    rows = asked_column(cap, asked_ref, 0)
    total = rows.shape[0]
    step = min(512, table_ref.shape[0])
    lane = iota((total, step), 1).astype(F32)
    acc = None
    for base in range(0, table_ref.shape[0], step):
        pick = jnp.where(rows - float(base) == lane, 1.0, 0.0).astype(BF16)
        part = dot_nn(pick, table_ref[base : base + step, :])
        acc = part if acc is None else acc + part
    served_ref[...] = acc.astype(BF16)


def counts_kernel(cap, items, asked_ref, counts_ref, new_ref, log_ref, row_ref):
    rows = asked_column(cap, asked_ref, 0)
    added = asked_column(cap, asked_ref, cap)
    total = rows.shape[0]
    lines = counts_ref.shape[0]
    line = jnp.floor(rows * (1.0 / LANES))
    lane = rows - line * LANES
    by_line = jnp.where(line == iota((total, lines), 1).astype(F32), added, 0.0).astype(BF16)
    by_lane = jnp.where(lane == iota((total, LANES), 1).astype(F32), 1.0, 0.0).astype(BF16)
    new = counts_ref[...].astype(F32) + dot_tn(by_line, by_lane)
    whole = jnp.sum(asked_ref[:, 2 * cap : 2 * cap + 1].astype(F32), axis=0, keepdims=True)
    new_ref[...] = new.astype(I32)
    log_ref[...] = jnp.log(new + 1.0) - jnp.log(whole + float(items))
    row_ref[...] = jnp.transpose(jnp.broadcast_to(rows, (total, LANES)))[0:8, :]


def take_kernel(slot_ref, fetched_ref, home_ref):
    total = fetched_ref.shape[0]
    pick = jnp.where(slot_ref[...] == iota((total, slot_ref.shape[1]), 0), 1.0, 0.0).astype(BF16)
    home_ref[...] = dot_tn(pick, fetched_ref[...]).astype(BF16)


def slot_sum_kernel(slot_ref, back_ref, sums_ref):
    total = sums_ref.shape[0]
    pick = jnp.where(slot_ref[...] == iota((total, slot_ref.shape[1]), 0), 1.0, 0.0).astype(BF16)
    sums_ref[...] = dot_nn(pick, back_ref[...]).astype(BF16)


def scatter_kernel(row_ref, got_ref, out_ref):
    block = out_ref.shape[0]
    total = got_ref.shape[0]
    here = row_ref[0:1, :] - (pl.program_id(0) * block).astype(F32)
    pick = jnp.where(here == iota((block, total), 0).astype(F32), 1.0, 0.0).astype(BF16)
    out_ref[...] = dot_nn(pick, got_ref[...])


def before_kernel(
    len_ref, dest_ref, time_ref, og_ref, wo_ref, pos_ref, timew_ref, bias_ref, go_ref, dmix_ref, valid_ref
):
    rows = time_ref.shape[1]
    heads, count = pos_ref.shape
    nhist = len_ref.shape[1]
    my_dp = lax.axis_index("dp")
    mine = jnp.where(dest_ref[...] == my_dp, len_ref[...], 0).astype(F32)
    later = iota((nhist, nhist), 0)
    other = iota((nhist, nhist), 1)
    ends = jnp.sum(jnp.where(other <= later, mine, 0.0), axis=1, keepdims=True)
    starts = jnp.sum(jnp.where(other < later, mine, 0.0), axis=1, keepdims=True)
    place = iota((nhist, rows), 1).astype(F32)
    label = iota((nhist, rows), 0).astype(F32) + 1.0
    inside = (starts <= place) & (place < ends)
    seg = jnp.sum(jnp.where(inside, label, 0.0), axis=0, keepdims=True) - 1.0
    seg_across = jnp.broadcast_to(seg, (rows, rows))
    seg_down = jnp.transpose(seg_across)
    stamp = jnp.broadcast_to(time_ref[...].astype(F32), (rows, rows))
    delta = jnp.transpose(stamp) - stamp
    dist = iota((rows, rows), 0) - iota((rows, rows), 1)
    mask = (seg_across == seg_down) & (seg_down >= 0.0) & (dist >= 0)
    valid = jnp.where(seg_down[:, 0:LANES] >= 0.0, 1.0, 0.0)
    valid_ref[...] = valid
    wide = og_ref.shape[1] // LANES
    go = og_ref[...].astype(F32) * jnp.concatenate([valid] * wide, axis=1)
    gob = go.astype(BF16)
    go_ref[...] = gob
    dmix_ref[...] = dot_nt(gob, wo_ref[...])
    for g in range(heads):
        bias = jnp.zeros((rows, rows), F32)
        for m in range(count):
            bias = bias + jnp.where(dist >= max(1, rows // 2 ** (count - m)), pos_ref[g, m], 0.0)
            bias = bias + jnp.where(delta >= float(4**m), timew_ref[g, m], 0.0)
        bias_ref[g] = jnp.where(mask, bias, MASKED)


def norm_of(value):
    centered = value - jnp.mean(value, axis=1, keepdims=True)
    scale = lax.rsqrt(jnp.mean(centered * centered, axis=1, keepdims=True) + EPSILON)
    return centered * scale, scale


def norm_back(grad_hat, normed, scale):
    first = jnp.mean(grad_hat, axis=1, keepdims=True)
    second = jnp.mean(grad_hat * normed, axis=1, keepdims=True)
    return scale * (grad_hat - first - normed * second)


def sigmoid(value):
    return 1.0 / (1.0 + jnp.exp(-value))


def layer_kernel(
    staged,
    x_ref,
    w_ref,
    b_ref,
    g1_ref,
    g2_ref,
    wo_ref,
    bo_ref,
    bias_ref,
    dmix_ref,
    valid_ref,
    lo_ref,
    n1_ref,
    y_ref,
    dh_ref,
    ds_ref,
    g2g_ref,
    msg_ref,
    h_ref,
    slope_ref,
    a_ref,
):
    rows, width = x_ref.shape
    heads = bias_ref.shape[0]
    pairs = heads // 2
    x = x_ref[...].astype(F32)
    xhat, _ = norm_of(x)
    n1 = (xhat * g1_ref[...]).astype(BF16)
    n1_ref[...] = n1
    acts = []
    for part in range(4):
        cols = slice(part * width, (part + 1) * width)
        h = dot_nn(n1, w_ref[:, cols]) + b_ref[:, cols]
        sig = sigmoid(h)
        acts.append(h * sig)
        h_ref[:, cols] = sig * (1.0 + h * (1.0 - sig))
    u = acts[0]
    v, q, k = (a.astype(BF16) for a in acts[1:])
    lane = iota((rows, LANES), 1)
    low = lane < LANES // 2
    zero = jnp.zeros((rows, LANES), BF16)

    def half(value, parity):
        return jnp.where(low if parity == 0 else ~low, value, zero)

    outs = []
    for pair in range(pairs):
        cols = slice(pair * LANES, (pair + 1) * LANES)
        total = None
        for parity in range(2):
            g = pair * 2 + parity
            s = dot_nt(half(q[:, cols], parity), k[:, cols]) * 0.125 + bias_ref[g]
            sig = sigmoid(s)
            a = (s * sig).astype(BF16)
            a_ref[g] = a
            slope_ref[g] = sig * (1.0 + s * (1.0 - sig))
            part = dot_nn(a, half(v[:, cols], parity))
            total = part if total is None else total + part
        outs.append(total)
    o = jnp.concatenate(outs, axis=1)
    ohat, scale2 = norm_of(o)
    g2 = g2_ref[...]
    n2 = ohat * g2
    y = (n2 * u).astype(BF16)
    y_ref[...] = y
    branch = dot_nn(y, wo_ref[...]) + bo_ref[...]
    valid = valid_ref[...]
    lo_ref[...] = (jnp.concatenate([valid] * (width // LANES), axis=1) * (x + branch)).astype(BF16)
    dmix = dmix_ref[...]
    du = dmix * n2
    e2 = dmix * u
    g2g_ref[...] = jnp.sum(e2 * ohat, axis=0, keepdims=True)
    do = norm_back(e2 * g2, ohat, scale2).astype(BF16)
    dh_ref[:, 0:width] = (du * h_ref[:, 0:width]).astype(BF16)
    for pair in range(pairs):
        cols = slice(pair * LANES, (pair + 1) * LANES)
        dv, dq, dk = None, None, None
        for parity in range(2):
            g = pair * 2 + parity
            dom = half(do[:, cols], parity)
            da = dot_nt(dom, v[:, cols])
            ds = (da * slope_ref[g]).astype(BF16)
            ds_ref[g] = ds
            parts = (
                dot_tn(a_ref[g], dom),
                dot_nn(ds, half(k[:, cols], parity)),
                dot_tn(ds, half(q[:, cols], parity)),
            )
            if parity == 0:
                dv, dq, dk = parts
            else:
                dv, dq, dk = dv + parts[0], dq + parts[1], dk + parts[2]
        for part, value in ((1, dv), (2, dq * 0.125), (3, dk * 0.125)):
            at = slice(part * width + pair * LANES, part * width + (pair + 1) * LANES)
            dh_ref[:, at] = (value * h_ref[:, at]).astype(BF16)
    if staged:
        other = 1 - lax.axis_index("table")
        half_cols = 2 * width
        msg_ref[:, 0:half_cols] = dh_ref[:, pl.ds(pl.multiple_of(other * half_cols, half_cols), half_cols)]
        msg_ref[:, half_cols : half_cols + width] = n1
        half_y = width // 2
        msg_ref[:, half_cols + width :] = y_ref[:, pl.ds(pl.multiple_of(other * half_y, half_y), half_y)]
    else:
        msg_ref[...] = jnp.zeros_like(msg_ref)


def dx_kernel(dh_ref, w_ref, x_ref, g1_ref, go_ref, dx_ref, g1g_ref):
    xhat, scale = norm_of(x_ref[...].astype(F32))
    dn1 = dot_nt(dh_ref[...], w_ref[...])
    g1g_ref[...] = jnp.sum(dn1 * xhat, axis=0, keepdims=True)
    dx = norm_back(dn1 * g1_ref[...], xhat, scale) + go_ref[...].astype(F32)
    dx_ref[...] = dx.astype(BF16)


SMALL_ROWS = 48


def small_kernel(count, ds_ref, time_ref, dh_ref, go_ref, g1g_ref, g2g_ref, out_ref):
    heads, rows, _ = ds_ref.shape
    width = go_ref.shape[1]
    stamp = jnp.broadcast_to(time_ref[...].astype(F32), (rows, rows))
    delta = jnp.transpose(stamp) - stamp
    dist = iota((rows, rows), 0) - iota((rows, rows), 1)
    out_ref[...] = jnp.zeros_like(out_ref)
    b_grad = jnp.sum(dh_ref[...].astype(F32), axis=0, keepdims=True)
    go_sum = jnp.sum(go_ref[...].astype(F32), axis=0, keepdims=True)
    at = 0
    for value in (b_grad, g1g_ref[...], g2g_ref[...], go_sum):
        for col in range(0, value.shape[1], LANES):
            out_ref[at : at + 1, :] = value[:, col : col + LANES]
            at += 1
    at = (at + 7) // 8 * 8
    lane = iota((heads, LANES), 1)
    for base, which, bounds in (
        (at, dist, [max(1, rows // 2 ** (count - m)) for m in range(count)]),
        (at + heads, delta, [float(4**m) for m in range(count)]),
    ):
        result = jnp.zeros((heads, LANES), F32)
        done = {}
        for m, bound in enumerate(bounds):
            if bound not in done:
                sums = [
                    jnp.sum(jnp.where(which >= bound, ds_ref[g].astype(F32), 0.0), axis=0, keepdims=True)
                    for g in range(heads)
                ]
                done[bound] = jnp.sum(jnp.concatenate(sums, axis=0), axis=1, keepdims=True)
            result = jnp.where(lane == m, done[bound], result)
        out_ref[base : base + heads, :] = result


def pack_kernel(
    planes, columns, dh_ref, n1_ref, y_ref, go_ref, got_ref, got_go_ref, small_ref, *rest
):
    outs, (uv_ref, wo_ref) = rest[:columns], rest[columns:]
    rows, width = n1_ref.shape
    core = lax.axis_index("table")
    my_dp = lax.axis_index("dp")
    my_xy = lax.rem(my_dp, columns)
    my_z = lax.div(my_dp, columns)
    half_cols = 2 * width
    half_y = width // 2
    dh = jnp.concatenate(
        [dh_ref[:, pl.ds(pl.multiple_of(core * half_cols, half_cols), half_cols)], got_ref[:, 0:half_cols]],
        axis=0,
    )
    n1 = jnp.concatenate([n1_ref[...], got_ref[:, half_cols : half_cols + width]], axis=0)
    y = jnp.concatenate(
        [y_ref[:, pl.ds(pl.multiple_of(core * half_y, half_y), half_y)], got_ref[:, half_cols + width :]],
        axis=0,
    )
    go = jnp.concatenate([go_ref[...], got_go_ref[...]], axis=0)
    uv_ref[...] = dot_tn(n1, dh)
    wo_ref[...] = dot_tn(y, go)
    chunks = planes * columns
    tall = width // chunks
    short = tall // 2
    for rel_xy in range(columns):
        xy = jnp.bitwise_xor(my_xy, rel_xy)
        for rel_z in range(planes):
            z = jnp.bitwise_xor(my_z, rel_z)
            chunk = xy * planes + z
            at = pl.multiple_of(chunk * tall, tall)
            out = outs[rel_xy].at[rel_z]
            out[:, 0:half_cols] = uv_ref[pl.ds(at, short), :].astype(BF16)
            out[:, half_cols : 2 * half_cols] = uv_ref[
                pl.ds(pl.multiple_of(at + short, short), short), :
            ].astype(BF16)
            at = pl.multiple_of(chunk * short, short)
            out[:, 2 * half_cols : 2 * half_cols + width] = wo_ref[pl.ds(at, short), :].astype(BF16)
            out[:, 2 * half_cols + width :] = small_ref[pl.ds(at, short), :].astype(BF16)


def unpack_kernel(
    planes,
    columns,
    mine_ref,
    theirs_ref,
    uvqk_ref,
    wout_ref,
    b_ref,
    g1_ref,
    g2_ref,
    bo_ref,
    pos_ref,
    time_ref,
    small_ref,
):
    width = wout_ref.shape[0]
    core = lax.axis_index("table")
    my_dp = lax.axis_index("dp")
    my_xy = lax.rem(my_dp, columns)
    my_z = lax.div(my_dp, columns)
    half_cols = 2 * width
    half_y = width // 2
    tall = width // (planes * columns)
    short = tall // 2
    for rel_xy in range(columns):
        xy = jnp.bitwise_xor(my_xy, rel_xy)
        for rel_z in range(planes):
            z = jnp.bitwise_xor(my_z, rel_z)
            chunk = xy * planes + z
            at = pl.multiple_of(chunk * short, short)
            last = slice(2 * half_cols + width, 2 * half_cols + width + LANES)
            small_ref[pl.ds(at, short), :] = (
                mine_ref[rel_xy, rel_z, :, last].astype(F32) + theirs_ref[rel_xy, rel_z, :, last].astype(F32)
            )
            for ref, side in ((mine_ref, core), (theirs_ref, 1 - core)):
                cols = pl.ds(pl.multiple_of(side * half_cols, half_cols), half_cols)
                at = pl.multiple_of(chunk * tall, tall)
                uvqk_ref[pl.ds(at, short), cols] = ref[rel_xy, rel_z, :, 0:half_cols].astype(F32)
                at = pl.multiple_of(chunk * tall + short, short)
                uvqk_ref[pl.ds(at, short), cols] = ref[
                    rel_xy, rel_z, :, half_cols : 2 * half_cols
                ].astype(F32)
                at = pl.multiple_of(side * half_y + chunk * short, short)
                wout_ref[pl.ds(at, short), :] = ref[
                    rel_xy, rel_z, :, 2 * half_cols : 2 * half_cols + width
                ].astype(F32)
    at = 0
    for out in (b_ref, g1_ref, g2_ref, bo_ref):
        for col in range(0, out.shape[1], LANES):
            out[:, col : col + LANES] = small_ref[at : at + 1, :]
            at += 1
    at = (at + 7) // 8 * 8
    heads, count = pos_ref.shape
    pos_ref[...] = small_ref[at : at + heads, 0:count]
    time_ref[...] = small_ref[at + heads : at + 2 * heads, 0:count]


def add_up(first, *rest):
    total = first.astype(F32)
    for other in rest:
        total = total + other.astype(F32)
    return total.astype(BF16)


def xor_step(value, size, step):
    return lax.ppermute(value, "dp", [(i, i ^ step) for i in range(size)])


def staged_sum(pieces, planes, columns):
    size = planes * columns
    got = [xor_step(pieces[k], size, k) for k in range(1, columns)]
    line = add_up(pieces[0], *got)
    got = [xor_step(line[k], size, k * columns) for k in range(1, planes)]
    own = add_up(line[0], *got)
    line = jnp.stack([own] + [xor_step(own, size, k * columns) for k in range(1, planes)])
    return jnp.stack([line] + [xor_step(line, size, k) for k in range(1, columns)])


def swap_cores(value):
    return lax.ppermute(value, "table", [(0, 1), (1, 0)])


def on_device(
    item_table,
    token_request_slot,
    request_rows,
    lengths,
    assignment,
    timestamps,
    item_counts,
    first_norm_gain,
    w_uvqk,
    b_uvqk,
    norm2_gain,
    w_out,
    b_out,
    pos_weight,
    time_weight,
    out_grad,
):
    rows = token_request_slot.shape[0]
    rows_dev, width = item_table.shape
    replicas = lax.axis_size("dp")
    groups = lax.axis_size("table")
    devices = replicas * groups
    cap = request_rows.shape[2]
    piece = rows // replicas
    heads, count = pos_weight.shape
    slots = devices * cap
    columns = 4
    planes = replicas // columns
    staged = (
        groups == 2
        and replicas in (4, 8, 16)
        and width % (32 * replicas) == 0
        and (2 * heads + SMALL_ROWS - 16) <= width // 2
    )
    mb = 1 << 20

    slot_row = token_request_slot.reshape(1, rows)
    time_row = timestamps.reshape(1, rows)
    counts_2d = item_counts.reshape(rows_dev // LANES, LANES)
    msg = call(
        functools.partial(request_kernel, piece, cap),
        shape_of((devices, LANES), I32),
        [VMEM] * 5,
        mb,
        mb // 8,
    )(request_rows.reshape(devices, cap), slot_row, lengths, assignment, counts_2d)
    asked = lax.all_to_all(msg.reshape(devices, 1, LANES), BOTH, 0, 0, tiled=True).reshape(devices, LANES)
    bias, go, dmix, valid = call(
        before_kernel,
        (
            shape_of((heads, rows, rows), F32),
            shape_of((rows, width), BF16),
            shape_of((rows, width), F32),
            shape_of((rows, LANES), F32),
        ),
        [VMEM] * 5 + [SMEM] * 2,
        1 << 30,
        4 * mb,
    )(lengths, assignment, time_row, out_grad, w_out, pos_weight, time_weight)
    served = call(
        functools.partial(serve_kernel, cap), shape_of((slots, width), BF16), [VMEM] * 2, 1 << 30, 5 * mb
    )(asked, item_table)
    fetched = lax.all_to_all(served.reshape(devices, cap, width), BOTH, 0, 0, tiled=True)
    new_counts, log_q, asked_row = call(
        functools.partial(counts_kernel, cap, rows_dev * devices),
        (
            shape_of((rows_dev // LANES, LANES), I32),
            shape_of((rows_dev // LANES, LANES), F32),
            shape_of((8, slots), F32),
        ),
        [VMEM] * 2,
        64 * mb,
        mb,
    )(asked, counts_2d)
    home = call(take_kernel, shape_of((rows, width), BF16), [VMEM] * 2, 64 * mb, mb)(
        slot_row, fetched.reshape(slots, width)
    )
    x = lax.all_to_all(home.reshape(replicas, piece, width), "dp", 0, 0, tiled=True).reshape(rows, width)

    half_cols = 2 * width
    g1, g2 = first_norm_gain.reshape(1, width), norm2_gain.reshape(1, width)
    msg_cols = half_cols + width + width // 2 if staged else LANES
    layer_out, n1, y, dh, ds, g2_grad, to_core = call(
        functools.partial(layer_kernel, staged),
        (
            shape_of((rows, width), BF16),
            shape_of((rows, width), BF16),
            shape_of((rows, width), BF16),
            shape_of((rows, 4 * width), BF16),
            shape_of((heads, rows, rows), BF16),
            shape_of((1, width), F32),
            shape_of((rows, msg_cols), BF16),
        ),
        [VMEM] * 10,
        2 << 30,
        8 * mb,
        scratch=(
            pltpu.VMEM((rows, 4 * width), F32),
            pltpu.VMEM((heads, rows, rows), F32),
            pltpu.VMEM((heads, rows, rows), BF16),
        ),
    )(
        x,
        w_uvqk,
        b_uvqk.reshape(1, 4 * width),
        g1,
        g2,
        w_out,
        b_out.reshape(1, width),
        bias,
        dmix,
        valid,
    )
    if staged:
        got_go = swap_cores(go)
        got = swap_cores(to_core)
    dx, g1_grad = call(
        dx_kernel, (shape_of((rows, width), BF16), shape_of((1, width), F32)), [VMEM] * 5, 1 << 29, 4 * mb
    )(dh, w_uvqk, x, g1, go)
    back = lax.all_to_all(dx.reshape(replicas, piece, width), "dp", 0, 0, tiled=True).reshape(rows, width)
    small = call(
        functools.partial(small_kernel, count),
        shape_of((width // 2, LANES), F32),
        [VMEM] * 6,
        1 << 28,
        2 * mb,
    )(ds, time_row, dh, go, g1_grad, g2_grad)
    if staged:
        short = width // replicas // 2
        pack_cols = 2 * half_cols + width + LANES
        pieces = call(
            functools.partial(pack_kernel, planes, columns),
            tuple(shape_of((planes, short, pack_cols), BF16) for _ in range(columns)),
            [VMEM] * 7,
            1 << 30,
            6 * mb,
            scratch=(pltpu.VMEM((width, half_cols), F32), pltpu.VMEM((width // 2, width), F32)),
        )(dh, n1, y, go, got, got_go, small)
        mine = staged_sum(pieces, planes, columns)
        theirs = swap_cores(mine)
        w_uvqk_sum, w_out_sum, b_sum, g1_sum, g2_sum, bo_sum, pos_sum, time_sum = call(
            functools.partial(unpack_kernel, planes, columns),
            (
                shape_of((width, 4 * width), F32),
                shape_of((width, width), F32),
                shape_of((1, 4 * width), F32),
                shape_of((1, width), F32),
                shape_of((1, width), F32),
                shape_of((1, width), F32),
                shape_of((heads, count), F32),
                shape_of((heads, count), F32),
            ),
            [VMEM] * 2,
            mb,
            8 * mb,
            scratch=(pltpu.VMEM((width // 2, LANES), F32),),
        )(mine, theirs)
    else:
        w_uvqk_sum, w_out_sum, parts = lax.psum((dot_tn(n1, dh), dot_tn(y, go), small[0:SMALL_ROWS]), BOTH)
        at = 4 * width // LANES
        step = width // LANES
        b_sum = parts[0:at]
        g1_sum, g2_sum, bo_sum = (parts[at + n * step : at + (n + 1) * step] for n in range(3))
        at = (at + 3 * step + 7) // 8 * 8
        pos_sum = parts[at : at + heads, 0:count]
        time_sum = parts[at + heads : at + 2 * heads, 0:count]
    sums = call(slot_sum_kernel, shape_of((slots, width), BF16), [VMEM] * 2, 64 * mb, mb)(slot_row, back)
    got_sums = lax.all_to_all(sums.reshape(devices, cap, width), BOTH, 0, 0, tiled=True).reshape(slots, width)
    block = min(512, rows_dev)
    table_grad = pl.pallas_call(
        scatter_kernel,
        grid=(rows_dev // block,),
        out_shape=shape_of((rows_dev, width), F32),
        in_specs=[pl.BlockSpec((8, slots), lambda i: (0, 0)), pl.BlockSpec((slots, width), lambda i: (0, 0))],
        out_specs=pl.BlockSpec((block, width), lambda i: (i, 0)),
        compiler_params=PARAMS,
        cost_estimate=cost(1 << 30, 8 * mb),
    )(asked_row, got_sums)
    return (
        layer_out,
        table_grad,
        g1_sum.reshape(width),
        w_uvqk_sum,
        b_sum.reshape(4 * width),
        g2_sum.reshape(width),
        w_out_sum,
        bo_sum.reshape(width),
        pos_sum,
        time_sum,
        new_counts.reshape(rows_dev),
        log_q.reshape(rows_dev),
    )


def solution(mesh):
    split = P(("dp", "table"))
    rows_split = P(("dp", "table"), None)
    placed = (
        rows_split,
        split,
        P(("dp", "table"), None, None),
        P("table", None),
        P("table", None),
        split,
        split,
        P(),
        P(),
        P(),
        P(),
        P(),
        P(),
        P(),
        P(),
        rows_split,
    )
    return jax.shard_map(
        on_device,
        mesh=mesh,
        in_specs=placed,
        out_specs=(rows_split, rows_split, P(), P(), P(), P(), P(), P(), P(), P(), split, split),
        check_vma=False,
    )
```

time: 275 us -> 156 us (0.57)
  matrix products: 32.2 us -> 0 us
  waiting for transfers between devices: 87.2 us -> 55.5 us
  Pallas kernels: 0 us -> 28.9 us
  other arithmetic: 26.2 us -> 0.49 us
  local copies, waits for them, and re-layouts: 26.9 us -> 7.08 us
  between operations: 16.6 us -> 0.96 us
  blocking collectives: 53.2 us -> 40.6 us
  starting transfers between devices: 31.5 us -> 22 us
    psum x1 -> x0, waiting for transfers between devices: 49.5 us -> none  [on_device(): lax.psum((first_gain_gradient, w_uvqk_grad, b_uvqk_grad, gain2_grad, w_ou...]
    psum x1 -> x0, blocking collectives: 41.7 us -> none  [on_device(): lax.psum((first_gain_gradient, w_uvqk_grad, b_uvqk_grad, gain2_grad, w_ou...]
    ppermute x0 -> x15, waiting for transfers between devices: none -> 40.9 us  [the longest x12 40.9 us: xor_step(): return lax.ppermute(value, 'dp', [(i, i ^ step) for i in range(size)])]
    dot_general x14 -> x0, matrix products: 32.2 us -> none  [the longest x1 7.65 us: on_device(): jnp.einsum('qhd,khd->hqk', queries, keys, preferred_element_type=jnp.floa...]
    all_to_all x3, blocking collectives: 11.5 us -> 40.6 us  [the longest x1 14.2 us: on_device(): lax.all_to_all(msg.reshape(devices, 1, LANES), BOTH, 0, 0, tiled=True)]
    pallas_call x0 -> x12, Pallas kernels: none -> 28.9 us  [the longest x1 7.06 us: on_device(): call(functools.partial(layer_kernel, staged), (shape_of((rows, width), BF...]
    all_to_all x7 -> x2, starting transfers between devices: 31.3 us -> 6.3 us  [the longest x1 3.71 us: on_device(): lax.all_to_all(home.reshape(replicas, piece, width), 'dp', 0, 0, tiled=True)]
    all_to_all x7 -> x2, waiting for transfers between devices: 37.6 us -> 14.6 us  [the longest x1 9.45 us: on_device(): lax.all_to_all(sums.reshape(devices, cap, width), BOTH, 0, 0, tiled=True)]
  transfers between devices with their start and end apart: 8 -> 17, of which waited for: 7 -> 12; matrix products, arithmetic and copies ran while one was open for 11% -> 0% of each run, Pallas kernels for 0% -> 10%
where the time goes in v1:
time: 156 us
  waiting for transfers between devices  55.5 us (36%)
  blocking collectives  40.6 us (26%)
  Pallas kernels  28.9 us (19%)
  starting transfers between devices  22 us (14%)
  local copies, waits for them, and re-layouts  7.08 us (5%)
    ppermute x12, waiting for transfers between devices, xor_step(): return lax.ppermute(value, 'dp', [(i, i ^ step) for i in range(size)])  40.9 us
    ppermute x12, starting transfers between devices, xor_step(): return lax.ppermute(value, 'dp', [(i, i ^ step) for i in range(size)])  15.1 us
    all_to_all x1, blocking collectives, on_device(): lax.all_to_all(msg.reshape(devices, 1, LANES), BOTH, 0, 0, tiled=True)  14.2 us
    all_to_all x1, blocking collectives, on_device(): lax.all_to_all(dx.reshape(replicas, piece, width), 'dp', 0, 0, tiled=True)  13.9 us
    all_to_all x1, blocking collectives, on_device(): lax.all_to_all(served.reshape(devices, cap, width), BOTH, 0, 0, tiled=True)  12.4 us
    all_to_all x1, waiting for transfers between devices, on_device(): lax.all_to_all(sums.reshape(devices, cap, width), BOTH, 0, 0, tiled=True)  9.45 us
    pallas_call x1, Pallas kernels, on_device(): call(functools.partial(layer_kernel, staged), (shape_of((rows, width), BF...  7.06 us
    unnamed x41, local copies, waits for them, and re-layouts  7.05 us
  transfers between devices with their start and end apart: 17, of which 12 were waited for; matrix products, arithmetic and copies ran while one was open for 0% of the time, Pallas kernels for 10%

profile of v1, /device:TPU:0, one launch (start us, length us, event | category | flops | bytes accessed | tf_op | source)
XLA Modules:
  0.0 155.6 jit_solution(4958490517548130034)
XLA Ops:
  4.3 14.2 %all_to_all.25 = s32[32,1,128]{2,1,0:T(1,128)S(1)} all-to-all(s32[32,1,128]{2,1,0:T(1,128)S(1)} %bitcast.56), channel_id=1, replica_groups=mesh['dp'=16,'table'=2] {'dp','table'}, dimensions={0} | all-to-all | bytes 32768 | tf_op jit(solution)/shard_map/all_to_all | solution.py:522
  18.6 2.2 %copy-done = bf16[4096,512]{1,0:T(8,128)(2,1)S(1)} copy-done((bf16[4096,512]{1,0:T(8,128)(2,1)S(1)}, bf16[4096,512]{1,0:T(8,128)(2,1)}, u32[]{:S(2)}) %copy-start) | copy-done | bytes 4194328
  20.8 1.9 %shard_map.248 = bf16[256,512]{1,0:T(8,128)(2,1)S(1)} custom-call(s32[32,128]{1,0:T(8,128)S(1)} %bitcast.53, bf16[4096,512]{1,0:T(8,128)(2,1)S(1)} %copy-done), custom_call_target="tpu_custom_call" | custom-call | flops 1073741824 | bytes 5242880 | tf_op jit(solution)/shard_map/pallas_call | solution.py:535
  22.7 12.4 %all_to_all.26 = bf16[32,8,512]{2,1,0:T(8,128)(2,1)S(1)} all-to-all(bf16[32,8,512]{2,1,0:T(8,128)(2,1)S(1)} %bitcast.49), channel_id=1, replica_groups=mesh['dp'=16,'table'=2] {'dp','table'}, dimensions={0} | all-to-all | bytes 524288 | tf_op jit(solution)/shard_map/all_to_all | solution.py:538
  36.1 3.7 %all-to-all-start.2 = ((bf16[16,16,512]{2,1,0:T(8,128)(2,1)}), bf16[16,16,512]{2,1,0:T(8,128)(2,1)S(1)}, u32[]{:S(2)}, u32[]{:S(2)}) async-start(bf16[16,16,512]{2,1,0:T(8,128)(2,1)} %bitcast.8), calls=%async_computation.2 | async-start | bytes 524288 | tf_op jit(solution)/shard_map/all_to_all | solution.py:553
  40.0 3.4 %shard_map.250 = (f32[8,256,256]{2,1,0:T(8,128)S(1)}, bf16[256,512]{1,0:T(8,128)(2,1)S(1)}, f32[256,512]{1,0:T(8,128)S(1)}, f32[256,128]{1,0:T(8,128)S(1)}) custom-call(s32[1,64]{1,0:T(1,128)S(1)} %copy-done.9, s32[1,64]{1,0:T(1,128)S(1)} %copy-done.11, s32[1,256]{1,0:T(1,128)S(1)} %bitcast.64, bf16[256,512]{1,0:T(8,128)(2,1)S(1)} %copy-done.13, ...), custom_call_target="tpu_custom_call" | custom-call | flops 1073741824 | bytes 4194304 | tf_op jit(solution)/shard_map/pallas_call | solution.py:523
  43.4 1.3 copy-done.19
  44.7 5.1 %all-to-all-done.2 = bf16[16,16,512]{2,1,0:T(8,128)(2,1)S(1)} async-done(((bf16[16,16,512]{2,1,0:T(8,128)(2,1)}), bf16[16,16,512]{2,1,0:T(8,128)(2,1)S(1)}, u32[]{:S(2)}, u32[]{:S(2)}) %all-to-all-start.2) | async-done | bytes 262176 | tf_op jit(solution)/shard_map/all_to_all | solution.py:553
  49.9 7.1 %shard_map.251 = (bf16[256,512]{1,0:T(8,128)(2,1)}, bf16[256,512]{1,0:T(8,128)(2,1)S(1)}, bf16[256,512]{1,0:T(8,128)(2,1)S(1)}, bf16[256,2048]{1,0:T(8,128)(2,1)...) custom-call(bf16[256,512]{1,0:T(8,128)(2,1)S(1)} %bitcast.46, ...), custom_call_target="tpu_custom_call" | custom-call | flops 2147483648 | bytes 8388608 | tf_op jit(solution)/shard_map/pallas_call | solution.py:558
  58.4 3.4 %shard_map.256.small_ref = f32[256,128]{1,0:T(8,128)S(1)} custom-call(bf16[8,256,256]{2,1,0:T(8,128)(2,1)S(1)} %get-tuple-element.51.ds_ref, s32[1,256]{1,0:T(1,128)S(1)} %bitcast.65, bf16[256,2048]{1,0:T(8,128)(2,1)S(1)} %get-tuple-element.45.dh_ref, bf16[256,512]{1,0:T(8,128)(2,1)S(1)} %get-tuple-element.46.go_ref, ...), custom_call_target="tpu_custom_call" | custom-call | flops 268435456 | bytes 2097152 | tf_op jit(solution)/shard_map/pallas_call | solution.py:596
  61.8 1.2 shard_map.257
  64.5 2.0 %collective-permute-start.4 = (bf16[4,16,2688]{2,1,0:T(8,128)(2,1)S(1)}, bf16[4,16,2688]{2,1,0:T(8,128)(2,1)S(1)}, u32[]{:S(2)}, u32[]{:S(2)}) collective-permute-start(bf16[4,16,2688]{2,1,0:T(8,128)(2,1)S(1)} %get-tuple-element.57), channel_id=1, source_target_pairs={{0,6},{2,4},{4,2},{6,0},{8,14},{10,12},{12,10},{14,8},{16,22},{18,... | collective-permute-start | bytes 1032200 | tf_op jit(solution)/shard_map/ppermute | solution.py:458
  66.5 7.4 %collective-permute-done.2 = bf16[4,16,2688]{2,1,0:T(8,128)(2,1)S(1)} collective-permute-done((bf16[4,16,2688]{2,1,0:T(8,128)(2,1)S(1)}, bf16[4,16,2688]{2,1,0:T(8,128)(2,1)S(1)}, u32[]{:S(2)}, u32[]{:S(2)}) %collective-permute-start.2) | collective-permute-done | bytes 344096 | tf_op jit(solution)/shard_map/ppermute | solution.py:458
  74.0 7.0 %collective-permute-done.3 = bf16[4,16,2688]{2,1,0:T(8,128)(2,1)S(1)} collective-permute-done((bf16[4,16,2688]{2,1,0:T(8,128)(2,1)S(1)}, bf16[4,16,2688]{2,1,0:T(8,128)(2,1)S(1)}, u32[]{:S(2)}, u32[]{:S(2)}) %collective-permute-start.3) | collective-permute-done | bytes 344096 | tf_op jit(solution)/shard_map/ppermute | solution.py:458
  82.1 1.6 %collective-permute-start.7 = (bf16[16,2688]{1,0:T(8,128)(2,1)S(1)}, bf16[16,2688]{1,0:T(8,128)(2,1)S(1)}, u32[]{:S(2)}, u32[]{:S(2)}) collective-permute-start(bf16[16,2688]{1,0:T(8,128)(2,1)S(1)} %get-tuple-element.71), channel_id=1, source_target_pairs={{0,24},{2,26},{4,28},{6,30},{8,16},{10,18},{12,20},{14,22},{16,8},... | collective-permute-start | bytes 258056 | tf_op jit(solution)/shard_map/ppermute | solution.py:458
  84.7 2.5 %collective-permute-done.5 = bf16[16,2688]{1,0:T(8,128)(2,1)S(1)} collective-permute-done((bf16[16,2688]{1,0:T(8,128)(2,1)S(1)}, bf16[16,2688]{1,0:T(8,128)(2,1)S(1)}, u32[]{:S(2)}, u32[]{:S(2)}) %collective-permute-start.5) | collective-permute-done | bytes 86048 | tf_op jit(solution)/shard_map/ppermute | solution.py:458
  87.3 1.8 %collective-permute-done.7 = bf16[16,2688]{1,0:T(8,128)(2,1)S(1)} collective-permute-done((bf16[16,2688]{1,0:T(8,128)(2,1)S(1)}, bf16[16,2688]{1,0:T(8,128)(2,1)S(1)}, u32[]{:S(2)}, u32[]{:S(2)}) %collective-permute-start.7) | collective-permute-done | bytes 86048 | tf_op jit(solution)/shard_map/ppermute | solution.py:458
  89.0 2.8 %collective-permute-done.6 = bf16[16,2688]{1,0:T(8,128)(2,1)S(1)} collective-permute-done((bf16[16,2688]{1,0:T(8,128)(2,1)S(1)}, bf16[16,2688]{1,0:T(8,128)(2,1)S(1)}, u32[]{:S(2)}, u32[]{:S(2)}) %collective-permute-start.6) | collective-permute-done | bytes 86048 | tf_op jit(solution)/shard_map/ppermute | solution.py:458
  91.9 1.5 collective-permute-start.10
  93.4 2.9 %collective-permute-start.8 = (bf16[16,2688]{1,0:T(8,128)(2,1)S(1)}, bf16[16,2688]{1,0:T(8,128)(2,1)S(1)}, u32[]{:S(2)}, u32[]{:S(2)}) collective-permute-start(bf16[16,2688]{1,0:T(8,128)(2,1)S(1)} %fusion.2), channel_id=1, source_target_pairs={{0,8},{2,10},{4,12},{6,14},{8,0},{10,2},{12,4},{14,6},{16,24},{18,... | collective-permute-start | bytes 258056 | tf_op jit(solution)/shard_map/ppermute | solution.py:458
  96.4 2.7 %collective-permute-done.10 = bf16[16,2688]{1,0:T(8,128)(2,1)S(1)} collective-permute-done((bf16[16,2688]{1,0:T(8,128)(2,1)S(1)}, bf16[16,2688]{1,0:T(8,128)(2,1)S(1)}, u32[]{:S(2)}, u32[]{:S(2)}) %collective-permute-start.10) | collective-permute-done | bytes 86048 | tf_op jit(solution)/shard_map/ppermute | solution.py:458
  99.1 2.0 %collective-permute-done.9 = bf16[16,2688]{1,0:T(8,128)(2,1)S(1)} collective-permute-done((bf16[16,2688]{1,0:T(8,128)(2,1)S(1)}, bf16[16,2688]{1,0:T(8,128)(2,1)S(1)}, u32[]{:S(2)}, u32[]{:S(2)}) %collective-permute-start.9) | collective-permute-done | bytes 86048 | tf_op jit(solution)/shard_map/ppermute | solution.py:458
  101.2 1.2 collective-permute-start.12
  103.2 1.5 collective-permute-start.13
  104.7 6.6 %collective-permute-done.12 = bf16[4,16,2688]{2,1,0:T(8,128)(2,1)S(1)} collective-permute-done((bf16[4,16,2688]{2,1,0:T(8,128)(2,1)S(1)}, bf16[4,16,2688]{2,1,0:T(8,128)(2,1)S(1)}, u32[]{:S(2)}, u32[]{:S(2)}) %collective-permute-start.12) | collective-permute-done | bytes 344096 | tf_op jit(solution)/shard_map/ppermute | solution.py:458
  111.3 2.0 %collective-permute-done.11 = bf16[4,16,2688]{2,1,0:T(8,128)(2,1)S(1)} collective-permute-done((bf16[4,16,2688]{2,1,0:T(8,128)(2,1)S(1)}, bf16[4,16,2688]{2,1,0:T(8,128)(2,1)S(1)}, u32[]{:S(2)}, u32[]{:S(2)}) %collective-permute-start.11) | collective-permute-done | bytes 344096 | tf_op jit(solution)/shard_map/ppermute | solution.py:458
  113.3 6.0 %collective-permute-done.13 = bf16[4,16,2688]{2,1,0:T(8,128)(2,1)S(1)} collective-permute-done((bf16[4,16,2688]{2,1,0:T(8,128)(2,1)S(1)}, bf16[4,16,2688]{2,1,0:T(8,128)(2,1)S(1)}, u32[]{:S(2)}, u32[]{:S(2)}) %collective-permute-start.13) | collective-permute-done | bytes 344096 | tf_op jit(solution)/shard_map/ppermute | solution.py:458
  119.6 13.9 %all_to_all.27 = bf16[16,16,512]{2,1,0:T(8,128)(2,1)S(1)} all-to-all(bf16[16,16,512]{2,1,0:T(8,128)(2,1)S(1)} %bitcast.52), channel_id=1, replica_groups=mesh['dp'=16,'table'=2] {'dp'}, dimensions={0} | all-to-all | bytes 524288 | tf_op jit(solution)/shard_map/all_to_all | solution.py:595
  134.5 2.6 %all-to-all-start.4 = ((bf16[32,8,512]{2,1,0:T(8,128)(2,1)}), bf16[32,8,512]{2,1,0:T(8,128)(2,1)S(1)}, u32[]{:S(2)}, u32[]{:S(2)}) async-start(bf16[32,8,512]{2,1,0:T(8,128)(2,1)} %bitcast.17), calls=%async_computation.4 | async-start | bytes 524288 | tf_op jit(solution)/shard_map/all_to_all | solution.py:643
  138.2 9.5 %all-to-all-done.4 = bf16[32,8,512]{2,1,0:T(8,128)(2,1)S(1)} async-done(((bf16[32,8,512]{2,1,0:T(8,128)(2,1)}), bf16[32,8,512]{2,1,0:T(8,128)(2,1)S(1)}, u32[]{:S(2)}, u32[]{:S(2)}) %all-to-all-start.4) | async-done | bytes 262176 | tf_op jit(solution)/shard_map/all_to_all | solution.py:643
  147.7 5.4 %shard_map.255 = f32[4096,512]{1,0:T(8,128)} custom-call(f32[8,256]{1,0:T(8,128)S(1)} %get-tuple-element.44.row_ref, bf16[256,512]{1,0:T(8,128)(2,1)S(1)} %bitcast.48), custom_call_target="tpu_custom_call" | custom-call | flops 1073741824 | bytes 8388608 | tf_op jit(solution)/shard_map/pallas_call | solution.py:645
  153.1 2.5 %shard_map.258 = (f32[512,2048]{1,0:T(8,128)}, f32[512,512]{1,0:T(8,128)}, f32[1,2048]{1,0:T(1,128)}, f32[1,512]{1,0:T(1,128)}, f32[1,512]{1,0:T(1,128)}, /*inde...) custom-call(bf16[4,4,16,2688]{3,2,1,0:T(8,128)(2,1)S(1)} %pad_maximum_fusion.mine_ref, ...), custom_call_target="tpu_custom_call" | custom-call | flops 1048576 | bytes 8388608 | tf_op jit(solution)/shard_map/pallas_call | solution.py:616
  (63 shorter events, 13.2 us)
Async XLA Ops:
  18.6 2.2 %copy-start = (bf16[4096,512]{1,0:T(8,128)(2,1)S(1)}, bf16[4096,512]{1,0:T(8,128)(2,1)}, u32[]{:S(2)}) copy-start(bf16[4096,512]{1,0:T(8,128)(2,1)} %table_ref.1) | copy-start | bytes 12582916
  20.8 14.4 %copy-start.5 = (s32[256]{0:T(256)S(1)}, s32[256]{0:T(256)}, u32[]{:S(2)}) copy-start(s32[256]{0:T(256)} %param.17) | copy-start | bytes 3076
  22.6 17.2 %copy-start.7 = (s32[256]{0:T(256)S(1)}, s32[256]{0:T(256)}, u32[]{:S(2)}) copy-start(s32[256]{0:T(256)} %param.21) | copy-start | bytes 3076
  22.6 17.2 %copy-start.9 = (s32[1,64]{1,0:T(1,128)S(1)}, s32[1,64]{1,0:T(1,128)}, u32[]{:S(2)}) copy-start(s32[1,64]{1,0:T(1,128)} %len_ref.3) | copy-start | bytes 772
  22.6 17.2 %copy-start.11 = (s32[1,64]{1,0:T(1,128)S(1)}, s32[1,64]{1,0:T(1,128)}, u32[]{:S(2)}) copy-start(s32[1,64]{1,0:T(1,128)} %dest_ref.3) | copy-start | bytes 772
  22.7 17.2 %copy-start.12 = (bf16[512,512]{1,0:T(8,128)(2,1)S(1)}, bf16[512,512]{1,0:T(8,128)(2,1)}, u32[]{:S(2)}) copy-start(bf16[512,512]{1,0:T(8,128)(2,1)} %wo_ref.3) | copy-start | bytes 1572868
  22.7 17.2 %copy-start.13 = (bf16[256,512]{1,0:T(8,128)(2,1)S(1)}, bf16[256,512]{1,0:T(8,128)(2,1)}, u32[]{:S(2)}) copy-start(bf16[256,512]{1,0:T(8,128)(2,1)} %og_ref.1) | copy-start | bytes 786436
  22.7 17.2 %copy-start.15 = (f32[8,10]{1,0:T(8,128)S(1)}, f32[8,10]{1,0:T(8,128)}, u32[]{:S(2)}) copy-start(f32[8,10]{1,0:T(8,128)} %pos_ref.1) | copy-start | bytes 964
  22.7 17.2 %copy-start.16 = (f32[8,10]{1,0:T(8,128)S(1)}, f32[8,10]{1,0:T(8,128)}, u32[]{:S(2)}) copy-start(f32[8,10]{1,0:T(8,128)} %timew_ref.1) | copy-start | bytes 964
  36.1 13.7 %all-to-all-start.2 = ((bf16[16,16,512]{2,1,0:T(8,128)(2,1)}), bf16[16,16,512]{2,1,0:T(8,128)(2,1)S(1)}, u32[]{:S(2)}, u32[]{:S(2)}) async-start(bf16[16,16,512]{2,1,0:T(8,128)(2,1)} %bitcast.8), calls=%async_computation.2 | async-start | bytes 524288 | tf_op jit(solution)/shard_map/all_to_all | solution.py:553
  39.9 9.9 %copy-start.6 = (f32[512]{0:T(512)S(1)}, f32[512]{0:T(512)}, u32[]{:S(2)}) copy-start(f32[512]{0:T(512)} %param.23) | copy-start | bytes 6148
  39.9 9.9 %copy-start.14 = (f32[2048]{0:T(1024)S(1)}, f32[2048]{0:T(1024)}, u32[]{:S(2)}) copy-start(f32[2048]{0:T(1024)} %param.25) | copy-start | bytes 24580
  39.9 9.9 %copy-start.17 = (f32[512]{0:T(512)S(1)}, f32[512]{0:T(512)}, u32[]{:S(2)}) copy-start(f32[512]{0:T(512)} %param.26) | copy-start | bytes 6148
  39.9 9.9 %copy-start.18 = (f32[512]{0:T(512)S(1)}, f32[512]{0:T(512)}, u32[]{:S(2)}) copy-start(f32[512]{0:T(512)} %param.28) | copy-start | bytes 6148
  49.8 7.6 %copy-start.1 = (bf16[512,2048]{1,0:T(8,128)(2,1)S(1)}, bf16[512,2048]{1,0:T(8,128)(2,1)}, u32[]{:S(2)}) copy-start(bf16[512,2048]{1,0:T(8,128)(2,1)} %w_ref.3) | copy-start | bytes 6291460
  56.9 4.9 %collective-permute-start = (bf16[256,1792]{1,0:T(8,128)(2,1)S(1)}, bf16[256,1792]{1,0:T(8,128)(2,1)S(1)}, u32[]{:S(2)}, u32[]{:S(2)}) collective-permute-start(bf16[256,1792]{1,0:T(8,128)(2,1)S(1)} %get-tuple-element.50), channel_id=1, source_target_pairs={{0,1},{1,0},{2,3},{3,2},{4,5},{5,4},{6,7},{7,6},{8,9},{9,8},{10,11... | collective-permute-start | bytes 2752520 | tf_op jit(solution)/shard_map/ppermute | solution.py:472
  57.0 4.8 %collective-permute-start.1 = (bf16[256,512]{1,0:T(8,128)(2,1)S(1)}, bf16[256,512]{1,0:T(8,128)(2,1)S(1)}, u32[]{:S(2)}, u32[]{:S(2)}) collective-permute-start(bf16[256,512]{1,0:T(8,128)(2,1)S(1)} %get-tuple-element.46.go_ref), channel_id=1, source_target_pairs={{0,1},{1,0},{2,3},{3,2},{4,5},{5,4},{6,7},{7,6},{8,9},{9,8},{10,11... | collective-permute-start | bytes 786440 | tf_op jit(solution)/shard_map/ppermute | solution.py:472
  63.0 11.0 %collective-permute-start.2 = (bf16[4,16,2688]{2,1,0:T(8,128)(2,1)S(1)}, bf16[4,16,2688]{2,1,0:T(8,128)(2,1)S(1)}, u32[]{:S(2)}, u32[]{:S(2)}) collective-permute-start(bf16[4,16,2688]{2,1,0:T(8,128)(2,1)S(1)} %get-tuple-element.55), channel_id=1, source_target_pairs={{0,2},{2,0},{4,6},{6,4},{8,10},{10,8},{12,14},{14,12},{16,18},{18,... | collective-permute-start | bytes 1032200 | tf_op jit(solution)/shard_map/ppermute | solution.py:458
  63.8 17.1 %collective-permute-start.3 = (bf16[4,16,2688]{2,1,0:T(8,128)(2,1)S(1)}, bf16[4,16,2688]{2,1,0:T(8,128)(2,1)S(1)}, u32[]{:S(2)}, u32[]{:S(2)}) collective-permute-start(bf16[4,16,2688]{2,1,0:T(8,128)(2,1)S(1)} %get-tuple-element.56), channel_id=1, source_target_pairs={{0,4},{2,6},{4,0},{6,2},{8,12},{10,14},{12,8},{14,10},{16,20},{18,... | collective-permute-start | bytes 1032200 | tf_op jit(solution)/shard_map/ppermute | solution.py:458
  64.5 16.5 %collective-permute-start.4 = (bf16[4,16,2688]{2,1,0:T(8,128)(2,1)S(1)}, bf16[4,16,2688]{2,1,0:T(8,128)(2,1)S(1)}, u32[]{:S(2)}, u32[]{:S(2)}) collective-permute-start(bf16[4,16,2688]{2,1,0:T(8,128)(2,1)S(1)} %get-tuple-element.57), channel_id=1, source_target_pairs={{0,6},{2,4},{4,2},{6,0},{8,14},{10,12},{12,10},{14,8},{16,22},{18,... | collective-permute-start | bytes 1032200 | tf_op jit(solution)/shard_map/ppermute | solution.py:458
  81.2 6.1 %collective-permute-start.5 = (bf16[16,2688]{1,0:T(8,128)(2,1)S(1)}, bf16[16,2688]{1,0:T(8,128)(2,1)S(1)}, u32[]{:S(2)}, u32[]{:S(2)}) collective-permute-start(bf16[16,2688]{1,0:T(8,128)(2,1)S(1)} %get-tuple-element.70), channel_id=1, source_target_pairs={{0,8},{2,10},{4,12},{6,14},{8,0},{10,2},{12,4},{14,6},{16,24},{18,... | collective-permute-start | bytes 258056 | tf_op jit(solution)/shard_map/ppermute | solution.py:458
  82.1 6.9 %collective-permute-start.7 = (bf16[16,2688]{1,0:T(8,128)(2,1)S(1)}, bf16[16,2688]{1,0:T(8,128)(2,1)S(1)}, u32[]{:S(2)}, u32[]{:S(2)}) collective-permute-start(bf16[16,2688]{1,0:T(8,128)(2,1)S(1)} %get-tuple-element.71), channel_id=1, source_target_pairs={{0,24},{2,26},{4,28},{6,30},{8,16},{10,18},{12,20},{14,22},{16,8},... | collective-permute-start | bytes 258056 | tf_op jit(solution)/shard_map/ppermute | solution.py:458
  83.7 8.1 %collective-permute-start.6 = (bf16[16,2688]{1,0:T(8,128)(2,1)S(1)}, bf16[16,2688]{1,0:T(8,128)(2,1)S(1)}, u32[]{:S(2)}, u32[]{:S(2)}) collective-permute-start(bf16[16,2688]{1,0:T(8,128)(2,1)S(1)} %get-tuple-element.72), channel_id=1, source_target_pairs={{0,16},{2,18},{4,20},{6,22},{8,24},{10,26},{12,28},{14,30},{16,0},... | collective-permute-start | bytes 258056 | tf_op jit(solution)/shard_map/ppermute | solution.py:458
  91.9 7.2 %collective-permute-start.10 = (bf16[16,2688]{1,0:T(8,128)(2,1)S(1)}, bf16[16,2688]{1,0:T(8,128)(2,1)S(1)}, u32[]{:S(2)}, u32[]{:S(2)}) collective-permute-start(bf16[16,2688]{1,0:T(8,128)(2,1)S(1)} %fusion.2), channel_id=1, source_target_pairs={{0,24},{2,26},{4,28},{6,30},{8,16},{10,18},{12,20},{14,22},{16,8},... | collective-permute-start | bytes 258056 | tf_op jit(solution)/shard_map/ppermute | solution.py:458
  93.4 7.7 %collective-permute-start.9 = (bf16[16,2688]{1,0:T(8,128)(2,1)S(1)}, bf16[16,2688]{1,0:T(8,128)(2,1)S(1)}, u32[]{:S(2)}, u32[]{:S(2)}) collective-permute-start(bf16[16,2688]{1,0:T(8,128)(2,1)S(1)} %fusion.2), channel_id=1, source_target_pairs={{0,16},{2,18},{4,20},{6,22},{8,24},{10,26},{12,28},{14,30},{16,0},... | collective-permute-start | bytes 258056 | tf_op jit(solution)/shard_map/ppermute | solution.py:458
  93.4 7.7 %collective-permute-start.8 = (bf16[16,2688]{1,0:T(8,128)(2,1)S(1)}, bf16[16,2688]{1,0:T(8,128)(2,1)S(1)}, u32[]{:S(2)}, u32[]{:S(2)}) collective-permute-start(bf16[16,2688]{1,0:T(8,128)(2,1)S(1)} %fusion.2), channel_id=1, source_target_pairs={{0,8},{2,10},{4,12},{6,14},{8,0},{10,2},{12,4},{14,6},{16,24},{18,... | collective-permute-start | bytes 258056 | tf_op jit(solution)/shard_map/ppermute | solution.py:458
  101.2 10.2 %collective-permute-start.12 = (bf16[4,16,2688]{2,1,0:T(8,128)(2,1)S(1)}, bf16[4,16,2688]{2,1,0:T(8,128)(2,1)S(1)}, u32[]{:S(2)}, u32[]{:S(2)}) collective-permute-start(bf16[4,16,2688]{2,1,0:T(8,128)(2,1)S(1)} %get-tuple-element.69), channel_id=1, source_target_pairs={{0,4},{2,6},{4,0},{6,2},{8,12},{10,14},{12,8},{14,10},{16,20},{18,... | collective-permute-start | bytes 1032200 | tf_op jit(solution)/shard_map/ppermute | solution.py:458
  102.3 11.0 %collective-permute-start.11 = (bf16[4,16,2688]{2,1,0:T(8,128)(2,1)S(1)}, bf16[4,16,2688]{2,1,0:T(8,128)(2,1)S(1)}, u32[]{:S(2)}, u32[]{:S(2)}) collective-permute-start(bf16[4,16,2688]{2,1,0:T(8,128)(2,1)S(1)} %get-tuple-element.69), channel_id=1, source_target_pairs={{0,2},{2,0},{4,6},{6,4},{8,10},{10,8},{12,14},{14,12},{16,18},{18,... | collective-permute-start | bytes 1032200 | tf_op jit(solution)/shard_map/ppermute | solution.py:458
  103.2 16.1 %collective-permute-start.13 = (bf16[4,16,2688]{2,1,0:T(8,128)(2,1)S(1)}, bf16[4,16,2688]{2,1,0:T(8,128)(2,1)S(1)}, u32[]{:S(2)}, u32[]{:S(2)}) collective-permute-start(bf16[4,16,2688]{2,1,0:T(8,128)(2,1)S(1)} %get-tuple-element.69), channel_id=1, source_target_pairs={{0,6},{2,4},{4,2},{6,0},{8,14},{10,12},{12,10},{14,8},{16,22},{18,... | collective-permute-start | bytes 1032200 | tf_op jit(solution)/shard_map/ppermute | solution.py:458
  119.5 17.5 %copy-start.3 = (s32[4096]{0:T(1024)S(1)}, s32[4096]{0:T(1024)}, u32[]{:S(2)}) copy-start(s32[4096]{0:T(1024)} %param.22) | copy-start | bytes 49156
  119.5 33.5 %collective-permute-start.14 = (bf16[4,4,16,2688]{3,2,1,0:T(8,128)(2,1)S(1)}, bf16[4,4,16,2688]{3,2,1,0:T(8,128)(2,1)S(1)}, u32[]{:S(2)}, u32[]{:S(2)}) collective-permute-start(bf16[4,4,16,2688]{3,2,1,0:T(8,128)(2,1)S(1)} %pad_maximum_fusion.mine_ref), channel_id=1, source_target_pairs={{0,1},{1,0},{2,3},{3,2},{4,5},{5,4},{6,7},{7,6},{8,9},{9,8},{10,11... | collective-permute-start | bytes 4128776 | tf_op jit(solution)/shard_map/ppermute | solution.py:472
  134.5 13.2 %all-to-all-start.4 = ((bf16[32,8,512]{2,1,0:T(8,128)(2,1)}), bf16[32,8,512]{2,1,0:T(8,128)(2,1)S(1)}, u32[]{:S(2)}, u32[]{:S(2)}) async-start(bf16[32,8,512]{2,1,0:T(8,128)(2,1)} %bitcast.17), calls=%async_computation.4 | async-start | bytes 524288 | tf_op jit(solution)/shard_map/all_to_all | solution.py:643
  (5 other events, 4.0 us)

commit v2 on v1

--- a/solution.py
+++ b/solution.py
@@ -16,7 +16,8 @@
 LANES = 128
 VMEM = pl.BlockSpec(memory_space=pltpu.VMEM)
 SMEM = pl.BlockSpec(memory_space=pltpu.SMEM)
-PARAMS = pltpu.CompilerParams(vmem_limit_bytes=48 * 1024 * 1024)
+HBM = pl.BlockSpec(memory_space=pltpu.HBM)
+MIB = 1 << 20
 
 
 def dot_nn(a, b):
@@ -49,21 +50,37 @@
     return pl.CostEstimate(flops=int(flops), bytes_accessed=int(moved), transcendentals=0)
 
 
-def call(body, outs, specs, flops, moved, scratch=()):
-    many = isinstance(outs, tuple)
+def params(mib):
+    return pltpu.CompilerParams(vmem_limit_bytes=mib * MIB)
+
+
+def call(body, outs, specs, flops, moved, scratch=(), room=16, out_specs=None):
+    if out_specs is None:
+        out_specs = tuple(VMEM for _ in outs) if isinstance(outs, tuple) else VMEM
     return pl.pallas_call(
         body,
         out_shape=outs,
         in_specs=specs,
-        out_specs=tuple(VMEM for _ in outs) if many else VMEM,
+        out_specs=out_specs,
         scratch_shapes=list(scratch),
-        compiler_params=PARAMS,
+        compiler_params=params(room),
         cost_estimate=cost(flops, moved),
     )
 
 
-def request_kernel(piece, cap, rows_ref, slot_ref, len_ref, dest_ref, counts_ref, msg_ref):
-    owners = rows_ref.shape[0]
+def start_all(sources, targets, sems):
+    copies = [pltpu.make_async_copy(a, b, sems.at[n]) for n, (a, b) in enumerate(zip(sources, targets))]
+    for copy in copies:
+        copy.start()
+    return copies
+
+
+def request_kernel(piece, cap, *refs):
+    sources, msg_ref, held, sems = refs[:5], refs[5], refs[6:11], refs[11]
+    for copy in start_all(sources, held, sems):
+        copy.wait()
+    rows_ref, slot_ref, len_ref, dest_ref, counts_ref = held
+    owners = rows_ref.shape[1]
     tokens = slot_ref.shape[1]
     replicas = tokens // piece
     my_dp = lax.axis_index("dp")
@@ -82,8 +99,9 @@
     old = jnp.sum(counts_ref[...].astype(F32), axis=0, keepdims=True)
     total = jnp.sum(old, axis=1, keepdims=True) + jnp.sum(valid, axis=1, keepdims=True)
     lane = iota((owners, LANES), 1)
-    msg_ref[...] = jnp.where(lane == 2 * cap, total, counts).astype(I32)
-    msg_ref[:, 0:cap] = rows_ref[...]
+    place = jnp.where(iota((cap, LANES), 0) == iota((cap, LANES), 1), 1.0, 0.0)
+    wanted = dot_exact(jnp.transpose(rows_ref[...].astype(F32)), place)
+    msg_ref[...] = (jnp.where(lane == 2 * cap, total, counts) + wanted).astype(I32)
 
 
 def asked_column(cap, asked_ref, first):
@@ -144,41 +162,88 @@
     out_ref[...] = dot_nn(pick, got_ref[...])
 
 
-def before_kernel(
-    len_ref, dest_ref, time_ref, og_ref, wo_ref, pos_ref, timew_ref, bias_ref, go_ref, dmix_ref, valid_ref
-):
-    rows = time_ref.shape[1]
-    heads, count = pos_ref.shape
+def segments(len_ref, dest_ref, rows):
     nhist = len_ref.shape[1]
-    my_dp = lax.axis_index("dp")
-    mine = jnp.where(dest_ref[...] == my_dp, len_ref[...], 0).astype(F32)
+    mine = jnp.where(dest_ref[...] == lax.axis_index("dp"), len_ref[...], 0).astype(F32)
     later = iota((nhist, nhist), 0)
     other = iota((nhist, nhist), 1)
     ends = jnp.sum(jnp.where(other <= later, mine, 0.0), axis=1, keepdims=True)
     starts = jnp.sum(jnp.where(other < later, mine, 0.0), axis=1, keepdims=True)
     place = iota((nhist, rows), 1).astype(F32)
     label = iota((nhist, rows), 0).astype(F32) + 1.0
-    inside = (starts <= place) & (place < ends)
-    seg = jnp.sum(jnp.where(inside, label, 0.0), axis=0, keepdims=True) - 1.0
-    seg_across = jnp.broadcast_to(seg, (rows, rows))
-    seg_down = jnp.transpose(seg_across)
+    return jnp.sum(jnp.where((starts <= place) & (place < ends), label, 0.0), axis=0, keepdims=True)
+
+
+def valid_rows(seg, rows):
+    return jnp.transpose(jnp.broadcast_to(jnp.where(seg > 0.0, 1.0, 0.0), (LANES, rows)))
+
+
+def masked_grad(og_ref, valid):
+    wide = og_ref.shape[1] // LANES
+    return (og_ref[...].astype(F32) * jnp.concatenate([valid] * wide, axis=1)).astype(BF16)
+
+
+def go_kernel(len_ref, dest_ref, og_ref, go_ref):
+    rows = og_ref.shape[0]
+    go_ref[...] = masked_grad(og_ref, valid_rows(segments(len_ref, dest_ref, rows), rows))
+
+
+def hold_kernel(table_ref, held_ref, sems):
+    parts = sems.shape[0]
+    step = table_ref.shape[0] // parts
+    blocks = [pl.ds(n * step, step) for n in range(parts)]
+    for copy in start_all([table_ref.at[b, :] for b in blocks], [held_ref.at[b, :] for b in blocks], sems):
+        copy.wait()
+
+
+def pos_bounds(rows, count):
+    return [max(1, rows // 2 ** (count - m)) for m in range(count)]
+
+
+def time_bounds(count):
+    return [float(4**m) for m in range(count)]
+
+
+def time_gaps(time_ref, rows):
     stamp = jnp.broadcast_to(time_ref[...].astype(F32), (rows, rows))
-    delta = jnp.transpose(stamp) - stamp
+    return jnp.transpose(stamp) - stamp
+
+
+def steps_passed(value, bounds):
+    total = jnp.where(value >= bounds[0], 1, 0)
+    for bound in bounds[1:]:
+        total = total + jnp.where(value >= bound, 1, 0)
+    return total
+
+
+def bias_index(seg, time_ref, rows, count):
+    across = jnp.broadcast_to(seg, (rows, rows))
+    down = jnp.transpose(across)
     dist = iota((rows, rows), 0) - iota((rows, rows), 1)
-    mask = (seg_across == seg_down) & (seg_down >= 0.0) & (dist >= 0)
-    valid = jnp.where(seg_down[:, 0:LANES] >= 0.0, 1.0, 0.0)
-    valid_ref[...] = valid
-    wide = og_ref.shape[1] // LANES
-    go = og_ref[...].astype(F32) * jnp.concatenate([valid] * wide, axis=1)
-    gob = go.astype(BF16)
-    go_ref[...] = gob
-    dmix_ref[...] = dot_nt(gob, wo_ref[...])
-    for g in range(heads):
-        bias = jnp.zeros((rows, rows), F32)
-        for m in range(count):
-            bias = bias + jnp.where(dist >= max(1, rows // 2 ** (count - m)), pos_ref[g, m], 0.0)
-            bias = bias + jnp.where(delta >= float(4**m), timew_ref[g, m], 0.0)
-        bias_ref[g] = jnp.where(mask, bias, MASKED)
+    near = steps_passed(dist, pos_bounds(rows, count))
+    late = steps_passed(time_gaps(time_ref, rows), time_bounds(count))
+    mask = (across == down) & (down > 0.0) & (dist >= 0)
+    return jnp.where(mask, near * (count + 1) + late, LANES - 1)
+
+
+def bias_table(pos_ref, timew_ref):
+    heads, count = pos_ref.shape
+    entry = iota((heads, LANES), 1)
+    near = entry // (count + 1)
+    late = entry - near * (count + 1)
+    table = jnp.zeros((heads, LANES), F32)
+    for m in range(count):
+        table = table + jnp.where(near > m, pos_ref[:, m : m + 1], 0.0)
+        table = table + jnp.where(late > m, timew_ref[:, m : m + 1], 0.0)
+    return jnp.where(entry == LANES - 1, MASKED, table)
+
+
+def look_up(table_row, index):
+    rows, cols = index.shape
+    spread = jnp.broadcast_to(table_row, (rows, LANES))
+    return jnp.concatenate(
+        [jnp.take_along_axis(spread, index[:, at : at + LANES], axis=1) for at in range(0, cols, LANES)], axis=1
+    )
 
 
 def norm_of(value):
@@ -206,9 +271,12 @@
     g2_ref,
     wo_ref,
     bo_ref,
-    bias_ref,
-    dmix_ref,
-    valid_ref,
+    len_ref,
+    dest_ref,
+    time_ref,
+    og_ref,
+    pos_ref,
+    timew_ref,
     lo_ref,
     n1_ref,
     y_ref,
@@ -221,8 +289,13 @@
     a_ref,
 ):
     rows, width = x_ref.shape
-    heads = bias_ref.shape[0]
+    heads, count = pos_ref.shape
     pairs = heads // 2
+    seg = segments(len_ref, dest_ref, rows)
+    valid = valid_rows(seg, rows)
+    dmix = dot_nt(masked_grad(og_ref, valid), wo_ref[...])
+    index = bias_index(seg, time_ref, rows, count)
+    table = bias_table(pos_ref, timew_ref)
     x = x_ref[...].astype(F32)
     xhat, _ = norm_of(x)
     n1 = (xhat * g1_ref[...]).astype(BF16)
@@ -249,7 +322,7 @@
         total = None
         for parity in range(2):
             g = pair * 2 + parity
-            s = dot_nt(half(q[:, cols], parity), k[:, cols]) * 0.125 + bias_ref[g]
+            s = dot_nt(half(q[:, cols], parity), k[:, cols]) * 0.125 + look_up(table[g : g + 1, :], index)
             sig = sigmoid(s)
             a = (s * sig).astype(BF16)
             a_ref[g] = a
@@ -264,9 +337,7 @@
     y = (n2 * u).astype(BF16)
     y_ref[...] = y
     branch = dot_nn(y, wo_ref[...]) + bo_ref[...]
-    valid = valid_ref[...]
     lo_ref[...] = (jnp.concatenate([valid] * (width // LANES), axis=1) * (x + branch)).astype(BF16)
-    dmix = dmix_ref[...]
     du = dmix * n2
     e2 = dmix * u
     g2g_ref[...] = jnp.sum(e2 * ohat, axis=0, keepdims=True)
@@ -318,8 +389,7 @@
 def small_kernel(count, ds_ref, time_ref, dh_ref, go_ref, g1g_ref, g2g_ref, out_ref):
     heads, rows, _ = ds_ref.shape
     width = go_ref.shape[1]
-    stamp = jnp.broadcast_to(time_ref[...].astype(F32), (rows, rows))
-    delta = jnp.transpose(stamp) - stamp
+    delta = time_gaps(time_ref, rows)
     dist = iota((rows, rows), 0) - iota((rows, rows), 1)
     out_ref[...] = jnp.zeros_like(out_ref)
     b_grad = jnp.sum(dh_ref[...].astype(F32), axis=0, keepdims=True)
@@ -332,8 +402,8 @@
     at = (at + 7) // 8 * 8
     lane = iota((heads, LANES), 1)
     for base, which, bounds in (
-        (at, dist, [max(1, rows // 2 ** (count - m)) for m in range(count)]),
-        (at + heads, delta, [float(4**m) for m in range(count)]),
+        (at, dist, pos_bounds(rows, count)),
+        (at + heads, delta, time_bounds(count)),
     ):
         result = jnp.zeros((heads, LANES), F32)
         done = {}
@@ -348,15 +418,16 @@
         out_ref[base : base + heads, :] = result
 
 
-def pack_kernel(
-    planes, columns, dh_ref, n1_ref, y_ref, go_ref, got_ref, got_go_ref, small_ref, *rest
-):
+def place_of(columns):
+    my_dp = lax.axis_index("dp")
+    return lax.rem(my_dp, columns), lax.div(my_dp, columns)
+
+
+def pack_kernel(planes, columns, dh_ref, n1_ref, y_ref, go_ref, got_ref, got_go_ref, small_ref, *rest):
     outs, (uv_ref, wo_ref) = rest[:columns], rest[columns:]
-    rows, width = n1_ref.shape
+    width = n1_ref.shape[1]
     core = lax.axis_index("table")
-    my_dp = lax.axis_index("dp")
-    my_xy = lax.rem(my_dp, columns)
-    my_z = lax.div(my_dp, columns)
+    my_xy, my_z = place_of(columns)
     half_cols = 2 * width
     half_y = width // 2
     dh = jnp.concatenate(
@@ -371,71 +442,46 @@
     go = jnp.concatenate([go_ref[...], got_go_ref[...]], axis=0)
     uv_ref[...] = dot_tn(n1, dh)
     wo_ref[...] = dot_tn(y, go)
-    chunks = planes * columns
-    tall = width // chunks
-    short = tall // 2
+    short = half_y // (planes * columns)
     for rel_xy in range(columns):
-        xy = jnp.bitwise_xor(my_xy, rel_xy)
         for rel_z in range(planes):
-            z = jnp.bitwise_xor(my_z, rel_z)
-            chunk = xy * planes + z
-            at = pl.multiple_of(chunk * tall, tall)
+            chunk = jnp.bitwise_xor(my_xy, rel_xy) * planes + jnp.bitwise_xor(my_z, rel_z)
             out = outs[rel_xy].at[rel_z]
-            out[:, 0:half_cols] = uv_ref[pl.ds(at, short), :].astype(BF16)
-            out[:, half_cols : 2 * half_cols] = uv_ref[
-                pl.ds(pl.multiple_of(at + short, short), short), :
-            ].astype(BF16)
+            for part in range(2):
+                at = pl.multiple_of((2 * chunk + part) * short, short)
+                out[:, part * half_cols : (part + 1) * half_cols] = uv_ref[pl.ds(at, short), :].astype(BF16)
             at = pl.multiple_of(chunk * short, short)
             out[:, 2 * half_cols : 2 * half_cols + width] = wo_ref[pl.ds(at, short), :].astype(BF16)
             out[:, 2 * half_cols + width :] = small_ref[pl.ds(at, short), :].astype(BF16)
 
 
-def unpack_kernel(
-    planes,
-    columns,
-    mine_ref,
-    theirs_ref,
-    uvqk_ref,
-    wout_ref,
-    b_ref,
-    g1_ref,
-    g2_ref,
-    bo_ref,
-    pos_ref,
-    time_ref,
-    small_ref,
-):
+def unpack_kernel(planes, columns, *refs):
+    pieces = refs[: 2 * columns]
+    uvqk_ref, wout_ref, b_ref, g1_ref, g2_ref, bo_ref, pos_ref, time_ref, small_ref = refs[2 * columns :]
     width = wout_ref.shape[0]
     core = lax.axis_index("table")
-    my_dp = lax.axis_index("dp")
-    my_xy = lax.rem(my_dp, columns)
-    my_z = lax.div(my_dp, columns)
+    my_xy, my_z = place_of(columns)
     half_cols = 2 * width
     half_y = width // 2
-    tall = width // (planes * columns)
-    short = tall // 2
+    short = half_y // (planes * columns)
+    wout_lanes = slice(2 * half_cols, 2 * half_cols + width)
+    small_lanes = slice(2 * half_cols + width, 2 * half_cols + width + LANES)
     for rel_xy in range(columns):
-        xy = jnp.bitwise_xor(my_xy, rel_xy)
         for rel_z in range(planes):
-            z = jnp.bitwise_xor(my_z, rel_z)
-            chunk = xy * planes + z
-            at = pl.multiple_of(chunk * short, short)
-            last = slice(2 * half_cols + width, 2 * half_cols + width + LANES)
-            small_ref[pl.ds(at, short), :] = (
-                mine_ref[rel_xy, rel_z, :, last].astype(F32) + theirs_ref[rel_xy, rel_z, :, last].astype(F32)
-            )
-            for ref, side in ((mine_ref, core), (theirs_ref, 1 - core)):
+            chunk = jnp.bitwise_xor(my_xy, rel_xy) * planes + jnp.bitwise_xor(my_z, rel_z)
+            mine, theirs = (pieces[which * columns + rel_xy].at[rel_z] for which in range(2))
+            for ref, side in ((mine, core), (theirs, 1 - core)):
                 cols = pl.ds(pl.multiple_of(side * half_cols, half_cols), half_cols)
-                at = pl.multiple_of(chunk * tall, tall)
-                uvqk_ref[pl.ds(at, short), cols] = ref[rel_xy, rel_z, :, 0:half_cols].astype(F32)
-                at = pl.multiple_of(chunk * tall + short, short)
-                uvqk_ref[pl.ds(at, short), cols] = ref[
-                    rel_xy, rel_z, :, half_cols : 2 * half_cols
-                ].astype(F32)
+                for part in range(2):
+                    at = pl.multiple_of((2 * chunk + part) * short, short)
+                    uvqk_ref[pl.ds(at, short), cols] = ref[
+                        :, part * half_cols : (part + 1) * half_cols
+                    ].astype(F32)
                 at = pl.multiple_of(side * half_y + chunk * short, short)
-                wout_ref[pl.ds(at, short), :] = ref[
-                    rel_xy, rel_z, :, 2 * half_cols : 2 * half_cols + width
-                ].astype(F32)
+                wout_ref[pl.ds(at, short), :] = ref[:, wout_lanes].astype(F32)
+            small_ref[pl.ds(pl.multiple_of(chunk * short, short), short), :] = mine[:, small_lanes].astype(
+                F32
+            ) + theirs[:, small_lanes].astype(F32)
     at = 0
     for out in (b_ref, g1_ref, g2_ref, bo_ref):
         for col in range(0, out.shape[1], LANES):
@@ -458,14 +504,12 @@
     return lax.ppermute(value, "dp", [(i, i ^ step) for i in range(size)])
 
 
-def staged_sum(pieces, planes, columns):
-    size = planes * columns
-    got = [xor_step(pieces[k], size, k) for k in range(1, columns)]
-    line = add_up(pieces[0], *got)
-    got = [xor_step(line[k], size, k * columns) for k in range(1, planes)]
-    own = add_up(line[0], *got)
-    line = jnp.stack([own] + [xor_step(own, size, k * columns) for k in range(1, planes)])
-    return jnp.stack([line] + [xor_step(line, size, k) for k in range(1, columns)])
+def reduce_step(pieces, size, stride):
+    return add_up(pieces[0], *(xor_step(pieces[k], size, k * stride) for k in range(1, len(pieces))))
+
+
+def gather_step(own, size, stride, peers):
+    return [own] + [xor_step(own, size, k * stride) for k in range(1, peers)]
 
 
 def swap_cores(value):
@@ -507,7 +551,7 @@
         and width % (32 * replicas) == 0
         and (2 * heads + SMALL_ROWS - 16) <= width // 2
     )
-    mb = 1 << 20
+    mb = MIB
 
     slot_row = token_request_slot.reshape(1, rows)
     time_row = timestamps.reshape(1, rows)
@@ -515,26 +559,33 @@
     msg = call(
         functools.partial(request_kernel, piece, cap),
         shape_of((devices, LANES), I32),
-        [VMEM] * 5,
+        [HBM] * 5,
         mb,
         mb // 8,
-    )(request_rows.reshape(devices, cap), slot_row, lengths, assignment, counts_2d)
+        scratch=(
+            pltpu.VMEM((cap, devices), I32),
+            pltpu.VMEM((1, rows), I32),
+            pltpu.VMEM(lengths.shape, I32),
+            pltpu.VMEM(lengths.shape, I32),
+            pltpu.VMEM(counts_2d.shape, I32),
+            pltpu.SemaphoreType.DMA((5,)),
+        ),
+        room=64,
+    )(request_rows.transpose(0, 2, 1).reshape(cap, devices), slot_row, lengths, assignment, counts_2d)
     asked = lax.all_to_all(msg.reshape(devices, 1, LANES), BOTH, 0, 0, tiled=True).reshape(devices, LANES)
-    bias, go, dmix, valid = call(
-        before_kernel,
-        (
-            shape_of((heads, rows, rows), F32),
-            shape_of((rows, width), BF16),
-            shape_of((rows, width), F32),
-            shape_of((rows, LANES), F32),
-        ),
-        [VMEM] * 5 + [SMEM] * 2,
-        1 << 30,
-        4 * mb,
-    )(lengths, assignment, time_row, out_grad, w_out, pos_weight, time_weight)
+    held = call(
+        hold_kernel,
+        shape_of(item_table.shape, BF16),
+        [HBM],
+        0,
+        8 * mb,
+        scratch=(pltpu.SemaphoreType.DMA((8,)),),
+    )(item_table)
+    asked, held = lax.optimization_barrier((asked, held))
     served = call(
         functools.partial(serve_kernel, cap), shape_of((slots, width), BF16), [VMEM] * 2, 1 << 30, 5 * mb
-    )(asked, item_table)
+    )(asked, held)
+    go = call(go_kernel, shape_of((rows, width), BF16), [VMEM] * 3, 64 * mb, mb)(lengths, assignment, out_grad)
     fetched = lax.all_to_all(served.reshape(devices, cap, width), BOTH, 0, 0, tiled=True)
     new_counts, log_q, asked_row = call(
         functools.partial(counts_kernel, cap, rows_dev * devices),
@@ -550,7 +601,11 @@
     home = call(take_kernel, shape_of((rows, width), BF16), [VMEM] * 2, 64 * mb, mb)(
         slot_row, fetched.reshape(slots, width)
     )
+    if staged:
+        got_go = swap_cores(go)
     x = lax.all_to_all(home.reshape(replicas, piece, width), "dp", 0, 0, tiled=True).reshape(rows, width)
+    if staged:
+        x, got_go = lax.optimization_barrier((x, got_go))
 
     half_cols = 2 * width
     g1, g2 = first_norm_gain.reshape(1, width), norm2_gain.reshape(1, width)
@@ -566,7 +621,7 @@
             shape_of((1, width), F32),
             shape_of((rows, msg_cols), BF16),
         ),
-        [VMEM] * 10,
+        [VMEM] * 13,
         2 << 30,
         8 * mb,
         scratch=(
@@ -574,6 +629,7 @@
             pltpu.VMEM((heads, rows, rows), F32),
             pltpu.VMEM((heads, rows, rows), BF16),
         ),
+        room=24,
     )(
         x,
         w_uvqk,
@@ -582,17 +638,38 @@
         g2,
         w_out,
         b_out.reshape(1, width),
-        bias,
-        dmix,
-        valid,
-    )
+        lengths,
+        assignment,
+        time_row,
+        out_grad,
+        pos_weight,
+        time_weight,
+    )
+    def home_again(dx):
+        return lax.all_to_all(dx.reshape(replicas, piece, width), "dp", 0, 0, tiled=True).reshape(rows, width)
+
+    def to_owners(back):
+        sums = call(slot_sum_kernel, shape_of((slots, width), BF16), [VMEM] * 2, 64 * mb, mb)(slot_row, back)
+        sums = lax.all_to_all(sums.reshape(devices, cap, width), BOTH, 0, 0, tiled=True)
+        return sums.reshape(slots, width)
+
+    def into_table(got_sums):
+        block = min(512, rows_dev)
+        return pl.pallas_call(
+            scatter_kernel,
+            grid=(rows_dev // block,),
+            out_shape=shape_of((rows_dev, width), F32),
+            in_specs=[pl.BlockSpec((8, slots), lambda i: (0, 0)), pl.BlockSpec((slots, width), lambda i: (0, 0))],
+            out_specs=pl.BlockSpec((block, width), lambda i: (i, 0)),
+            compiler_params=params(16),
+            cost_estimate=cost(1 << 30, 8 * mb),
+        )(asked_row, got_sums)
+
     if staged:
-        got_go = swap_cores(go)
         got = swap_cores(to_core)
     dx, g1_grad = call(
         dx_kernel, (shape_of((rows, width), BF16), shape_of((1, width), F32)), [VMEM] * 5, 1 << 29, 4 * mb
     )(dh, w_uvqk, x, g1, go)
-    back = lax.all_to_all(dx.reshape(replicas, piece, width), "dp", 0, 0, tiled=True).reshape(rows, width)
     small = call(
         functools.partial(small_kernel, count),
         shape_of((width // 2, LANES), F32),
@@ -602,17 +679,27 @@
     )(ds, time_row, dh, go, g1_grad, g2_grad)
     if staged:
         short = width // replicas // 2
-        pack_cols = 2 * half_cols + width + LANES
         pieces = call(
             functools.partial(pack_kernel, planes, columns),
-            tuple(shape_of((planes, short, pack_cols), BF16) for _ in range(columns)),
+            tuple(shape_of((planes, short, 5 * width + LANES), BF16) for _ in range(columns)),
             [VMEM] * 7,
             1 << 30,
             6 * mb,
             scratch=(pltpu.VMEM((width, half_cols), F32), pltpu.VMEM((width // 2, width), F32)),
         )(dh, n1, y, go, got, got_go, small)
-        mine = staged_sum(pieces, planes, columns)
-        theirs = swap_cores(mine)
+        dx, *pieces = lax.optimization_barrier((dx, *pieces))
+        back = home_again(dx)
+        line = reduce_step(pieces, replicas, 1)
+        line, back = lax.optimization_barrier((line, back))
+        got_sums = to_owners(back)
+        own = reduce_step(line, replicas, columns)
+        line = jnp.stack(gather_step(own, replicas, columns, planes))
+        line, got_sums = lax.optimization_barrier((line, got_sums))
+        table_grad = into_table(got_sums)
+        mine = gather_step(line, replicas, 1, columns)
+        theirs = [swap_cores(line)]
+        mine, theirs, table_grad = lax.optimization_barrier((mine, theirs, table_grad))
+        theirs += [swap_cores(piece) for piece in mine[1:]]
         w_uvqk_sum, w_out_sum, b_sum, g1_sum, g2_sum, bo_sum, pos_sum, time_sum = call(
             functools.partial(unpack_kernel, planes, columns),
             (
@@ -625,12 +712,13 @@
                 shape_of((heads, count), F32),
                 shape_of((heads, count), F32),
             ),
-            [VMEM] * 2,
+            [VMEM] * (2 * columns),
             mb,
             8 * mb,
             scratch=(pltpu.VMEM((width // 2, LANES), F32),),
-        )(mine, theirs)
+        )(*mine, *theirs)
     else:
+        table_grad = into_table(to_owners(home_again(dx)))
         w_uvqk_sum, w_out_sum, parts = lax.psum((dot_tn(n1, dh), dot_tn(y, go), small[0:SMALL_ROWS]), BOTH)
         at = 4 * width // LANES
         step = width // LANES
@@ -639,18 +727,6 @@
         at = (at + 3 * step + 7) // 8 * 8
         pos_sum = parts[at : at + heads, 0:count]
         time_sum = parts[at + heads : at + 2 * heads, 0:count]
-    sums = call(slot_sum_kernel, shape_of((slots, width), BF16), [VMEM] * 2, 64 * mb, mb)(slot_row, back)
-    got_sums = lax.all_to_all(sums.reshape(devices, cap, width), BOTH, 0, 0, tiled=True).reshape(slots, width)
-    block = min(512, rows_dev)
-    table_grad = pl.pallas_call(
-        scatter_kernel,
-        grid=(rows_dev // block,),
-        out_shape=shape_of((rows_dev, width), F32),
-        in_specs=[pl.BlockSpec((8, slots), lambda i: (0, 0)), pl.BlockSpec((slots, width), lambda i: (0, 0))],
-        out_specs=pl.BlockSpec((block, width), lambda i: (i, 0)),
-        compiler_params=PARAMS,
-        cost_estimate=cost(1 << 30, 8 * mb),
-    )(asked_row, got_sums)
     return (
         layer_out,
         table_grad,

time: 156 us -> 131 us (0.84)
  blocking collectives: 40.6 us -> 13.9 us
  starting transfers between devices: 22 us -> 33.6 us
  waiting for transfers between devices: 55.5 us -> 48.3 us
  Pallas kernels: 28.9 us -> 26.2 us
    all_to_all x2 -> x0, blocking collectives: 28.2 us -> none  [the longest x1 14.2 us: on_device(): lax.all_to_all(msg.reshape(devices, 1, LANES), BOTH, 0, 0, tiled=True)]
    all_to_all x1 -> x3, starting transfers between devices: 2.59 us -> 14.1 us  [the longest x1 7.3 us: on_device(): lax.all_to_all(msg.reshape(devices, 1, LANES), BOTH, 0, 0, tiled=True)]
    all_to_all x1 -> x3, waiting for transfers between devices: 9.45 us -> 2.48 us  [the longest x1 2.39 us: on_device(): lax.all_to_all(msg.reshape(devices, 1, LANES), BOTH, 0, 0, tiled=True)]
    ppermute x12, waiting for transfers between devices: 40.9 us -> 34.8 us  [xor_step(): return lax.ppermute(value, 'dp', [(i, i ^ step) for i in range(size)])]
    ppermute x3 -> x6, waiting for transfers between devices: 0.01 us -> 3.65 us  [swap_cores(): return lax.ppermute(value, 'table', [(0, 1), (1, 0)])]
    pallas_call x3 -> x4, Pallas kernels: 9.75 us -> 6.94 us  [the longest x1 5.41 us: into_table(): pl.pallas_call(scatter_kernel, grid=(rows_dev // block,), out_shape=shape...]
    all_to_all x1, waiting for transfers between devices: 5.14 us -> 7.42 us  [on_device(): lax.all_to_all(home.reshape(replicas, piece, width), 'dp', 0, 0, tiled=True)]
    pallas_call x1, Pallas kernels: 7.06 us -> 5.3 us  [on_device(): call(functools.partial(layer_kernel, staged), (shape_of((rows, width), BF...]
  transfers between devices with their start and end apart: 17 -> 22, of which waited for: 12 -> 17; matrix products, arithmetic and copies ran while one was open for 0% -> 0% of each run, Pallas kernels for 10% -> 10%
where the time goes in v2:
time: 131 us
  waiting for transfers between devices  48.3 us (37%)
  starting transfers between devices  33.6 us (26%)
  Pallas kernels  26.2 us (20%)
  blocking collectives  13.9 us (11%)
  local copies, waits for them, and re-layouts  7.18 us (5%)
    ppermute x12, waiting for transfers between devices, xor_step(): return lax.ppermute(value, 'dp', [(i, i ^ step) for i in range(size)])  34.8 us
    ppermute x12, starting transfers between devices, xor_step(): return lax.ppermute(value, 'dp', [(i, i ^ step) for i in range(size)])  15.1 us
    all_to_all x1, blocking collectives, on_device(): lax.all_to_all(served.reshape(devices, cap, width), BOTH, 0, 0, tiled=True)  13.9 us
    all_to_all x1, waiting for transfers between devices, on_device(): lax.all_to_all(home.reshape(replicas, piece, width), 'dp', 0, 0, tiled=True)  7.42 us
    all_to_all x1, starting transfers between devices, on_device(): lax.all_to_all(msg.reshape(devices, 1, LANES), BOTH, 0, 0, tiled=True)  7.3 us
    unnamed x38, local copies, waits for them, and re-layouts  7.16 us
    pallas_call x1, Pallas kernels, into_table(): pl.pallas_call(scatter_kernel, grid=(rows_dev // block,), out_shape=shape...  5.41 us
    pallas_call x1, Pallas kernels, on_device(): call(functools.partial(layer_kernel, staged), (shape_of((rows, width), BF...  5.3 us
  transfers between devices with their start and end apart: 22, of which 17 were waited for; matrix products, arithmetic and copies ran while one was open for 0% of the time, Pallas kernels for 10%

profile of v2, /device:TPU:0, one launch (start us, length us, event | category | flops | bytes accessed | tf_op | source)
XLA Modules:
  0.0 130.5 jit_solution(17411061938682779296)
XLA Ops:
  0.6 1.7 %shard_map.247 = s32[32,128]{1,0:T(8,128)} custom-call(s32[8,32]{1,0:T(8,128)} %bitcast.66, s32[1,256]{1,0:T(1,128)} %bitcast.51, s32[1,64]{1,0:T(1,128)} %len_ref.3, s32[1,64]{1,0:T(1,128)} %dest_ref.3, s32[32,128]{1,0:T(8,128)} %bitcast.49), custom_call_target="tpu_custom_call" | custom-call | flops 1048576 | bytes 131072 | tf_op jit(solution)/shard_map/pallas_call | solution.py:559
  2.3 7.3 %all-to-all-start = ((s32[32,1,128]{2,1,0:T(1,128)}), s32[32,1,128]{2,1,0:T(1,128)S(1)}, u32[]{:S(2)}, u32[]{:S(2)}) async-start(s32[32,1,128]{2,1,0:T(1,128)} %bitcast.65), calls=%async_computation | async-start | bytes 32768 | tf_op jit(solution)/shard_map/all_to_all | solution.py:575
  9.6 2.2 %copy-done.2 = bf16[4096,512]{1,0:T(8,128)(2,1)S(1)} copy-done((bf16[4096,512]{1,0:T(8,128)(2,1)S(1)}, bf16[4096,512]{1,0:T(8,128)(2,1)}, u32[]{:S(2)}) %copy-start.2) | copy-done | bytes 4194328
  12.3 2.0 %copy-done = bf16[4096,512]{1,0:T(8,128)(2,1)} copy-done((bf16[4096,512]{1,0:T(8,128)(2,1)}, bf16[4096,512]{1,0:T(8,128)(2,1)S(1)}, u32[]{:S(2)}) %copy-start) | copy-done | bytes 4194328
  14.3 2.4 %all-to-all-done = s32[32,1,128]{2,1,0:T(1,128)S(1)} async-done(((s32[32,1,128]{2,1,0:T(1,128)}), s32[32,1,128]{2,1,0:T(1,128)S(1)}, u32[]{:S(2)}, u32[]{:S(2)}) %all-to-all-start) | async-done | bytes 16416 | tf_op jit(solution)/shard_map/all_to_all | solution.py:575
  16.7 2.2 %copy-done.1 = bf16[4096,512]{1,0:T(8,128)(2,1)S(1)} copy-done((bf16[4096,512]{1,0:T(8,128)(2,1)S(1)}, bf16[4096,512]{1,0:T(8,128)(2,1)}, u32[]{:S(2)}) %copy-start.1) | copy-done | bytes 4194328
  18.9 1.9 %shard_map.249 = bf16[256,512]{1,0:T(8,128)(2,1)S(1)} custom-call(s32[32,128]{1,0:T(8,128)S(1)} %bitcast.47, bf16[4096,512]{1,0:T(8,128)(2,1)S(1)} %copy-done.1), custom_call_target="tpu_custom_call" | custom-call | flops 1073741824 | bytes 5242880 | tf_op jit(solution)/shard_map/pallas_call | solution.py:585
  20.8 13.9 %all_to_all.25 = bf16[32,8,512]{2,1,0:T(8,128)(2,1)S(1)} all-to-all(bf16[32,8,512]{2,1,0:T(8,128)(2,1)S(1)} %bitcast.44), channel_id=1, replica_groups=mesh['dp'=16,'table'=2] {'dp','table'}, dimensions={0} | all-to-all | bytes 524288 | tf_op jit(solution)/shard_map/all_to_all | solution.py:589
  35.6 3.7 %all-to-all-start.2 = ((bf16[16,16,512]{2,1,0:T(8,128)(2,1)}), bf16[16,16,512]{2,1,0:T(8,128)(2,1)S(1)}, u32[]{:S(2)}, u32[]{:S(2)}) async-start(bf16[16,16,512]{2,1,0:T(8,128)(2,1)} %bitcast.9), calls=%async_computation.2 | async-start | bytes 524288 | tf_op jit(solution)/shard_map/all_to_all | solution.py:606
  39.7 1.5 %collective-permute-done.got_go_ref = bf16[256,512]{1,0:T(8,128)(2,1)S(1)} collective-permute-done((bf16[256,512]{1,0:T(8,128)(2,1)S(1)}, bf16[256,512]{1,0:T(8,128)(2,1)S(1)}, u32[]{:S(2)}, u32[]{:S(2)}) %collective-permute-start) | collective-permute-done | bytes 262176 | tf_op jit(solution)/shard_map/ppermute | solution.py:516
  41.9 7.4 %all-to-all-done.2 = bf16[16,16,512]{2,1,0:T(8,128)(2,1)S(1)} async-done(((bf16[16,16,512]{2,1,0:T(8,128)(2,1)}), bf16[16,16,512]{2,1,0:T(8,128)(2,1)S(1)}, u32[]{:S(2)}, u32[]{:S(2)}) %all-to-all-start.2) | async-done | bytes 262176 | tf_op jit(solution)/shard_map/all_to_all | solution.py:606
  49.4 5.3 %shard_map.252 = (bf16[256,512]{1,0:T(8,128)(2,1)}, bf16[256,512]{1,0:T(8,128)(2,1)S(1)}, bf16[256,512]{1,0:T(8,128)(2,1)S(1)}, bf16[256,2048]{1,0:T(8,128)(2,1)...) custom-call(bf16[256,512]{1,0:T(8,128)(2,1)S(1)} %bitcast.42, ...), custom_call_target="tpu_custom_call" | custom-call | flops 2147483648 | bytes 8388608 | tf_op jit(solution)/shard_map/pallas_call | solution.py:613
  54.8 1.6 %shard_map.253 = (bf16[256,512]{1,0:T(8,128)(2,1)}, f32[1,512]{1,0:T(1,128)S(1)}) custom-call(bf16[256,2048]{1,0:T(8,128)(2,1)S(1)} %get-tuple-element.59.dh_ref, bf16[512,2048]{1,0:T(8,128)(2,1)S(1)} %copy-done.3, bf16[256,512]{1,0:T(8,128)(2,1)S(1)} %bitcast.43, f32[1,512]{1,0:T(1,128)S(1)} %bitcast.55, bf16[256,512]{1,0:T(8,128)(2,1)S(1)} %shard_map.251.go_ref), custom_call_target="tpu_custom_call" | custom-call | flops 536870912 | bytes 4194304 | tf_op jit(solution)/shard_map/pallas_call | solution.py:670
  56.4 3.4 %shard_map.254.small_ref = f32[256,128]{1,0:T(8,128)S(1)} custom-call(bf16[8,256,256]{2,1,0:T(8,128)(2,1)S(1)} %get-tuple-element.65.ds_ref, s32[1,256]{1,0:T(1,128)S(1)} %bitcast.57, bf16[256,2048]{1,0:T(8,128)(2,1)S(1)} %get-tuple-element.59.dh_ref, bf16[256,512]{1,0:T(8,128)(2,1)S(1)} %shard_map.251.go_ref, f32[1,512]{1,0:T(1,128)S(1)} %get-tuple-element.66.g1g_ref, ...), custom_call_target="tpu_custom_call" | custom-call | flops 268435456 | bytes 2097152 | tf_op jit(solution)/shard_map/pallas_call | solution.py:673
  62.3 2.0 %collective-permute-start.4 = (bf16[4,16,2688]{2,1,0:T(8,128)(2,1)S(1)}, bf16[4,16,2688]{2,1,0:T(8,128)(2,1)S(1)}, u32[]{:S(2)}, u32[]{:S(2)}) collective-permute-start(bf16[4,16,2688]{2,1,0:T(8,128)(2,1)S(1)} %get-tuple-element.75), channel_id=1, source_target_pairs={{0,6},{2,4},{4,2},{6,0},{8,14},{10,12},{12,10},{14,8},{16,22},{18,... | collective-permute-start | bytes 1032200 | tf_op jit(solution)/shard_map/ppermute | solution.py:504
  64.3 3.5 %all-to-all-start.3 = ((bf16[16,16,512]{2,1,0:T(8,128)(2,1)}), bf16[16,16,512]{2,1,0:T(8,128)(2,1)S(1)}, u32[]{:S(2)}, u32[]{:S(2)}) async-start(bf16[16,16,512]{2,1,0:T(8,128)(2,1)} %bitcast.16), calls=%async_computation.3 | async-start | bytes 524288 | tf_op jit(solution)/shard_map/all_to_all | solution.py:649
  67.8 4.2 %collective-permute-done.2 = bf16[4,16,2688]{2,1,0:T(8,128)(2,1)S(1)} collective-permute-done((bf16[4,16,2688]{2,1,0:T(8,128)(2,1)S(1)}, bf16[4,16,2688]{2,1,0:T(8,128)(2,1)S(1)}, u32[]{:S(2)}, u32[]{:S(2)}) %collective-permute-start.2) | collective-permute-done | bytes 344096 | tf_op jit(solution)/shard_map/ppermute | solution.py:504
  72.0 9.5 %collective-permute-done.3 = bf16[4,16,2688]{2,1,0:T(8,128)(2,1)S(1)} collective-permute-done((bf16[4,16,2688]{2,1,0:T(8,128)(2,1)S(1)}, bf16[4,16,2688]{2,1,0:T(8,128)(2,1)S(1)}, u32[]{:S(2)}, u32[]{:S(2)}) %collective-permute-start.3) | collective-permute-done | bytes 344096 | tf_op jit(solution)/shard_map/ppermute | solution.py:504
  83.0 1.5 %collective-permute-start.7 = (bf16[16,2688]{1,0:T(8,128)(2,1)S(1)}, bf16[16,2688]{1,0:T(8,128)(2,1)S(1)}, u32[]{:S(2)}, u32[]{:S(2)}) collective-permute-start(bf16[16,2688]{1,0:T(8,128)(2,1)S(1)} %get-tuple-element.99), channel_id=1, source_target_pairs={{0,24},{2,26},{4,28},{6,30},{8,16},{10,18},{12,20},{14,22},{16,8},... | collective-permute-start | bytes 258056 | tf_op jit(solution)/shard_map/ppermute | solution.py:504
  86.4 3.2 %all-to-all-start.4 = ((bf16[32,8,512]{2,1,0:T(8,128)(2,1)}), bf16[32,8,512]{2,1,0:T(8,128)(2,1)S(1)}, u32[]{:S(2)}, u32[]{:S(2)}) async-start(bf16[32,8,512]{2,1,0:T(8,128)(2,1)} %bitcast.26), calls=%async_computation.4 | async-start | bytes 524288 | tf_op jit(solution)/shard_map/all_to_all | solution.py:653
  89.8 3.3 %collective-permute-done.6 = bf16[16,2688]{1,0:T(8,128)(2,1)S(1)} collective-permute-done((bf16[16,2688]{1,0:T(8,128)(2,1)S(1)}, bf16[16,2688]{1,0:T(8,128)(2,1)S(1)}, u32[]{:S(2)}, u32[]{:S(2)}) %collective-permute-start.6) | collective-permute-done | bytes 86048 | tf_op jit(solution)/shard_map/ppermute | solution.py:504
  93.2 1.6 %collective-permute-start.10 = (bf16[16,2688]{1,0:T(8,128)(2,1)S(1)}, bf16[16,2688]{1,0:T(8,128)(2,1)S(1)}, u32[]{:S(2)}, u32[]{:S(2)}) collective-permute-start(bf16[16,2688]{1,0:T(8,128)(2,1)S(1)} %fusion.2), channel_id=1, source_target_pairs={{0,24},{2,26},{4,28},{6,30},{8,16},{10,18},{12,20},{14,22},{16,8},... | collective-permute-start | bytes 258056 | tf_op jit(solution)/shard_map/ppermute | solution.py:504
  94.8 2.8 %collective-permute-start.8 = (bf16[16,2688]{1,0:T(8,128)(2,1)S(1)}, bf16[16,2688]{1,0:T(8,128)(2,1)S(1)}, u32[]{:S(2)}, u32[]{:S(2)}) collective-permute-start(bf16[16,2688]{1,0:T(8,128)(2,1)S(1)} %fusion.2), channel_id=1, source_target_pairs={{0,8},{2,10},{4,12},{6,14},{8,0},{10,2},{12,4},{14,6},{16,24},{18,... | collective-permute-start | bytes 258056 | tf_op jit(solution)/shard_map/ppermute | solution.py:504
  97.6 3.3 %collective-permute-done.10 = bf16[16,2688]{1,0:T(8,128)(2,1)S(1)} collective-permute-done((bf16[16,2688]{1,0:T(8,128)(2,1)S(1)}, bf16[16,2688]{1,0:T(8,128)(2,1)S(1)}, u32[]{:S(2)}, u32[]{:S(2)}) %collective-permute-start.10) | collective-permute-done | bytes 86048 | tf_op jit(solution)/shard_map/ppermute | solution.py:504
  100.9 5.5 %collective-permute-done.9 = bf16[16,2688]{1,0:T(8,128)(2,1)S(1)} collective-permute-done((bf16[16,2688]{1,0:T(8,128)(2,1)S(1)}, bf16[16,2688]{1,0:T(8,128)(2,1)S(1)}, u32[]{:S(2)}, u32[]{:S(2)}) %collective-permute-start.9) | collective-permute-done | bytes 86048 | tf_op jit(solution)/shard_map/ppermute | solution.py:504
  106.6 2.5 %collective-permute-start.13 = (bf16[4,16,2688]{2,1,0:T(8,128)(2,1)S(1)}, bf16[4,16,2688]{2,1,0:T(8,128)(2,1)S(1)}, u32[]{:S(2)}, u32[]{:S(2)}) collective-permute-start(bf16[4,16,2688]{2,1,0:T(8,128)(2,1)S(1)} %pad_maximum_fusion.refs_0_), channel_id=1, source_target_pairs={{0,6},{2,4},{4,2},{6,0},{8,14},{10,12},{12,10},{14,8},{16,22},{18,... | collective-permute-start | bytes 1032200 | tf_op jit(solution)/shard_map/ppermute | solution.py:504
  110.1 1.1 shard_map.257
  111.3 5.4 %shard_map.258 = f32[4096,512]{1,0:T(8,128)} custom-call(f32[8,256]{1,0:T(8,128)S(1)} %get-tuple-element.80.row_ref, bf16[256,512]{1,0:T(8,128)(2,1)S(1)} %bitcast.41), custom_call_target="tpu_custom_call" | custom-call | flops 1073741824 | bytes 8388608 | tf_op jit(solution)/shard_map/pallas_call | solution.py:658
  116.7 1.8 %collective-permute-done.13.refs_3_ = bf16[4,16,2688]{2,1,0:T(8,128)(2,1)S(1)} collective-permute-done((bf16[4,16,2688]{2,1,0:T(8,128)(2,1)S(1)}, bf16[4,16,2688]{2,1,0:T(8,128)(2,1)S(1)}, u32[]{:S(2)}, u32[]{:S(2)}) %collective-permute-start.13) | collective-permute-done | bytes 344096 | tf_op jit(solution)/shard_map/ppermute | solution.py:504
  118.4 6.9 %collective-permute-done.12.refs_2_ = bf16[4,16,2688]{2,1,0:T(8,128)(2,1)S(1)} collective-permute-done((bf16[4,16,2688]{2,1,0:T(8,128)(2,1)S(1)}, bf16[4,16,2688]{2,1,0:T(8,128)(2,1)S(1)}, u32[]{:S(2)}, u32[]{:S(2)}) %collective-permute-start.12) | collective-permute-done | bytes 344096 | tf_op jit(solution)/shard_map/ppermute | solution.py:504
  125.9 1.1 collective-permute-done.15.refs_5_
  128.0 2.5 %shard_map.259 = (f32[512,2048]{1,0:T(8,128)}, f32[512,512]{1,0:T(8,128)}, f32[1,2048]{1,0:T(1,128)}, f32[1,512]{1,0:T(1,128)}, f32[1,512]{1,0:T(1,128)}, /*inde...) custom-call(bf16[4,16,2688]{2,1,0:T(8,128)(2,1)S(1)} %pad_maximum_fusion.refs_0_, ...), custom_call_target="tpu_custom_call" | custom-call | flops 1048576 | bytes 8388608 | tf_op jit(solution)/shard_map/pallas_call | solution.py:703
  (68 shorter events, 11.4 us)
Async XLA Ops:
  2.3 14.4 %all-to-all-start = ((s32[32,1,128]{2,1,0:T(1,128)}), s32[32,1,128]{2,1,0:T(1,128)S(1)}, u32[]{:S(2)}, u32[]{:S(2)}) async-start(s32[32,1,128]{2,1,0:T(1,128)} %bitcast.65), calls=%async_computation | async-start | bytes 32768 | tf_op jit(solution)/shard_map/all_to_all | solution.py:575
  11.8 37.5 %copy-start.3 = (bf16[512,2048]{1,0:T(8,128)(2,1)S(1)}, bf16[512,2048]{1,0:T(8,128)(2,1)}, u32[]{:S(2)}) copy-start(bf16[512,2048]{1,0:T(8,128)(2,1)} %w_ref.3) | copy-start | bytes 6291460
  11.8 37.5 %copy-start.7 = (f32[512]{0:T(512)S(1)}, f32[512]{0:T(512)}, u32[]{:S(2)}) copy-start(f32[512]{0:T(512)} %param.23) | copy-start | bytes 6148
  11.8 37.5 %copy-start.10 = (s32[256]{0:T(256)S(1)}, s32[256]{0:T(256)}, u32[]{:S(2)}) copy-start(s32[256]{0:T(256)} %param.21) | copy-start | bytes 3076
  11.8 37.5 %copy-start.11 = (bf16[512,512]{1,0:T(8,128)(2,1)S(1)}, bf16[512,512]{1,0:T(8,128)(2,1)}, u32[]{:S(2)}) copy-start(bf16[512,512]{1,0:T(8,128)(2,1)} %wo_ref.1) | copy-start | bytes 1572868
  11.9 37.5 %copy-start.14 = (f32[2048]{0:T(1024)S(1)}, f32[2048]{0:T(1024)}, u32[]{:S(2)}) copy-start(f32[2048]{0:T(1024)} %param.25) | copy-start | bytes 24580
  11.9 37.5 %copy-start.15 = (f32[8,10]{1,0:T(8,128)S(1)}, f32[8,10]{1,0:T(8,128)}, u32[]{:S(2)}) copy-start(f32[8,10]{1,0:T(8,128)} %pos_ref.1) | copy-start | bytes 964
  11.9 37.5 %copy-start.16 = (f32[8,10]{1,0:T(8,128)S(1)}, f32[8,10]{1,0:T(8,128)}, u32[]{:S(2)}) copy-start(f32[8,10]{1,0:T(8,128)} %timew_ref.1) | copy-start | bytes 964
  11.9 37.5 %copy-start.17 = (f32[512]{0:T(512)S(1)}, f32[512]{0:T(512)}, u32[]{:S(2)}) copy-start(f32[512]{0:T(512)} %param.26) | copy-start | bytes 6148
  11.9 37.5 %copy-start.18 = (f32[512]{0:T(512)S(1)}, f32[512]{0:T(512)}, u32[]{:S(2)}) copy-start(f32[512]{0:T(512)} %param.28) | copy-start | bytes 6148
  35.6 13.7 %all-to-all-start.2 = ((bf16[16,16,512]{2,1,0:T(8,128)(2,1)}), bf16[16,16,512]{2,1,0:T(8,128)(2,1)S(1)}, u32[]{:S(2)}, u32[]{:S(2)}) async-start(bf16[16,16,512]{2,1,0:T(8,128)(2,1)} %bitcast.9), calls=%async_computation.2 | async-start | bytes 524288 | tf_op jit(solution)/shard_map/all_to_all | solution.py:606
  39.6 1.6 %collective-permute-start = (bf16[256,512]{1,0:T(8,128)(2,1)S(1)}, bf16[256,512]{1,0:T(8,128)(2,1)S(1)}, u32[]{:S(2)}, u32[]{:S(2)}) collective-permute-start(bf16[256,512]{1,0:T(8,128)(2,1)S(1)} %shard_map.251.go_ref), channel_id=1, source_target_pairs={{0,1},{1,0},{2,3},{3,2},{4,5},{5,4},{6,7},{7,6},{8,9},{9,8},{10,11... | collective-permute-start | bytes 786440 | tf_op jit(solution)/shard_map/ppermute | solution.py:516
  54.7 5.1 %collective-permute-start.1 = (bf16[256,1792]{1,0:T(8,128)(2,1)S(1)}, bf16[256,1792]{1,0:T(8,128)(2,1)S(1)}, u32[]{:S(2)}, u32[]{:S(2)}) collective-permute-start(bf16[256,1792]{1,0:T(8,128)(2,1)S(1)} %get-tuple-element.63), channel_id=1, source_target_pairs={{0,1},{1,0},{2,3},{3,2},{4,5},{5,4},{6,7},{7,6},{8,9},{9,8},{10,11... | collective-permute-start | bytes 2752520 | tf_op jit(solution)/shard_map/ppermute | solution.py:516
  59.8 50.4 %copy-start.5 = (s32[4096]{0:T(1024)S(1)}, s32[4096]{0:T(1024)}, u32[]{:S(2)}) copy-start(s32[4096]{0:T(1024)} %param.22) | copy-start | bytes 49156
  60.7 11.3 %collective-permute-start.2 = (bf16[4,16,2688]{2,1,0:T(8,128)(2,1)S(1)}, bf16[4,16,2688]{2,1,0:T(8,128)(2,1)S(1)}, u32[]{:S(2)}, u32[]{:S(2)}) collective-permute-start(bf16[4,16,2688]{2,1,0:T(8,128)(2,1)S(1)} %get-tuple-element.73), channel_id=1, source_target_pairs={{0,2},{2,0},{4,6},{6,4},{8,10},{10,8},{12,14},{14,12},{16,18},{18,... | collective-permute-start | bytes 1032200 | tf_op jit(solution)/shard_map/ppermute | solution.py:504
  61.6 19.9 %collective-permute-start.3 = (bf16[4,16,2688]{2,1,0:T(8,128)(2,1)S(1)}, bf16[4,16,2688]{2,1,0:T(8,128)(2,1)S(1)}, u32[]{:S(2)}, u32[]{:S(2)}) collective-permute-start(bf16[4,16,2688]{2,1,0:T(8,128)(2,1)S(1)} %get-tuple-element.74), channel_id=1, source_target_pairs={{0,4},{2,6},{4,0},{6,2},{8,12},{10,14},{12,8},{14,10},{16,20},{18,... | collective-permute-start | bytes 1032200 | tf_op jit(solution)/shard_map/ppermute | solution.py:504
  62.3 19.4 %collective-permute-start.4 = (bf16[4,16,2688]{2,1,0:T(8,128)(2,1)S(1)}, bf16[4,16,2688]{2,1,0:T(8,128)(2,1)S(1)}, u32[]{:S(2)}, u32[]{:S(2)}) collective-permute-start(bf16[4,16,2688]{2,1,0:T(8,128)(2,1)S(1)} %get-tuple-element.75), channel_id=1, source_target_pairs={{0,6},{2,4},{4,2},{6,0},{8,14},{10,12},{12,10},{14,8},{16,22},{18,... | collective-permute-start | bytes 1032200 | tf_op jit(solution)/shard_map/ppermute | solution.py:504
  64.3 17.7 %all-to-all-start.3 = ((bf16[16,16,512]{2,1,0:T(8,128)(2,1)}), bf16[16,16,512]{2,1,0:T(8,128)(2,1)S(1)}, u32[]{:S(2)}, u32[]{:S(2)}) async-start(bf16[16,16,512]{2,1,0:T(8,128)(2,1)} %bitcast.16), calls=%async_computation.3 | async-start | bytes 524288 | tf_op jit(solution)/shard_map/all_to_all | solution.py:649
  81.9 7.7 %collective-permute-start.5 = (bf16[16,2688]{1,0:T(8,128)(2,1)S(1)}, bf16[16,2688]{1,0:T(8,128)(2,1)S(1)}, u32[]{:S(2)}, u32[]{:S(2)}) collective-permute-start(bf16[16,2688]{1,0:T(8,128)(2,1)S(1)} %get-tuple-element.98), channel_id=1, source_target_pairs={{0,8},{2,10},{4,12},{6,14},{8,0},{10,2},{12,4},{14,6},{16,24},{18,... | collective-permute-start | bytes 258056 | tf_op jit(solution)/shard_map/ppermute | solution.py:504
  83.0 6.9 %collective-permute-start.7 = (bf16[16,2688]{1,0:T(8,128)(2,1)S(1)}, bf16[16,2688]{1,0:T(8,128)(2,1)S(1)}, u32[]{:S(2)}, u32[]{:S(2)}) collective-permute-start(bf16[16,2688]{1,0:T(8,128)(2,1)S(1)} %get-tuple-element.99), channel_id=1, source_target_pairs={{0,24},{2,26},{4,28},{6,30},{8,16},{10,18},{12,20},{14,22},{16,8},... | collective-permute-start | bytes 258056 | tf_op jit(solution)/shard_map/ppermute | solution.py:504
  84.5 8.6 %collective-permute-start.6 = (bf16[16,2688]{1,0:T(8,128)(2,1)S(1)}, bf16[16,2688]{1,0:T(8,128)(2,1)S(1)}, u32[]{:S(2)}, u32[]{:S(2)}) collective-permute-start(bf16[16,2688]{1,0:T(8,128)(2,1)S(1)} %get-tuple-element.100), channel_id=1, source_target_pairs={{0,16},{2,18},{4,20},{6,22},{8,24},{10,26},{12,28},{14,30},{16,0},... | collective-permute-start | bytes 258056 | tf_op jit(solution)/shard_map/ppermute | solution.py:504
  86.4 20.1 %all-to-all-start.4 = ((bf16[32,8,512]{2,1,0:T(8,128)(2,1)}), bf16[32,8,512]{2,1,0:T(8,128)(2,1)S(1)}, u32[]{:S(2)}, u32[]{:S(2)}) async-start(bf16[32,8,512]{2,1,0:T(8,128)(2,1)} %bitcast.26), calls=%async_computation.4 | async-start | bytes 524288 | tf_op jit(solution)/shard_map/all_to_all | solution.py:653
  93.2 7.7 %collective-permute-start.10 = (bf16[16,2688]{1,0:T(8,128)(2,1)S(1)}, bf16[16,2688]{1,0:T(8,128)(2,1)S(1)}, u32[]{:S(2)}, u32[]{:S(2)}) collective-permute-start(bf16[16,2688]{1,0:T(8,128)(2,1)S(1)} %fusion.2), channel_id=1, source_target_pairs={{0,24},{2,26},{4,28},{6,30},{8,16},{10,18},{12,20},{14,22},{16,8},... | collective-permute-start | bytes 258056 | tf_op jit(solution)/shard_map/ppermute | solution.py:504
  94.8 11.6 %collective-permute-start.9 = (bf16[16,2688]{1,0:T(8,128)(2,1)S(1)}, bf16[16,2688]{1,0:T(8,128)(2,1)S(1)}, u32[]{:S(2)}, u32[]{:S(2)}) collective-permute-start(bf16[16,2688]{1,0:T(8,128)(2,1)S(1)} %fusion.2), channel_id=1, source_target_pairs={{0,16},{2,18},{4,20},{6,22},{8,24},{10,26},{12,28},{14,30},{16,0},... | collective-permute-start | bytes 258056 | tf_op jit(solution)/shard_map/ppermute | solution.py:504
  94.8 11.6 %collective-permute-start.8 = (bf16[16,2688]{1,0:T(8,128)(2,1)S(1)}, bf16[16,2688]{1,0:T(8,128)(2,1)S(1)}, u32[]{:S(2)}, u32[]{:S(2)}) collective-permute-start(bf16[16,2688]{1,0:T(8,128)(2,1)S(1)} %fusion.2), channel_id=1, source_target_pairs={{0,8},{2,10},{4,12},{6,14},{8,0},{10,2},{12,4},{14,6},{16,24},{18,... | collective-permute-start | bytes 258056 | tf_op jit(solution)/shard_map/ppermute | solution.py:504
  106.5 10.2 %collective-permute-start.14 = (bf16[4,16,2688]{2,1,0:T(8,128)(2,1)S(1)}, bf16[4,16,2688]{2,1,0:T(8,128)(2,1)S(1)}, u32[]{:S(2)}, u32[]{:S(2)}) collective-permute-start(bf16[4,16,2688]{2,1,0:T(8,128)(2,1)S(1)} %pad_maximum_fusion.refs_0_), channel_id=1, source_target_pairs={{0,1},{1,0},{2,3},{3,2},{4,5},{5,4},{6,7},{7,6},{8,9},{9,8},{10,11... | collective-permute-start | bytes 1032200 | tf_op jit(solution)/shard_map/ppermute | solution.py:516
  106.6 11.9 %collective-permute-start.13 = (bf16[4,16,2688]{2,1,0:T(8,128)(2,1)S(1)}, bf16[4,16,2688]{2,1,0:T(8,128)(2,1)S(1)}, u32[]{:S(2)}, u32[]{:S(2)}) collective-permute-start(bf16[4,16,2688]{2,1,0:T(8,128)(2,1)S(1)} %pad_maximum_fusion.refs_0_), channel_id=1, source_target_pairs={{0,6},{2,4},{4,2},{6,0},{8,14},{10,12},{12,10},{14,8},{16,22},{18,... | collective-permute-start | bytes 1032200 | tf_op jit(solution)/shard_map/ppermute | solution.py:504
  109.0 16.3 %collective-permute-start.12 = (bf16[4,16,2688]{2,1,0:T(8,128)(2,1)S(1)}, bf16[4,16,2688]{2,1,0:T(8,128)(2,1)S(1)}, u32[]{:S(2)}, u32[]{:S(2)}) collective-permute-start(bf16[4,16,2688]{2,1,0:T(8,128)(2,1)S(1)} %pad_maximum_fusion.refs_0_), channel_id=1, source_target_pairs={{0,4},{2,6},{4,0},{6,2},{8,12},{10,14},{12,8},{14,10},{16,20},{18,... | collective-permute-start | bytes 1032200 | tf_op jit(solution)/shard_map/ppermute | solution.py:504
  109.6 15.8 %collective-permute-start.11 = (bf16[4,16,2688]{2,1,0:T(8,128)(2,1)S(1)}, bf16[4,16,2688]{2,1,0:T(8,128)(2,1)S(1)}, u32[]{:S(2)}, u32[]{:S(2)}) collective-permute-start(bf16[4,16,2688]{2,1,0:T(8,128)(2,1)S(1)} %pad_maximum_fusion.refs_0_), channel_id=1, source_target_pairs={{0,2},{2,0},{4,6},{6,4},{8,10},{10,8},{12,14},{14,12},{16,18},{18,... | collective-permute-start | bytes 1032200 | tf_op jit(solution)/shard_map/ppermute | solution.py:504
  125.4 1.7 %collective-permute-start.15 = (bf16[4,16,2688]{2,1,0:T(8,128)(2,1)S(1)}, bf16[4,16,2688]{2,1,0:T(8,128)(2,1)S(1)}, u32[]{:S(2)}, u32[]{:S(2)}) collective-permute-start(bf16[4,16,2688]{2,1,0:T(8,128)(2,1)S(1)} %collective-permute-done.11.refs_1_), channel_id=1, source_target_pairs={{0,1},{1,0},{2,3},{3,2},{4,5},{5,4},{6,7},{7,6},{8,9},{9,8},{10,11... | collective-permute-start | bytes 1032200 | tf_op jit(solution)/shard_map/ppermute | solution.py:516
  125.4 2.1 %collective-permute-start.16 = (bf16[4,16,2688]{2,1,0:T(8,128)(2,1)S(1)}, bf16[4,16,2688]{2,1,0:T(8,128)(2,1)S(1)}, u32[]{:S(2)}, u32[]{:S(2)}) collective-permute-start(bf16[4,16,2688]{2,1,0:T(8,128)(2,1)S(1)} %collective-permute-done.12.refs_2_), channel_id=1, source_target_pairs={{0,1},{1,0},{2,3},{3,2},{4,5},{5,4},{6,7},{7,6},{8,9},{9,8},{10,11... | collective-permute-start | bytes 1032200 | tf_op jit(solution)/shard_map/ppermute | solution.py:516
  125.9 2.1 %collective-permute-start.17 = (bf16[4,16,2688]{2,1,0:T(8,128)(2,1)S(1)}, bf16[4,16,2688]{2,1,0:T(8,128)(2,1)S(1)}, u32[]{:S(2)}, u32[]{:S(2)}) collective-permute-start(bf16[4,16,2688]{2,1,0:T(8,128)(2,1)S(1)} %collective-permute-done.13.refs_3_), channel_id=1, source_target_pairs={{0,1},{1,0},{2,3},{3,2},{4,5},{5,4},{6,7},{7,6},{8,9},{9,8},{10,11... | collective-permute-start | bytes 1032200 | tf_op jit(solution)/shard_map/ppermute | solution.py:516
  (9 other events, 112.5 us)

commit v3 on v2

--- a/solution.py
+++ b/solution.py
@@ -54,7 +54,7 @@
     return pltpu.CompilerParams(vmem_limit_bytes=mib * MIB)
 
 
-def call(body, outs, specs, flops, moved, scratch=(), room=16, out_specs=None):
+def call(body, outs, specs, flops, moved, scratch=(), room=16, out_specs=None, aliases=None):
     if out_specs is None:
         out_specs = tuple(VMEM for _ in outs) if isinstance(outs, tuple) else VMEM
     return pl.pallas_call(
@@ -63,6 +63,7 @@
         in_specs=specs,
         out_specs=out_specs,
         scratch_shapes=list(scratch),
+        input_output_aliases=aliases or {},
         compiler_params=params(room),
         cost_estimate=cost(flops, moved),
     )
@@ -154,12 +155,19 @@
     sums_ref[...] = dot_nn(pick, back_ref[...]).astype(BF16)
 
 
-def scatter_kernel(row_ref, got_ref, out_ref):
-    block = out_ref.shape[0]
+def scatter_kernel(row_ref, got_ref, out_ref, held_ref, sems):
+    parts, block, _ = held_ref.shape
     total = got_ref.shape[0]
-    here = row_ref[0:1, :] - (pl.program_id(0) * block).astype(F32)
-    pick = jnp.where(here == iota((block, total), 0).astype(F32), 1.0, 0.0).astype(BF16)
-    out_ref[...] = dot_nn(pick, got_ref[...])
+    line = iota((block, total), 0).astype(F32)
+    copies = []
+    for n in range(parts):
+        pick = jnp.where(row_ref[0:1, :] - float(n * block) == line, 1.0, 0.0).astype(BF16)
+        held_ref[n] = dot_nn(pick, got_ref[...])
+        copies += start_all(
+            (held_ref.at[n],), (out_ref.at[pl.ds(n * block, block), :],), sems.at[pl.ds(n, 1)]
+        )
+    for copy in copies:
+        copy.wait()
 
 
 def segments(len_ref, dest_ref, rows):
@@ -186,14 +194,6 @@
 def go_kernel(len_ref, dest_ref, og_ref, go_ref):
     rows = og_ref.shape[0]
     go_ref[...] = masked_grad(og_ref, valid_rows(segments(len_ref, dest_ref, rows), rows))
-
-
-def hold_kernel(table_ref, held_ref, sems):
-    parts = sems.shape[0]
-    step = table_ref.shape[0] // parts
-    blocks = [pl.ds(n * step, step) for n in range(parts)]
-    for copy in start_all([table_ref.at[b, :] for b in blocks], [held_ref.at[b, :] for b in blocks], sems):
-        copy.wait()
 
 
 def pos_bounds(rows, count):
@@ -386,11 +386,22 @@
 SMALL_ROWS = 48
 
 
+def prefix_ends(time_ref, rows, count):
+    time_lane = 64
+    row = iota((1, rows), 1).astype(F32)
+    ends = [row - float(bound) for bound in pos_bounds(rows, count)]
+    ends += [jnp.full((time_lane - count, rows), -1.0, F32)]
+    stamp = jnp.broadcast_to(time_ref[...].astype(F32), (rows, rows))
+    gaps = stamp - jnp.transpose(stamp)
+    for bound in time_bounds(count):
+        ends.append(jnp.sum(jnp.where(gaps >= bound, 1.0, 0.0), axis=0, keepdims=True) - 1.0)
+    ends += [jnp.full((LANES - time_lane - count, rows), -1.0, F32)]
+    return jnp.transpose(jnp.concatenate(ends, axis=0)).astype(I32)
+
+
 def small_kernel(count, ds_ref, time_ref, dh_ref, go_ref, g1g_ref, g2g_ref, out_ref):
     heads, rows, _ = ds_ref.shape
     width = go_ref.shape[1]
-    delta = time_gaps(time_ref, rows)
-    dist = iota((rows, rows), 0) - iota((rows, rows), 1)
     out_ref[...] = jnp.zeros_like(out_ref)
     b_grad = jnp.sum(dh_ref[...].astype(F32), axis=0, keepdims=True)
     go_sum = jnp.sum(go_ref[...].astype(F32), axis=0, keepdims=True)
@@ -400,22 +411,22 @@
             out_ref[at : at + 1, :] = value[:, col : col + LANES]
             at += 1
     at = (at + 7) // 8 * 8
-    lane = iota((heads, LANES), 1)
-    for base, which, bounds in (
-        (at, dist, pos_bounds(rows, count)),
-        (at + heads, delta, time_bounds(count)),
-    ):
-        result = jnp.zeros((heads, LANES), F32)
-        done = {}
-        for m, bound in enumerate(bounds):
-            if bound not in done:
-                sums = [
-                    jnp.sum(jnp.where(which >= bound, ds_ref[g].astype(F32), 0.0), axis=0, keepdims=True)
-                    for g in range(heads)
-                ]
-                done[bound] = jnp.sum(jnp.concatenate(sums, axis=0), axis=1, keepdims=True)
-            result = jnp.where(lane == m, done[bound], result)
-        out_ref[base : base + heads, :] = result
+    ends = prefix_ends(time_ref, rows, count)
+    upto = jnp.where(iota((rows, rows), 0) <= iota((rows, rows), 1), 1.0, 0.0).astype(BF16)
+    sums = []
+    for g in range(heads):
+        prefix = dot_nn(ds_ref[g], upto)
+        found = jnp.zeros((rows, LANES), F32)
+        for first in range(0, rows, LANES):
+            here = (ends >= first) & (ends < first + LANES)
+            value = jnp.take_along_axis(
+                prefix[:, first : first + LANES], jnp.where(here, ends - first, 0), axis=1
+            )
+            found = found + jnp.where(here, value, 0.0)
+        sums.append(jnp.sum(found, axis=0, keepdims=True))
+    sums = jnp.concatenate(sums, axis=0)
+    out_ref[at : at + heads, :] = sums
+    out_ref[at + heads : at + 2 * heads, 0 : LANES // 2] = sums[:, LANES // 2 :]
 
 
 def place_of(columns):
@@ -424,7 +435,7 @@
 
 
 def pack_kernel(planes, columns, dh_ref, n1_ref, y_ref, go_ref, got_ref, got_go_ref, small_ref, *rest):
-    outs, (uv_ref, wo_ref) = rest[:columns], rest[columns:]
+    nears, fars, (uv_ref, wo_ref) = rest[:columns], rest[columns : 2 * columns], rest[2 * columns :]
     width = n1_ref.shape[1]
     core = lax.axis_index("table")
     my_xy, my_z = place_of(columns)
@@ -446,7 +457,7 @@
     for rel_xy in range(columns):
         for rel_z in range(planes):
             chunk = jnp.bitwise_xor(my_xy, rel_xy) * planes + jnp.bitwise_xor(my_z, rel_z)
-            out = outs[rel_xy].at[rel_z]
+            out = (nears, fars)[rel_z // 2][rel_xy].at[rel_z % 2]
             for part in range(2):
                 at = pl.multiple_of((2 * chunk + part) * short, short)
                 out[:, part * half_cols : (part + 1) * half_cols] = uv_ref[pl.ds(at, short), :].astype(BF16)
@@ -455,33 +466,70 @@
             out[:, 2 * half_cols + width :] = small_ref[pl.ds(at, short), :].astype(BF16)
 
 
-def unpack_kernel(planes, columns, *refs):
-    pieces = refs[: 2 * columns]
-    uvqk_ref, wout_ref, b_ref, g1_ref, g2_ref, bo_ref, pos_ref, time_ref, small_ref = refs[2 * columns :]
-    width = wout_ref.shape[0]
+def unpack(planes, columns, chunks, mine, theirs, uvqk_ref, wout_ref, small_ref, held_uvqk, held_wout, sems):
+    short = held_wout.shape[1]
+    width = held_wout.shape[2]
     core = lax.axis_index("table")
     my_xy, my_z = place_of(columns)
     half_cols = 2 * width
     half_y = width // 2
-    short = half_y // (planes * columns)
     wout_lanes = slice(2 * half_cols, 2 * half_cols + width)
     small_lanes = slice(2 * half_cols + width, 2 * half_cols + width + LANES)
-    for rel_xy in range(columns):
-        for rel_z in range(planes):
-            chunk = jnp.bitwise_xor(my_xy, rel_xy) * planes + jnp.bitwise_xor(my_z, rel_z)
-            mine, theirs = (pieces[which * columns + rel_xy].at[rel_z] for which in range(2))
-            for ref, side in ((mine, core), (theirs, 1 - core)):
-                cols = pl.ds(pl.multiple_of(side * half_cols, half_cols), half_cols)
-                for part in range(2):
-                    at = pl.multiple_of((2 * chunk + part) * short, short)
-                    uvqk_ref[pl.ds(at, short), cols] = ref[
-                        :, part * half_cols : (part + 1) * half_cols
-                    ].astype(F32)
-                at = pl.multiple_of(side * half_y + chunk * short, short)
-                wout_ref[pl.ds(at, short), :] = ref[:, wout_lanes].astype(F32)
-            small_ref[pl.ds(pl.multiple_of(chunk * short, short), short), :] = mine[:, small_lanes].astype(
-                F32
-            ) + theirs[:, small_lanes].astype(F32)
+    copies = []
+    for rel_xy, rel_z, ref, at in chunks:
+        chunk = jnp.bitwise_xor(my_xy, rel_xy) * planes + jnp.bitwise_xor(my_z, rel_z)
+        pieces = mine[ref].at[at], theirs[ref].at[at]
+        for piece, side in zip(pieces, (core, 1 - core)):
+            n = len(copies) // 2
+            for part in range(2):
+                held_uvqk[n, part * short : (part + 1) * short, :] = piece[
+                    :, part * half_cols : (part + 1) * half_cols
+                ].astype(F32)
+            held_wout[n] = piece[:, wout_lanes].astype(F32)
+            tall = pl.ds(pl.multiple_of(chunk * 2 * short, 2 * short), 2 * short)
+            cols = pl.ds(pl.multiple_of(side * half_cols, half_cols), half_cols)
+            rows = pl.ds(pl.multiple_of(side * half_y + chunk * short, short), short)
+            copies += start_all(
+                (held_uvqk.at[n], held_wout.at[n]),
+                (uvqk_ref.at[tall, cols], wout_ref.at[rows, :]),
+                sems.at[pl.ds(2 * n, 2)],
+            )
+        small_ref[pl.ds(pl.multiple_of(chunk * short, short), short), :] = pieces[0][:, small_lanes].astype(
+            F32
+        ) + pieces[1][:, small_lanes].astype(F32)
+    return copies
+
+
+def first_chunks(planes, columns):
+    near = [(xy, z, xy, z) for xy in range(columns) for z in range(2)]
+    return near + [(0, z, columns, z - 2) for z in range(2, planes)]
+
+
+def last_chunks(planes, columns):
+    return [(xy, z, xy - 1, z - 2) for xy in range(1, columns) for z in range(2, planes)]
+
+
+def unpack_first_kernel(planes, columns, *refs):
+    mine, theirs = refs[: columns + 1], refs[columns + 1 : 2 * columns + 2]
+    uvqk_ref, wout_ref, small_ref, held_uvqk, held_wout, sems = refs[2 * columns + 2 :]
+    small_ref[...] = jnp.zeros_like(small_ref)
+    chunks = first_chunks(planes, columns)
+    for copy in unpack(
+        planes, columns, chunks, mine, theirs, uvqk_ref, wout_ref, small_ref, held_uvqk, held_wout, sems
+    ):
+        copy.wait()
+
+
+def unpack_last_kernel(planes, columns, *refs):
+    peers = columns - 1
+    mine, theirs, first_ref = refs[:peers], refs[peers : 2 * peers], refs[2 * peers + 2]
+    uvqk_ref, wout_ref, b_ref, g1_ref, g2_ref, bo_ref, pos_ref, time_ref = refs[2 * peers + 3 : 2 * peers + 11]
+    small_ref, held_uvqk, held_wout, sems = refs[2 * peers + 11 :]
+    small_ref[...] = first_ref[...]
+    chunks = last_chunks(planes, columns)
+    copies = unpack(
+        planes, columns, chunks, mine, theirs, uvqk_ref, wout_ref, small_ref, held_uvqk, held_wout, sems
+    )
     at = 0
     for out in (b_ref, g1_ref, g2_ref, bo_ref):
         for col in range(0, out.shape[1], LANES):
@@ -491,6 +539,8 @@
     heads, count = pos_ref.shape
     pos_ref[...] = small_ref[at : at + heads, 0:count]
     time_ref[...] = small_ref[at + heads : at + 2 * heads, 0:count]
+    for copy in copies:
+        copy.wait()
 
 
 def add_up(first, *rest):
@@ -547,7 +597,7 @@
     planes = replicas // columns
     staged = (
         groups == 2
-        and replicas in (4, 8, 16)
+        and replicas == 16
         and width % (32 * replicas) == 0
         and (2 * heads + SMALL_ROWS - 16) <= width // 2
     )
@@ -573,18 +623,9 @@
         room=64,
     )(request_rows.transpose(0, 2, 1).reshape(cap, devices), slot_row, lengths, assignment, counts_2d)
     asked = lax.all_to_all(msg.reshape(devices, 1, LANES), BOTH, 0, 0, tiled=True).reshape(devices, LANES)
-    held = call(
-        hold_kernel,
-        shape_of(item_table.shape, BF16),
-        [HBM],
-        0,
-        8 * mb,
-        scratch=(pltpu.SemaphoreType.DMA((8,)),),
-    )(item_table)
-    asked, held = lax.optimization_barrier((asked, held))
     served = call(
         functools.partial(serve_kernel, cap), shape_of((slots, width), BF16), [VMEM] * 2, 1 << 30, 5 * mb
-    )(asked, held)
+    )(asked, item_table)
     go = call(go_kernel, shape_of((rows, width), BF16), [VMEM] * 3, 64 * mb, mb)(lengths, assignment, out_grad)
     fetched = lax.all_to_all(served.reshape(devices, cap, width), BOTH, 0, 0, tiled=True)
     new_counts, log_q, asked_row = call(
@@ -649,20 +690,28 @@
         return lax.all_to_all(dx.reshape(replicas, piece, width), "dp", 0, 0, tiled=True).reshape(rows, width)
 
     def to_owners(back):
-        sums = call(slot_sum_kernel, shape_of((slots, width), BF16), [VMEM] * 2, 64 * mb, mb)(slot_row, back)
+        return send_sums(slot_sums(back))
+
+    def slot_sums(back):
+        return call(slot_sum_kernel, shape_of((slots, width), BF16), [VMEM] * 2, 64 * mb, mb)(slot_row, back)
+    def send_sums(sums):
         sums = lax.all_to_all(sums.reshape(devices, cap, width), BOTH, 0, 0, tiled=True)
         return sums.reshape(slots, width)
 
     def into_table(got_sums):
         block = min(512, rows_dev)
-        return pl.pallas_call(
+        return call(
             scatter_kernel,
-            grid=(rows_dev // block,),
-            out_shape=shape_of((rows_dev, width), F32),
-            in_specs=[pl.BlockSpec((8, slots), lambda i: (0, 0)), pl.BlockSpec((slots, width), lambda i: (0, 0))],
-            out_specs=pl.BlockSpec((block, width), lambda i: (i, 0)),
-            compiler_params=params(16),
-            cost_estimate=cost(1 << 30, 8 * mb),
+            shape_of((rows_dev, width), F32),
+            [VMEM] * 2,
+            1 << 30,
+            8 * mb,
+            scratch=(
+                pltpu.VMEM((rows_dev // block, block, width), F32),
+                pltpu.SemaphoreType.DMA((rows_dev // block,)),
+            ),
+            room=24,
+            out_specs=HBM,
         )(asked_row, got_sums)
 
     if staged:
@@ -681,30 +730,63 @@
         short = width // replicas // 2
         pieces = call(
             functools.partial(pack_kernel, planes, columns),
-            tuple(shape_of((planes, short, 5 * width + LANES), BF16) for _ in range(columns)),
+            tuple(shape_of((2, short, 5 * width + LANES), BF16) for _ in range(2 * columns)),
             [VMEM] * 7,
             1 << 30,
             6 * mb,
             scratch=(pltpu.VMEM((width, half_cols), F32), pltpu.VMEM((width // 2, width), F32)),
         )(dh, n1, y, go, got, got_go, small)
         dx, *pieces = lax.optimization_barrier((dx, *pieces))
+        nears, fars = pieces[:columns], pieces[columns:]
         back = home_again(dx)
-        line = reduce_step(pieces, replicas, 1)
-        line, back = lax.optimization_barrier((line, back))
-        got_sums = to_owners(back)
-        own = reduce_step(line, replicas, columns)
-        line = jnp.stack(gather_step(own, replicas, columns, planes))
-        line, got_sums = lax.optimization_barrier((line, got_sums))
+        got_far = [xor_step(fars[k], replicas, k) for k in range(1, columns)]
+        nears, got_far[0] = lax.optimization_barrier((nears, got_far[0]))
+        far_line = add_up(fars[0], *got_far)
+        got_line = [xor_step(far_line[k - 2], replicas, k * columns) for k in range(2, planes)]
+        near_line = reduce_step(nears, replicas, 1)
+        near_line, back = lax.optimization_barrier((near_line, back))
+        got_next = xor_step(near_line[1], replicas, columns)
+        sums = slot_sums(back)
+        own = add_up(near_line[0], got_next, *got_line)
+        own, sums = lax.optimization_barrier((own, sums))
+        next_own = xor_step(own, replicas, columns)
+        far = [xor_step(own, replicas, k * columns) for k in range(2, planes)]
+        near = jnp.stack([own, next_own])
+        nears = gather_step(near, replicas, 1, columns)
+        nears[1], sums = lax.optimization_barrier((nears[1], sums))
+        got_sums = send_sums(sums)
+        far = jnp.stack(far)
+        far, nears = lax.optimization_barrier((far, nears))
         table_grad = into_table(got_sums)
-        mine = gather_step(line, replicas, 1, columns)
-        theirs = [swap_cores(line)]
-        mine, theirs, table_grad = lax.optimization_barrier((mine, theirs, table_grad))
-        theirs += [swap_cores(piece) for piece in mine[1:]]
+        fars = gather_step(far, replicas, 1, columns)
+        their_nears = [swap_cores(piece) for piece in nears]
+        their_far = swap_cores(far)
+        small_shape = shape_of((width // 2, LANES), F32)
+        wide_shapes = (shape_of((width, 4 * width), F32), shape_of((width, width), F32))
+
+        def unpack_scratch(chunks):
+            n = 2 * len(chunks)
+            return (
+                pltpu.VMEM((n, 2 * short, half_cols), F32),
+                pltpu.VMEM((n, short, width), F32),
+                pltpu.SemaphoreType.DMA((2 * n,)),
+            )
+
+        w_uvqk_sum, w_out_sum, small_sum = call(
+            functools.partial(unpack_first_kernel, planes, columns),
+            wide_shapes + (small_shape,),
+            [VMEM] * (2 * columns + 2),
+            mb,
+            5 * mb,
+            scratch=unpack_scratch(first_chunks(planes, columns)),
+            out_specs=(HBM, HBM, VMEM),
+        )(*nears, far, *their_nears, their_far)
+        fars, small_sum, table_grad = lax.optimization_barrier((fars, small_sum, table_grad))
+        their_fars = [swap_cores(piece) for piece in fars[1:]]
         w_uvqk_sum, w_out_sum, b_sum, g1_sum, g2_sum, bo_sum, pos_sum, time_sum = call(
-            functools.partial(unpack_kernel, planes, columns),
-            (
-                shape_of((width, 4 * width), F32),
-                shape_of((width, width), F32),
+            functools.partial(unpack_last_kernel, planes, columns),
+            wide_shapes
+            + (
                 shape_of((1, 4 * width), F32),
                 shape_of((1, width), F32),
                 shape_of((1, width), F32),
@@ -712,11 +794,13 @@
                 shape_of((heads, count), F32),
                 shape_of((heads, count), F32),
             ),
-            [VMEM] * (2 * columns),
+            [VMEM] * (2 * columns - 2) + [HBM, HBM, VMEM],
             mb,
-            8 * mb,
-            scratch=(pltpu.VMEM((width // 2, LANES), F32),),
-        )(*mine, *theirs)
+            3 * mb,
+            scratch=(pltpu.VMEM(small_shape.shape, F32),) + unpack_scratch(last_chunks(planes, columns)),
+            out_specs=(HBM, HBM) + (VMEM,) * 6,
+            aliases={2 * columns - 2: 0, 2 * columns - 1: 1},
+        )(*fars[1:], *their_fars, w_uvqk_sum, w_out_sum, small_sum)
     else:
         table_grad = into_table(to_owners(home_again(dx)))
         w_uvqk_sum, w_out_sum, parts = lax.psum((dot_tn(n1, dh), dot_tn(y, go), small[0:SMALL_ROWS]), BOTH)

time: 131 us -> 119 us (0.908)
  waiting for transfers between devices: 48.3 us -> 26.7 us
  blocking collectives: 13.9 us -> 26.7 us
  local copies, waits for them, and re-layouts: 7.18 us -> 2.99 us
  starting transfers between devices: 33.6 us -> 35.7 us
  Pallas kernels: 26.2 us -> 24.6 us
    ppermute x12 -> x18, waiting for transfers between devices: 34.8 us -> 15.6 us  [xor_step(): return lax.ppermute(value, 'dp', [(i, i ^ step) for i in range(size)])]
    all_to_all x0 -> x1, blocking collectives: none -> 14.4 us  [on_device(): lax.all_to_all(msg.reshape(devices, 1, LANES), BOTH, 0, 0, tiled=True)]
    ppermute x12 -> x18, starting transfers between devices: 15.1 us -> 23.5 us  [xor_step(): return lax.ppermute(value, 'dp', [(i, i ^ step) for i in range(size)])]
    all_to_all x2 -> x1, starting transfers between devices: 10.5 us -> 3.23 us  [send_sums(): lax.all_to_all(sums.reshape(devices, cap, width), BOTH, 0, 0, tiled=True)]
    unnamed x38 -> x34, local copies, waits for them, and re-layouts: 7.16 us -> 2.97 us
    all_to_all x2 -> x1, waiting for transfers between devices: 2.39 us -> 0.19 us  [send_sums(): lax.all_to_all(sums.reshape(devices, cap, width), BOTH, 0, 0, tiled=True)]
    all_to_all x1, blocking collectives: 13.9 us -> 12.3 us  [on_device(): lax.all_to_all(served.reshape(devices, cap, width), BOTH, 0, 0, tiled=True)]
    ppermute x6 -> x10, waiting for transfers between devices: 3.65 us -> 3.3 us  [swap_cores(): return lax.ppermute(value, 'table', [(0, 1), (1, 0)])]
  transfers between devices with their start and end apart: 22 -> 31, of which waited for: 17 -> 15; matrix products, arithmetic and copies ran while one was open for 0% -> 0% of each run, Pallas kernels for 10% -> 10%
where the time goes in v3:
time: 119 us; the launch traced here: 118 us
  starting transfers between devices  35.7 us (30%)
  blocking collectives  26.7 us (22%)
  waiting for transfers between devices  26.7 us (22%)
  Pallas kernels  24.6 us (21%)
  local copies, waits for them, and re-layouts  2.99 us (3%)
    ppermute x18, starting transfers between devices, xor_step(): return lax.ppermute(value, 'dp', [(i, i ^ step) for i in range(size)])  23.5 us
    ppermute x18, waiting for transfers between devices, xor_step(): return lax.ppermute(value, 'dp', [(i, i ^ step) for i in range(size)])  15.6 us
    all_to_all x1, blocking collectives, on_device(): lax.all_to_all(msg.reshape(devices, 1, LANES), BOTH, 0, 0, tiled=True)  14.4 us
    all_to_all x1, blocking collectives, on_device(): lax.all_to_all(served.reshape(devices, cap, width), BOTH, 0, 0, tiled=True)  12.3 us
    all_to_all x1, waiting for transfers between devices, on_device(): lax.all_to_all(home.reshape(replicas, piece, width), 'dp', 0, 0, tiled=True)  7.6 us
    pallas_call x1, Pallas kernels, on_device(): call(functools.partial(layer_kernel, staged), (shape_of((rows, width), BF...  5.33 us
    all_to_all x1, starting transfers between devices, home_again(): lax.all_to_all(dx.reshape(replicas, piece, width), 'dp', 0, 0, tiled=True)  3.71 us
    pallas_call x1, Pallas kernels, into_table(): call(scatter_kernel, shape_of((rows_dev, width), F32), [VMEM] * 2, 1 << 3...  3.67 us
  transfers between devices with their start and end apart: 31, of which 15 were waited for; matrix products, arithmetic and copies ran while one was open for 0% of the time, Pallas kernels for 10%

profile of v3, /device:TPU:0, one launch (start us, length us, event | category | flops | bytes accessed | tf_op | source)
XLA Modules:
  0.0 118.2 jit_solution(13135087299010009742)
XLA Ops:
  0.6 1.7 %shard_map.247 = s32[32,128]{1,0:T(8,128)} custom-call(s32[8,32]{1,0:T(8,128)} %bitcast.66, s32[1,256]{1,0:T(1,128)} %bitcast.51, s32[1,64]{1,0:T(1,128)} %len_ref.3, s32[1,64]{1,0:T(1,128)} %dest_ref.3, s32[32,128]{1,0:T(8,128)} %bitcast.49), custom_call_target="tpu_custom_call" | custom-call | flops 1048576 | bytes 131072 | tf_op jit(solution)/shard_map/pallas_call | solution.py:609
  2.4 14.4 %all_to_all.25 = s32[32,1,128]{2,1,0:T(1,128)S(1)} all-to-all(s32[32,1,128]{2,1,0:T(1,128)} %bitcast.65), channel_id=1, replica_groups=mesh['dp'=16,'table'=2] {'dp','table'}, dimensions={0} | all-to-all | bytes 32768 | tf_op jit(solution)/shard_map/all_to_all | solution.py:625
  16.8 2.2 %copy-done = bf16[4096,512]{1,0:T(8,128)(2,1)S(1)} copy-done((bf16[4096,512]{1,0:T(8,128)(2,1)S(1)}, bf16[4096,512]{1,0:T(8,128)(2,1)}, u32[]{:S(2)}) %copy-start) | copy-done | bytes 4194328
  19.0 1.9 %shard_map.248 = bf16[256,512]{1,0:T(8,128)(2,1)S(1)} custom-call(s32[32,128]{1,0:T(8,128)S(1)} %bitcast.47, bf16[4096,512]{1,0:T(8,128)(2,1)S(1)} %copy-done), custom_call_target="tpu_custom_call" | custom-call | flops 1073741824 | bytes 5242880 | tf_op jit(solution)/shard_map/pallas_call | solution.py:626
  20.9 12.3 %all_to_all.26 = bf16[32,8,512]{2,1,0:T(8,128)(2,1)S(1)} all-to-all(bf16[32,8,512]{2,1,0:T(8,128)(2,1)S(1)} %bitcast.44), channel_id=1, replica_groups=mesh['dp'=16,'table'=2] {'dp','table'}, dimensions={0} | all-to-all | bytes 524288 | tf_op jit(solution)/shard_map/all_to_all | solution.py:630
  34.2 3.5 %all-to-all-start.2 = ((bf16[16,16,512]{2,1,0:T(8,128)(2,1)}), bf16[16,16,512]{2,1,0:T(8,128)(2,1)S(1)}, u32[]{:S(2)}, u32[]{:S(2)}) async-start(bf16[16,16,512]{2,1,0:T(8,128)(2,1)} %bitcast.9), calls=%async_computation.2 | async-start | bytes 524288 | tf_op jit(solution)/shard_map/all_to_all | solution.py:647
  38.0 1.5 %collective-permute-done.got_go_ref = bf16[256,512]{1,0:T(8,128)(2,1)S(1)} collective-permute-done((bf16[256,512]{1,0:T(8,128)(2,1)S(1)}, bf16[256,512]{1,0:T(8,128)(2,1)S(1)}, u32[]{:S(2)}, u32[]{:S(2)}) %collective-permute-start) | collective-permute-done | bytes 262176 | tf_op jit(solution)/shard_map/ppermute | solution.py:566
  40.3 7.6 %all-to-all-done.2 = bf16[16,16,512]{2,1,0:T(8,128)(2,1)S(1)} async-done(((bf16[16,16,512]{2,1,0:T(8,128)(2,1)}), bf16[16,16,512]{2,1,0:T(8,128)(2,1)S(1)}, u32[]{:S(2)}, u32[]{:S(2)}) %all-to-all-start.2) | async-done | bytes 262176 | tf_op jit(solution)/shard_map/all_to_all | solution.py:647
  47.9 5.3 %shard_map.251 = (bf16[256,512]{1,0:T(8,128)(2,1)}, bf16[256,512]{1,0:T(8,128)(2,1)S(1)}, bf16[256,512]{1,0:T(8,128)(2,1)S(1)}, bf16[256,2048]{1,0:T(8,128)(2,1)...) custom-call(bf16[256,512]{1,0:T(8,128)(2,1)S(1)} %bitcast.42, ...), custom_call_target="tpu_custom_call" | custom-call | flops 2147483648 | bytes 8388608 | tf_op jit(solution)/shard_map/pallas_call | solution.py:654
  53.3 1.6 %shard_map.252 = (bf16[256,512]{1,0:T(8,128)(2,1)}, f32[1,512]{1,0:T(1,128)S(1)}) custom-call(bf16[256,2048]{1,0:T(8,128)(2,1)S(1)} %get-tuple-element.77.dh_ref, bf16[512,2048]{1,0:T(8,128)(2,1)S(1)} %copy-done.1, bf16[256,512]{1,0:T(8,128)(2,1)S(1)} %bitcast.43, f32[1,512]{1,0:T(1,128)S(1)} %bitcast.55, bf16[256,512]{1,0:T(8,128)(2,1)S(1)} %shard_map.250.go_ref), custom_call_target="tpu_custom_call" | custom-call | flops 536870912 | bytes 4194304 | tf_op jit(solution)/shard_map/pallas_call | solution.py:719
  55.0 2.2 %shard_map.253.small_ref = f32[256,128]{1,0:T(8,128)S(1)} custom-call(bf16[8,256,256]{2,1,0:T(8,128)(2,1)S(1)} %get-tuple-element.83.ds_ref, s32[1,256]{1,0:T(1,128)S(1)} %bitcast.57, bf16[256,2048]{1,0:T(8,128)(2,1)S(1)} %get-tuple-element.77.dh_ref, bf16[256,512]{1,0:T(8,128)(2,1)S(1)} %shard_map.250.go_ref, f32[1,512]{1,0:T(1,128)S(1)} %get-tuple-element.84.g1g_ref, ...), custom_call_target="tpu_custom_call" | custom-call | flops 268435456 | bytes 2097152 | tf_op jit(solution)/shard_map/pallas_call | solution.py:722
  59.6 2.0 %collective-permute-start.8 = (bf16[2,16,2688]{2,1,0:T(8,128)(2,1)S(1)}, bf16[2,16,2688]{2,1,0:T(8,128)(2,1)S(1)}, u32[]{:S(2)}, u32[]{:S(2)}) collective-permute-start(bf16[2,16,2688]{2,1,0:T(8,128)(2,1)S(1)} %get-tuple-element.108), channel_id=1, source_target_pairs={{0,6},{2,4},{4,2},{6,0},{8,14},{10,12},{12,10},{14,8},{16,22},{18,... | collective-permute-start | bytes 516104 | tf_op jit(solution)/shard_map/ppermute | solution.py:554
  61.7 3.7 %all-to-all-start.3 = ((bf16[16,16,512]{2,1,0:T(8,128)(2,1)}), bf16[16,16,512]{2,1,0:T(8,128)(2,1)S(1)}, u32[]{:S(2)}, u32[]{:S(2)}) async-start(bf16[16,16,512]{2,1,0:T(8,128)(2,1)} %bitcast.16), calls=%async_computation.3 | async-start | bytes 524288 | tf_op jit(solution)/shard_map/all_to_all | solution.py:690
  65.4 1.8 %collective-permute-start.3 = (bf16[2,16,2688]{2,1,0:T(8,128)(2,1)S(1)}, bf16[2,16,2688]{2,1,0:T(8,128)(2,1)S(1)}, u32[]{:S(2)}, u32[]{:S(2)}) collective-permute-start(bf16[2,16,2688]{2,1,0:T(8,128)(2,1)S(1)} %get-tuple-element.100), channel_id=1, source_target_pairs={{0,2},{2,0},{4,6},{6,4},{8,10},{10,8},{12,14},{14,12},{16,18},{18,... | collective-permute-start | bytes 516104 | tf_op jit(solution)/shard_map/ppermute | solution.py:554
  67.2 1.5 %collective-permute-start.4 = (bf16[2,16,2688]{2,1,0:T(8,128)(2,1)S(1)}, bf16[2,16,2688]{2,1,0:T(8,128)(2,1)S(1)}, u32[]{:S(2)}, u32[]{:S(2)}) collective-permute-start(bf16[2,16,2688]{2,1,0:T(8,128)(2,1)S(1)} %get-tuple-element.101), channel_id=1, source_target_pairs={{0,4},{2,6},{4,0},{6,2},{8,12},{10,14},{12,8},{14,10},{16,20},{18,... | collective-permute-start | bytes 516104 | tf_op jit(solution)/shard_map/ppermute | solution.py:554
  69.8 2.0 %collective-permute-start.9 = (bf16[16,2688]{1,0:T(8,128)(2,1)S(1)}, bf16[16,2688]{1,0:T(8,128)(2,1)S(1)}, u32[]{:S(2)}, u32[]{:S(2)}) collective-permute-start(bf16[16,2688]{1,0:T(8,128)(2,1)S(1)} %get-tuple-element.138), channel_id=1, source_target_pairs={{0,16},{2,18},{4,20},{6,22},{8,24},{10,26},{12,28},{14,30},{16,0},... | collective-permute-start | bytes 258056 | tf_op jit(solution)/shard_map/ppermute | solution.py:554
  71.8 1.5 %collective-permute-start.10 = (bf16[16,2688]{1,0:T(8,128)(2,1)S(1)}, bf16[16,2688]{1,0:T(8,128)(2,1)S(1)}, u32[]{:S(2)}, u32[]{:S(2)}) collective-permute-start(bf16[16,2688]{1,0:T(8,128)(2,1)S(1)} %get-tuple-element.139), channel_id=1, source_target_pairs={{0,24},{2,26},{4,28},{6,30},{8,16},{10,18},{12,20},{14,22},{16,8},... | collective-permute-start | bytes 258056 | tf_op jit(solution)/shard_map/ppermute | solution.py:554
  73.2 2.0 %collective-permute-done.3 = bf16[2,16,2688]{2,1,0:T(8,128)(2,1)S(1)} collective-permute-done((bf16[2,16,2688]{2,1,0:T(8,128)(2,1)S(1)}, bf16[2,16,2688]{2,1,0:T(8,128)(2,1)S(1)}, u32[]{:S(2)}, u32[]{:S(2)}) %collective-permute-start.3) | collective-permute-done | bytes 172064 | tf_op jit(solution)/shard_map/ppermute | solution.py:554
  75.2 4.1 %collective-permute-done.4 = bf16[2,16,2688]{2,1,0:T(8,128)(2,1)S(1)} collective-permute-done((bf16[2,16,2688]{2,1,0:T(8,128)(2,1)S(1)}, bf16[2,16,2688]{2,1,0:T(8,128)(2,1)S(1)}, u32[]{:S(2)}, u32[]{:S(2)}) %collective-permute-start.4) | collective-permute-done | bytes 172064 | tf_op jit(solution)/shard_map/ppermute | solution.py:554
  79.5 1.4 %collective-permute-start.6 = (bf16[16,2688]{1,0:T(8,128)(2,1)S(1)}, bf16[16,2688]{1,0:T(8,128)(2,1)S(1)}, u32[]{:S(2)}, u32[]{:S(2)}) collective-permute-start(bf16[16,2688]{1,0:T(8,128)(2,1)S(1)} %slice_bitcast_fusion.2), channel_id=1, source_target_pairs={{0,8},{2,10},{4,12},{6,14},{8,0},{10,2},{12,4},{14,6},{16,24},{18,... | collective-permute-start | bytes 258056 | tf_op jit(solution)/shard_map/ppermute | solution.py:554
  81.8 2.2 %collective-permute-done.6 = bf16[16,2688]{1,0:T(8,128)(2,1)S(1)} collective-permute-done((bf16[16,2688]{1,0:T(8,128)(2,1)S(1)}, bf16[16,2688]{1,0:T(8,128)(2,1)S(1)}, u32[]{:S(2)}, u32[]{:S(2)}) %collective-permute-start.6) | collective-permute-done | bytes 86048 | tf_op jit(solution)/shard_map/ppermute | solution.py:554
  84.1 1.6 %collective-permute-start.13 = (bf16[16,2688]{1,0:T(8,128)(2,1)S(1)}, bf16[16,2688]{1,0:T(8,128)(2,1)S(1)}, u32[]{:S(2)}, u32[]{:S(2)}) collective-permute-start(bf16[16,2688]{1,0:T(8,128)(2,1)S(1)} %fusion.2), channel_id=1, source_target_pairs={{0,8},{2,10},{4,12},{6,14},{8,0},{10,2},{12,4},{14,6},{16,24},{18,... | collective-permute-start | bytes 258056 | tf_op jit(solution)/shard_map/ppermute | solution.py:554
  85.6 3.0 %collective-permute-done.13 = bf16[16,2688]{1,0:T(8,128)(2,1)S(1)} collective-permute-done((bf16[16,2688]{1,0:T(8,128)(2,1)S(1)}, bf16[16,2688]{1,0:T(8,128)(2,1)S(1)}, u32[]{:S(2)}, u32[]{:S(2)}) %collective-permute-start.13) | collective-permute-done | bytes 86048 | tf_op jit(solution)/shard_map/ppermute | solution.py:554
  88.6 1.3 %collective-permute-start.14 = (bf16[2,16,2688]{2,1,0:T(8,128)(2,1)S(1)}, bf16[2,16,2688]{2,1,0:T(8,128)(2,1)S(1)}, u32[]{:S(2)}, u32[]{:S(2)}) collective-permute-start(bf16[2,16,2688]{2,1,0:T(8,128)(2,1)S(1)} %pad_maximum_fusion.1.refs_0_), channel_id=1, source_target_pairs={{0,2},{2,0},{4,6},{6,4},{8,10},{10,8},{12,14},{14,12},{16,18},{18,... | collective-permute-start | bytes 516104 | tf_op jit(solution)/shard_map/ppermute | solution.py:554
  89.9 2.2 %collective-permute-start.12 = (bf16[16,2688]{1,0:T(8,128)(2,1)S(1)}, bf16[16,2688]{1,0:T(8,128)(2,1)S(1)}, u32[]{:S(2)}, u32[]{:S(2)}) collective-permute-start(bf16[16,2688]{1,0:T(8,128)(2,1)S(1)} %fusion.2), channel_id=1, source_target_pairs={{0,24},{2,26},{4,28},{6,30},{8,16},{10,18},{12,20},{14,22},{16,8},... | collective-permute-start | bytes 258056 | tf_op jit(solution)/shard_map/ppermute | solution.py:554
  93.9 1.3 %collective-permute-start.15 = (bf16[2,16,2688]{2,1,0:T(8,128)(2,1)S(1)}, bf16[2,16,2688]{2,1,0:T(8,128)(2,1)S(1)}, u32[]{:S(2)}, u32[]{:S(2)}) collective-permute-start(bf16[2,16,2688]{2,1,0:T(8,128)(2,1)S(1)} %pad_maximum_fusion.1.refs_0_), channel_id=1, source_target_pairs={{0,4},{2,6},{4,0},{6,2},{8,12},{10,14},{12,8},{14,10},{16,20},{18,... | collective-permute-start | bytes 516104 | tf_op jit(solution)/shard_map/ppermute | solution.py:554
  95.2 3.2 %all-to-all-start.4 = ((bf16[32,8,512]{2,1,0:T(8,128)(2,1)}), bf16[32,8,512]{2,1,0:T(8,128)(2,1)S(1)}, u32[]{:S(2)}, u32[]{:S(2)}) async-start(bf16[32,8,512]{2,1,0:T(8,128)(2,1)} %bitcast.26), calls=%async_computation.4 | async-start | bytes 524288 | tf_op jit(solution)/shard_map/all_to_all | solution.py:698
  99.0 1.7 %collective-permute-done.15.refs_2_ = bf16[2,16,2688]{2,1,0:T(8,128)(2,1)S(1)} collective-permute-done((bf16[2,16,2688]{2,1,0:T(8,128)(2,1)S(1)}, bf16[2,16,2688]{2,1,0:T(8,128)(2,1)S(1)}, u32[]{:S(2)}, u32[]{:S(2)}) %collective-permute-start.15) | collective-permute-done | bytes 172064 | tf_op jit(solution)/shard_map/ppermute | solution.py:554
  103.4 1.3 %collective-permute-start.18 = (bf16[2,16,2688]{2,1,0:T(8,128)(2,1)S(1)}, bf16[2,16,2688]{2,1,0:T(8,128)(2,1)S(1)}, u32[]{:S(2)}, u32[]{:S(2)}) collective-permute-start(bf16[2,16,2688]{2,1,0:T(8,128)(2,1)S(1)} %pad_maximum_fusion.refs_4_), channel_id=1, source_target_pairs={{0,4},{2,6},{4,0},{6,2},{8,12},{10,14},{12,8},{14,10},{16,20},{18,... | collective-permute-start | bytes 516104 | tf_op jit(solution)/shard_map/ppermute | solution.py:554
  106.8 2.1 %shard_map.256 = (f32[512,2048]{1,0:T(8,128)}, f32[512,512]{1,0:T(8,128)}, f32[256,128]{1,0:T(8,128)S(1)}) custom-call(bf16[2,16,2688]{2,1,0:T(8,128)(2,1)S(1)} %pad_maximum_fusion.1.refs_0_, bf16[2,16,2688]{2,1,0:T(8,128)(2,1)S(1)} %collective-permute-done.14.refs_1_, bf16[2,16,2688]{2,1,0:T(8,128)(2,1)S(1)} %collective-permute-done.15.refs_2_, ...), custom_call_target="tpu_custom_call" | custom-call | flops 1048576 | bytes 5242880 | tf_op jit(solution)/shard_map/pallas_call | solution.py:775
  109.1 3.7 %shard_map.258 = f32[4096,512]{1,0:T(8,128)} custom-call(f32[8,256]{1,0:T(8,128)S(1)} %get-tuple-element.119.row_ref, bf16[256,512]{1,0:T(8,128)(2,1)S(1)} %bitcast.41), custom_call_target="tpu_custom_call" | custom-call | flops 1073741824 | bytes 8388608 | tf_op jit(solution)/shard_map/pallas_call | solution.py:703
  116.0 2.1 %shard_map.259 = (f32[512,2048]{1,0:T(8,128)}, f32[512,512]{1,0:T(8,128)}, f32[1,2048]{1,0:T(1,128)}, f32[1,512]{1,0:T(1,128)}, f32[1,512]{1,0:T(1,128)}, /*inde...) custom-call(bf16[2,16,2688]{2,1,0:T(8,128)(2,1)S(1)} %collective-permute-done.1, ...), custom_call_target="tpu_custom_call", output_to_operand_aliasing={{0}: (6, {}), {1}: (7, {})} | custom-call | flops 1048576 | bytes 3145728 | tf_op jit(solution)/shard_map/pallas_call | solution.py:786
  (86 shorter events, 17.3 us)
Async XLA Ops:
  34.2 13.7 %all-to-all-start.2 = ((bf16[16,16,512]{2,1,0:T(8,128)(2,1)}), bf16[16,16,512]{2,1,0:T(8,128)(2,1)S(1)}, u32[]{:S(2)}, u32[]{:S(2)}) async-start(bf16[16,16,512]{2,1,0:T(8,128)(2,1)} %bitcast.9), calls=%async_computation.2 | async-start | bytes 524288 | tf_op jit(solution)/shard_map/all_to_all | solution.py:647
  38.0 1.6 %collective-permute-start = (bf16[256,512]{1,0:T(8,128)(2,1)S(1)}, bf16[256,512]{1,0:T(8,128)(2,1)S(1)}, u32[]{:S(2)}, u32[]{:S(2)}) collective-permute-start(bf16[256,512]{1,0:T(8,128)(2,1)S(1)} %shard_map.250.go_ref), channel_id=1, source_target_pairs={{0,1},{1,0},{2,3},{3,2},{4,5},{5,4},{6,7},{7,6},{8,9},{9,8},{10,11... | collective-permute-start | bytes 786440 | tf_op jit(solution)/shard_map/ppermute | solution.py:566
  53.3 3.9 %collective-permute-start.1 = (bf16[256,1792]{1,0:T(8,128)(2,1)S(1)}, bf16[256,1792]{1,0:T(8,128)(2,1)S(1)}, u32[]{:S(2)}, u32[]{:S(2)}) collective-permute-start(bf16[256,1792]{1,0:T(8,128)(2,1)S(1)} %get-tuple-element.81), channel_id=1, source_target_pairs={{0,1},{1,0},{2,3},{3,2},{4,5},{5,4},{6,7},{7,6},{8,9},{9,8},{10,11... | collective-permute-start | bytes 2752520 | tf_op jit(solution)/shard_map/ppermute | solution.py:566
  57.2 48.5 %copy-start.3 = (s32[4096]{0:T(1024)S(1)}, s32[4096]{0:T(1024)}, u32[]{:S(2)}) copy-start(s32[4096]{0:T(1024)} %param.22) | copy-start | bytes 49156
  58.1 7.3 %collective-permute-start.2 = (bf16[2,16,2688]{2,1,0:T(8,128)(2,1)S(1)}, bf16[2,16,2688]{2,1,0:T(8,128)(2,1)S(1)}, u32[]{:S(2)}, u32[]{:S(2)}) collective-permute-start(bf16[2,16,2688]{2,1,0:T(8,128)(2,1)S(1)} %get-tuple-element.98), channel_id=1, source_target_pairs={{0,2},{2,0},{4,6},{6,4},{8,10},{10,8},{12,14},{14,12},{16,18},{18,... | collective-permute-start | bytes 516104 | tf_op jit(solution)/shard_map/ppermute | solution.py:554
  59.0 10.7 %collective-permute-start.7 = (bf16[2,16,2688]{2,1,0:T(8,128)(2,1)S(1)}, bf16[2,16,2688]{2,1,0:T(8,128)(2,1)S(1)}, u32[]{:S(2)}, u32[]{:S(2)}) collective-permute-start(bf16[2,16,2688]{2,1,0:T(8,128)(2,1)S(1)} %get-tuple-element.107), channel_id=1, source_target_pairs={{0,4},{2,6},{4,0},{6,2},{8,12},{10,14},{12,8},{14,10},{16,20},{18,... | collective-permute-start | bytes 516104 | tf_op jit(solution)/shard_map/ppermute | solution.py:554
  59.6 10.0 %collective-permute-start.8 = (bf16[2,16,2688]{2,1,0:T(8,128)(2,1)S(1)}, bf16[2,16,2688]{2,1,0:T(8,128)(2,1)S(1)}, u32[]{:S(2)}, u32[]{:S(2)}) collective-permute-start(bf16[2,16,2688]{2,1,0:T(8,128)(2,1)S(1)} %get-tuple-element.108), channel_id=1, source_target_pairs={{0,6},{2,4},{4,2},{6,0},{8,14},{10,12},{12,10},{14,8},{16,22},{18,... | collective-permute-start | bytes 516104 | tf_op jit(solution)/shard_map/ppermute | solution.py:554
  61.7 17.8 %all-to-all-start.3 = ((bf16[16,16,512]{2,1,0:T(8,128)(2,1)}), bf16[16,16,512]{2,1,0:T(8,128)(2,1)S(1)}, u32[]{:S(2)}, u32[]{:S(2)}) async-start(bf16[16,16,512]{2,1,0:T(8,128)(2,1)} %bitcast.16), calls=%async_computation.3 | async-start | bytes 524288 | tf_op jit(solution)/shard_map/all_to_all | solution.py:690
  65.4 9.8 %collective-permute-start.3 = (bf16[2,16,2688]{2,1,0:T(8,128)(2,1)S(1)}, bf16[2,16,2688]{2,1,0:T(8,128)(2,1)S(1)}, u32[]{:S(2)}, u32[]{:S(2)}) collective-permute-start(bf16[2,16,2688]{2,1,0:T(8,128)(2,1)S(1)} %get-tuple-element.100), channel_id=1, source_target_pairs={{0,2},{2,0},{4,6},{6,4},{8,10},{10,8},{12,14},{14,12},{16,18},{18,... | collective-permute-start | bytes 516104 | tf_op jit(solution)/shard_map/ppermute | solution.py:554
  67.2 12.2 %collective-permute-start.4 = (bf16[2,16,2688]{2,1,0:T(8,128)(2,1)S(1)}, bf16[2,16,2688]{2,1,0:T(8,128)(2,1)S(1)}, u32[]{:S(2)}, u32[]{:S(2)}) collective-permute-start(bf16[2,16,2688]{2,1,0:T(8,128)(2,1)S(1)} %get-tuple-element.101), channel_id=1, source_target_pairs={{0,4},{2,6},{4,0},{6,2},{8,12},{10,14},{12,8},{14,10},{16,20},{18,... | collective-permute-start | bytes 516104 | tf_op jit(solution)/shard_map/ppermute | solution.py:554
  68.6 10.7 %collective-permute-start.5 = (bf16[2,16,2688]{2,1,0:T(8,128)(2,1)S(1)}, bf16[2,16,2688]{2,1,0:T(8,128)(2,1)S(1)}, u32[]{:S(2)}, u32[]{:S(2)}) collective-permute-start(bf16[2,16,2688]{2,1,0:T(8,128)(2,1)S(1)} %get-tuple-element.102), channel_id=1, source_target_pairs={{0,6},{2,4},{4,2},{6,0},{8,14},{10,12},{12,10},{14,8},{16,22},{18,... | collective-permute-start | bytes 516104 | tf_op jit(solution)/shard_map/ppermute | solution.py:554
  69.8 12.0 %collective-permute-start.9 = (bf16[16,2688]{1,0:T(8,128)(2,1)S(1)}, bf16[16,2688]{1,0:T(8,128)(2,1)S(1)}, u32[]{:S(2)}, u32[]{:S(2)}) collective-permute-start(bf16[16,2688]{1,0:T(8,128)(2,1)S(1)} %get-tuple-element.138), channel_id=1, source_target_pairs={{0,16},{2,18},{4,20},{6,22},{8,24},{10,26},{12,28},{14,30},{16,0},... | collective-permute-start | bytes 258056 | tf_op jit(solution)/shard_map/ppermute | solution.py:554
  71.8 10.0 %collective-permute-start.10 = (bf16[16,2688]{1,0:T(8,128)(2,1)S(1)}, bf16[16,2688]{1,0:T(8,128)(2,1)S(1)}, u32[]{:S(2)}, u32[]{:S(2)}) collective-permute-start(bf16[16,2688]{1,0:T(8,128)(2,1)S(1)} %get-tuple-element.139), channel_id=1, source_target_pairs={{0,24},{2,26},{4,28},{6,30},{8,16},{10,18},{12,20},{14,22},{16,8},... | collective-permute-start | bytes 258056 | tf_op jit(solution)/shard_map/ppermute | solution.py:554
  79.5 4.6 %collective-permute-start.6 = (bf16[16,2688]{1,0:T(8,128)(2,1)S(1)}, bf16[16,2688]{1,0:T(8,128)(2,1)S(1)}, u32[]{:S(2)}, u32[]{:S(2)}) collective-permute-start(bf16[16,2688]{1,0:T(8,128)(2,1)S(1)} %slice_bitcast_fusion.2), channel_id=1, source_target_pairs={{0,8},{2,10},{4,12},{6,14},{8,0},{10,2},{12,4},{14,6},{16,24},{18,... | collective-permute-start | bytes 258056 | tf_op jit(solution)/shard_map/ppermute | solution.py:554
  84.1 4.6 %collective-permute-start.13 = (bf16[16,2688]{1,0:T(8,128)(2,1)S(1)}, bf16[16,2688]{1,0:T(8,128)(2,1)S(1)}, u32[]{:S(2)}, u32[]{:S(2)}) collective-permute-start(bf16[16,2688]{1,0:T(8,128)(2,1)S(1)} %fusion.2), channel_id=1, source_target_pairs={{0,8},{2,10},{4,12},{6,14},{8,0},{10,2},{12,4},{14,6},{16,24},{18,... | collective-permute-start | bytes 258056 | tf_op jit(solution)/shard_map/ppermute | solution.py:554
  88.6 6.5 %collective-permute-start.14 = (bf16[2,16,2688]{2,1,0:T(8,128)(2,1)S(1)}, bf16[2,16,2688]{2,1,0:T(8,128)(2,1)S(1)}, u32[]{:S(2)}, u32[]{:S(2)}) collective-permute-start(bf16[2,16,2688]{2,1,0:T(8,128)(2,1)S(1)} %pad_maximum_fusion.1.refs_0_), channel_id=1, source_target_pairs={{0,2},{2,0},{4,6},{6,4},{8,10},{10,8},{12,14},{14,12},{16,18},{18,... | collective-permute-start | bytes 516104 | tf_op jit(solution)/shard_map/ppermute | solution.py:554
  89.9 8.5 %collective-permute-start.12 = (bf16[16,2688]{1,0:T(8,128)(2,1)S(1)}, bf16[16,2688]{1,0:T(8,128)(2,1)S(1)}, u32[]{:S(2)}, u32[]{:S(2)}) collective-permute-start(bf16[16,2688]{1,0:T(8,128)(2,1)S(1)} %fusion.2), channel_id=1, source_target_pairs={{0,24},{2,26},{4,28},{6,30},{8,16},{10,18},{12,20},{14,22},{16,8},... | collective-permute-start | bytes 258056 | tf_op jit(solution)/shard_map/ppermute | solution.py:554
  92.2 6.2 %collective-permute-start.11 = (bf16[16,2688]{1,0:T(8,128)(2,1)S(1)}, bf16[16,2688]{1,0:T(8,128)(2,1)S(1)}, u32[]{:S(2)}, u32[]{:S(2)}) collective-permute-start(bf16[16,2688]{1,0:T(8,128)(2,1)S(1)} %fusion.2), channel_id=1, source_target_pairs={{0,16},{2,18},{4,20},{6,22},{8,24},{10,26},{12,28},{14,30},{16,0},... | collective-permute-start | bytes 258056 | tf_op jit(solution)/shard_map/ppermute | solution.py:554
  92.6 6.4 %collective-permute-start.16 = (bf16[2,16,2688]{2,1,0:T(8,128)(2,1)S(1)}, bf16[2,16,2688]{2,1,0:T(8,128)(2,1)S(1)}, u32[]{:S(2)}, u32[]{:S(2)}) collective-permute-start(bf16[2,16,2688]{2,1,0:T(8,128)(2,1)S(1)} %pad_maximum_fusion.1.refs_0_), channel_id=1, source_target_pairs={{0,6},{2,4},{4,2},{6,0},{8,14},{10,12},{12,10},{14,8},{16,22},{18,... | collective-permute-start | bytes 516104 | tf_op jit(solution)/shard_map/ppermute | solution.py:554
  93.9 6.9 %collective-permute-start.15 = (bf16[2,16,2688]{2,1,0:T(8,128)(2,1)S(1)}, bf16[2,16,2688]{2,1,0:T(8,128)(2,1)S(1)}, u32[]{:S(2)}, u32[]{:S(2)}) collective-permute-start(bf16[2,16,2688]{2,1,0:T(8,128)(2,1)S(1)} %pad_maximum_fusion.1.refs_0_), channel_id=1, source_target_pairs={{0,4},{2,6},{4,0},{6,2},{8,12},{10,14},{12,8},{14,10},{16,20},{18,... | collective-permute-start | bytes 516104 | tf_op jit(solution)/shard_map/ppermute | solution.py:554
  95.2 13.9 %all-to-all-start.4 = ((bf16[32,8,512]{2,1,0:T(8,128)(2,1)}), bf16[32,8,512]{2,1,0:T(8,128)(2,1)S(1)}, u32[]{:S(2)}, u32[]{:S(2)}) async-start(bf16[32,8,512]{2,1,0:T(8,128)(2,1)} %bitcast.26), calls=%async_computation.4 | async-start | bytes 524288 | tf_op jit(solution)/shard_map/all_to_all | solution.py:698
  100.8 1.4 %collective-permute-start.20 = (bf16[2,16,2688]{2,1,0:T(8,128)(2,1)S(1)}, bf16[2,16,2688]{2,1,0:T(8,128)(2,1)S(1)}, u32[]{:S(2)}, u32[]{:S(2)}) collective-permute-start(bf16[2,16,2688]{2,1,0:T(8,128)(2,1)S(1)} %pad_maximum_fusion.1.refs_0_), channel_id=1, source_target_pairs={{0,1},{1,0},{2,3},{3,2},{4,5},{5,4},{6,7},{7,6},{8,9},{9,8},{10,11... | collective-permute-start | bytes 516104 | tf_op jit(solution)/shard_map/ppermute | solution.py:566
  100.8 2.7 %collective-permute-start.21 = (bf16[2,16,2688]{2,1,0:T(8,128)(2,1)S(1)}, bf16[2,16,2688]{2,1,0:T(8,128)(2,1)S(1)}, u32[]{:S(2)}, u32[]{:S(2)}) collective-permute-start(bf16[2,16,2688]{2,1,0:T(8,128)(2,1)S(1)} %collective-permute-done.14.refs_1_), channel_id=1, source_target_pairs={{0,1},{1,0},{2,3},{3,2},{4,5},{5,4},{6,7},{7,6},{8,9},{9,8},{10,11... | collective-permute-start | bytes 516104 | tf_op jit(solution)/shard_map/ppermute | solution.py:566
  101.3 3.5 %collective-permute-start.22 = (bf16[2,16,2688]{2,1,0:T(8,128)(2,1)S(1)}, bf16[2,16,2688]{2,1,0:T(8,128)(2,1)S(1)}, u32[]{:S(2)}, u32[]{:S(2)}) collective-permute-start(bf16[2,16,2688]{2,1,0:T(8,128)(2,1)S(1)} %collective-permute-done.15.refs_2_), channel_id=1, source_target_pairs={{0,1},{1,0},{2,3},{3,2},{4,5},{5,4},{6,7},{7,6},{8,9},{9,8},{10,11... | collective-permute-start | bytes 516104 | tf_op jit(solution)/shard_map/ppermute | solution.py:566
  101.3 5.5 %collective-permute-start.23 = (bf16[2,16,2688]{2,1,0:T(8,128)(2,1)S(1)}, bf16[2,16,2688]{2,1,0:T(8,128)(2,1)S(1)}, u32[]{:S(2)}, u32[]{:S(2)}) collective-permute-start(bf16[2,16,2688]{2,1,0:T(8,128)(2,1)S(1)} %collective-permute-done.16.refs_3_), channel_id=1, source_target_pairs={{0,1},{1,0},{2,3},{3,2},{4,5},{5,4},{6,7},{7,6},{8,9},{9,8},{10,11... | collective-permute-start | bytes 516104 | tf_op jit(solution)/shard_map/ppermute | solution.py:566
  101.8 5.0 %collective-permute-start.24 = (bf16[2,16,2688]{2,1,0:T(8,128)(2,1)S(1)}, bf16[2,16,2688]{2,1,0:T(8,128)(2,1)S(1)}, u32[]{:S(2)}, u32[]{:S(2)}) collective-permute-start(bf16[2,16,2688]{2,1,0:T(8,128)(2,1)S(1)} %pad_maximum_fusion.refs_4_), channel_id=1, source_target_pairs={{0,1},{1,0},{2,3},{3,2},{4,5},{5,4},{6,7},{7,6},{8,9},{9,8},{10,11... | collective-permute-start | bytes 516104 | tf_op jit(solution)/shard_map/ppermute | solution.py:566
  102.2 10.6 %collective-permute-start.19 = (bf16[2,16,2688]{2,1,0:T(8,128)(2,1)S(1)}, bf16[2,16,2688]{2,1,0:T(8,128)(2,1)S(1)}, u32[]{:S(2)}, u32[]{:S(2)}) collective-permute-start(bf16[2,16,2688]{2,1,0:T(8,128)(2,1)S(1)} %pad_maximum_fusion.refs_4_), channel_id=1, source_target_pairs={{0,6},{2,4},{4,2},{6,0},{8,14},{10,12},{12,10},{14,8},{16,22},{18,... | collective-permute-start | bytes 516104 | tf_op jit(solution)/shard_map/ppermute | solution.py:554
  103.4 10.6 %collective-permute-start.18 = (bf16[2,16,2688]{2,1,0:T(8,128)(2,1)S(1)}, bf16[2,16,2688]{2,1,0:T(8,128)(2,1)S(1)}, u32[]{:S(2)}, u32[]{:S(2)}) collective-permute-start(bf16[2,16,2688]{2,1,0:T(8,128)(2,1)S(1)} %pad_maximum_fusion.refs_4_), channel_id=1, source_target_pairs={{0,4},{2,6},{4,0},{6,2},{8,12},{10,14},{12,8},{14,10},{16,20},{18,... | collective-permute-start | bytes 516104 | tf_op jit(solution)/shard_map/ppermute | solution.py:554
  104.7 9.3 %collective-permute-start.17 = (bf16[2,16,2688]{2,1,0:T(8,128)(2,1)S(1)}, bf16[2,16,2688]{2,1,0:T(8,128)(2,1)S(1)}, u32[]{:S(2)}, u32[]{:S(2)}) collective-permute-start(bf16[2,16,2688]{2,1,0:T(8,128)(2,1)S(1)} %pad_maximum_fusion.refs_4_), channel_id=1, source_target_pairs={{0,2},{2,0},{4,6},{6,4},{8,10},{10,8},{12,14},{14,12},{16,18},{18,... | collective-permute-start | bytes 516104 | tf_op jit(solution)/shard_map/ppermute | solution.py:554
  114.0 1.4 %collective-permute-start.25 = (bf16[2,16,2688]{2,1,0:T(8,128)(2,1)S(1)}, bf16[2,16,2688]{2,1,0:T(8,128)(2,1)S(1)}, u32[]{:S(2)}, u32[]{:S(2)}) collective-permute-start(bf16[2,16,2688]{2,1,0:T(8,128)(2,1)S(1)} %collective-permute-done.17.refs_0_), channel_id=1, source_target_pairs={{0,1},{1,0},{2,3},{3,2},{4,5},{5,4},{6,7},{7,6},{8,9},{9,8},{10,11... | collective-permute-start | bytes 516104 | tf_op jit(solution)/shard_map/ppermute | solution.py:566
  114.1 1.6 %collective-permute-start.26 = (bf16[2,16,2688]{2,1,0:T(8,128)(2,1)S(1)}, bf16[2,16,2688]{2,1,0:T(8,128)(2,1)S(1)}, u32[]{:S(2)}, u32[]{:S(2)}) collective-permute-start(bf16[2,16,2688]{2,1,0:T(8,128)(2,1)S(1)} %collective-permute-done.18.refs_1_), channel_id=1, source_target_pairs={{0,1},{1,0},{2,3},{3,2},{4,5},{5,4},{6,7},{7,6},{8,9},{9,8},{10,11... | collective-permute-start | bytes 516104 | tf_op jit(solution)/shard_map/ppermute | solution.py:566
  114.5 1.4 %collective-permute-start.27 = (bf16[2,16,2688]{2,1,0:T(8,128)(2,1)S(1)}, bf16[2,16,2688]{2,1,0:T(8,128)(2,1)S(1)}, u32[]{:S(2)}, u32[]{:S(2)}) collective-permute-start(bf16[2,16,2688]{2,1,0:T(8,128)(2,1)S(1)} %collective-permute-done.19.refs_2_), channel_id=1, source_target_pairs={{0,1},{1,0},{2,3},{3,2},{4,5},{5,4},{6,7},{7,6},{8,9},{9,8},{10,11... | collective-permute-start | bytes 516104 | tf_op jit(solution)/shard_map/ppermute | solution.py:566
  (16 other events, 503.3 us)

commit v4 on v3

--- a/solution.py
+++ b/solution.py
@@ -259,7 +259,7 @@
 
 
 def sigmoid(value):
-    return 1.0 / (1.0 + jnp.exp(-value))
+    return 0.5 * jnp.tanh(0.5 * value) + 0.5
 
 
 def layer_kernel(
@@ -466,7 +466,7 @@
             out[:, 2 * half_cols + width :] = small_ref[pl.ds(at, short), :].astype(BF16)
 
 
-def unpack(planes, columns, chunks, mine, theirs, uvqk_ref, wout_ref, small_ref, held_uvqk, held_wout, sems):
+def unpack(planes, columns, chunks, uvqk_ref, wout_ref, small_ref, held_uvqk, held_wout, sems):
     short = held_wout.shape[1]
     width = held_wout.shape[2]
     core = lax.axis_index("table")
@@ -476,60 +476,62 @@
     wout_lanes = slice(2 * half_cols, 2 * half_cols + width)
     small_lanes = slice(2 * half_cols + width, 2 * half_cols + width + LANES)
     copies = []
-    for rel_xy, rel_z, ref, at in chunks:
+    for n, (rel_xy, rel_z, whose, piece) in enumerate(chunks):
         chunk = jnp.bitwise_xor(my_xy, rel_xy) * planes + jnp.bitwise_xor(my_z, rel_z)
-        pieces = mine[ref].at[at], theirs[ref].at[at]
-        for piece, side in zip(pieces, (core, 1 - core)):
-            n = len(copies) // 2
-            for part in range(2):
-                held_uvqk[n, part * short : (part + 1) * short, :] = piece[
-                    :, part * half_cols : (part + 1) * half_cols
-                ].astype(F32)
-            held_wout[n] = piece[:, wout_lanes].astype(F32)
-            tall = pl.ds(pl.multiple_of(chunk * 2 * short, 2 * short), 2 * short)
-            cols = pl.ds(pl.multiple_of(side * half_cols, half_cols), half_cols)
-            rows = pl.ds(pl.multiple_of(side * half_y + chunk * short, short), short)
-            copies += start_all(
-                (held_uvqk.at[n], held_wout.at[n]),
-                (uvqk_ref.at[tall, cols], wout_ref.at[rows, :]),
-                sems.at[pl.ds(2 * n, 2)],
-            )
-        small_ref[pl.ds(pl.multiple_of(chunk * short, short), short), :] = pieces[0][:, small_lanes].astype(
-            F32
-        ) + pieces[1][:, small_lanes].astype(F32)
+        side = jnp.bitwise_xor(core, whose)
+        for part in range(2):
+            held_uvqk[n, part * short : (part + 1) * short, :] = piece[
+                :, part * half_cols : (part + 1) * half_cols
+            ].astype(F32)
+        held_wout[n] = piece[:, wout_lanes].astype(F32)
+        tall = pl.ds(pl.multiple_of(chunk * 2 * short, 2 * short), 2 * short)
+        cols = pl.ds(pl.multiple_of(side * half_cols, half_cols), half_cols)
+        rows = pl.ds(pl.multiple_of(side * half_y + chunk * short, short), short)
+        copies += start_all(
+            (held_uvqk.at[n], held_wout.at[n]),
+            (uvqk_ref.at[tall, cols], wout_ref.at[rows, :]),
+            sems.at[pl.ds(2 * n, 2)],
+        )
+        small_ref[pl.ds(pl.multiple_of(chunk * short, short), short), :] += piece[:, small_lanes].astype(F32)
     return copies
 
 
-def first_chunks(planes, columns):
-    near = [(xy, z, xy, z) for xy in range(columns) for z in range(2)]
-    return near + [(0, z, columns, z - 2) for z in range(2, planes)]
-
-
-def last_chunks(planes, columns):
-    return [(xy, z, xy - 1, z - 2) for xy in range(1, columns) for z in range(2, planes)]
+def chunks_of(planes, first_z, pieces, whose, first_xy=0):
+    return [
+        (first_xy + xy, first_z + z, whose, piece.at[z])
+        for xy, piece in enumerate(pieces)
+        for z in range(min(2, planes - first_z))
+    ]
 
 
 def unpack_first_kernel(planes, columns, *refs):
     mine, theirs = refs[: columns + 1], refs[columns + 1 : 2 * columns + 2]
-    uvqk_ref, wout_ref, small_ref, held_uvqk, held_wout, sems = refs[2 * columns + 2 :]
+    uvqk_ref, wout_ref, small_ref, *scratch = refs[2 * columns + 2 :]
     small_ref[...] = jnp.zeros_like(small_ref)
-    chunks = first_chunks(planes, columns)
-    for copy in unpack(
-        planes, columns, chunks, mine, theirs, uvqk_ref, wout_ref, small_ref, held_uvqk, held_wout, sems
-    ):
+    chunks = []
+    for whose, pieces in enumerate((mine, theirs)):
+        chunks += chunks_of(planes, 0, pieces[:columns], whose) + chunks_of(planes, 2, pieces[columns:], whose)
+    for copy in unpack(planes, columns, chunks, uvqk_ref, wout_ref, small_ref, *scratch):
+        copy.wait()
+
+
+def unpack_next_kernel(planes, columns, *refs):
+    peers = columns - 1
+    mine, before_ref = refs[:peers], refs[peers + 2]
+    uvqk_ref, wout_ref, small_ref, *scratch = refs[peers + 3 :]
+    small_ref[...] = before_ref[...]
+    chunks = chunks_of(planes, 2, mine, 0, 1)
+    for copy in unpack(planes, columns, chunks, uvqk_ref, wout_ref, small_ref, *scratch):
         copy.wait()
 
 
 def unpack_last_kernel(planes, columns, *refs):
     peers = columns - 1
-    mine, theirs, first_ref = refs[:peers], refs[peers : 2 * peers], refs[2 * peers + 2]
-    uvqk_ref, wout_ref, b_ref, g1_ref, g2_ref, bo_ref, pos_ref, time_ref = refs[2 * peers + 3 : 2 * peers + 11]
-    small_ref, held_uvqk, held_wout, sems = refs[2 * peers + 11 :]
-    small_ref[...] = first_ref[...]
-    chunks = last_chunks(planes, columns)
-    copies = unpack(
-        planes, columns, chunks, mine, theirs, uvqk_ref, wout_ref, small_ref, held_uvqk, held_wout, sems
-    )
+    theirs, before_ref = refs[:peers], refs[peers + 2]
+    uvqk_ref, wout_ref, b_ref, g1_ref, g2_ref, bo_ref, pos_ref, time_ref, small_ref, *scratch = refs[peers + 3 :]
+    small_ref[...] = before_ref[...]
+    chunks = chunks_of(planes, 2, theirs, 1, 1)
+    copies = unpack(planes, columns, chunks, uvqk_ref, wout_ref, small_ref, *scratch)
     at = 0
     for out in (b_ref, g1_ref, g2_ref, bo_ref):
         for col in range(0, out.shape[1], LANES):
@@ -753,10 +755,9 @@
         far = [xor_step(own, replicas, k * columns) for k in range(2, planes)]
         near = jnp.stack([own, next_own])
         nears = gather_step(near, replicas, 1, columns)
-        nears[1], sums = lax.optimization_barrier((nears[1], sums))
+        far[1], sums = lax.optimization_barrier((far[1], sums))
         got_sums = send_sums(sums)
         far = jnp.stack(far)
-        far, nears = lax.optimization_barrier((far, nears))
         table_grad = into_table(got_sums)
         fars = gather_step(far, replicas, 1, columns)
         their_nears = [swap_cores(piece) for piece in nears]
@@ -764,29 +765,38 @@
         small_shape = shape_of((width // 2, LANES), F32)
         wide_shapes = (shape_of((width, 4 * width), F32), shape_of((width, width), F32))
 
-        def unpack_scratch(chunks):
-            n = 2 * len(chunks)
-            return (
-                pltpu.VMEM((n, 2 * short, half_cols), F32),
-                pltpu.VMEM((n, short, width), F32),
-                pltpu.SemaphoreType.DMA((2 * n,)),
+        def unpack_call(body, specs, outs, chunks, scratch=(), aliases=None):
+            return call(
+                functools.partial(body, planes, columns),
+                wide_shapes + outs,
+                specs,
+                mb,
+                3 * mb,
+                scratch=scratch
+                + (
+                    pltpu.VMEM((chunks, 2 * short, half_cols), F32),
+                    pltpu.VMEM((chunks, short, width), F32),
+                    pltpu.SemaphoreType.DMA((2 * chunks,)),
+                ),
+                out_specs=(HBM, HBM) + (VMEM,) * len(outs),
+                aliases=aliases,
             )
 
-        w_uvqk_sum, w_out_sum, small_sum = call(
-            functools.partial(unpack_first_kernel, planes, columns),
-            wide_shapes + (small_shape,),
-            [VMEM] * (2 * columns + 2),
-            mb,
-            5 * mb,
-            scratch=unpack_scratch(first_chunks(planes, columns)),
-            out_specs=(HBM, HBM, VMEM),
+        peers = columns - 1
+        wides = {peers: 0, peers + 1: 1}
+        wide_specs = [VMEM] * peers + [HBM, HBM, VMEM]
+        *sums_so_far, small_sum = unpack_call(
+            unpack_first_kernel, [VMEM] * (2 * columns + 2), (small_shape,), 2 * (2 * columns + 2)
         )(*nears, far, *their_nears, their_far)
         fars, small_sum, table_grad = lax.optimization_barrier((fars, small_sum, table_grad))
         their_fars = [swap_cores(piece) for piece in fars[1:]]
-        w_uvqk_sum, w_out_sum, b_sum, g1_sum, g2_sum, bo_sum, pos_sum, time_sum = call(
-            functools.partial(unpack_last_kernel, planes, columns),
-            wide_shapes
-            + (
+        *sums_so_far, small_sum = unpack_call(
+            unpack_next_kernel, wide_specs, (small_shape,), 2 * peers, aliases=wides
+        )(*fars[1:], *sums_so_far, small_sum)
+        w_uvqk_sum, w_out_sum, b_sum, g1_sum, g2_sum, bo_sum, pos_sum, time_sum = unpack_call(
+            unpack_last_kernel,
+            wide_specs,
+            (
                 shape_of((1, 4 * width), F32),
                 shape_of((1, width), F32),
                 shape_of((1, width), F32),
@@ -794,13 +804,10 @@
                 shape_of((heads, count), F32),
                 shape_of((heads, count), F32),
             ),
-            [VMEM] * (2 * columns - 2) + [HBM, HBM, VMEM],
-            mb,
-            3 * mb,
-            scratch=(pltpu.VMEM(small_shape.shape, F32),) + unpack_scratch(last_chunks(planes, columns)),
-            out_specs=(HBM, HBM) + (VMEM,) * 6,
-            aliases={2 * columns - 2: 0, 2 * columns - 1: 1},
-        )(*fars[1:], *their_fars, w_uvqk_sum, w_out_sum, small_sum)
+            2 * peers,
+            scratch=(pltpu.VMEM(small_shape.shape, F32),),
+            aliases=wides,
+        )(*their_fars, *sums_so_far, small_sum)
     else:
         table_grad = into_table(to_owners(home_again(dx)))
         w_uvqk_sum, w_out_sum, parts = lax.psum((dot_tn(n1, dh), dot_tn(y, go), small[0:SMALL_ROWS]), BOTH)

time: 119 us -> 115 us (0.966)
  waiting for transfers between devices: 26.7 us -> 22.8 us
    ppermute x18, waiting for transfers between devices: 15.6 us -> 10.8 us  [xor_step(): return lax.ppermute(value, 'dp', [(i, i ^ step) for i in range(size)])]
    all_to_all x1, waiting for transfers between devices: 0.19 us -> 2.44 us  [send_sums(): lax.all_to_all(sums.reshape(devices, cap, width), BOTH, 0, 0, tiled=True)]
    ppermute x10, waiting for transfers between devices: 3.3 us -> 1.96 us  [swap_cores(): return lax.ppermute(value, 'table', [(0, 1), (1, 0)])]
    pallas_call x2 -> x3, Pallas kernels: 4.14 us -> 4.76 us  [the longest x1 2.05 us: on_device(): unpack_call(unpack_first_kernel, [VMEM] * (2 * columns + 2), (small_shape...]
  transfers between devices with their start and end apart: 31 -> 31, of which waited for: 15 -> 12; matrix products, arithmetic and copies ran while one was open for 0% -> 0% of each run, Pallas kernels for 10% -> 11%
where the time goes in v4:
time: 115 us
  starting transfers between devices  35.7 us (31%)
  blocking collectives  26.7 us (23%)
  Pallas kernels  25.1 us (22%)
  waiting for transfers between devices  22.8 us (20%)
  local copies, waits for them, and re-layouts  2.99 us (3%)
  between operations  1.17 us (1%)
    ppermute x18, starting transfers between devices, xor_step(): return lax.ppermute(value, 'dp', [(i, i ^ step) for i in range(size)])  22.8 us
    all_to_all x1, blocking collectives, on_device(): lax.all_to_all(msg.reshape(devices, 1, LANES), BOTH, 0, 0, tiled=True)  14.4 us
    all_to_all x1, blocking collectives, on_device(): lax.all_to_all(served.reshape(devices, cap, width), BOTH, 0, 0, tiled=True)  12.3 us
    ppermute x18, waiting for transfers between devices, xor_step(): return lax.ppermute(value, 'dp', [(i, i ^ step) for i in range(size)])  10.8 us
    all_to_all x1, waiting for transfers between devices, on_device(): lax.all_to_all(home.reshape(replicas, piece, width), 'dp', 0, 0, tiled=True)  7.6 us
    pallas_call x1, Pallas kernels, on_device(): call(functools.partial(layer_kernel, staged), (shape_of((rows, width), BF...  5.18 us
    all_to_all x1, starting transfers between devices, send_sums(): lax.all_to_all(sums.reshape(devices, cap, width), BOTH, 0, 0, tiled=True)  3.89 us
    all_to_all x1, starting transfers between devices, home_again(): lax.all_to_all(dx.reshape(replicas, piece, width), 'dp', 0, 0, tiled=True)  3.71 us
  transfers between devices with their start and end apart: 31, of which 12 were waited for; matrix products, arithmetic and copies ran while one was open for 0% of the time, Pallas kernels for 11%

profile of v4, /device:TPU:0, one launch (start us, length us, event | category | flops | bytes accessed | tf_op | source)
XLA Modules:
  0.0 114.7 jit_solution(17628947430049648089)
XLA Ops:
  0.6 1.7 %shard_map.247 = s32[32,128]{1,0:T(8,128)} custom-call(s32[8,32]{1,0:T(8,128)} %bitcast.66, s32[1,256]{1,0:T(1,128)} %bitcast.51, s32[1,64]{1,0:T(1,128)} %len_ref.3, s32[1,64]{1,0:T(1,128)} %dest_ref.3, s32[32,128]{1,0:T(8,128)} %bitcast.49), custom_call_target="tpu_custom_call" | custom-call | flops 1048576 | bytes 131072 | tf_op jit(solution)/shard_map/pallas_call | solution.py:611
  2.4 14.4 %all_to_all.25 = s32[32,1,128]{2,1,0:T(1,128)S(1)} all-to-all(s32[32,1,128]{2,1,0:T(1,128)} %bitcast.65), channel_id=1, replica_groups=mesh['dp'=16,'table'=2] {'dp','table'}, dimensions={0} | all-to-all | bytes 32768 | tf_op jit(solution)/shard_map/all_to_all | solution.py:627
  16.8 2.2 %copy-done = bf16[4096,512]{1,0:T(8,128)(2,1)S(1)} copy-done((bf16[4096,512]{1,0:T(8,128)(2,1)S(1)}, bf16[4096,512]{1,0:T(8,128)(2,1)}, u32[]{:S(2)}) %copy-start) | copy-done | bytes 4194328
  19.0 1.9 %shard_map.248 = bf16[256,512]{1,0:T(8,128)(2,1)S(1)} custom-call(s32[32,128]{1,0:T(8,128)S(1)} %bitcast.47, bf16[4096,512]{1,0:T(8,128)(2,1)S(1)} %copy-done), custom_call_target="tpu_custom_call" | custom-call | flops 1073741824 | bytes 5242880 | tf_op jit(solution)/shard_map/pallas_call | solution.py:628
  20.9 12.3 %all_to_all.26 = bf16[32,8,512]{2,1,0:T(8,128)(2,1)S(1)} all-to-all(bf16[32,8,512]{2,1,0:T(8,128)(2,1)S(1)} %bitcast.44), channel_id=1, replica_groups=mesh['dp'=16,'table'=2] {'dp','table'}, dimensions={0} | all-to-all | bytes 524288 | tf_op jit(solution)/shard_map/all_to_all | solution.py:632
  34.2 3.5 %all-to-all-start.2 = ((bf16[16,16,512]{2,1,0:T(8,128)(2,1)}), bf16[16,16,512]{2,1,0:T(8,128)(2,1)S(1)}, u32[]{:S(2)}, u32[]{:S(2)}) async-start(bf16[16,16,512]{2,1,0:T(8,128)(2,1)} %bitcast.9), calls=%async_computation.2 | async-start | bytes 524288 | tf_op jit(solution)/shard_map/all_to_all | solution.py:649
  38.0 1.5 %collective-permute-done.got_go_ref = bf16[256,512]{1,0:T(8,128)(2,1)S(1)} collective-permute-done((bf16[256,512]{1,0:T(8,128)(2,1)S(1)}, bf16[256,512]{1,0:T(8,128)(2,1)S(1)}, u32[]{:S(2)}, u32[]{:S(2)}) %collective-permute-start) | collective-permute-done | bytes 262176 | tf_op jit(solution)/shard_map/ppermute | solution.py:568
  40.3 7.6 %all-to-all-done.2 = bf16[16,16,512]{2,1,0:T(8,128)(2,1)S(1)} async-done(((bf16[16,16,512]{2,1,0:T(8,128)(2,1)}), bf16[16,16,512]{2,1,0:T(8,128)(2,1)S(1)}, u32[]{:S(2)}, u32[]{:S(2)}) %all-to-all-start.2) | async-done | bytes 262176 | tf_op jit(solution)/shard_map/all_to_all | solution.py:649
  47.9 5.2 %shard_map.251 = (bf16[256,512]{1,0:T(8,128)(2,1)}, bf16[256,512]{1,0:T(8,128)(2,1)S(1)}, bf16[256,512]{1,0:T(8,128)(2,1)S(1)}, bf16[256,2048]{1,0:T(8,128)(2,1)...) custom-call(bf16[256,512]{1,0:T(8,128)(2,1)S(1)} %bitcast.42, ...), custom_call_target="tpu_custom_call" | custom-call | flops 2147483648 | bytes 8388608 | tf_op jit(solution)/shard_map/pallas_call | solution.py:656
  53.2 1.6 %shard_map.252 = (bf16[256,512]{1,0:T(8,128)(2,1)}, f32[1,512]{1,0:T(1,128)S(1)}) custom-call(bf16[256,2048]{1,0:T(8,128)(2,1)S(1)} %get-tuple-element.75.dh_ref, bf16[512,2048]{1,0:T(8,128)(2,1)S(1)} %copy-done.1, bf16[256,512]{1,0:T(8,128)(2,1)S(1)} %bitcast.43, f32[1,512]{1,0:T(1,128)S(1)} %bitcast.55, bf16[256,512]{1,0:T(8,128)(2,1)S(1)} %shard_map.250.go_ref), custom_call_target="tpu_custom_call" | custom-call | flops 536870912 | bytes 4194304 | tf_op jit(solution)/shard_map/pallas_call | solution.py:721
  54.8 2.2 %shard_map.253.small_ref = f32[256,128]{1,0:T(8,128)S(1)} custom-call(bf16[8,256,256]{2,1,0:T(8,128)(2,1)S(1)} %get-tuple-element.81.ds_ref, s32[1,256]{1,0:T(1,128)S(1)} %bitcast.57, bf16[256,2048]{1,0:T(8,128)(2,1)S(1)} %get-tuple-element.75.dh_ref, bf16[256,512]{1,0:T(8,128)(2,1)S(1)} %shard_map.250.go_ref, f32[1,512]{1,0:T(1,128)S(1)} %get-tuple-element.82.g1g_ref, ...), custom_call_target="tpu_custom_call" | custom-call | flops 268435456 | bytes 2097152 | tf_op jit(solution)/shard_map/pallas_call | solution.py:724
  59.5 2.0 %collective-permute-start.8 = (bf16[2,16,2688]{2,1,0:T(8,128)(2,1)S(1)}, bf16[2,16,2688]{2,1,0:T(8,128)(2,1)S(1)}, u32[]{:S(2)}, u32[]{:S(2)}) collective-permute-start(bf16[2,16,2688]{2,1,0:T(8,128)(2,1)S(1)} %get-tuple-element.106), channel_id=1, source_target_pairs={{0,6},{2,4},{4,2},{6,0},{8,14},{10,12},{12,10},{14,8},{16,22},{18,... | collective-permute-start | bytes 516104 | tf_op jit(solution)/shard_map/ppermute | solution.py:556
  61.5 3.7 %all-to-all-start.3 = ((bf16[16,16,512]{2,1,0:T(8,128)(2,1)}), bf16[16,16,512]{2,1,0:T(8,128)(2,1)S(1)}, u32[]{:S(2)}, u32[]{:S(2)}) async-start(bf16[16,16,512]{2,1,0:T(8,128)(2,1)} %bitcast.16), calls=%async_computation.3 | async-start | bytes 524288 | tf_op jit(solution)/shard_map/all_to_all | solution.py:692
  65.2 1.8 %collective-permute-start.3 = (bf16[2,16,2688]{2,1,0:T(8,128)(2,1)S(1)}, bf16[2,16,2688]{2,1,0:T(8,128)(2,1)S(1)}, u32[]{:S(2)}, u32[]{:S(2)}) collective-permute-start(bf16[2,16,2688]{2,1,0:T(8,128)(2,1)S(1)} %get-tuple-element.98), channel_id=1, source_target_pairs={{0,2},{2,0},{4,6},{6,4},{8,10},{10,8},{12,14},{14,12},{16,18},{18,... | collective-permute-start | bytes 516104 | tf_op jit(solution)/shard_map/ppermute | solution.py:556
  67.0 1.5 %collective-permute-start.4 = (bf16[2,16,2688]{2,1,0:T(8,128)(2,1)S(1)}, bf16[2,16,2688]{2,1,0:T(8,128)(2,1)S(1)}, u32[]{:S(2)}, u32[]{:S(2)}) collective-permute-start(bf16[2,16,2688]{2,1,0:T(8,128)(2,1)S(1)} %get-tuple-element.99), channel_id=1, source_target_pairs={{0,4},{2,6},{4,0},{6,2},{8,12},{10,14},{12,8},{14,10},{16,20},{18,... | collective-permute-start | bytes 516104 | tf_op jit(solution)/shard_map/ppermute | solution.py:556
  69.7 1.9 %collective-permute-start.9 = (bf16[16,2688]{1,0:T(8,128)(2,1)S(1)}, bf16[16,2688]{1,0:T(8,128)(2,1)S(1)}, u32[]{:S(2)}, u32[]{:S(2)}) collective-permute-start(bf16[16,2688]{1,0:T(8,128)(2,1)S(1)} %get-tuple-element.134), channel_id=1, source_target_pairs={{0,16},{2,18},{4,20},{6,22},{8,24},{10,26},{12,28},{14,30},{16,0},... | collective-permute-start | bytes 258056 | tf_op jit(solution)/shard_map/ppermute | solution.py:556
  71.6 1.5 %collective-permute-start.10 = (bf16[16,2688]{1,0:T(8,128)(2,1)S(1)}, bf16[16,2688]{1,0:T(8,128)(2,1)S(1)}, u32[]{:S(2)}, u32[]{:S(2)}) collective-permute-start(bf16[16,2688]{1,0:T(8,128)(2,1)S(1)} %get-tuple-element.135), channel_id=1, source_target_pairs={{0,24},{2,26},{4,28},{6,30},{8,16},{10,18},{12,20},{14,22},{16,8},... | collective-permute-start | bytes 258056 | tf_op jit(solution)/shard_map/ppermute | solution.py:556
  73.1 2.0 %collective-permute-done.3 = bf16[2,16,2688]{2,1,0:T(8,128)(2,1)S(1)} collective-permute-done((bf16[2,16,2688]{2,1,0:T(8,128)(2,1)S(1)}, bf16[2,16,2688]{2,1,0:T(8,128)(2,1)S(1)}, u32[]{:S(2)}, u32[]{:S(2)}) %collective-permute-start.3) | collective-permute-done | bytes 172064 | tf_op jit(solution)/shard_map/ppermute | solution.py:556
  75.1 4.1 %collective-permute-done.4 = bf16[2,16,2688]{2,1,0:T(8,128)(2,1)S(1)} collective-permute-done((bf16[2,16,2688]{2,1,0:T(8,128)(2,1)S(1)}, bf16[2,16,2688]{2,1,0:T(8,128)(2,1)S(1)}, u32[]{:S(2)}, u32[]{:S(2)}) %collective-permute-start.4) | collective-permute-done | bytes 172064 | tf_op jit(solution)/shard_map/ppermute | solution.py:556
  79.3 1.4 %collective-permute-start.6 = (bf16[16,2688]{1,0:T(8,128)(2,1)S(1)}, bf16[16,2688]{1,0:T(8,128)(2,1)S(1)}, u32[]{:S(2)}, u32[]{:S(2)}) collective-permute-start(bf16[16,2688]{1,0:T(8,128)(2,1)S(1)} %slice_bitcast_fusion.2), channel_id=1, source_target_pairs={{0,8},{2,10},{4,12},{6,14},{8,0},{10,2},{12,4},{14,6},{16,24},{18,... | collective-permute-start | bytes 258056 | tf_op jit(solution)/shard_map/ppermute | solution.py:556
  81.6 2.2 %collective-permute-done.6 = bf16[16,2688]{1,0:T(8,128)(2,1)S(1)} collective-permute-done((bf16[16,2688]{1,0:T(8,128)(2,1)S(1)}, bf16[16,2688]{1,0:T(8,128)(2,1)S(1)}, u32[]{:S(2)}, u32[]{:S(2)}) %collective-permute-start.6) | collective-permute-done | bytes 86048 | tf_op jit(solution)/shard_map/ppermute | solution.py:556
  83.9 1.6 %collective-permute-start.16 = (bf16[16,2688]{1,0:T(8,128)(2,1)S(1)}, bf16[16,2688]{1,0:T(8,128)(2,1)S(1)}, u32[]{:S(2)}, u32[]{:S(2)}) collective-permute-start(bf16[16,2688]{1,0:T(8,128)(2,1)S(1)} %fusion.2), channel_id=1, source_target_pairs={{0,8},{2,10},{4,12},{6,14},{8,0},{10,2},{12,4},{14,6},{16,24},{18,... | collective-permute-start | bytes 258056 | tf_op jit(solution)/shard_map/ppermute | solution.py:556
  85.5 1.7 %collective-permute-start.12 = (bf16[16,2688]{1,0:T(8,128)(2,1)S(1)}, bf16[16,2688]{1,0:T(8,128)(2,1)S(1)}, u32[]{:S(2)}, u32[]{:S(2)}) collective-permute-start(bf16[16,2688]{1,0:T(8,128)(2,1)S(1)} %fusion.2), channel_id=1, source_target_pairs={{0,24},{2,26},{4,28},{6,30},{8,16},{10,18},{12,20},{14,22},{16,8},... | collective-permute-start | bytes 258056 | tf_op jit(solution)/shard_map/ppermute | solution.py:556
  87.5 1.3 %collective-permute-done.16 = bf16[16,2688]{1,0:T(8,128)(2,1)S(1)} collective-permute-done((bf16[16,2688]{1,0:T(8,128)(2,1)S(1)}, bf16[16,2688]{1,0:T(8,128)(2,1)S(1)}, u32[]{:S(2)}, u32[]{:S(2)}) %collective-permute-start.16) | collective-permute-done | bytes 86048 | tf_op jit(solution)/shard_map/ppermute | solution.py:556
  88.8 2.3 %collective-permute-start.19 = (bf16[2,16,2688]{2,1,0:T(8,128)(2,1)S(1)}, bf16[2,16,2688]{2,1,0:T(8,128)(2,1)S(1)}, u32[]{:S(2)}, u32[]{:S(2)}) collective-permute-start(bf16[2,16,2688]{2,1,0:T(8,128)(2,1)S(1)} %pad_maximum_fusion.1.refs_0_), channel_id=1, source_target_pairs={{0,6},{2,4},{4,2},{6,0},{8,14},{10,12},{12,10},{14,8},{16,22},{18,... | collective-permute-start | bytes 516104 | tf_op jit(solution)/shard_map/ppermute | solution.py:556
  92.6 3.9 %all-to-all-start.4 = ((bf16[32,8,512]{2,1,0:T(8,128)(2,1)}), bf16[32,8,512]{2,1,0:T(8,128)(2,1)S(1)}, u32[]{:S(2)}, u32[]{:S(2)}) async-start(bf16[32,8,512]{2,1,0:T(8,128)(2,1)} %bitcast.26), calls=%async_computation.4 | async-start | bytes 524288 | tf_op jit(solution)/shard_map/all_to_all | solution.py:700
  98.0 2.7 %collective-permute-start.15 = (bf16[2,16,2688]{2,1,0:T(8,128)(2,1)S(1)}, bf16[2,16,2688]{2,1,0:T(8,128)(2,1)S(1)}, u32[]{:S(2)}, u32[]{:S(2)}) collective-permute-start(bf16[2,16,2688]{2,1,0:T(8,128)(2,1)S(1)} %pad_maximum_fusion.refs_4_), channel_id=1, source_target_pairs={{0,6},{2,4},{4,2},{6,0},{8,14},{10,12},{12,10},{14,8},{16,22},{18,... | collective-permute-start | bytes 516104 | tf_op jit(solution)/shard_map/ppermute | solution.py:556
  101.5 1.1 shard_map.257
  102.7 2.0 %shard_map.256 = (f32[512,2048]{1,0:T(8,128)}, f32[512,512]{1,0:T(8,128)}, f32[256,128]{1,0:T(8,128)S(1)}) custom-call(bf16[2,16,2688]{2,1,0:T(8,128)(2,1)S(1)} %pad_maximum_fusion.1.refs_0_, bf16[2,16,2688]{2,1,0:T(8,128)(2,1)S(1)} %collective-permute-done.17.refs_1_, bf16[2,16,2688]{2,1,0:T(8,128)(2,1)S(1)} %collective-permute-done.18.refs_2_, ...), custom_call_target="tpu_custom_call" | custom-call | flops 1048576 | bytes 3145728 | tf_op jit(solution)/shard_map/pallas_call | solution.py:788
  104.7 2.4 %all-to-all-done.4 = bf16[32,8,512]{2,1,0:T(8,128)(2,1)S(1)} async-done(((bf16[32,8,512]{2,1,0:T(8,128)(2,1)}), bf16[32,8,512]{2,1,0:T(8,128)(2,1)S(1)}, u32[]{:S(2)}, u32[]{:S(2)}) %all-to-all-start.4) | async-done | bytes 262176 | tf_op jit(solution)/shard_map/all_to_all | solution.py:700
  107.2 3.7 %shard_map.258 = f32[4096,512]{1,0:T(8,128)} custom-call(f32[8,256]{1,0:T(8,128)S(1)} %get-tuple-element.112.row_ref, bf16[256,512]{1,0:T(8,128)(2,1)S(1)} %bitcast.41), custom_call_target="tpu_custom_call" | custom-call | flops 1073741824 | bytes 8388608 | tf_op jit(solution)/shard_map/pallas_call | solution.py:705
  112.9 1.7 %shard_map.260 = (f32[512,2048]{1,0:T(8,128)}, f32[512,512]{1,0:T(8,128)}, f32[1,2048]{1,0:T(1,128)}, f32[1,512]{1,0:T(1,128)}, f32[1,512]{1,0:T(1,128)}, /*inde...) custom-call(bf16[2,16,2688]{2,1,0:T(8,128)(2,1)S(1)} %collective-permute-done.2, ...), custom_call_target="tpu_custom_call", output_to_operand_aliasing={{0}: (3, {}), {1}: (4, {})} | custom-call | flops 1048576 | bytes 3145728 | tf_op jit(solution)/shard_map/pallas_call | solution.py:796
  (87 shorter events, 13.1 us)
Async XLA Ops:
  2.4 45.5 %copy-start.5 = (f32[512]{0:T(512)S(1)}, f32[512]{0:T(512)}, u32[]{:S(2)}) copy-start(f32[512]{0:T(512)} %param.23) | copy-start | bytes 6148
  34.2 13.7 %all-to-all-start.2 = ((bf16[16,16,512]{2,1,0:T(8,128)(2,1)}), bf16[16,16,512]{2,1,0:T(8,128)(2,1)S(1)}, u32[]{:S(2)}, u32[]{:S(2)}) async-start(bf16[16,16,512]{2,1,0:T(8,128)(2,1)} %bitcast.9), calls=%async_computation.2 | async-start | bytes 524288 | tf_op jit(solution)/shard_map/all_to_all | solution.py:649
  38.0 1.6 %collective-permute-start = (bf16[256,512]{1,0:T(8,128)(2,1)S(1)}, bf16[256,512]{1,0:T(8,128)(2,1)S(1)}, u32[]{:S(2)}, u32[]{:S(2)}) collective-permute-start(bf16[256,512]{1,0:T(8,128)(2,1)S(1)} %shard_map.250.go_ref), channel_id=1, source_target_pairs={{0,1},{1,0},{2,3},{3,2},{4,5},{5,4},{6,7},{7,6},{8,9},{9,8},{10,11... | collective-permute-start | bytes 786440 | tf_op jit(solution)/shard_map/ppermute | solution.py:568
  53.1 3.9 %collective-permute-start.1 = (bf16[256,1792]{1,0:T(8,128)(2,1)S(1)}, bf16[256,1792]{1,0:T(8,128)(2,1)S(1)}, u32[]{:S(2)}, u32[]{:S(2)}) collective-permute-start(bf16[256,1792]{1,0:T(8,128)(2,1)S(1)} %get-tuple-element.79), channel_id=1, source_target_pairs={{0,1},{1,0},{2,3},{3,2},{4,5},{5,4},{6,7},{7,6},{8,9},{9,8},{10,11... | collective-permute-start | bytes 2752520 | tf_op jit(solution)/shard_map/ppermute | solution.py:568
  58.0 7.3 %collective-permute-start.2 = (bf16[2,16,2688]{2,1,0:T(8,128)(2,1)S(1)}, bf16[2,16,2688]{2,1,0:T(8,128)(2,1)S(1)}, u32[]{:S(2)}, u32[]{:S(2)}) collective-permute-start(bf16[2,16,2688]{2,1,0:T(8,128)(2,1)S(1)} %get-tuple-element.96), channel_id=1, source_target_pairs={{0,2},{2,0},{4,6},{6,4},{8,10},{10,8},{12,14},{14,12},{16,18},{18,... | collective-permute-start | bytes 516104 | tf_op jit(solution)/shard_map/ppermute | solution.py:556
  58.8 10.7 %collective-permute-start.7 = (bf16[2,16,2688]{2,1,0:T(8,128)(2,1)S(1)}, bf16[2,16,2688]{2,1,0:T(8,128)(2,1)S(1)}, u32[]{:S(2)}, u32[]{:S(2)}) collective-permute-start(bf16[2,16,2688]{2,1,0:T(8,128)(2,1)S(1)} %get-tuple-element.105), channel_id=1, source_target_pairs={{0,4},{2,6},{4,0},{6,2},{8,12},{10,14},{12,8},{14,10},{16,20},{18,... | collective-permute-start | bytes 516104 | tf_op jit(solution)/shard_map/ppermute | solution.py:556
  59.5 10.0 %collective-permute-start.8 = (bf16[2,16,2688]{2,1,0:T(8,128)(2,1)S(1)}, bf16[2,16,2688]{2,1,0:T(8,128)(2,1)S(1)}, u32[]{:S(2)}, u32[]{:S(2)}) collective-permute-start(bf16[2,16,2688]{2,1,0:T(8,128)(2,1)S(1)} %get-tuple-element.106), channel_id=1, source_target_pairs={{0,6},{2,4},{4,2},{6,0},{8,14},{10,12},{12,10},{14,8},{16,22},{18,... | collective-permute-start | bytes 516104 | tf_op jit(solution)/shard_map/ppermute | solution.py:556
  61.5 17.8 %all-to-all-start.3 = ((bf16[16,16,512]{2,1,0:T(8,128)(2,1)}), bf16[16,16,512]{2,1,0:T(8,128)(2,1)S(1)}, u32[]{:S(2)}, u32[]{:S(2)}) async-start(bf16[16,16,512]{2,1,0:T(8,128)(2,1)} %bitcast.16), calls=%async_computation.3 | async-start | bytes 524288 | tf_op jit(solution)/shard_map/all_to_all | solution.py:692
  65.2 9.8 %collective-permute-start.3 = (bf16[2,16,2688]{2,1,0:T(8,128)(2,1)S(1)}, bf16[2,16,2688]{2,1,0:T(8,128)(2,1)S(1)}, u32[]{:S(2)}, u32[]{:S(2)}) collective-permute-start(bf16[2,16,2688]{2,1,0:T(8,128)(2,1)S(1)} %get-tuple-element.98), channel_id=1, source_target_pairs={{0,2},{2,0},{4,6},{6,4},{8,10},{10,8},{12,14},{14,12},{16,18},{18,... | collective-permute-start | bytes 516104 | tf_op jit(solution)/shard_map/ppermute | solution.py:556
  67.0 12.2 %collective-permute-start.4 = (bf16[2,16,2688]{2,1,0:T(8,128)(2,1)S(1)}, bf16[2,16,2688]{2,1,0:T(8,128)(2,1)S(1)}, u32[]{:S(2)}, u32[]{:S(2)}) collective-permute-start(bf16[2,16,2688]{2,1,0:T(8,128)(2,1)S(1)} %get-tuple-element.99), channel_id=1, source_target_pairs={{0,4},{2,6},{4,0},{6,2},{8,12},{10,14},{12,8},{14,10},{16,20},{18,... | collective-permute-start | bytes 516104 | tf_op jit(solution)/shard_map/ppermute | solution.py:556
  68.5 10.7 %collective-permute-start.5 = (bf16[2,16,2688]{2,1,0:T(8,128)(2,1)S(1)}, bf16[2,16,2688]{2,1,0:T(8,128)(2,1)S(1)}, u32[]{:S(2)}, u32[]{:S(2)}) collective-permute-start(bf16[2,16,2688]{2,1,0:T(8,128)(2,1)S(1)} %get-tuple-element.100), channel_id=1, source_target_pairs={{0,6},{2,4},{4,2},{6,0},{8,14},{10,12},{12,10},{14,8},{16,22},{18,... | collective-permute-start | bytes 516104 | tf_op jit(solution)/shard_map/ppermute | solution.py:556
  69.7 12.0 %collective-permute-start.9 = (bf16[16,2688]{1,0:T(8,128)(2,1)S(1)}, bf16[16,2688]{1,0:T(8,128)(2,1)S(1)}, u32[]{:S(2)}, u32[]{:S(2)}) collective-permute-start(bf16[16,2688]{1,0:T(8,128)(2,1)S(1)} %get-tuple-element.134), channel_id=1, source_target_pairs={{0,16},{2,18},{4,20},{6,22},{8,24},{10,26},{12,28},{14,30},{16,0},... | collective-permute-start | bytes 258056 | tf_op jit(solution)/shard_map/ppermute | solution.py:556
  71.6 10.0 %collective-permute-start.10 = (bf16[16,2688]{1,0:T(8,128)(2,1)S(1)}, bf16[16,2688]{1,0:T(8,128)(2,1)S(1)}, u32[]{:S(2)}, u32[]{:S(2)}) collective-permute-start(bf16[16,2688]{1,0:T(8,128)(2,1)S(1)} %get-tuple-element.135), channel_id=1, source_target_pairs={{0,24},{2,26},{4,28},{6,30},{8,16},{10,18},{12,20},{14,22},{16,8},... | collective-permute-start | bytes 258056 | tf_op jit(solution)/shard_map/ppermute | solution.py:556
  79.3 4.6 %collective-permute-start.6 = (bf16[16,2688]{1,0:T(8,128)(2,1)S(1)}, bf16[16,2688]{1,0:T(8,128)(2,1)S(1)}, u32[]{:S(2)}, u32[]{:S(2)}) collective-permute-start(bf16[16,2688]{1,0:T(8,128)(2,1)S(1)} %slice_bitcast_fusion.2), channel_id=1, source_target_pairs={{0,8},{2,10},{4,12},{6,14},{8,0},{10,2},{12,4},{14,6},{16,24},{18,... | collective-permute-start | bytes 258056 | tf_op jit(solution)/shard_map/ppermute | solution.py:556
  83.9 4.9 %collective-permute-start.16 = (bf16[16,2688]{1,0:T(8,128)(2,1)S(1)}, bf16[16,2688]{1,0:T(8,128)(2,1)S(1)}, u32[]{:S(2)}, u32[]{:S(2)}) collective-permute-start(bf16[16,2688]{1,0:T(8,128)(2,1)S(1)} %fusion.2), channel_id=1, source_target_pairs={{0,8},{2,10},{4,12},{6,14},{8,0},{10,2},{12,4},{14,6},{16,24},{18,... | collective-permute-start | bytes 258056 | tf_op jit(solution)/shard_map/ppermute | solution.py:556
  85.5 7.1 %collective-permute-start.12 = (bf16[16,2688]{1,0:T(8,128)(2,1)S(1)}, bf16[16,2688]{1,0:T(8,128)(2,1)S(1)}, u32[]{:S(2)}, u32[]{:S(2)}) collective-permute-start(bf16[16,2688]{1,0:T(8,128)(2,1)S(1)} %fusion.2), channel_id=1, source_target_pairs={{0,24},{2,26},{4,28},{6,30},{8,16},{10,18},{12,20},{14,22},{16,8},... | collective-permute-start | bytes 258056 | tf_op jit(solution)/shard_map/ppermute | solution.py:556
  87.2 9.3 %collective-permute-start.11 = (bf16[16,2688]{1,0:T(8,128)(2,1)S(1)}, bf16[16,2688]{1,0:T(8,128)(2,1)S(1)}, u32[]{:S(2)}, u32[]{:S(2)}) collective-permute-start(bf16[16,2688]{1,0:T(8,128)(2,1)S(1)} %fusion.2), channel_id=1, source_target_pairs={{0,16},{2,18},{4,20},{6,22},{8,24},{10,26},{12,28},{14,30},{16,0},... | collective-permute-start | bytes 258056 | tf_op jit(solution)/shard_map/ppermute | solution.py:556
  88.8 8.3 %collective-permute-start.19 = (bf16[2,16,2688]{2,1,0:T(8,128)(2,1)S(1)}, bf16[2,16,2688]{2,1,0:T(8,128)(2,1)S(1)}, u32[]{:S(2)}, u32[]{:S(2)}) collective-permute-start(bf16[2,16,2688]{2,1,0:T(8,128)(2,1)S(1)} %pad_maximum_fusion.1.refs_0_), channel_id=1, source_target_pairs={{0,6},{2,4},{4,2},{6,0},{8,14},{10,12},{12,10},{14,8},{16,22},{18,... | collective-permute-start | bytes 516104 | tf_op jit(solution)/shard_map/ppermute | solution.py:556
  91.1 6.2 %collective-permute-start.18 = (bf16[2,16,2688]{2,1,0:T(8,128)(2,1)S(1)}, bf16[2,16,2688]{2,1,0:T(8,128)(2,1)S(1)}, u32[]{:S(2)}, u32[]{:S(2)}) collective-permute-start(bf16[2,16,2688]{2,1,0:T(8,128)(2,1)S(1)} %pad_maximum_fusion.1.refs_0_), channel_id=1, source_target_pairs={{0,4},{2,6},{4,0},{6,2},{8,12},{10,14},{12,8},{14,10},{16,20},{18,... | collective-permute-start | bytes 516104 | tf_op jit(solution)/shard_map/ppermute | solution.py:556
  91.5 6.4 %collective-permute-start.17 = (bf16[2,16,2688]{2,1,0:T(8,128)(2,1)S(1)}, bf16[2,16,2688]{2,1,0:T(8,128)(2,1)S(1)}, u32[]{:S(2)}, u32[]{:S(2)}) collective-permute-start(bf16[2,16,2688]{2,1,0:T(8,128)(2,1)S(1)} %pad_maximum_fusion.1.refs_0_), channel_id=1, source_target_pairs={{0,2},{2,0},{4,6},{6,4},{8,10},{10,8},{12,14},{14,12},{16,18},{18,... | collective-permute-start | bytes 516104 | tf_op jit(solution)/shard_map/ppermute | solution.py:556
  92.6 14.6 %all-to-all-start.4 = ((bf16[32,8,512]{2,1,0:T(8,128)(2,1)}), bf16[32,8,512]{2,1,0:T(8,128)(2,1)S(1)}, u32[]{:S(2)}, u32[]{:S(2)}) async-start(bf16[32,8,512]{2,1,0:T(8,128)(2,1)} %bitcast.26), calls=%async_computation.4 | async-start | bytes 524288 | tf_op jit(solution)/shard_map/all_to_all | solution.py:700
  96.5 1.5 %collective-permute-start.24 = (bf16[2,16,2688]{2,1,0:T(8,128)(2,1)S(1)}, bf16[2,16,2688]{2,1,0:T(8,128)(2,1)S(1)}, u32[]{:S(2)}, u32[]{:S(2)}) collective-permute-start(bf16[2,16,2688]{2,1,0:T(8,128)(2,1)S(1)} %pad_maximum_fusion.refs_4_), channel_id=1, source_target_pairs={{0,1},{1,0},{2,3},{3,2},{4,5},{5,4},{6,7},{7,6},{8,9},{9,8},{10,11... | collective-permute-start | bytes 516104 | tf_op jit(solution)/shard_map/ppermute | solution.py:568
  96.9 3.8 %collective-permute-start.20 = (bf16[2,16,2688]{2,1,0:T(8,128)(2,1)S(1)}, bf16[2,16,2688]{2,1,0:T(8,128)(2,1)S(1)}, u32[]{:S(2)}, u32[]{:S(2)}) collective-permute-start(bf16[2,16,2688]{2,1,0:T(8,128)(2,1)S(1)} %pad_maximum_fusion.1.refs_0_), channel_id=1, source_target_pairs={{0,1},{1,0},{2,3},{3,2},{4,5},{5,4},{6,7},{7,6},{8,9},{9,8},{10,11... | collective-permute-start | bytes 516104 | tf_op jit(solution)/shard_map/ppermute | solution.py:568
  97.1 4.1 %collective-permute-start.23 = (bf16[2,16,2688]{2,1,0:T(8,128)(2,1)S(1)}, bf16[2,16,2688]{2,1,0:T(8,128)(2,1)S(1)}, u32[]{:S(2)}, u32[]{:S(2)}) collective-permute-start(bf16[2,16,2688]{2,1,0:T(8,128)(2,1)S(1)} %collective-permute-done.19.refs_3_), channel_id=1, source_target_pairs={{0,1},{1,0},{2,3},{3,2},{4,5},{5,4},{6,7},{7,6},{8,9},{9,8},{10,11... | collective-permute-start | bytes 516104 | tf_op jit(solution)/shard_map/ppermute | solution.py:568
  97.4 5.3 %collective-permute-start.22 = (bf16[2,16,2688]{2,1,0:T(8,128)(2,1)S(1)}, bf16[2,16,2688]{2,1,0:T(8,128)(2,1)S(1)}, u32[]{:S(2)}, u32[]{:S(2)}) collective-permute-start(bf16[2,16,2688]{2,1,0:T(8,128)(2,1)S(1)} %collective-permute-done.18.refs_2_), channel_id=1, source_target_pairs={{0,1},{1,0},{2,3},{3,2},{4,5},{5,4},{6,7},{7,6},{8,9},{9,8},{10,11... | collective-permute-start | bytes 516104 | tf_op jit(solution)/shard_map/ppermute | solution.py:568
  97.9 4.8 %collective-permute-start.21 = (bf16[2,16,2688]{2,1,0:T(8,128)(2,1)S(1)}, bf16[2,16,2688]{2,1,0:T(8,128)(2,1)S(1)}, u32[]{:S(2)}, u32[]{:S(2)}) collective-permute-start(bf16[2,16,2688]{2,1,0:T(8,128)(2,1)S(1)} %collective-permute-done.17.refs_1_), channel_id=1, source_target_pairs={{0,1},{1,0},{2,3},{3,2},{4,5},{5,4},{6,7},{7,6},{8,9},{9,8},{10,11... | collective-permute-start | bytes 516104 | tf_op jit(solution)/shard_map/ppermute | solution.py:568
  98.0 12.8 %collective-permute-start.15 = (bf16[2,16,2688]{2,1,0:T(8,128)(2,1)S(1)}, bf16[2,16,2688]{2,1,0:T(8,128)(2,1)S(1)}, u32[]{:S(2)}, u32[]{:S(2)}) collective-permute-start(bf16[2,16,2688]{2,1,0:T(8,128)(2,1)S(1)} %pad_maximum_fusion.refs_4_), channel_id=1, source_target_pairs={{0,6},{2,4},{4,2},{6,0},{8,14},{10,12},{12,10},{14,8},{16,22},{18,... | collective-permute-start | bytes 516104 | tf_op jit(solution)/shard_map/ppermute | solution.py:556
  100.7 10.3 %collective-permute-start.14 = (bf16[2,16,2688]{2,1,0:T(8,128)(2,1)S(1)}, bf16[2,16,2688]{2,1,0:T(8,128)(2,1)S(1)}, u32[]{:S(2)}, u32[]{:S(2)}) collective-permute-start(bf16[2,16,2688]{2,1,0:T(8,128)(2,1)S(1)} %pad_maximum_fusion.refs_4_), channel_id=1, source_target_pairs={{0,4},{2,6},{4,0},{6,2},{8,12},{10,14},{12,8},{14,10},{16,20},{18,... | collective-permute-start | bytes 516104 | tf_op jit(solution)/shard_map/ppermute | solution.py:556
  101.3 9.7 %collective-permute-start.13 = (bf16[2,16,2688]{2,1,0:T(8,128)(2,1)S(1)}, bf16[2,16,2688]{2,1,0:T(8,128)(2,1)S(1)}, u32[]{:S(2)}, u32[]{:S(2)}) collective-permute-start(bf16[2,16,2688]{2,1,0:T(8,128)(2,1)S(1)} %pad_maximum_fusion.refs_4_), channel_id=1, source_target_pairs={{0,2},{2,0},{4,6},{6,4},{8,10},{10,8},{12,14},{14,12},{16,18},{18,... | collective-permute-start | bytes 516104 | tf_op jit(solution)/shard_map/ppermute | solution.py:556
  111.0 1.6 %collective-permute-start.25 = (bf16[2,16,2688]{2,1,0:T(8,128)(2,1)S(1)}, bf16[2,16,2688]{2,1,0:T(8,128)(2,1)S(1)}, u32[]{:S(2)}, u32[]{:S(2)}) collective-permute-start(bf16[2,16,2688]{2,1,0:T(8,128)(2,1)S(1)} %collective-permute-done.13.refs_0_), channel_id=1, source_target_pairs={{0,1},{1,0},{2,3},{3,2},{4,5},{5,4},{6,7},{7,6},{8,9},{9,8},{10,11... | collective-permute-start | bytes 516104 | tf_op jit(solution)/shard_map/ppermute | solution.py:568
  111.0 1.7 %collective-permute-start.26 = (bf16[2,16,2688]{2,1,0:T(8,128)(2,1)S(1)}, bf16[2,16,2688]{2,1,0:T(8,128)(2,1)S(1)}, u32[]{:S(2)}, u32[]{:S(2)}) collective-permute-start(bf16[2,16,2688]{2,1,0:T(8,128)(2,1)S(1)} %collective-permute-done.14.refs_1_), channel_id=1, source_target_pairs={{0,1},{1,0},{2,3},{3,2},{4,5},{5,4},{6,7},{7,6},{8,9},{9,8},{10,11... | collective-permute-start | bytes 516104 | tf_op jit(solution)/shard_map/ppermute | solution.py:568
  111.5 1.4 %collective-permute-start.27 = (bf16[2,16,2688]{2,1,0:T(8,128)(2,1)S(1)}, bf16[2,16,2688]{2,1,0:T(8,128)(2,1)S(1)}, u32[]{:S(2)}, u32[]{:S(2)}) collective-permute-start(bf16[2,16,2688]{2,1,0:T(8,128)(2,1)S(1)} %collective-permute-done.15.refs_2_), channel_id=1, source_target_pairs={{0,1},{1,0},{2,3},{3,2},{4,5},{5,4},{6,7},{7,6},{8,9},{9,8},{10,11... | collective-permute-start | bytes 516104 | tf_op jit(solution)/shard_map/ppermute | solution.py:568
  (16 other events, 502.3 us)

commit v5 on v4

--- a/solution.py
+++ b/solution.py
@@ -191,11 +191,6 @@
     return (og_ref[...].astype(F32) * jnp.concatenate([valid] * wide, axis=1)).astype(BF16)
 
 
-def go_kernel(len_ref, dest_ref, og_ref, go_ref):
-    rows = og_ref.shape[0]
-    go_ref[...] = masked_grad(og_ref, valid_rows(segments(len_ref, dest_ref, rows), rows))
-
-
 def pos_bounds(rows, count):
     return [max(1, rows // 2 ** (count - m)) for m in range(count)]
 
@@ -280,6 +275,7 @@
     lo_ref,
     n1_ref,
     y_ref,
+    go_ref,
     dh_ref,
     ds_ref,
     g2g_ref,
@@ -293,7 +289,8 @@
     pairs = heads // 2
     seg = segments(len_ref, dest_ref, rows)
     valid = valid_rows(seg, rows)
-    dmix = dot_nt(masked_grad(og_ref, valid), wo_ref[...])
+    go_ref[...] = masked_grad(og_ref, valid)
+    dmix = dot_nt(go_ref[...], wo_ref[...])
     index = bias_index(seg, time_ref, rows, count)
     table = bias_table(pos_ref, timew_ref)
     x = x_ref[...].astype(F32)
@@ -316,20 +313,22 @@
     def half(value, parity):
         return jnp.where(low if parity == 0 else ~low, value, zero)
 
+    def stacked(value):
+        return jnp.concatenate([half(value, 0), half(value, 1)], axis=0)
+
+    def abreast(value):
+        return jnp.concatenate([value[:rows], value[rows:]], axis=1)
+
     outs = []
     for pair in range(pairs):
         cols = slice(pair * LANES, (pair + 1) * LANES)
-        total = None
-        for parity in range(2):
-            g = pair * 2 + parity
-            s = dot_nt(half(q[:, cols], parity), k[:, cols]) * 0.125 + look_up(table[g : g + 1, :], index)
-            sig = sigmoid(s)
-            a = (s * sig).astype(BF16)
-            a_ref[g] = a
-            slope_ref[g] = sig * (1.0 + s * (1.0 - sig))
-            part = dot_nn(a, half(v[:, cols], parity))
-            total = part if total is None else total + part
-        outs.append(total)
+        bias = jnp.concatenate([look_up(table[g : g + 1, :], index) for g in (2 * pair, 2 * pair + 1)], axis=0)
+        s = dot_nt(stacked(q[:, cols]), k[:, cols]) * 0.125 + bias
+        sig = sigmoid(s)
+        a = (s * sig).astype(BF16)
+        a_ref[pair] = a
+        slope_ref[pair] = sig * (1.0 + s * (1.0 - sig))
+        outs.append(dot_nn(abreast(a), stacked(v[:, cols])))
     o = jnp.concatenate(outs, axis=1)
     ohat, scale2 = norm_of(o)
     g2 = g2_ref[...]
@@ -345,22 +344,13 @@
     dh_ref[:, 0:width] = (du * h_ref[:, 0:width]).astype(BF16)
     for pair in range(pairs):
         cols = slice(pair * LANES, (pair + 1) * LANES)
-        dv, dq, dk = None, None, None
-        for parity in range(2):
-            g = pair * 2 + parity
-            dom = half(do[:, cols], parity)
-            da = dot_nt(dom, v[:, cols])
-            ds = (da * slope_ref[g]).astype(BF16)
-            ds_ref[g] = ds
-            parts = (
-                dot_tn(a_ref[g], dom),
-                dot_nn(ds, half(k[:, cols], parity)),
-                dot_tn(ds, half(q[:, cols], parity)),
-            )
-            if parity == 0:
-                dv, dq, dk = parts
-            else:
-                dv, dq, dk = dv + parts[0], dq + parts[1], dk + parts[2]
+        dom = stacked(do[:, cols])
+        ds = (dot_nt(dom, v[:, cols]) * slope_ref[pair]).astype(BF16)
+        ds_ref[2 * pair] = ds[:rows]
+        ds_ref[2 * pair + 1] = ds[rows:]
+        dv = dot_tn(a_ref[pair], dom)
+        dq = dot_nn(abreast(ds), stacked(k[:, cols]))
+        dk = dot_tn(ds, stacked(q[:, cols]))
         for part, value in ((1, dv), (2, dq * 0.125), (3, dk * 0.125)):
             at = slice(part * width + pair * LANES, part * width + (pair + 1) * LANES)
             dh_ref[:, at] = (value * h_ref[:, at]).astype(BF16)
@@ -370,17 +360,11 @@
         msg_ref[:, 0:half_cols] = dh_ref[:, pl.ds(pl.multiple_of(other * half_cols, half_cols), half_cols)]
         msg_ref[:, half_cols : half_cols + width] = n1
         half_y = width // 2
-        msg_ref[:, half_cols + width :] = y_ref[:, pl.ds(pl.multiple_of(other * half_y, half_y), half_y)]
+        y_half = y_ref[:, pl.ds(pl.multiple_of(other * half_y, half_y), half_y)].astype(F32)
+        y_half = y_half * jnp.concatenate([valid] * (half_y // LANES), axis=1)
+        msg_ref[:, half_cols + width :] = y_half.astype(BF16)
     else:
         msg_ref[...] = jnp.zeros_like(msg_ref)
-
-
-def dx_kernel(dh_ref, w_ref, x_ref, g1_ref, go_ref, dx_ref, g1g_ref):
-    xhat, scale = norm_of(x_ref[...].astype(F32))
-    dn1 = dot_nt(dh_ref[...], w_ref[...])
-    g1g_ref[...] = jnp.sum(dn1 * xhat, axis=0, keepdims=True)
-    dx = norm_back(dn1 * g1_ref[...], xhat, scale) + go_ref[...].astype(F32)
-    dx_ref[...] = dx.astype(BF16)
 
 
 SMALL_ROWS = 48
@@ -399,34 +383,43 @@
     return jnp.transpose(jnp.concatenate(ends, axis=0)).astype(I32)
 
 
-def small_kernel(count, ds_ref, time_ref, dh_ref, go_ref, g1g_ref, g2g_ref, out_ref):
+def after_kernel(count, dh_ref, w_ref, x_ref, g1_ref, go_ref, ds_ref, time_ref, g2g_ref, *rest):
+    dx_out, out_ref, dx_ref, sem = rest
     heads, rows, _ = ds_ref.shape
-    width = go_ref.shape[1]
+    xhat, scale = norm_of(x_ref[...].astype(F32))
+    dn1 = dot_nt(dh_ref[...], w_ref[...])
+    go = go_ref[...].astype(F32)
+    dx_ref[...] = (norm_back(dn1 * g1_ref[...], xhat, scale) + go).astype(BF16)
+    copy = pltpu.make_async_copy(dx_ref, dx_out, sem)
+    copy.start()
     out_ref[...] = jnp.zeros_like(out_ref)
+    g1_grad = jnp.sum(dn1 * xhat, axis=0, keepdims=True)
     b_grad = jnp.sum(dh_ref[...].astype(F32), axis=0, keepdims=True)
-    go_sum = jnp.sum(go_ref[...].astype(F32), axis=0, keepdims=True)
+    go_sum = jnp.sum(go, axis=0, keepdims=True)
     at = 0
-    for value in (b_grad, g1g_ref[...], g2g_ref[...], go_sum):
+    for value in (b_grad, g1_grad, g2g_ref[...], go_sum):
         for col in range(0, value.shape[1], LANES):
             out_ref[at : at + 1, :] = value[:, col : col + LANES]
             at += 1
     at = (at + 7) // 8 * 8
     ends = prefix_ends(time_ref, rows, count)
     upto = jnp.where(iota((rows, rows), 0) <= iota((rows, rows), 1), 1.0, 0.0).astype(BF16)
+    prefix = dot_nn(ds_ref[...].reshape(heads * rows, rows), upto)
+    tables = [
+        ((ends >= first) & (ends < first + LANES), jnp.clip(ends - first, 0, LANES - 1))
+        for first in range(0, rows, LANES)
+    ]
     sums = []
     for g in range(heads):
-        prefix = dot_nn(ds_ref[g], upto)
         found = jnp.zeros((rows, LANES), F32)
-        for first in range(0, rows, LANES):
-            here = (ends >= first) & (ends < first + LANES)
-            value = jnp.take_along_axis(
-                prefix[:, first : first + LANES], jnp.where(here, ends - first, 0), axis=1
-            )
-            found = found + jnp.where(here, value, 0.0)
+        for n, (here, index) in enumerate(tables):
+            value = prefix[g * rows : (g + 1) * rows, n * LANES : (n + 1) * LANES]
+            found = found + jnp.where(here, jnp.take_along_axis(value, index, axis=1), 0.0)
         sums.append(jnp.sum(found, axis=0, keepdims=True))
     sums = jnp.concatenate(sums, axis=0)
     out_ref[at : at + heads, :] = sums
     out_ref[at + heads : at + 2 * heads, 0 : LANES // 2] = sums[:, LANES // 2 :]
+    copy.wait()
 
 
 def place_of(columns):
@@ -434,7 +427,7 @@
     return lax.rem(my_dp, columns), lax.div(my_dp, columns)
 
 
-def pack_kernel(planes, columns, dh_ref, n1_ref, y_ref, go_ref, got_ref, got_go_ref, small_ref, *rest):
+def pack_kernel(planes, columns, dh_ref, n1_ref, y_ref, go_ref, got_ref, got_grad_ref, small_ref, *rest):
     nears, fars, (uv_ref, wo_ref) = rest[:columns], rest[columns : 2 * columns], rest[2 * columns :]
     width = n1_ref.shape[1]
     core = lax.axis_index("table")
@@ -450,7 +443,7 @@
         [y_ref[:, pl.ds(pl.multiple_of(core * half_y, half_y), half_y)], got_ref[:, half_cols + width :]],
         axis=0,
     )
-    go = jnp.concatenate([go_ref[...], got_go_ref[...]], axis=0)
+    go = jnp.concatenate([go_ref[...], got_grad_ref[...]], axis=0)
     uv_ref[...] = dot_tn(n1, dh)
     wo_ref[...] = dot_tn(y, go)
     short = half_y // (planes * columns)
@@ -624,11 +617,15 @@
         ),
         room=64,
     )(request_rows.transpose(0, 2, 1).reshape(cap, devices), slot_row, lengths, assignment, counts_2d)
+    if staged:
+        msg, other_grad = lax.optimization_barrier((msg, out_grad))
+        got_grad = swap_cores(other_grad)
     asked = lax.all_to_all(msg.reshape(devices, 1, LANES), BOTH, 0, 0, tiled=True).reshape(devices, LANES)
+    if staged:
+        asked, got_grad = lax.optimization_barrier((asked, got_grad))
     served = call(
         functools.partial(serve_kernel, cap), shape_of((slots, width), BF16), [VMEM] * 2, 1 << 30, 5 * mb
     )(asked, item_table)
-    go = call(go_kernel, shape_of((rows, width), BF16), [VMEM] * 3, 64 * mb, mb)(lengths, assignment, out_grad)
     fetched = lax.all_to_all(served.reshape(devices, cap, width), BOTH, 0, 0, tiled=True)
     new_counts, log_q, asked_row = call(
         functools.partial(counts_kernel, cap, rows_dev * devices),
@@ -644,18 +641,15 @@
     home = call(take_kernel, shape_of((rows, width), BF16), [VMEM] * 2, 64 * mb, mb)(
         slot_row, fetched.reshape(slots, width)
     )
-    if staged:
-        got_go = swap_cores(go)
     x = lax.all_to_all(home.reshape(replicas, piece, width), "dp", 0, 0, tiled=True).reshape(rows, width)
-    if staged:
-        x, got_go = lax.optimization_barrier((x, got_go))
 
     half_cols = 2 * width
     g1, g2 = first_norm_gain.reshape(1, width), norm2_gain.reshape(1, width)
     msg_cols = half_cols + width + width // 2 if staged else LANES
-    layer_out, n1, y, dh, ds, g2_grad, to_core = call(
+    layer_out, n1, y, go, dh, ds, g2_grad, to_core = call(
         functools.partial(layer_kernel, staged),
         (
+            shape_of((rows, width), BF16),
             shape_of((rows, width), BF16),
             shape_of((rows, width), BF16),
             shape_of((rows, width), BF16),
@@ -669,8 +663,8 @@
         8 * mb,
         scratch=(
             pltpu.VMEM((rows, 4 * width), F32),
-            pltpu.VMEM((heads, rows, rows), F32),
-            pltpu.VMEM((heads, rows, rows), BF16),
+            pltpu.VMEM((heads // 2, 2 * rows, rows), F32),
+            pltpu.VMEM((heads // 2, 2 * rows, rows), BF16),
         ),
         room=24,
     )(
@@ -718,16 +712,15 @@
 
     if staged:
         got = swap_cores(to_core)
-    dx, g1_grad = call(
-        dx_kernel, (shape_of((rows, width), BF16), shape_of((1, width), F32)), [VMEM] * 5, 1 << 29, 4 * mb
-    )(dh, w_uvqk, x, g1, go)
-    small = call(
-        functools.partial(small_kernel, count),
-        shape_of((width // 2, LANES), F32),
-        [VMEM] * 6,
-        1 << 28,
-        2 * mb,
-    )(ds, time_row, dh, go, g1_grad, g2_grad)
+    dx, small = call(
+        functools.partial(after_kernel, count),
+        (shape_of((rows, width), BF16), shape_of((width // 2, LANES), F32)),
+        [VMEM] * 8,
+        1 << 29,
+        4 * mb,
+        scratch=(pltpu.VMEM((rows, width), BF16), pltpu.SemaphoreType.DMA),
+        out_specs=(HBM, VMEM),
+    )(dh, w_uvqk, x, g1, go, ds, time_row, g2_grad)
     if staged:
         short = width // replicas // 2
         pieces = call(
@@ -737,7 +730,7 @@
             1 << 30,
             6 * mb,
             scratch=(pltpu.VMEM((width, half_cols), F32), pltpu.VMEM((width // 2, width), F32)),
-        )(dh, n1, y, go, got, got_go, small)
+        )(dh, n1, y, go, got, got_grad, small)
         dx, *pieces = lax.optimization_barrier((dx, *pieces))
         nears, fars = pieces[:columns], pieces[columns:]
         back = home_again(dx)

time: 115 us -> 113 us (0.983)
  blocking collectives: 26.7 us -> 39.3 us
  waiting for transfers between devices: 22.8 us -> 13.6 us
  starting transfers between devices: 35.7 us -> 32.6 us
  Pallas kernels: 25.1 us -> 23.2 us
    all_to_all x0 -> x1, blocking collectives: none -> 13 us  [on_device(): lax.all_to_all(home.reshape(replicas, piece, width), 'dp', 0, 0, tiled=True)]
    all_to_all x1 -> x0, waiting for transfers between devices: 7.6 us -> none  [on_device(): lax.all_to_all(home.reshape(replicas, piece, width), 'dp', 0, 0, tiled=True)]
    all_to_all x1 -> x0, starting transfers between devices: 3.53 us -> none  [on_device(): lax.all_to_all(home.reshape(replicas, piece, width), 'dp', 0, 0, tiled=True)]
    ppermute x10, waiting for transfers between devices: 1.96 us -> 0.44 us  [swap_cores(): return lax.ppermute(value, 'table', [(0, 1), (1, 0)])]
    pallas_call x3 -> x1, Pallas kernels: 4.03 us -> 2.84 us  [on_device(): call(functools.partial(after_kernel, count), (shape_of((rows, width), BF1...]
    unnamed x34 -> x30, local copies, waits for them, and re-layouts: 2.97 us -> 2.27 us
  transfers between devices with their start and end apart: 31 -> 30, of which waited for: 12 -> 10; matrix products, arithmetic and copies ran while one was open for 0% -> 0% of each run, Pallas kernels for 11% -> 10%
where the time goes in v5:
time: 113 us; the launch traced here: 112 us
  blocking collectives  39.3 us (35%)
  starting transfers between devices  32.6 us (29%)
  Pallas kernels  23.2 us (21%)
  waiting for transfers between devices  13.6 us (12%)
  local copies, waits for them, and re-layouts  2.29 us (2%)
  between operations  1.16 us (1%)
    ppermute x18, starting transfers between devices, xor_step(): return lax.ppermute(value, 'dp', [(i, i ^ step) for i in range(size)])  22.9 us
    all_to_all x1, blocking collectives, on_device(): lax.all_to_all(msg.reshape(devices, 1, LANES), BOTH, 0, 0, tiled=True)  14 us
    all_to_all x1, blocking collectives, on_device(): lax.all_to_all(home.reshape(replicas, piece, width), 'dp', 0, 0, tiled=True)  13 us
    all_to_all x1, blocking collectives, on_device(): lax.all_to_all(served.reshape(devices, cap, width), BOTH, 0, 0, tiled=True)  12.3 us
    ppermute x18, waiting for transfers between devices, xor_step(): return lax.ppermute(value, 'dp', [(i, i ^ step) for i in range(size)])  10.7 us
    pallas_call x1, Pallas kernels, on_device(): call(functools.partial(layer_kernel, staged), (shape_of((rows, width), BF...  5.16 us
    all_to_all x1, starting transfers between devices, send_sums(): lax.all_to_all(sums.reshape(devices, cap, width), BOTH, 0, 0, tiled=True)  3.87 us
    all_to_all x1, starting transfers between devices, home_again(): lax.all_to_all(dx.reshape(replicas, piece, width), 'dp', 0, 0, tiled=True)  3.72 us
  transfers between devices with their start and end apart: 30, of which 10 were waited for; matrix products, arithmetic and copies ran while one was open for 0% of the time, Pallas kernels for 10%

profile of v5, /device:TPU:0, one launch (start us, length us, event | category | flops | bytes accessed | tf_op | source)
XLA Modules:
  0.0 112.5 jit_solution(1809652895158975528)
XLA Ops:
  0.6 1.7 %shard_map.247 = s32[32,128]{1,0:T(8,128)} custom-call(s32[8,32]{1,0:T(8,128)} %bitcast.67, s32[1,256]{1,0:T(1,128)} %bitcast.52, s32[1,64]{1,0:T(1,128)} %len_ref.1, s32[1,64]{1,0:T(1,128)} %dest_ref.1, s32[32,128]{1,0:T(8,128)} %bitcast.50), custom_call_target="tpu_custom_call" | custom-call | flops 1048576 | bytes 131072 | tf_op jit(solution)/shard_map/pallas_call | solution.py:604
  3.0 14.0 %all_to_all.25 = s32[32,1,128]{2,1,0:T(1,128)S(1)} all-to-all(s32[32,1,128]{2,1,0:T(1,128)} %bitcast.66), channel_id=1, replica_groups=mesh['dp'=16,'table'=2] {'dp','table'}, dimensions={0} | all-to-all | bytes 32768 | tf_op jit(solution)/shard_map/all_to_all | solution.py:623
  17.0 2.2 %copy-done = bf16[4096,512]{1,0:T(8,128)(2,1)S(1)} copy-done((bf16[4096,512]{1,0:T(8,128)(2,1)S(1)}, bf16[4096,512]{1,0:T(8,128)(2,1)}, u32[]{:S(2)}) %copy-start) | copy-done | bytes 4194328
  19.2 1.9 %shard_map.248 = bf16[256,512]{1,0:T(8,128)(2,1)S(1)} custom-call(s32[32,128]{1,0:T(8,128)S(1)} %bitcast.48, bf16[4096,512]{1,0:T(8,128)(2,1)S(1)} %copy-done), custom_call_target="tpu_custom_call" | custom-call | flops 1073741824 | bytes 5242880 | tf_op jit(solution)/shard_map/pallas_call | solution.py:626
  21.1 12.3 %all_to_all.26 = bf16[32,8,512]{2,1,0:T(8,128)(2,1)S(1)} all-to-all(bf16[32,8,512]{2,1,0:T(8,128)(2,1)S(1)} %bitcast.44), channel_id=1, replica_groups=mesh['dp'=16,'table'=2] {'dp','table'}, dimensions={0} | all-to-all | bytes 524288 | tf_op jit(solution)/shard_map/all_to_all | solution.py:629
  33.6 13.0 %all_to_all.27 = bf16[16,16,512]{2,1,0:T(8,128)(2,1)S(1)} all-to-all(bf16[16,16,512]{2,1,0:T(8,128)(2,1)S(1)} %bitcast.47), channel_id=1, replica_groups=mesh['dp'=16,'table'=2] {'dp'}, dimensions={0} | all-to-all | bytes 524288 | tf_op jit(solution)/shard_map/all_to_all | solution.py:644
  46.7 5.2 %shard_map.250 = (bf16[256,512]{1,0:T(8,128)(2,1)}, bf16[256,512]{1,0:T(8,128)(2,1)S(1)}, bf16[256,512]{1,0:T(8,128)(2,1)S(1)}, bf16[256,512]{1,0:T(8,128)(2,1)S...) custom-call(bf16[256,512]{1,0:T(8,128)(2,1)S(1)} %bitcast.42, ...), custom_call_target="tpu_custom_call" | custom-call | flops 2147483648 | bytes 8388608 | tf_op jit(solution)/shard_map/pallas_call | solution.py:649
  51.9 2.8 %shard_map.251 = (bf16[256,512]{1,0:T(8,128)(2,1)}, f32[256,128]{1,0:T(8,128)S(1)}) custom-call(bf16[256,2048]{1,0:T(8,128)(2,1)S(1)} %get-tuple-element.80.dh_ref, bf16[512,2048]{1,0:T(8,128)(2,1)S(1)} %copy-done.1, bf16[256,512]{1,0:T(8,128)(2,1)S(1)} %bitcast.43, f32[1,512]{1,0:T(1,128)S(1)} %bitcast.56, bf16[256,512]{1,0:T(8,128)(2,1)S(1)} %get-tuple-element.81.go_ref, ...), custom_call_target="tpu_custom_call" | custom-call | flops 536870912 | bytes 4194304 | tf_op jit(solution)/shard_map/pallas_call | solution.py:715
  54.7 0.9 shard_map.252
  57.2 2.0 %collective-permute-start.8 = (bf16[2,16,2688]{2,1,0:T(8,128)(2,1)S(1)}, bf16[2,16,2688]{2,1,0:T(8,128)(2,1)S(1)}, u32[]{:S(2)}, u32[]{:S(2)}) collective-permute-start(bf16[2,16,2688]{2,1,0:T(8,128)(2,1)S(1)} %get-tuple-element.112), channel_id=1, source_target_pairs={{0,6},{2,4},{4,2},{6,0},{8,14},{10,12},{12,10},{14,8},{16,22},{18,... | collective-permute-start | bytes 516104 | tf_op jit(solution)/shard_map/ppermute | solution.py:549
  59.2 3.7 %all-to-all-start.3 = ((bf16[16,16,512]{2,1,0:T(8,128)(2,1)}), bf16[16,16,512]{2,1,0:T(8,128)(2,1)S(1)}, u32[]{:S(2)}, u32[]{:S(2)}) async-start(bf16[16,16,512]{2,1,0:T(8,128)(2,1)} %bitcast.16), calls=%async_computation.3 | async-start | bytes 524288 | tf_op jit(solution)/shard_map/all_to_all | solution.py:686
  63.0 1.8 %collective-permute-start.3 = (bf16[2,16,2688]{2,1,0:T(8,128)(2,1)S(1)}, bf16[2,16,2688]{2,1,0:T(8,128)(2,1)S(1)}, u32[]{:S(2)}, u32[]{:S(2)}) collective-permute-start(bf16[2,16,2688]{2,1,0:T(8,128)(2,1)S(1)} %get-tuple-element.104), channel_id=1, source_target_pairs={{0,2},{2,0},{4,6},{6,4},{8,10},{10,8},{12,14},{14,12},{16,18},{18,... | collective-permute-start | bytes 516104 | tf_op jit(solution)/shard_map/ppermute | solution.py:549
  64.8 1.5 %collective-permute-start.4 = (bf16[2,16,2688]{2,1,0:T(8,128)(2,1)S(1)}, bf16[2,16,2688]{2,1,0:T(8,128)(2,1)S(1)}, u32[]{:S(2)}, u32[]{:S(2)}) collective-permute-start(bf16[2,16,2688]{2,1,0:T(8,128)(2,1)S(1)} %get-tuple-element.105), channel_id=1, source_target_pairs={{0,4},{2,6},{4,0},{6,2},{8,12},{10,14},{12,8},{14,10},{16,20},{18,... | collective-permute-start | bytes 516104 | tf_op jit(solution)/shard_map/ppermute | solution.py:549
  67.4 2.0 %collective-permute-start.9 = (bf16[16,2688]{1,0:T(8,128)(2,1)S(1)}, bf16[16,2688]{1,0:T(8,128)(2,1)S(1)}, u32[]{:S(2)}, u32[]{:S(2)}) collective-permute-start(bf16[16,2688]{1,0:T(8,128)(2,1)S(1)} %get-tuple-element.140), channel_id=1, source_target_pairs={{0,16},{2,18},{4,20},{6,22},{8,24},{10,26},{12,28},{14,30},{16,0},... | collective-permute-start | bytes 258056 | tf_op jit(solution)/shard_map/ppermute | solution.py:549
  69.4 1.5 %collective-permute-start.10 = (bf16[16,2688]{1,0:T(8,128)(2,1)S(1)}, bf16[16,2688]{1,0:T(8,128)(2,1)S(1)}, u32[]{:S(2)}, u32[]{:S(2)}) collective-permute-start(bf16[16,2688]{1,0:T(8,128)(2,1)S(1)} %get-tuple-element.141), channel_id=1, source_target_pairs={{0,24},{2,26},{4,28},{6,30},{8,16},{10,18},{12,20},{14,22},{16,8},... | collective-permute-start | bytes 258056 | tf_op jit(solution)/shard_map/ppermute | solution.py:549
  70.8 2.0 %collective-permute-done.3 = bf16[2,16,2688]{2,1,0:T(8,128)(2,1)S(1)} collective-permute-done((bf16[2,16,2688]{2,1,0:T(8,128)(2,1)S(1)}, bf16[2,16,2688]{2,1,0:T(8,128)(2,1)S(1)}, u32[]{:S(2)}, u32[]{:S(2)}) %collective-permute-start.3) | collective-permute-done | bytes 172064 | tf_op jit(solution)/shard_map/ppermute | solution.py:549
  72.8 4.1 %collective-permute-done.4 = bf16[2,16,2688]{2,1,0:T(8,128)(2,1)S(1)} collective-permute-done((bf16[2,16,2688]{2,1,0:T(8,128)(2,1)S(1)}, bf16[2,16,2688]{2,1,0:T(8,128)(2,1)S(1)}, u32[]{:S(2)}, u32[]{:S(2)}) %collective-permute-start.4) | collective-permute-done | bytes 172064 | tf_op jit(solution)/shard_map/ppermute | solution.py:549
  77.0 1.4 %collective-permute-start.6 = (bf16[16,2688]{1,0:T(8,128)(2,1)S(1)}, bf16[16,2688]{1,0:T(8,128)(2,1)S(1)}, u32[]{:S(2)}, u32[]{:S(2)}) collective-permute-start(bf16[16,2688]{1,0:T(8,128)(2,1)S(1)} %slice_bitcast_fusion.2), channel_id=1, source_target_pairs={{0,8},{2,10},{4,12},{6,14},{8,0},{10,2},{12,4},{14,6},{16,24},{18,... | collective-permute-start | bytes 258056 | tf_op jit(solution)/shard_map/ppermute | solution.py:549
  79.4 2.2 %collective-permute-done.6 = bf16[16,2688]{1,0:T(8,128)(2,1)S(1)} collective-permute-done((bf16[16,2688]{1,0:T(8,128)(2,1)S(1)}, bf16[16,2688]{1,0:T(8,128)(2,1)S(1)}, u32[]{:S(2)}, u32[]{:S(2)}) %collective-permute-start.6) | collective-permute-done | bytes 86048 | tf_op jit(solution)/shard_map/ppermute | solution.py:549
  81.6 1.7 %collective-permute-start.16 = (bf16[16,2688]{1,0:T(8,128)(2,1)S(1)}, bf16[16,2688]{1,0:T(8,128)(2,1)S(1)}, u32[]{:S(2)}, u32[]{:S(2)}) collective-permute-start(bf16[16,2688]{1,0:T(8,128)(2,1)S(1)} %fusion.2), channel_id=1, source_target_pairs={{0,8},{2,10},{4,12},{6,14},{8,0},{10,2},{12,4},{14,6},{16,24},{18,... | collective-permute-start | bytes 258056 | tf_op jit(solution)/shard_map/ppermute | solution.py:549
  83.3 1.6 %collective-permute-start.12 = (bf16[16,2688]{1,0:T(8,128)(2,1)S(1)}, bf16[16,2688]{1,0:T(8,128)(2,1)S(1)}, u32[]{:S(2)}, u32[]{:S(2)}) collective-permute-start(bf16[16,2688]{1,0:T(8,128)(2,1)S(1)} %fusion.2), channel_id=1, source_target_pairs={{0,24},{2,26},{4,28},{6,30},{8,16},{10,18},{12,20},{14,22},{16,8},... | collective-permute-start | bytes 258056 | tf_op jit(solution)/shard_map/ppermute | solution.py:549
  85.2 1.3 %collective-permute-done.16 = bf16[16,2688]{1,0:T(8,128)(2,1)S(1)} collective-permute-done((bf16[16,2688]{1,0:T(8,128)(2,1)S(1)}, bf16[16,2688]{1,0:T(8,128)(2,1)S(1)}, u32[]{:S(2)}, u32[]{:S(2)}) %collective-permute-start.16) | collective-permute-done | bytes 86048 | tf_op jit(solution)/shard_map/ppermute | solution.py:549
  86.5 2.3 %collective-permute-start.19 = (bf16[2,16,2688]{2,1,0:T(8,128)(2,1)S(1)}, bf16[2,16,2688]{2,1,0:T(8,128)(2,1)S(1)}, u32[]{:S(2)}, u32[]{:S(2)}) collective-permute-start(bf16[2,16,2688]{2,1,0:T(8,128)(2,1)S(1)} %pad_maximum_fusion.1.refs_0_), channel_id=1, source_target_pairs={{0,6},{2,4},{4,2},{6,0},{8,14},{10,12},{12,10},{14,8},{16,22},{18,... | collective-permute-start | bytes 516104 | tf_op jit(solution)/shard_map/ppermute | solution.py:549
  89.2 1.1 collective-permute-start.17
  90.4 3.9 %all-to-all-start.4 = ((bf16[32,8,512]{2,1,0:T(8,128)(2,1)}), bf16[32,8,512]{2,1,0:T(8,128)(2,1)S(1)}, u32[]{:S(2)}, u32[]{:S(2)}) async-start(bf16[32,8,512]{2,1,0:T(8,128)(2,1)} %bitcast.26), calls=%async_computation.4 | async-start | bytes 524288 | tf_op jit(solution)/shard_map/all_to_all | solution.py:694
  95.8 2.7 %collective-permute-start.15 = (bf16[2,16,2688]{2,1,0:T(8,128)(2,1)S(1)}, bf16[2,16,2688]{2,1,0:T(8,128)(2,1)S(1)}, u32[]{:S(2)}, u32[]{:S(2)}) collective-permute-start(bf16[2,16,2688]{2,1,0:T(8,128)(2,1)S(1)} %pad_maximum_fusion.refs_4_), channel_id=1, source_target_pairs={{0,6},{2,4},{4,2},{6,0},{8,14},{10,12},{12,10},{14,8},{16,22},{18,... | collective-permute-start | bytes 516104 | tf_op jit(solution)/shard_map/ppermute | solution.py:549
  99.3 1.1 %shard_map.255 = (s32[32,128]{1,0:T(8,128)}, f32[32,128]{1,0:T(8,128)}, f32[8,256]{1,0:T(8,128)S(1)}) custom-call(s32[32,128]{1,0:T(8,128)S(1)} %bitcast.49, s32[32,128]{1,0:T(8,128)S(1)} %bitcast.51), custom_call_target="tpu_custom_call" | custom-call | flops 67108864 | bytes 1048576 | tf_op jit(solution)/shard_map/pallas_call | solution.py:630
  100.4 2.0 %shard_map.254 = (f32[512,2048]{1,0:T(8,128)}, f32[512,512]{1,0:T(8,128)}, f32[256,128]{1,0:T(8,128)S(1)}) custom-call(bf16[2,16,2688]{2,1,0:T(8,128)(2,1)S(1)} %pad_maximum_fusion.1.refs_0_, bf16[2,16,2688]{2,1,0:T(8,128)(2,1)S(1)} %collective-permute-done.17.refs_1_, bf16[2,16,2688]{2,1,0:T(8,128)(2,1)S(1)} %collective-permute-done.18.refs_2_, ...), custom_call_target="tpu_custom_call" | custom-call | flops 1048576 | bytes 3145728 | tf_op jit(solution)/shard_map/pallas_call | solution.py:781
  102.5 2.4 %all-to-all-done.4 = bf16[32,8,512]{2,1,0:T(8,128)(2,1)S(1)} async-done(((bf16[32,8,512]{2,1,0:T(8,128)(2,1)}), bf16[32,8,512]{2,1,0:T(8,128)(2,1)S(1)}, u32[]{:S(2)}, u32[]{:S(2)}) %all-to-all-start.4) | async-done | bytes 262176 | tf_op jit(solution)/shard_map/all_to_all | solution.py:694
  104.9 3.7 %shard_map.256 = f32[4096,512]{1,0:T(8,128)} custom-call(f32[8,256]{1,0:T(8,128)S(1)} %get-tuple-element.118.row_ref, bf16[256,512]{1,0:T(8,128)(2,1)S(1)} %bitcast.41), custom_call_target="tpu_custom_call" | custom-call | flops 1073741824 | bytes 8388608 | tf_op jit(solution)/shard_map/pallas_call | solution.py:699
  109.3 1.1 shard_map.257
  110.7 1.7 %shard_map.258 = (f32[512,2048]{1,0:T(8,128)}, f32[512,512]{1,0:T(8,128)}, f32[1,2048]{1,0:T(1,128)}, f32[1,512]{1,0:T(1,128)}, f32[1,512]{1,0:T(1,128)}, /*inde...) custom-call(bf16[2,16,2688]{2,1,0:T(8,128)(2,1)S(1)} %collective-permute-done.2, ...), custom_call_target="tpu_custom_call", output_to_operand_aliasing={{0}: (3, {}), {1}: (4, {})} | custom-call | flops 1048576 | bytes 3145728 | tf_op jit(solution)/shard_map/pallas_call | solution.py:789
  (80 shorter events, 8.7 us)
Async XLA Ops:
  2.3 44.3 %copy-start.4 = (f32[512]{0:T(512)S(1)}, f32[512]{0:T(512)}, u32[]{:S(2)}) copy-start(f32[512]{0:T(512)} %param.23) | copy-start | bytes 6148
  2.4 14.6 %collective-permute-start = (bf16[256,512]{1,0:T(8,128)(2,1)}, bf16[256,512]{1,0:T(8,128)(2,1)S(1)}, u32[]{:S(2)}, u32[]{:S(2)}) collective-permute-start(bf16[256,512]{1,0:T(8,128)(2,1)} %og_ref.1), channel_id=1, source_target_pairs={{0,1},{1,0},{2,3},{3,2},{4,5},{5,4},{6,7},{7,6},{8,9},{9,8},{10,11... | collective-permute-start | bytes 786440 | tf_op jit(solution)/shard_map/ppermute | solution.py:561
  51.9 2.9 %collective-permute-start.1 = (bf16[256,1792]{1,0:T(8,128)(2,1)S(1)}, bf16[256,1792]{1,0:T(8,128)(2,1)S(1)}, u32[]{:S(2)}, u32[]{:S(2)}) collective-permute-start(bf16[256,1792]{1,0:T(8,128)(2,1)S(1)} %get-tuple-element.87), channel_id=1, source_target_pairs={{0,1},{1,0},{2,3},{3,2},{4,5},{5,4},{6,7},{7,6},{8,9},{9,8},{10,11... | collective-permute-start | bytes 2752520 | tf_op jit(solution)/shard_map/ppermute | solution.py:561
  54.7 44.6 %copy-start.2 = (s32[4096]{0:T(1024)S(1)}, s32[4096]{0:T(1024)}, u32[]{:S(2)}) copy-start(s32[4096]{0:T(1024)} %param.22) | copy-start | bytes 49156
  55.7 7.3 %collective-permute-start.2 = (bf16[2,16,2688]{2,1,0:T(8,128)(2,1)S(1)}, bf16[2,16,2688]{2,1,0:T(8,128)(2,1)S(1)}, u32[]{:S(2)}, u32[]{:S(2)}) collective-permute-start(bf16[2,16,2688]{2,1,0:T(8,128)(2,1)S(1)} %get-tuple-element.102), channel_id=1, source_target_pairs={{0,2},{2,0},{4,6},{6,4},{8,10},{10,8},{12,14},{14,12},{16,18},{18,... | collective-permute-start | bytes 516104 | tf_op jit(solution)/shard_map/ppermute | solution.py:549
  56.5 10.7 %collective-permute-start.7 = (bf16[2,16,2688]{2,1,0:T(8,128)(2,1)S(1)}, bf16[2,16,2688]{2,1,0:T(8,128)(2,1)S(1)}, u32[]{:S(2)}, u32[]{:S(2)}) collective-permute-start(bf16[2,16,2688]{2,1,0:T(8,128)(2,1)S(1)} %get-tuple-element.111), channel_id=1, source_target_pairs={{0,4},{2,6},{4,0},{6,2},{8,12},{10,14},{12,8},{14,10},{16,20},{18,... | collective-permute-start | bytes 516104 | tf_op jit(solution)/shard_map/ppermute | solution.py:549
  57.2 10.0 %collective-permute-start.8 = (bf16[2,16,2688]{2,1,0:T(8,128)(2,1)S(1)}, bf16[2,16,2688]{2,1,0:T(8,128)(2,1)S(1)}, u32[]{:S(2)}, u32[]{:S(2)}) collective-permute-start(bf16[2,16,2688]{2,1,0:T(8,128)(2,1)S(1)} %get-tuple-element.112), channel_id=1, source_target_pairs={{0,6},{2,4},{4,2},{6,0},{8,14},{10,12},{12,10},{14,8},{16,22},{18,... | collective-permute-start | bytes 516104 | tf_op jit(solution)/shard_map/ppermute | solution.py:549
  59.2 17.8 %all-to-all-start.3 = ((bf16[16,16,512]{2,1,0:T(8,128)(2,1)}), bf16[16,16,512]{2,1,0:T(8,128)(2,1)S(1)}, u32[]{:S(2)}, u32[]{:S(2)}) async-start(bf16[16,16,512]{2,1,0:T(8,128)(2,1)} %bitcast.16), calls=%async_computation.3 | async-start | bytes 524288 | tf_op jit(solution)/shard_map/all_to_all | solution.py:686
  63.0 9.8 %collective-permute-start.3 = (bf16[2,16,2688]{2,1,0:T(8,128)(2,1)S(1)}, bf16[2,16,2688]{2,1,0:T(8,128)(2,1)S(1)}, u32[]{:S(2)}, u32[]{:S(2)}) collective-permute-start(bf16[2,16,2688]{2,1,0:T(8,128)(2,1)S(1)} %get-tuple-element.104), channel_id=1, source_target_pairs={{0,2},{2,0},{4,6},{6,4},{8,10},{10,8},{12,14},{14,12},{16,18},{18,... | collective-permute-start | bytes 516104 | tf_op jit(solution)/shard_map/ppermute | solution.py:549
  64.8 12.1 %collective-permute-start.4 = (bf16[2,16,2688]{2,1,0:T(8,128)(2,1)S(1)}, bf16[2,16,2688]{2,1,0:T(8,128)(2,1)S(1)}, u32[]{:S(2)}, u32[]{:S(2)}) collective-permute-start(bf16[2,16,2688]{2,1,0:T(8,128)(2,1)S(1)} %get-tuple-element.105), channel_id=1, source_target_pairs={{0,4},{2,6},{4,0},{6,2},{8,12},{10,14},{12,8},{14,10},{16,20},{18,... | collective-permute-start | bytes 516104 | tf_op jit(solution)/shard_map/ppermute | solution.py:549
  66.2 10.6 %collective-permute-start.5 = (bf16[2,16,2688]{2,1,0:T(8,128)(2,1)S(1)}, bf16[2,16,2688]{2,1,0:T(8,128)(2,1)S(1)}, u32[]{:S(2)}, u32[]{:S(2)}) collective-permute-start(bf16[2,16,2688]{2,1,0:T(8,128)(2,1)S(1)} %get-tuple-element.106), channel_id=1, source_target_pairs={{0,6},{2,4},{4,2},{6,0},{8,14},{10,12},{12,10},{14,8},{16,22},{18,... | collective-permute-start | bytes 516104 | tf_op jit(solution)/shard_map/ppermute | solution.py:549
  67.4 12.0 %collective-permute-start.9 = (bf16[16,2688]{1,0:T(8,128)(2,1)S(1)}, bf16[16,2688]{1,0:T(8,128)(2,1)S(1)}, u32[]{:S(2)}, u32[]{:S(2)}) collective-permute-start(bf16[16,2688]{1,0:T(8,128)(2,1)S(1)} %get-tuple-element.140), channel_id=1, source_target_pairs={{0,16},{2,18},{4,20},{6,22},{8,24},{10,26},{12,28},{14,30},{16,0},... | collective-permute-start | bytes 258056 | tf_op jit(solution)/shard_map/ppermute | solution.py:549
  69.4 10.0 %collective-permute-start.10 = (bf16[16,2688]{1,0:T(8,128)(2,1)S(1)}, bf16[16,2688]{1,0:T(8,128)(2,1)S(1)}, u32[]{:S(2)}, u32[]{:S(2)}) collective-permute-start(bf16[16,2688]{1,0:T(8,128)(2,1)S(1)} %get-tuple-element.141), channel_id=1, source_target_pairs={{0,24},{2,26},{4,28},{6,30},{8,16},{10,18},{12,20},{14,22},{16,8},... | collective-permute-start | bytes 258056 | tf_op jit(solution)/shard_map/ppermute | solution.py:549
  77.0 4.6 %collective-permute-start.6 = (bf16[16,2688]{1,0:T(8,128)(2,1)S(1)}, bf16[16,2688]{1,0:T(8,128)(2,1)S(1)}, u32[]{:S(2)}, u32[]{:S(2)}) collective-permute-start(bf16[16,2688]{1,0:T(8,128)(2,1)S(1)} %slice_bitcast_fusion.2), channel_id=1, source_target_pairs={{0,8},{2,10},{4,12},{6,14},{8,0},{10,2},{12,4},{14,6},{16,24},{18,... | collective-permute-start | bytes 258056 | tf_op jit(solution)/shard_map/ppermute | solution.py:549
  81.6 4.9 %collective-permute-start.16 = (bf16[16,2688]{1,0:T(8,128)(2,1)S(1)}, bf16[16,2688]{1,0:T(8,128)(2,1)S(1)}, u32[]{:S(2)}, u32[]{:S(2)}) collective-permute-start(bf16[16,2688]{1,0:T(8,128)(2,1)S(1)} %fusion.2), channel_id=1, source_target_pairs={{0,8},{2,10},{4,12},{6,14},{8,0},{10,2},{12,4},{14,6},{16,24},{18,... | collective-permute-start | bytes 258056 | tf_op jit(solution)/shard_map/ppermute | solution.py:549
  83.3 7.1 %collective-permute-start.12 = (bf16[16,2688]{1,0:T(8,128)(2,1)S(1)}, bf16[16,2688]{1,0:T(8,128)(2,1)S(1)}, u32[]{:S(2)}, u32[]{:S(2)}) collective-permute-start(bf16[16,2688]{1,0:T(8,128)(2,1)S(1)} %fusion.2), channel_id=1, source_target_pairs={{0,24},{2,26},{4,28},{6,30},{8,16},{10,18},{12,20},{14,22},{16,8},... | collective-permute-start | bytes 258056 | tf_op jit(solution)/shard_map/ppermute | solution.py:549
  84.9 9.3 %collective-permute-start.11 = (bf16[16,2688]{1,0:T(8,128)(2,1)S(1)}, bf16[16,2688]{1,0:T(8,128)(2,1)S(1)}, u32[]{:S(2)}, u32[]{:S(2)}) collective-permute-start(bf16[16,2688]{1,0:T(8,128)(2,1)S(1)} %fusion.2), channel_id=1, source_target_pairs={{0,16},{2,18},{4,20},{6,22},{8,24},{10,26},{12,28},{14,30},{16,0},... | collective-permute-start | bytes 258056 | tf_op jit(solution)/shard_map/ppermute | solution.py:549
  86.5 8.3 %collective-permute-start.19 = (bf16[2,16,2688]{2,1,0:T(8,128)(2,1)S(1)}, bf16[2,16,2688]{2,1,0:T(8,128)(2,1)S(1)}, u32[]{:S(2)}, u32[]{:S(2)}) collective-permute-start(bf16[2,16,2688]{2,1,0:T(8,128)(2,1)S(1)} %pad_maximum_fusion.1.refs_0_), channel_id=1, source_target_pairs={{0,6},{2,4},{4,2},{6,0},{8,14},{10,12},{12,10},{14,8},{16,22},{18,... | collective-permute-start | bytes 516104 | tf_op jit(solution)/shard_map/ppermute | solution.py:549
  88.8 6.3 %collective-permute-start.18 = (bf16[2,16,2688]{2,1,0:T(8,128)(2,1)S(1)}, bf16[2,16,2688]{2,1,0:T(8,128)(2,1)S(1)}, u32[]{:S(2)}, u32[]{:S(2)}) collective-permute-start(bf16[2,16,2688]{2,1,0:T(8,128)(2,1)S(1)} %pad_maximum_fusion.1.refs_0_), channel_id=1, source_target_pairs={{0,4},{2,6},{4,0},{6,2},{8,12},{10,14},{12,8},{14,10},{16,20},{18,... | collective-permute-start | bytes 516104 | tf_op jit(solution)/shard_map/ppermute | solution.py:549
  89.2 6.4 %collective-permute-start.17 = (bf16[2,16,2688]{2,1,0:T(8,128)(2,1)S(1)}, bf16[2,16,2688]{2,1,0:T(8,128)(2,1)S(1)}, u32[]{:S(2)}, u32[]{:S(2)}) collective-permute-start(bf16[2,16,2688]{2,1,0:T(8,128)(2,1)S(1)} %pad_maximum_fusion.1.refs_0_), channel_id=1, source_target_pairs={{0,2},{2,0},{4,6},{6,4},{8,10},{10,8},{12,14},{14,12},{16,18},{18,... | collective-permute-start | bytes 516104 | tf_op jit(solution)/shard_map/ppermute | solution.py:549
  90.4 14.5 %all-to-all-start.4 = ((bf16[32,8,512]{2,1,0:T(8,128)(2,1)}), bf16[32,8,512]{2,1,0:T(8,128)(2,1)S(1)}, u32[]{:S(2)}, u32[]{:S(2)}) async-start(bf16[32,8,512]{2,1,0:T(8,128)(2,1)} %bitcast.26), calls=%async_computation.4 | async-start | bytes 524288 | tf_op jit(solution)/shard_map/all_to_all | solution.py:694
  94.3 1.5 %collective-permute-start.24 = (bf16[2,16,2688]{2,1,0:T(8,128)(2,1)S(1)}, bf16[2,16,2688]{2,1,0:T(8,128)(2,1)S(1)}, u32[]{:S(2)}, u32[]{:S(2)}) collective-permute-start(bf16[2,16,2688]{2,1,0:T(8,128)(2,1)S(1)} %pad_maximum_fusion.refs_4_), channel_id=1, source_target_pairs={{0,1},{1,0},{2,3},{3,2},{4,5},{5,4},{6,7},{7,6},{8,9},{9,8},{10,11... | collective-permute-start | bytes 516104 | tf_op jit(solution)/shard_map/ppermute | solution.py:561
  94.6 3.8 %collective-permute-start.20 = (bf16[2,16,2688]{2,1,0:T(8,128)(2,1)S(1)}, bf16[2,16,2688]{2,1,0:T(8,128)(2,1)S(1)}, u32[]{:S(2)}, u32[]{:S(2)}) collective-permute-start(bf16[2,16,2688]{2,1,0:T(8,128)(2,1)S(1)} %pad_maximum_fusion.1.refs_0_), channel_id=1, source_target_pairs={{0,1},{1,0},{2,3},{3,2},{4,5},{5,4},{6,7},{7,6},{8,9},{9,8},{10,11... | collective-permute-start | bytes 516104 | tf_op jit(solution)/shard_map/ppermute | solution.py:561
  94.9 4.1 %collective-permute-start.23 = (bf16[2,16,2688]{2,1,0:T(8,128)(2,1)S(1)}, bf16[2,16,2688]{2,1,0:T(8,128)(2,1)S(1)}, u32[]{:S(2)}, u32[]{:S(2)}) collective-permute-start(bf16[2,16,2688]{2,1,0:T(8,128)(2,1)S(1)} %collective-permute-done.19.refs_3_), channel_id=1, source_target_pairs={{0,1},{1,0},{2,3},{3,2},{4,5},{5,4},{6,7},{7,6},{8,9},{9,8},{10,11... | collective-permute-start | bytes 516104 | tf_op jit(solution)/shard_map/ppermute | solution.py:561
  95.1 5.3 %collective-permute-start.22 = (bf16[2,16,2688]{2,1,0:T(8,128)(2,1)S(1)}, bf16[2,16,2688]{2,1,0:T(8,128)(2,1)S(1)}, u32[]{:S(2)}, u32[]{:S(2)}) collective-permute-start(bf16[2,16,2688]{2,1,0:T(8,128)(2,1)S(1)} %collective-permute-done.18.refs_2_), channel_id=1, source_target_pairs={{0,1},{1,0},{2,3},{3,2},{4,5},{5,4},{6,7},{7,6},{8,9},{9,8},{10,11... | collective-permute-start | bytes 516104 | tf_op jit(solution)/shard_map/ppermute | solution.py:561
  95.6 4.8 %collective-permute-start.21 = (bf16[2,16,2688]{2,1,0:T(8,128)(2,1)S(1)}, bf16[2,16,2688]{2,1,0:T(8,128)(2,1)S(1)}, u32[]{:S(2)}, u32[]{:S(2)}) collective-permute-start(bf16[2,16,2688]{2,1,0:T(8,128)(2,1)S(1)} %collective-permute-done.17.refs_1_), channel_id=1, source_target_pairs={{0,1},{1,0},{2,3},{3,2},{4,5},{5,4},{6,7},{7,6},{8,9},{9,8},{10,11... | collective-permute-start | bytes 516104 | tf_op jit(solution)/shard_map/ppermute | solution.py:561
  95.8 12.8 %collective-permute-start.15 = (bf16[2,16,2688]{2,1,0:T(8,128)(2,1)S(1)}, bf16[2,16,2688]{2,1,0:T(8,128)(2,1)S(1)}, u32[]{:S(2)}, u32[]{:S(2)}) collective-permute-start(bf16[2,16,2688]{2,1,0:T(8,128)(2,1)S(1)} %pad_maximum_fusion.refs_4_), channel_id=1, source_target_pairs={{0,6},{2,4},{4,2},{6,0},{8,14},{10,12},{12,10},{14,8},{16,22},{18,... | collective-permute-start | bytes 516104 | tf_op jit(solution)/shard_map/ppermute | solution.py:549
  98.4 10.3 %collective-permute-start.14 = (bf16[2,16,2688]{2,1,0:T(8,128)(2,1)S(1)}, bf16[2,16,2688]{2,1,0:T(8,128)(2,1)S(1)}, u32[]{:S(2)}, u32[]{:S(2)}) collective-permute-start(bf16[2,16,2688]{2,1,0:T(8,128)(2,1)S(1)} %pad_maximum_fusion.refs_4_), channel_id=1, source_target_pairs={{0,4},{2,6},{4,0},{6,2},{8,12},{10,14},{12,8},{14,10},{16,20},{18,... | collective-permute-start | bytes 516104 | tf_op jit(solution)/shard_map/ppermute | solution.py:549
  99.0 9.7 %collective-permute-start.13 = (bf16[2,16,2688]{2,1,0:T(8,128)(2,1)S(1)}, bf16[2,16,2688]{2,1,0:T(8,128)(2,1)S(1)}, u32[]{:S(2)}, u32[]{:S(2)}) collective-permute-start(bf16[2,16,2688]{2,1,0:T(8,128)(2,1)S(1)} %pad_maximum_fusion.refs_4_), channel_id=1, source_target_pairs={{0,2},{2,0},{4,6},{6,4},{8,10},{10,8},{12,14},{14,12},{16,18},{18,... | collective-permute-start | bytes 516104 | tf_op jit(solution)/shard_map/ppermute | solution.py:549
  108.7 1.6 %collective-permute-start.25 = (bf16[2,16,2688]{2,1,0:T(8,128)(2,1)S(1)}, bf16[2,16,2688]{2,1,0:T(8,128)(2,1)S(1)}, u32[]{:S(2)}, u32[]{:S(2)}) collective-permute-start(bf16[2,16,2688]{2,1,0:T(8,128)(2,1)S(1)} %collective-permute-done.13.refs_0_), channel_id=1, source_target_pairs={{0,1},{1,0},{2,3},{3,2},{4,5},{5,4},{6,7},{7,6},{8,9},{9,8},{10,11... | collective-permute-start | bytes 516104 | tf_op jit(solution)/shard_map/ppermute | solution.py:561
  108.7 1.7 %collective-permute-start.26 = (bf16[2,16,2688]{2,1,0:T(8,128)(2,1)S(1)}, bf16[2,16,2688]{2,1,0:T(8,128)(2,1)S(1)}, u32[]{:S(2)}, u32[]{:S(2)}) collective-permute-start(bf16[2,16,2688]{2,1,0:T(8,128)(2,1)S(1)} %collective-permute-done.14.refs_1_), channel_id=1, source_target_pairs={{0,1},{1,0},{2,3},{3,2},{4,5},{5,4},{6,7},{7,6},{8,9},{9,8},{10,11... | collective-permute-start | bytes 516104 | tf_op jit(solution)/shard_map/ppermute | solution.py:561
  109.2 1.4 %collective-permute-start.27 = (bf16[2,16,2688]{2,1,0:T(8,128)(2,1)S(1)}, bf16[2,16,2688]{2,1,0:T(8,128)(2,1)S(1)}, u32[]{:S(2)}, u32[]{:S(2)}) collective-permute-start(bf16[2,16,2688]{2,1,0:T(8,128)(2,1)S(1)} %collective-permute-done.15.refs_2_), channel_id=1, source_target_pairs={{0,1},{1,0},{2,3},{3,2},{4,5},{5,4},{6,7},{7,6},{8,9},{9,8},{10,11... | collective-permute-start | bytes 516104 | tf_op jit(solution)/shard_map/ppermute | solution.py:561
  (13 other events, 469.6 us)

commit v6 on v5

--- a/solution.py
+++ b/solution.py
@@ -272,7 +272,7 @@
     og_ref,
     pos_ref,
     timew_ref,
-    lo_ref,
+    lo_out,
     n1_ref,
     y_ref,
     go_ref,
@@ -283,6 +283,8 @@
     h_ref,
     slope_ref,
     a_ref,
+    lo_ref,
+    sem,
 ):
     rows, width = x_ref.shape
     heads, count = pos_ref.shape
@@ -337,6 +339,8 @@
     y_ref[...] = y
     branch = dot_nn(y, wo_ref[...]) + bo_ref[...]
     lo_ref[...] = (jnp.concatenate([valid] * (width // LANES), axis=1) * (x + branch)).astype(BF16)
+    out_copy = pltpu.make_async_copy(lo_ref, lo_out, sem)
+    out_copy.start()
     du = dmix * n2
     e2 = dmix * u
     g2g_ref[...] = jnp.sum(e2 * ohat, axis=0, keepdims=True)
@@ -365,6 +369,7 @@
         msg_ref[:, half_cols + width :] = y_half.astype(BF16)
     else:
         msg_ref[...] = jnp.zeros_like(msg_ref)
+    out_copy.wait()
 
 
 SMALL_ROWS = 48
@@ -521,7 +526,10 @@
 def unpack_last_kernel(planes, columns, *refs):
     peers = columns - 1
     theirs, before_ref = refs[:peers], refs[peers + 2]
-    uvqk_ref, wout_ref, b_ref, g1_ref, g2_ref, bo_ref, pos_ref, time_ref, small_ref, *scratch = refs[peers + 3 :]
+    uvqk_ref, wout_ref, *small_outs = refs[peers + 3 : peers + 11]
+    small_ref, *held, small_sems = refs[peers + 11 : peers + 19]
+    b_ref, g1_ref, g2_ref, bo_ref, pos_ref, time_ref = held
+    scratch = refs[peers + 19 :]
     small_ref[...] = before_ref[...]
     chunks = chunks_of(planes, 2, theirs, 1, 1)
     copies = unpack(planes, columns, chunks, uvqk_ref, wout_ref, small_ref, *scratch)
@@ -534,7 +542,7 @@
     heads, count = pos_ref.shape
     pos_ref[...] = small_ref[at : at + heads, 0:count]
     time_ref[...] = small_ref[at + heads : at + 2 * heads, 0:count]
-    for copy in copies:
+    for copy in copies + start_all(held, small_outs, small_sems):
         copy.wait()
 
 
@@ -665,8 +673,11 @@
             pltpu.VMEM((rows, 4 * width), F32),
             pltpu.VMEM((heads // 2, 2 * rows, rows), F32),
             pltpu.VMEM((heads // 2, 2 * rows, rows), BF16),
+            pltpu.VMEM((rows, width), BF16),
+            pltpu.SemaphoreType.DMA,
         ),
         room=24,
+        out_specs=(HBM,) + (VMEM,) * 7,
     )(
         x,
         w_uvqk,
@@ -758,7 +769,7 @@
         small_shape = shape_of((width // 2, LANES), F32)
         wide_shapes = (shape_of((width, 4 * width), F32), shape_of((width, width), F32))
 
-        def unpack_call(body, specs, outs, chunks, scratch=(), aliases=None):
+        def unpack_call(body, specs, outs, chunks, scratch=(), aliases=None, place=VMEM):
             return call(
                 functools.partial(body, planes, columns),
                 wide_shapes + outs,
@@ -771,7 +782,7 @@
                     pltpu.VMEM((chunks, short, width), F32),
                     pltpu.SemaphoreType.DMA((2 * chunks,)),
                 ),
-                out_specs=(HBM, HBM) + (VMEM,) * len(outs),
+                out_specs=(HBM, HBM) + (place,) * len(outs),
                 aliases=aliases,
             )
 
@@ -786,20 +797,19 @@
         *sums_so_far, small_sum = unpack_call(
             unpack_next_kernel, wide_specs, (small_shape,), 2 * peers, aliases=wides
         )(*fars[1:], *sums_so_far, small_sum)
+        small_outs = ((1, 4 * width),) + ((1, width),) * 3 + ((heads, count),) * 2
         w_uvqk_sum, w_out_sum, b_sum, g1_sum, g2_sum, bo_sum, pos_sum, time_sum = unpack_call(
             unpack_last_kernel,
             wide_specs,
-            (
-                shape_of((1, 4 * width), F32),
-                shape_of((1, width), F32),
-                shape_of((1, width), F32),
-                shape_of((1, width), F32),
-                shape_of((heads, count), F32),
-                shape_of((heads, count), F32),
+            tuple(shape_of(shape, F32) for shape in small_outs),
+            2 * peers,
+            scratch=(
+                pltpu.VMEM(small_shape.shape, F32),
+                *(pltpu.VMEM(shape, F32) for shape in small_outs),
+                pltpu.SemaphoreType.DMA((len(small_outs),)),
             ),
-            2 * peers,
-            scratch=(pltpu.VMEM(small_shape.shape, F32),),
             aliases=wides,
+            place=HBM,
         )(*their_fars, *sums_so_far, small_sum)
     else:
         table_grad = into_table(to_owners(home_again(dx)))

time: 113 us -> 112 us (level)
  no operation moved by 1% of the time
where the time goes in v6:
time: 112 us
  blocking collectives  39.3 us (35%)
  starting transfers between devices  32.7 us (29%)
  Pallas kernels  22.3 us (20%)
  waiting for transfers between devices  13.5 us (12%)
  local copies, waits for them, and re-layouts  2.29 us (2%)
  between operations  1.18 us (1%)
    ppermute x18, starting transfers between devices, xor_step(): return lax.ppermute(value, 'dp', [(i, i ^ step) for i in range(size)])  22.9 us
    all_to_all x1, blocking collectives, on_device(): lax.all_to_all(msg.reshape(devices, 1, LANES), BOTH, 0, 0, tiled=True)  14 us
    all_to_all x1, blocking collectives, on_device(): lax.all_to_all(home.reshape(replicas, piece, width), 'dp', 0, 0, tiled=True)  13 us
    all_to_all x1, blocking collectives, on_device(): lax.all_to_all(served.reshape(devices, cap, width), BOTH, 0, 0, tiled=True)  12.3 us
    ppermute x18, waiting for transfers between devices, xor_step(): return lax.ppermute(value, 'dp', [(i, i ^ step) for i in range(size)])  10.6 us
    pallas_call x1, Pallas kernels, on_device(): call(functools.partial(layer_kernel, staged), (shape_of((rows, width), BF...  4.8 us
    all_to_all x1, starting transfers between devices, send_sums(): lax.all_to_all(sums.reshape(devices, cap, width), BOTH, 0, 0, tiled=True)  3.9 us
    all_to_all x1, starting transfers between devices, home_again(): lax.all_to_all(dx.reshape(replicas, piece, width), 'dp', 0, 0, tiled=True)  3.72 us
  transfers between devices with their start and end apart: 30, of which 10 were waited for; matrix products, arithmetic and copies ran while one was open for 0% of the time, Pallas kernels for 10%

profile of v6, /device:TPU:0, one launch (start us, length us, event | category | flops | bytes accessed | tf_op | source)
XLA Modules:
  0.0 111.6 jit_solution(1558923119723499473)
XLA Ops:
  0.6 1.7 %shard_map.247 = s32[32,128]{1,0:T(8,128)} custom-call(s32[8,32]{1,0:T(8,128)} %bitcast.67, s32[1,256]{1,0:T(1,128)} %bitcast.52, s32[1,64]{1,0:T(1,128)} %len_ref.1, s32[1,64]{1,0:T(1,128)} %dest_ref.1, s32[32,128]{1,0:T(8,128)} %bitcast.50), custom_call_target="tpu_custom_call" | custom-call | flops 1048576 | bytes 131072 | tf_op jit(solution)/shard_map/pallas_call | solution.py:612
  3.0 14.0 %all_to_all.25 = s32[32,1,128]{2,1,0:T(1,128)S(1)} all-to-all(s32[32,1,128]{2,1,0:T(1,128)} %bitcast.66), channel_id=1, replica_groups=mesh['dp'=16,'table'=2] {'dp','table'}, dimensions={0} | all-to-all | bytes 32768 | tf_op jit(solution)/shard_map/all_to_all | solution.py:631
  17.0 2.2 %copy-done = bf16[4096,512]{1,0:T(8,128)(2,1)S(1)} copy-done((bf16[4096,512]{1,0:T(8,128)(2,1)S(1)}, bf16[4096,512]{1,0:T(8,128)(2,1)}, u32[]{:S(2)}) %copy-start) | copy-done | bytes 4194328
  19.2 1.9 %shard_map.248 = bf16[256,512]{1,0:T(8,128)(2,1)S(1)} custom-call(s32[32,128]{1,0:T(8,128)S(1)} %bitcast.48, bf16[4096,512]{1,0:T(8,128)(2,1)S(1)} %copy-done), custom_call_target="tpu_custom_call" | custom-call | flops 1073741824 | bytes 5242880 | tf_op jit(solution)/shard_map/pallas_call | solution.py:634
  21.1 12.3 %all_to_all.26 = bf16[32,8,512]{2,1,0:T(8,128)(2,1)S(1)} all-to-all(bf16[32,8,512]{2,1,0:T(8,128)(2,1)S(1)} %bitcast.44), channel_id=1, replica_groups=mesh['dp'=16,'table'=2] {'dp','table'}, dimensions={0} | all-to-all | bytes 524288 | tf_op jit(solution)/shard_map/all_to_all | solution.py:637
  33.6 13.0 %all_to_all.27 = bf16[16,16,512]{2,1,0:T(8,128)(2,1)S(1)} all-to-all(bf16[16,16,512]{2,1,0:T(8,128)(2,1)S(1)} %bitcast.47), channel_id=1, replica_groups=mesh['dp'=16,'table'=2] {'dp'}, dimensions={0} | all-to-all | bytes 524288 | tf_op jit(solution)/shard_map/all_to_all | solution.py:652
  46.7 4.8 %shard_map.250 = (bf16[256,512]{1,0:T(8,128)(2,1)}, bf16[256,512]{1,0:T(8,128)(2,1)S(1)}, bf16[256,512]{1,0:T(8,128)(2,1)S(1)}, bf16[256,512]{1,0:T(8,128)(2,1)S...) custom-call(bf16[256,512]{1,0:T(8,128)(2,1)S(1)} %bitcast.42, ...), custom_call_target="tpu_custom_call" | custom-call | flops 2147483648 | bytes 8388608 | tf_op jit(solution)/shard_map/pallas_call | solution.py:657
  51.6 2.8 %shard_map.251 = (bf16[256,512]{1,0:T(8,128)(2,1)}, f32[256,128]{1,0:T(8,128)S(1)}) custom-call(bf16[256,2048]{1,0:T(8,128)(2,1)S(1)} %get-tuple-element.80.dh_ref, bf16[512,2048]{1,0:T(8,128)(2,1)S(1)} %copy-done.1, bf16[256,512]{1,0:T(8,128)(2,1)S(1)} %bitcast.43, f32[1,512]{1,0:T(1,128)S(1)} %bitcast.56, bf16[256,512]{1,0:T(8,128)(2,1)S(1)} %get-tuple-element.81.go_ref, ...), custom_call_target="tpu_custom_call" | custom-call | flops 536870912 | bytes 4194304 | tf_op jit(solution)/shard_map/pallas_call | solution.py:726
  54.5 0.9 shard_map.252
  56.9 2.0 %collective-permute-start.8 = (bf16[2,16,2688]{2,1,0:T(8,128)(2,1)S(1)}, bf16[2,16,2688]{2,1,0:T(8,128)(2,1)S(1)}, u32[]{:S(2)}, u32[]{:S(2)}) collective-permute-start(bf16[2,16,2688]{2,1,0:T(8,128)(2,1)S(1)} %get-tuple-element.112), channel_id=1, source_target_pairs={{0,6},{2,4},{4,2},{6,0},{8,14},{10,12},{12,10},{14,8},{16,22},{18,... | collective-permute-start | bytes 516104 | tf_op jit(solution)/shard_map/ppermute | solution.py:557
  58.9 3.7 %all-to-all-start.3 = ((bf16[16,16,512]{2,1,0:T(8,128)(2,1)}), bf16[16,16,512]{2,1,0:T(8,128)(2,1)S(1)}, u32[]{:S(2)}, u32[]{:S(2)}) async-start(bf16[16,16,512]{2,1,0:T(8,128)(2,1)} %bitcast.16), calls=%async_computation.3 | async-start | bytes 524288 | tf_op jit(solution)/shard_map/all_to_all | solution.py:697
  62.7 1.8 %collective-permute-start.3 = (bf16[2,16,2688]{2,1,0:T(8,128)(2,1)S(1)}, bf16[2,16,2688]{2,1,0:T(8,128)(2,1)S(1)}, u32[]{:S(2)}, u32[]{:S(2)}) collective-permute-start(bf16[2,16,2688]{2,1,0:T(8,128)(2,1)S(1)} %get-tuple-element.104), channel_id=1, source_target_pairs={{0,2},{2,0},{4,6},{6,4},{8,10},{10,8},{12,14},{14,12},{16,18},{18,... | collective-permute-start | bytes 516104 | tf_op jit(solution)/shard_map/ppermute | solution.py:557
  64.5 1.5 %collective-permute-start.4 = (bf16[2,16,2688]{2,1,0:T(8,128)(2,1)S(1)}, bf16[2,16,2688]{2,1,0:T(8,128)(2,1)S(1)}, u32[]{:S(2)}, u32[]{:S(2)}) collective-permute-start(bf16[2,16,2688]{2,1,0:T(8,128)(2,1)S(1)} %get-tuple-element.105), channel_id=1, source_target_pairs={{0,4},{2,6},{4,0},{6,2},{8,12},{10,14},{12,8},{14,10},{16,20},{18,... | collective-permute-start | bytes 516104 | tf_op jit(solution)/shard_map/ppermute | solution.py:557
  67.1 2.0 %collective-permute-start.9 = (bf16[16,2688]{1,0:T(8,128)(2,1)S(1)}, bf16[16,2688]{1,0:T(8,128)(2,1)S(1)}, u32[]{:S(2)}, u32[]{:S(2)}) collective-permute-start(bf16[16,2688]{1,0:T(8,128)(2,1)S(1)} %get-tuple-element.140), channel_id=1, source_target_pairs={{0,16},{2,18},{4,20},{6,22},{8,24},{10,26},{12,28},{14,30},{16,0},... | collective-permute-start | bytes 258056 | tf_op jit(solution)/shard_map/ppermute | solution.py:557
  69.1 1.5 %collective-permute-start.10 = (bf16[16,2688]{1,0:T(8,128)(2,1)S(1)}, bf16[16,2688]{1,0:T(8,128)(2,1)S(1)}, u32[]{:S(2)}, u32[]{:S(2)}) collective-permute-start(bf16[16,2688]{1,0:T(8,128)(2,1)S(1)} %get-tuple-element.141), channel_id=1, source_target_pairs={{0,24},{2,26},{4,28},{6,30},{8,16},{10,18},{12,20},{14,22},{16,8},... | collective-permute-start | bytes 258056 | tf_op jit(solution)/shard_map/ppermute | solution.py:557
  70.6 2.0 %collective-permute-done.3 = bf16[2,16,2688]{2,1,0:T(8,128)(2,1)S(1)} collective-permute-done((bf16[2,16,2688]{2,1,0:T(8,128)(2,1)S(1)}, bf16[2,16,2688]{2,1,0:T(8,128)(2,1)S(1)}, u32[]{:S(2)}, u32[]{:S(2)}) %collective-permute-start.3) | collective-permute-done | bytes 172064 | tf_op jit(solution)/shard_map/ppermute | solution.py:557
  72.5 4.1 %collective-permute-done.4 = bf16[2,16,2688]{2,1,0:T(8,128)(2,1)S(1)} collective-permute-done((bf16[2,16,2688]{2,1,0:T(8,128)(2,1)S(1)}, bf16[2,16,2688]{2,1,0:T(8,128)(2,1)S(1)}, u32[]{:S(2)}, u32[]{:S(2)}) %collective-permute-start.4) | collective-permute-done | bytes 172064 | tf_op jit(solution)/shard_map/ppermute | solution.py:557
  76.7 1.4 %collective-permute-start.6 = (bf16[16,2688]{1,0:T(8,128)(2,1)S(1)}, bf16[16,2688]{1,0:T(8,128)(2,1)S(1)}, u32[]{:S(2)}, u32[]{:S(2)}) collective-permute-start(bf16[16,2688]{1,0:T(8,128)(2,1)S(1)} %slice_bitcast_fusion.2), channel_id=1, source_target_pairs={{0,8},{2,10},{4,12},{6,14},{8,0},{10,2},{12,4},{14,6},{16,24},{18,... | collective-permute-start | bytes 258056 | tf_op jit(solution)/shard_map/ppermute | solution.py:557
  79.1 2.2 %collective-permute-done.6 = bf16[16,2688]{1,0:T(8,128)(2,1)S(1)} collective-permute-done((bf16[16,2688]{1,0:T(8,128)(2,1)S(1)}, bf16[16,2688]{1,0:T(8,128)(2,1)S(1)}, u32[]{:S(2)}, u32[]{:S(2)}) %collective-permute-start.6) | collective-permute-done | bytes 86048 | tf_op jit(solution)/shard_map/ppermute | solution.py:557
  81.3 1.7 %collective-permute-start.16 = (bf16[16,2688]{1,0:T(8,128)(2,1)S(1)}, bf16[16,2688]{1,0:T(8,128)(2,1)S(1)}, u32[]{:S(2)}, u32[]{:S(2)}) collective-permute-start(bf16[16,2688]{1,0:T(8,128)(2,1)S(1)} %fusion.2), channel_id=1, source_target_pairs={{0,8},{2,10},{4,12},{6,14},{8,0},{10,2},{12,4},{14,6},{16,24},{18,... | collective-permute-start | bytes 258056 | tf_op jit(solution)/shard_map/ppermute | solution.py:557
  83.0 1.6 %collective-permute-start.12 = (bf16[16,2688]{1,0:T(8,128)(2,1)S(1)}, bf16[16,2688]{1,0:T(8,128)(2,1)S(1)}, u32[]{:S(2)}, u32[]{:S(2)}) collective-permute-start(bf16[16,2688]{1,0:T(8,128)(2,1)S(1)} %fusion.2), channel_id=1, source_target_pairs={{0,24},{2,26},{4,28},{6,30},{8,16},{10,18},{12,20},{14,22},{16,8},... | collective-permute-start | bytes 258056 | tf_op jit(solution)/shard_map/ppermute | solution.py:557
  84.9 1.3 %collective-permute-done.16 = bf16[16,2688]{1,0:T(8,128)(2,1)S(1)} collective-permute-done((bf16[16,2688]{1,0:T(8,128)(2,1)S(1)}, bf16[16,2688]{1,0:T(8,128)(2,1)S(1)}, u32[]{:S(2)}, u32[]{:S(2)}) %collective-permute-start.16) | collective-permute-done | bytes 86048 | tf_op jit(solution)/shard_map/ppermute | solution.py:557
  86.2 2.3 %collective-permute-start.19 = (bf16[2,16,2688]{2,1,0:T(8,128)(2,1)S(1)}, bf16[2,16,2688]{2,1,0:T(8,128)(2,1)S(1)}, u32[]{:S(2)}, u32[]{:S(2)}) collective-permute-start(bf16[2,16,2688]{2,1,0:T(8,128)(2,1)S(1)} %pad_maximum_fusion.1.refs_0_), channel_id=1, source_target_pairs={{0,6},{2,4},{4,2},{6,0},{8,14},{10,12},{12,10},{14,8},{16,22},{18,... | collective-permute-start | bytes 516104 | tf_op jit(solution)/shard_map/ppermute | solution.py:557
  88.9 1.1 collective-permute-start.17
  90.0 3.9 %all-to-all-start.4 = ((bf16[32,8,512]{2,1,0:T(8,128)(2,1)}), bf16[32,8,512]{2,1,0:T(8,128)(2,1)S(1)}, u32[]{:S(2)}, u32[]{:S(2)}) async-start(bf16[32,8,512]{2,1,0:T(8,128)(2,1)} %bitcast.26), calls=%async_computation.4 | async-start | bytes 524288 | tf_op jit(solution)/shard_map/all_to_all | solution.py:705
  95.5 2.7 %collective-permute-start.15 = (bf16[2,16,2688]{2,1,0:T(8,128)(2,1)S(1)}, bf16[2,16,2688]{2,1,0:T(8,128)(2,1)S(1)}, u32[]{:S(2)}, u32[]{:S(2)}) collective-permute-start(bf16[2,16,2688]{2,1,0:T(8,128)(2,1)S(1)} %pad_maximum_fusion.refs_4_), channel_id=1, source_target_pairs={{0,6},{2,4},{4,2},{6,0},{8,14},{10,12},{12,10},{14,8},{16,22},{18,... | collective-permute-start | bytes 516104 | tf_op jit(solution)/shard_map/ppermute | solution.py:557
  99.0 1.1 %shard_map.255 = (s32[32,128]{1,0:T(8,128)}, f32[32,128]{1,0:T(8,128)}, f32[8,256]{1,0:T(8,128)S(1)}) custom-call(s32[32,128]{1,0:T(8,128)S(1)} %bitcast.49, s32[32,128]{1,0:T(8,128)S(1)} %bitcast.51), custom_call_target="tpu_custom_call" | custom-call | flops 67108864 | bytes 1048576 | tf_op jit(solution)/shard_map/pallas_call | solution.py:638
  100.1 2.0 %shard_map.254 = (f32[512,2048]{1,0:T(8,128)}, f32[512,512]{1,0:T(8,128)}, f32[256,128]{1,0:T(8,128)S(1)}) custom-call(bf16[2,16,2688]{2,1,0:T(8,128)(2,1)S(1)} %pad_maximum_fusion.1.refs_0_, bf16[2,16,2688]{2,1,0:T(8,128)(2,1)S(1)} %collective-permute-done.17.refs_1_, bf16[2,16,2688]{2,1,0:T(8,128)(2,1)S(1)} %collective-permute-done.18.refs_2_, ...), custom_call_target="tpu_custom_call" | custom-call | flops 1048576 | bytes 3145728 | tf_op jit(solution)/shard_map/pallas_call | solution.py:792
  102.2 2.4 %all-to-all-done.4 = bf16[32,8,512]{2,1,0:T(8,128)(2,1)S(1)} async-done(((bf16[32,8,512]{2,1,0:T(8,128)(2,1)}), bf16[32,8,512]{2,1,0:T(8,128)(2,1)S(1)}, u32[]{:S(2)}, u32[]{:S(2)}) %all-to-all-start.4) | async-done | bytes 262176 | tf_op jit(solution)/shard_map/all_to_all | solution.py:705
  104.6 3.7 %shard_map.256 = f32[4096,512]{1,0:T(8,128)} custom-call(f32[8,256]{1,0:T(8,128)S(1)} %get-tuple-element.118.row_ref, bf16[256,512]{1,0:T(8,128)(2,1)S(1)} %bitcast.41), custom_call_target="tpu_custom_call" | custom-call | flops 1073741824 | bytes 8388608 | tf_op jit(solution)/shard_map/pallas_call | solution.py:710
  109.0 1.1 shard_map.257
  110.4 1.1 shard_map.258
  (80 shorter events, 8.7 us)
Async XLA Ops:
  2.3 44.3 %copy-start.4 = (f32[512]{0:T(512)S(1)}, f32[512]{0:T(512)}, u32[]{:S(2)}) copy-start(f32[512]{0:T(512)} %param.23) | copy-start | bytes 6148
  2.4 14.6 %collective-permute-start = (bf16[256,512]{1,0:T(8,128)(2,1)}, bf16[256,512]{1,0:T(8,128)(2,1)S(1)}, u32[]{:S(2)}, u32[]{:S(2)}) collective-permute-start(bf16[256,512]{1,0:T(8,128)(2,1)} %og_ref.1), channel_id=1, source_target_pairs={{0,1},{1,0},{2,3},{3,2},{4,5},{5,4},{6,7},{7,6},{8,9},{9,8},{10,11... | collective-permute-start | bytes 786440 | tf_op jit(solution)/shard_map/ppermute | solution.py:569
  51.5 2.9 %collective-permute-start.1 = (bf16[256,1792]{1,0:T(8,128)(2,1)S(1)}, bf16[256,1792]{1,0:T(8,128)(2,1)S(1)}, u32[]{:S(2)}, u32[]{:S(2)}) collective-permute-start(bf16[256,1792]{1,0:T(8,128)(2,1)S(1)} %get-tuple-element.87), channel_id=1, source_target_pairs={{0,1},{1,0},{2,3},{3,2},{4,5},{5,4},{6,7},{7,6},{8,9},{9,8},{10,11... | collective-permute-start | bytes 2752520 | tf_op jit(solution)/shard_map/ppermute | solution.py:569
  54.4 44.5 %copy-start.2 = (s32[4096]{0:T(1024)S(1)}, s32[4096]{0:T(1024)}, u32[]{:S(2)}) copy-start(s32[4096]{0:T(1024)} %param.22) | copy-start | bytes 49156
  55.4 7.3 %collective-permute-start.2 = (bf16[2,16,2688]{2,1,0:T(8,128)(2,1)S(1)}, bf16[2,16,2688]{2,1,0:T(8,128)(2,1)S(1)}, u32[]{:S(2)}, u32[]{:S(2)}) collective-permute-start(bf16[2,16,2688]{2,1,0:T(8,128)(2,1)S(1)} %get-tuple-element.102), channel_id=1, source_target_pairs={{0,2},{2,0},{4,6},{6,4},{8,10},{10,8},{12,14},{14,12},{16,18},{18,... | collective-permute-start | bytes 516104 | tf_op jit(solution)/shard_map/ppermute | solution.py:557
  56.2 10.7 %collective-permute-start.7 = (bf16[2,16,2688]{2,1,0:T(8,128)(2,1)S(1)}, bf16[2,16,2688]{2,1,0:T(8,128)(2,1)S(1)}, u32[]{:S(2)}, u32[]{:S(2)}) collective-permute-start(bf16[2,16,2688]{2,1,0:T(8,128)(2,1)S(1)} %get-tuple-element.111), channel_id=1, source_target_pairs={{0,4},{2,6},{4,0},{6,2},{8,12},{10,14},{12,8},{14,10},{16,20},{18,... | collective-permute-start | bytes 516104 | tf_op jit(solution)/shard_map/ppermute | solution.py:557
  56.9 10.0 %collective-permute-start.8 = (bf16[2,16,2688]{2,1,0:T(8,128)(2,1)S(1)}, bf16[2,16,2688]{2,1,0:T(8,128)(2,1)S(1)}, u32[]{:S(2)}, u32[]{:S(2)}) collective-permute-start(bf16[2,16,2688]{2,1,0:T(8,128)(2,1)S(1)} %get-tuple-element.112), channel_id=1, source_target_pairs={{0,6},{2,4},{4,2},{6,0},{8,14},{10,12},{12,10},{14,8},{16,22},{18,... | collective-permute-start | bytes 516104 | tf_op jit(solution)/shard_map/ppermute | solution.py:557
  58.9 17.8 %all-to-all-start.3 = ((bf16[16,16,512]{2,1,0:T(8,128)(2,1)}), bf16[16,16,512]{2,1,0:T(8,128)(2,1)S(1)}, u32[]{:S(2)}, u32[]{:S(2)}) async-start(bf16[16,16,512]{2,1,0:T(8,128)(2,1)} %bitcast.16), calls=%async_computation.3 | async-start | bytes 524288 | tf_op jit(solution)/shard_map/all_to_all | solution.py:697
  62.7 9.8 %collective-permute-start.3 = (bf16[2,16,2688]{2,1,0:T(8,128)(2,1)S(1)}, bf16[2,16,2688]{2,1,0:T(8,128)(2,1)S(1)}, u32[]{:S(2)}, u32[]{:S(2)}) collective-permute-start(bf16[2,16,2688]{2,1,0:T(8,128)(2,1)S(1)} %get-tuple-element.104), channel_id=1, source_target_pairs={{0,2},{2,0},{4,6},{6,4},{8,10},{10,8},{12,14},{14,12},{16,18},{18,... | collective-permute-start | bytes 516104 | tf_op jit(solution)/shard_map/ppermute | solution.py:557
  64.5 12.1 %collective-permute-start.4 = (bf16[2,16,2688]{2,1,0:T(8,128)(2,1)S(1)}, bf16[2,16,2688]{2,1,0:T(8,128)(2,1)S(1)}, u32[]{:S(2)}, u32[]{:S(2)}) collective-permute-start(bf16[2,16,2688]{2,1,0:T(8,128)(2,1)S(1)} %get-tuple-element.105), channel_id=1, source_target_pairs={{0,4},{2,6},{4,0},{6,2},{8,12},{10,14},{12,8},{14,10},{16,20},{18,... | collective-permute-start | bytes 516104 | tf_op jit(solution)/shard_map/ppermute | solution.py:557
  66.0 10.6 %collective-permute-start.5 = (bf16[2,16,2688]{2,1,0:T(8,128)(2,1)S(1)}, bf16[2,16,2688]{2,1,0:T(8,128)(2,1)S(1)}, u32[]{:S(2)}, u32[]{:S(2)}) collective-permute-start(bf16[2,16,2688]{2,1,0:T(8,128)(2,1)S(1)} %get-tuple-element.106), channel_id=1, source_target_pairs={{0,6},{2,4},{4,2},{6,0},{8,14},{10,12},{12,10},{14,8},{16,22},{18,... | collective-permute-start | bytes 516104 | tf_op jit(solution)/shard_map/ppermute | solution.py:557
  67.1 12.0 %collective-permute-start.9 = (bf16[16,2688]{1,0:T(8,128)(2,1)S(1)}, bf16[16,2688]{1,0:T(8,128)(2,1)S(1)}, u32[]{:S(2)}, u32[]{:S(2)}) collective-permute-start(bf16[16,2688]{1,0:T(8,128)(2,1)S(1)} %get-tuple-element.140), channel_id=1, source_target_pairs={{0,16},{2,18},{4,20},{6,22},{8,24},{10,26},{12,28},{14,30},{16,0},... | collective-permute-start | bytes 258056 | tf_op jit(solution)/shard_map/ppermute | solution.py:557
  69.1 10.0 %collective-permute-start.10 = (bf16[16,2688]{1,0:T(8,128)(2,1)S(1)}, bf16[16,2688]{1,0:T(8,128)(2,1)S(1)}, u32[]{:S(2)}, u32[]{:S(2)}) collective-permute-start(bf16[16,2688]{1,0:T(8,128)(2,1)S(1)} %get-tuple-element.141), channel_id=1, source_target_pairs={{0,24},{2,26},{4,28},{6,30},{8,16},{10,18},{12,20},{14,22},{16,8},... | collective-permute-start | bytes 258056 | tf_op jit(solution)/shard_map/ppermute | solution.py:557
  76.7 4.6 %collective-permute-start.6 = (bf16[16,2688]{1,0:T(8,128)(2,1)S(1)}, bf16[16,2688]{1,0:T(8,128)(2,1)S(1)}, u32[]{:S(2)}, u32[]{:S(2)}) collective-permute-start(bf16[16,2688]{1,0:T(8,128)(2,1)S(1)} %slice_bitcast_fusion.2), channel_id=1, source_target_pairs={{0,8},{2,10},{4,12},{6,14},{8,0},{10,2},{12,4},{14,6},{16,24},{18,... | collective-permute-start | bytes 258056 | tf_op jit(solution)/shard_map/ppermute | solution.py:557
  81.3 4.9 %collective-permute-start.16 = (bf16[16,2688]{1,0:T(8,128)(2,1)S(1)}, bf16[16,2688]{1,0:T(8,128)(2,1)S(1)}, u32[]{:S(2)}, u32[]{:S(2)}) collective-permute-start(bf16[16,2688]{1,0:T(8,128)(2,1)S(1)} %fusion.2), channel_id=1, source_target_pairs={{0,8},{2,10},{4,12},{6,14},{8,0},{10,2},{12,4},{14,6},{16,24},{18,... | collective-permute-start | bytes 258056 | tf_op jit(solution)/shard_map/ppermute | solution.py:557
  83.0 7.0 %collective-permute-start.12 = (bf16[16,2688]{1,0:T(8,128)(2,1)S(1)}, bf16[16,2688]{1,0:T(8,128)(2,1)S(1)}, u32[]{:S(2)}, u32[]{:S(2)}) collective-permute-start(bf16[16,2688]{1,0:T(8,128)(2,1)S(1)} %fusion.2), channel_id=1, source_target_pairs={{0,24},{2,26},{4,28},{6,30},{8,16},{10,18},{12,20},{14,22},{16,8},... | collective-permute-start | bytes 258056 | tf_op jit(solution)/shard_map/ppermute | solution.py:557
  84.6 9.3 %collective-permute-start.11 = (bf16[16,2688]{1,0:T(8,128)(2,1)S(1)}, bf16[16,2688]{1,0:T(8,128)(2,1)S(1)}, u32[]{:S(2)}, u32[]{:S(2)}) collective-permute-start(bf16[16,2688]{1,0:T(8,128)(2,1)S(1)} %fusion.2), channel_id=1, source_target_pairs={{0,16},{2,18},{4,20},{6,22},{8,24},{10,26},{12,28},{14,30},{16,0},... | collective-permute-start | bytes 258056 | tf_op jit(solution)/shard_map/ppermute | solution.py:557
  86.2 8.3 %collective-permute-start.19 = (bf16[2,16,2688]{2,1,0:T(8,128)(2,1)S(1)}, bf16[2,16,2688]{2,1,0:T(8,128)(2,1)S(1)}, u32[]{:S(2)}, u32[]{:S(2)}) collective-permute-start(bf16[2,16,2688]{2,1,0:T(8,128)(2,1)S(1)} %pad_maximum_fusion.1.refs_0_), channel_id=1, source_target_pairs={{0,6},{2,4},{4,2},{6,0},{8,14},{10,12},{12,10},{14,8},{16,22},{18,... | collective-permute-start | bytes 516104 | tf_op jit(solution)/shard_map/ppermute | solution.py:557
  88.5 6.3 %collective-permute-start.18 = (bf16[2,16,2688]{2,1,0:T(8,128)(2,1)S(1)}, bf16[2,16,2688]{2,1,0:T(8,128)(2,1)S(1)}, u32[]{:S(2)}, u32[]{:S(2)}) collective-permute-start(bf16[2,16,2688]{2,1,0:T(8,128)(2,1)S(1)} %pad_maximum_fusion.1.refs_0_), channel_id=1, source_target_pairs={{0,4},{2,6},{4,0},{6,2},{8,12},{10,14},{12,8},{14,10},{16,20},{18,... | collective-permute-start | bytes 516104 | tf_op jit(solution)/shard_map/ppermute | solution.py:557
  88.9 6.3 %collective-permute-start.17 = (bf16[2,16,2688]{2,1,0:T(8,128)(2,1)S(1)}, bf16[2,16,2688]{2,1,0:T(8,128)(2,1)S(1)}, u32[]{:S(2)}, u32[]{:S(2)}) collective-permute-start(bf16[2,16,2688]{2,1,0:T(8,128)(2,1)S(1)} %pad_maximum_fusion.1.refs_0_), channel_id=1, source_target_pairs={{0,2},{2,0},{4,6},{6,4},{8,10},{10,8},{12,14},{14,12},{16,18},{18,... | collective-permute-start | bytes 516104 | tf_op jit(solution)/shard_map/ppermute | solution.py:557
  90.0 14.6 %all-to-all-start.4 = ((bf16[32,8,512]{2,1,0:T(8,128)(2,1)}), bf16[32,8,512]{2,1,0:T(8,128)(2,1)S(1)}, u32[]{:S(2)}, u32[]{:S(2)}) async-start(bf16[32,8,512]{2,1,0:T(8,128)(2,1)} %bitcast.26), calls=%async_computation.4 | async-start | bytes 524288 | tf_op jit(solution)/shard_map/all_to_all | solution.py:705
  94.0 1.5 %collective-permute-start.24 = (bf16[2,16,2688]{2,1,0:T(8,128)(2,1)S(1)}, bf16[2,16,2688]{2,1,0:T(8,128)(2,1)S(1)}, u32[]{:S(2)}, u32[]{:S(2)}) collective-permute-start(bf16[2,16,2688]{2,1,0:T(8,128)(2,1)S(1)} %pad_maximum_fusion.refs_4_), channel_id=1, source_target_pairs={{0,1},{1,0},{2,3},{3,2},{4,5},{5,4},{6,7},{7,6},{8,9},{9,8},{10,11... | collective-permute-start | bytes 516104 | tf_op jit(solution)/shard_map/ppermute | solution.py:569
  94.3 3.8 %collective-permute-start.20 = (bf16[2,16,2688]{2,1,0:T(8,128)(2,1)S(1)}, bf16[2,16,2688]{2,1,0:T(8,128)(2,1)S(1)}, u32[]{:S(2)}, u32[]{:S(2)}) collective-permute-start(bf16[2,16,2688]{2,1,0:T(8,128)(2,1)S(1)} %pad_maximum_fusion.1.refs_0_), channel_id=1, source_target_pairs={{0,1},{1,0},{2,3},{3,2},{4,5},{5,4},{6,7},{7,6},{8,9},{9,8},{10,11... | collective-permute-start | bytes 516104 | tf_op jit(solution)/shard_map/ppermute | solution.py:569
  94.6 4.1 %collective-permute-start.23 = (bf16[2,16,2688]{2,1,0:T(8,128)(2,1)S(1)}, bf16[2,16,2688]{2,1,0:T(8,128)(2,1)S(1)}, u32[]{:S(2)}, u32[]{:S(2)}) collective-permute-start(bf16[2,16,2688]{2,1,0:T(8,128)(2,1)S(1)} %collective-permute-done.19.refs_3_), channel_id=1, source_target_pairs={{0,1},{1,0},{2,3},{3,2},{4,5},{5,4},{6,7},{7,6},{8,9},{9,8},{10,11... | collective-permute-start | bytes 516104 | tf_op jit(solution)/shard_map/ppermute | solution.py:569
  94.8 5.3 %collective-permute-start.22 = (bf16[2,16,2688]{2,1,0:T(8,128)(2,1)S(1)}, bf16[2,16,2688]{2,1,0:T(8,128)(2,1)S(1)}, u32[]{:S(2)}, u32[]{:S(2)}) collective-permute-start(bf16[2,16,2688]{2,1,0:T(8,128)(2,1)S(1)} %collective-permute-done.18.refs_2_), channel_id=1, source_target_pairs={{0,1},{1,0},{2,3},{3,2},{4,5},{5,4},{6,7},{7,6},{8,9},{9,8},{10,11... | collective-permute-start | bytes 516104 | tf_op jit(solution)/shard_map/ppermute | solution.py:569
  95.3 4.8 %collective-permute-start.21 = (bf16[2,16,2688]{2,1,0:T(8,128)(2,1)S(1)}, bf16[2,16,2688]{2,1,0:T(8,128)(2,1)S(1)}, u32[]{:S(2)}, u32[]{:S(2)}) collective-permute-start(bf16[2,16,2688]{2,1,0:T(8,128)(2,1)S(1)} %collective-permute-done.17.refs_1_), channel_id=1, source_target_pairs={{0,1},{1,0},{2,3},{3,2},{4,5},{5,4},{6,7},{7,6},{8,9},{9,8},{10,11... | collective-permute-start | bytes 516104 | tf_op jit(solution)/shard_map/ppermute | solution.py:569
  95.5 12.8 %collective-permute-start.15 = (bf16[2,16,2688]{2,1,0:T(8,128)(2,1)S(1)}, bf16[2,16,2688]{2,1,0:T(8,128)(2,1)S(1)}, u32[]{:S(2)}, u32[]{:S(2)}) collective-permute-start(bf16[2,16,2688]{2,1,0:T(8,128)(2,1)S(1)} %pad_maximum_fusion.refs_4_), channel_id=1, source_target_pairs={{0,6},{2,4},{4,2},{6,0},{8,14},{10,12},{12,10},{14,8},{16,22},{18,... | collective-permute-start | bytes 516104 | tf_op jit(solution)/shard_map/ppermute | solution.py:557
  98.1 10.3 %collective-permute-start.14 = (bf16[2,16,2688]{2,1,0:T(8,128)(2,1)S(1)}, bf16[2,16,2688]{2,1,0:T(8,128)(2,1)S(1)}, u32[]{:S(2)}, u32[]{:S(2)}) collective-permute-start(bf16[2,16,2688]{2,1,0:T(8,128)(2,1)S(1)} %pad_maximum_fusion.refs_4_), channel_id=1, source_target_pairs={{0,4},{2,6},{4,0},{6,2},{8,12},{10,14},{12,8},{14,10},{16,20},{18,... | collective-permute-start | bytes 516104 | tf_op jit(solution)/shard_map/ppermute | solution.py:557
  98.7 9.7 %collective-permute-start.13 = (bf16[2,16,2688]{2,1,0:T(8,128)(2,1)S(1)}, bf16[2,16,2688]{2,1,0:T(8,128)(2,1)S(1)}, u32[]{:S(2)}, u32[]{:S(2)}) collective-permute-start(bf16[2,16,2688]{2,1,0:T(8,128)(2,1)S(1)} %pad_maximum_fusion.refs_4_), channel_id=1, source_target_pairs={{0,2},{2,0},{4,6},{6,4},{8,10},{10,8},{12,14},{14,12},{16,18},{18,... | collective-permute-start | bytes 516104 | tf_op jit(solution)/shard_map/ppermute | solution.py:557
  108.4 1.6 %collective-permute-start.25 = (bf16[2,16,2688]{2,1,0:T(8,128)(2,1)S(1)}, bf16[2,16,2688]{2,1,0:T(8,128)(2,1)S(1)}, u32[]{:S(2)}, u32[]{:S(2)}) collective-permute-start(bf16[2,16,2688]{2,1,0:T(8,128)(2,1)S(1)} %collective-permute-done.13.refs_0_), channel_id=1, source_target_pairs={{0,1},{1,0},{2,3},{3,2},{4,5},{5,4},{6,7},{7,6},{8,9},{9,8},{10,11... | collective-permute-start | bytes 516104 | tf_op jit(solution)/shard_map/ppermute | solution.py:569
  108.4 1.7 %collective-permute-start.26 = (bf16[2,16,2688]{2,1,0:T(8,128)(2,1)S(1)}, bf16[2,16,2688]{2,1,0:T(8,128)(2,1)S(1)}, u32[]{:S(2)}, u32[]{:S(2)}) collective-permute-start(bf16[2,16,2688]{2,1,0:T(8,128)(2,1)S(1)} %collective-permute-done.14.refs_1_), channel_id=1, source_target_pairs={{0,1},{1,0},{2,3},{3,2},{4,5},{5,4},{6,7},{7,6},{8,9},{9,8},{10,11... | collective-permute-start | bytes 516104 | tf_op jit(solution)/shard_map/ppermute | solution.py:569
  108.9 1.4 %collective-permute-start.27 = (bf16[2,16,2688]{2,1,0:T(8,128)(2,1)S(1)}, bf16[2,16,2688]{2,1,0:T(8,128)(2,1)S(1)}, u32[]{:S(2)}, u32[]{:S(2)}) collective-permute-start(bf16[2,16,2688]{2,1,0:T(8,128)(2,1)S(1)} %collective-permute-done.15.refs_2_), channel_id=1, source_target_pairs={{0,1},{1,0},{2,3},{3,2},{4,5},{5,4},{6,7},{7,6},{8,9},{9,8},{10,11... | collective-permute-start | bytes 516104 | tf_op jit(solution)/shard_map/ppermute | solution.py:569
  (13 other events, 469.6 us)

commit v7 on v6

--- a/solution.py
+++ b/solution.py
@@ -108,8 +108,12 @@
 def asked_column(cap, asked_ref, first):
     askers = asked_ref.shape[0]
     total = askers * cap
-    spread = jnp.where(iota((total, askers), 0) // cap == iota((total, askers), 1), 1.0, 0.0)
-    each = dot_exact(spread, asked_ref[...].astype(F32))
+    ahead = iota((total, askers), 0) - iota((total, askers), 1) * cap
+    spread = jnp.where((ahead >= 0) & (ahead < cap), 1.0, 0.0).astype(BF16)
+    asked = asked_ref[...].astype(F32)
+    high = jnp.floor(asked * (1.0 / LANES))
+    low = asked - high * LANES
+    each = dot_nn(spread, high.astype(BF16)) * LANES + dot_nn(spread, low.astype(BF16))
     pick = iota((total, LANES), 1) == iota((total, LANES), 0) % cap + first
     return jnp.sum(jnp.where(pick, each, 0.0), axis=1, keepdims=True)
 
@@ -117,7 +121,7 @@
 def serve_kernel(cap, asked_ref, table_ref, served_ref):
     rows = asked_column(cap, asked_ref, 0)
     total = rows.shape[0]
-    step = min(512, table_ref.shape[0])
+    step = min(256, table_ref.shape[0])
     lane = iota((total, step), 1).astype(F32)
     acc = None
     for base in range(0, table_ref.shape[0], step):

time: 112 us -> 112 us (level)
  transfers between devices with their start and end apart: 30 -> 30, of which waited for: 10 -> 11; matrix products, arithmetic and copies ran while one was open for 0% -> 0% of each run, Pallas kernels for 10% -> 10%
where the time goes in v7:
time: 112 us; the launch traced here: 111 us
  blocking collectives  39.3 us (35%)
  starting transfers between devices  32.7 us (29%)
  Pallas kernels  21.8 us (19%)
  waiting for transfers between devices  13.7 us (12%)
  local copies, waits for them, and re-layouts  2.29 us (2%)
  between operations  1.17 us (1%)
    ppermute x18, starting transfers between devices, xor_step(): return lax.ppermute(value, 'dp', [(i, i ^ step) for i in range(size)])  22.8 us
    all_to_all x1, blocking collectives, on_device(): lax.all_to_all(msg.reshape(devices, 1, LANES), BOTH, 0, 0, tiled=True)  14 us
    all_to_all x1, blocking collectives, on_device(): lax.all_to_all(home.reshape(replicas, piece, width), 'dp', 0, 0, tiled=True)  13 us
    all_to_all x1, blocking collectives, on_device(): lax.all_to_all(served.reshape(devices, cap, width), BOTH, 0, 0, tiled=True)  12.3 us
    ppermute x18, waiting for transfers between devices, xor_step(): return lax.ppermute(value, 'dp', [(i, i ^ step) for i in range(size)])  10.7 us
    pallas_call x1, Pallas kernels, on_device(): call(functools.partial(layer_kernel, staged), (shape_of((rows, width), BF...  4.8 us
    all_to_all x1, starting transfers between devices, send_sums(): lax.all_to_all(sums.reshape(devices, cap, width), BOTH, 0, 0, tiled=True)  4.06 us
    pallas_call x1, Pallas kernels, into_table(): call(scatter_kernel, shape_of((rows_dev, width), F32), [VMEM] * 2, 1 << 3...  3.67 us
  transfers between devices with their start and end apart: 30, of which 11 were waited for; matrix products, arithmetic and copies ran while one was open for 0% of the time, Pallas kernels for 10%

profile of v7, /device:TPU:0, one launch (start us, length us, event | category | flops | bytes accessed | tf_op | source)
XLA Modules:
  0.0 111.2 jit_solution(3032476556952485075)
XLA Ops:
  0.6 1.7 %shard_map.247 = s32[32,128]{1,0:T(8,128)} custom-call(s32[8,32]{1,0:T(8,128)} %bitcast.67, s32[1,256]{1,0:T(1,128)} %bitcast.52, s32[1,64]{1,0:T(1,128)} %len_ref.1, s32[1,64]{1,0:T(1,128)} %dest_ref.1, s32[32,128]{1,0:T(8,128)} %bitcast.50), custom_call_target="tpu_custom_call" | custom-call | flops 1048576 | bytes 131072 | tf_op jit(solution)/shard_map/pallas_call | solution.py:616
  3.0 14.0 %all_to_all.25 = s32[32,1,128]{2,1,0:T(1,128)S(1)} all-to-all(s32[32,1,128]{2,1,0:T(1,128)} %bitcast.66), channel_id=1, replica_groups=mesh['dp'=16,'table'=2] {'dp','table'}, dimensions={0} | all-to-all | bytes 32768 | tf_op jit(solution)/shard_map/all_to_all | solution.py:635
  17.0 2.2 %copy-done = bf16[4096,512]{1,0:T(8,128)(2,1)S(1)} copy-done((bf16[4096,512]{1,0:T(8,128)(2,1)S(1)}, bf16[4096,512]{1,0:T(8,128)(2,1)}, u32[]{:S(2)}) %copy-start) | copy-done | bytes 4194328
  19.2 1.4 %shard_map.248 = bf16[256,512]{1,0:T(8,128)(2,1)S(1)} custom-call(s32[32,128]{1,0:T(8,128)S(1)} %bitcast.48, bf16[4096,512]{1,0:T(8,128)(2,1)S(1)} %copy-done), custom_call_target="tpu_custom_call" | custom-call | flops 1073741824 | bytes 5242880 | tf_op jit(solution)/shard_map/pallas_call | solution.py:638
  20.6 12.3 %all_to_all.26 = bf16[32,8,512]{2,1,0:T(8,128)(2,1)S(1)} all-to-all(bf16[32,8,512]{2,1,0:T(8,128)(2,1)S(1)} %bitcast.44), channel_id=1, replica_groups=mesh['dp'=16,'table'=2] {'dp','table'}, dimensions={0} | all-to-all | bytes 524288 | tf_op jit(solution)/shard_map/all_to_all | solution.py:641
  33.2 13.0 %all_to_all.27 = bf16[16,16,512]{2,1,0:T(8,128)(2,1)S(1)} all-to-all(bf16[16,16,512]{2,1,0:T(8,128)(2,1)S(1)} %bitcast.47), channel_id=1, replica_groups=mesh['dp'=16,'table'=2] {'dp'}, dimensions={0} | all-to-all | bytes 524288 | tf_op jit(solution)/shard_map/all_to_all | solution.py:656
  46.3 4.8 %shard_map.250 = (bf16[256,512]{1,0:T(8,128)(2,1)}, bf16[256,512]{1,0:T(8,128)(2,1)S(1)}, bf16[256,512]{1,0:T(8,128)(2,1)S(1)}, bf16[256,512]{1,0:T(8,128)(2,1)S...) custom-call(bf16[256,512]{1,0:T(8,128)(2,1)S(1)} %bitcast.42, ...), custom_call_target="tpu_custom_call" | custom-call | flops 2147483648 | bytes 8388608 | tf_op jit(solution)/shard_map/pallas_call | solution.py:661
  51.1 2.8 %shard_map.251 = (bf16[256,512]{1,0:T(8,128)(2,1)}, f32[256,128]{1,0:T(8,128)S(1)}) custom-call(bf16[256,2048]{1,0:T(8,128)(2,1)S(1)} %get-tuple-element.80.dh_ref, bf16[512,2048]{1,0:T(8,128)(2,1)S(1)} %copy-done.1, bf16[256,512]{1,0:T(8,128)(2,1)S(1)} %bitcast.43, f32[1,512]{1,0:T(1,128)S(1)} %bitcast.56, bf16[256,512]{1,0:T(8,128)(2,1)S(1)} %get-tuple-element.81.go_ref, ...), custom_call_target="tpu_custom_call" | custom-call | flops 536870912 | bytes 4194304 | tf_op jit(solution)/shard_map/pallas_call | solution.py:730
  54.0 0.9 shard_map.252
  56.5 2.0 %collective-permute-start.8 = (bf16[2,16,2688]{2,1,0:T(8,128)(2,1)S(1)}, bf16[2,16,2688]{2,1,0:T(8,128)(2,1)S(1)}, u32[]{:S(2)}, u32[]{:S(2)}) collective-permute-start(bf16[2,16,2688]{2,1,0:T(8,128)(2,1)S(1)} %get-tuple-element.112), channel_id=1, source_target_pairs={{0,6},{2,4},{4,2},{6,0},{8,14},{10,12},{12,10},{14,8},{16,22},{18,... | collective-permute-start | bytes 516104 | tf_op jit(solution)/shard_map/ppermute | solution.py:561
  58.5 3.5 %all-to-all-start.3 = ((bf16[16,16,512]{2,1,0:T(8,128)(2,1)}), bf16[16,16,512]{2,1,0:T(8,128)(2,1)S(1)}, u32[]{:S(2)}, u32[]{:S(2)}) async-start(bf16[16,16,512]{2,1,0:T(8,128)(2,1)} %bitcast.16), calls=%async_computation.3 | async-start | bytes 524288 | tf_op jit(solution)/shard_map/all_to_all | solution.py:701
  62.2 1.9 %collective-permute-start.3 = (bf16[2,16,2688]{2,1,0:T(8,128)(2,1)S(1)}, bf16[2,16,2688]{2,1,0:T(8,128)(2,1)S(1)}, u32[]{:S(2)}, u32[]{:S(2)}) collective-permute-start(bf16[2,16,2688]{2,1,0:T(8,128)(2,1)S(1)} %get-tuple-element.104), channel_id=1, source_target_pairs={{0,2},{2,0},{4,6},{6,4},{8,10},{10,8},{12,14},{14,12},{16,18},{18,... | collective-permute-start | bytes 516104 | tf_op jit(solution)/shard_map/ppermute | solution.py:561
  64.1 1.5 %collective-permute-start.4 = (bf16[2,16,2688]{2,1,0:T(8,128)(2,1)S(1)}, bf16[2,16,2688]{2,1,0:T(8,128)(2,1)S(1)}, u32[]{:S(2)}, u32[]{:S(2)}) collective-permute-start(bf16[2,16,2688]{2,1,0:T(8,128)(2,1)S(1)} %get-tuple-element.105), channel_id=1, source_target_pairs={{0,4},{2,6},{4,0},{6,2},{8,12},{10,14},{12,8},{14,10},{16,20},{18,... | collective-permute-start | bytes 516104 | tf_op jit(solution)/shard_map/ppermute | solution.py:561
  66.6 2.0 %collective-permute-start.9 = (bf16[16,2688]{1,0:T(8,128)(2,1)S(1)}, bf16[16,2688]{1,0:T(8,128)(2,1)S(1)}, u32[]{:S(2)}, u32[]{:S(2)}) collective-permute-start(bf16[16,2688]{1,0:T(8,128)(2,1)S(1)} %get-tuple-element.140), channel_id=1, source_target_pairs={{0,16},{2,18},{4,20},{6,22},{8,24},{10,26},{12,28},{14,30},{16,0},... | collective-permute-start | bytes 258056 | tf_op jit(solution)/shard_map/ppermute | solution.py:561
  68.7 1.5 %collective-permute-start.10 = (bf16[16,2688]{1,0:T(8,128)(2,1)S(1)}, bf16[16,2688]{1,0:T(8,128)(2,1)S(1)}, u32[]{:S(2)}, u32[]{:S(2)}) collective-permute-start(bf16[16,2688]{1,0:T(8,128)(2,1)S(1)} %get-tuple-element.141), channel_id=1, source_target_pairs={{0,24},{2,26},{4,28},{6,30},{8,16},{10,18},{12,20},{14,22},{16,8},... | collective-permute-start | bytes 258056 | tf_op jit(solution)/shard_map/ppermute | solution.py:561
  70.1 2.0 %collective-permute-done.3 = bf16[2,16,2688]{2,1,0:T(8,128)(2,1)S(1)} collective-permute-done((bf16[2,16,2688]{2,1,0:T(8,128)(2,1)S(1)}, bf16[2,16,2688]{2,1,0:T(8,128)(2,1)S(1)}, u32[]{:S(2)}, u32[]{:S(2)}) %collective-permute-start.3) | collective-permute-done | bytes 172064 | tf_op jit(solution)/shard_map/ppermute | solution.py:561
  72.1 4.1 %collective-permute-done.4 = bf16[2,16,2688]{2,1,0:T(8,128)(2,1)S(1)} collective-permute-done((bf16[2,16,2688]{2,1,0:T(8,128)(2,1)S(1)}, bf16[2,16,2688]{2,1,0:T(8,128)(2,1)S(1)}, u32[]{:S(2)}, u32[]{:S(2)}) %collective-permute-start.4) | collective-permute-done | bytes 172064 | tf_op jit(solution)/shard_map/ppermute | solution.py:561
  76.3 1.4 %collective-permute-start.6 = (bf16[16,2688]{1,0:T(8,128)(2,1)S(1)}, bf16[16,2688]{1,0:T(8,128)(2,1)S(1)}, u32[]{:S(2)}, u32[]{:S(2)}) collective-permute-start(bf16[16,2688]{1,0:T(8,128)(2,1)S(1)} %slice_bitcast_fusion.2), channel_id=1, source_target_pairs={{0,8},{2,10},{4,12},{6,14},{8,0},{10,2},{12,4},{14,6},{16,24},{18,... | collective-permute-start | bytes 258056 | tf_op jit(solution)/shard_map/ppermute | solution.py:561
  78.7 2.2 %collective-permute-done.6 = bf16[16,2688]{1,0:T(8,128)(2,1)S(1)} collective-permute-done((bf16[16,2688]{1,0:T(8,128)(2,1)S(1)}, bf16[16,2688]{1,0:T(8,128)(2,1)S(1)}, u32[]{:S(2)}, u32[]{:S(2)}) %collective-permute-start.6) | collective-permute-done | bytes 86048 | tf_op jit(solution)/shard_map/ppermute | solution.py:561
  80.9 1.7 %collective-permute-start.16 = (bf16[16,2688]{1,0:T(8,128)(2,1)S(1)}, bf16[16,2688]{1,0:T(8,128)(2,1)S(1)}, u32[]{:S(2)}, u32[]{:S(2)}) collective-permute-start(bf16[16,2688]{1,0:T(8,128)(2,1)S(1)} %fusion.2), channel_id=1, source_target_pairs={{0,8},{2,10},{4,12},{6,14},{8,0},{10,2},{12,4},{14,6},{16,24},{18,... | collective-permute-start | bytes 258056 | tf_op jit(solution)/shard_map/ppermute | solution.py:561
  82.6 1.6 %collective-permute-start.12 = (bf16[16,2688]{1,0:T(8,128)(2,1)S(1)}, bf16[16,2688]{1,0:T(8,128)(2,1)S(1)}, u32[]{:S(2)}, u32[]{:S(2)}) collective-permute-start(bf16[16,2688]{1,0:T(8,128)(2,1)S(1)} %fusion.2), channel_id=1, source_target_pairs={{0,24},{2,26},{4,28},{6,30},{8,16},{10,18},{12,20},{14,22},{16,8},... | collective-permute-start | bytes 258056 | tf_op jit(solution)/shard_map/ppermute | solution.py:561
  84.5 1.3 %collective-permute-done.16 = bf16[16,2688]{1,0:T(8,128)(2,1)S(1)} collective-permute-done((bf16[16,2688]{1,0:T(8,128)(2,1)S(1)}, bf16[16,2688]{1,0:T(8,128)(2,1)S(1)}, u32[]{:S(2)}, u32[]{:S(2)}) %collective-permute-start.16) | collective-permute-done | bytes 86048 | tf_op jit(solution)/shard_map/ppermute | solution.py:561
  85.8 2.3 %collective-permute-start.19 = (bf16[2,16,2688]{2,1,0:T(8,128)(2,1)S(1)}, bf16[2,16,2688]{2,1,0:T(8,128)(2,1)S(1)}, u32[]{:S(2)}, u32[]{:S(2)}) collective-permute-start(bf16[2,16,2688]{2,1,0:T(8,128)(2,1)S(1)} %pad_maximum_fusion.1.refs_0_), channel_id=1, source_target_pairs={{0,6},{2,4},{4,2},{6,0},{8,14},{10,12},{12,10},{14,8},{16,22},{18,... | collective-permute-start | bytes 516104 | tf_op jit(solution)/shard_map/ppermute | solution.py:561
  88.5 1.1 collective-permute-start.17
  89.6 4.1 %all-to-all-start.4 = ((bf16[32,8,512]{2,1,0:T(8,128)(2,1)}), bf16[32,8,512]{2,1,0:T(8,128)(2,1)S(1)}, u32[]{:S(2)}, u32[]{:S(2)}) async-start(bf16[32,8,512]{2,1,0:T(8,128)(2,1)} %bitcast.26), calls=%async_computation.4 | async-start | bytes 524288 | tf_op jit(solution)/shard_map/all_to_all | solution.py:709
  95.2 2.5 %collective-permute-start.15 = (bf16[2,16,2688]{2,1,0:T(8,128)(2,1)S(1)}, bf16[2,16,2688]{2,1,0:T(8,128)(2,1)S(1)}, u32[]{:S(2)}, u32[]{:S(2)}) collective-permute-start(bf16[2,16,2688]{2,1,0:T(8,128)(2,1)S(1)} %pad_maximum_fusion.refs_4_), channel_id=1, source_target_pairs={{0,6},{2,4},{4,2},{6,0},{8,14},{10,12},{12,10},{14,8},{16,22},{18,... | collective-permute-start | bytes 516104 | tf_op jit(solution)/shard_map/ppermute | solution.py:561
  98.7 1.1 shard_map.255
  99.8 2.0 %shard_map.254 = (f32[512,2048]{1,0:T(8,128)}, f32[512,512]{1,0:T(8,128)}, f32[256,128]{1,0:T(8,128)S(1)}) custom-call(bf16[2,16,2688]{2,1,0:T(8,128)(2,1)S(1)} %pad_maximum_fusion.1.refs_0_, bf16[2,16,2688]{2,1,0:T(8,128)(2,1)S(1)} %collective-permute-done.17.refs_1_, bf16[2,16,2688]{2,1,0:T(8,128)(2,1)S(1)} %collective-permute-done.18.refs_2_, ...), custom_call_target="tpu_custom_call" | custom-call | flops 1048576 | bytes 3145728 | tf_op jit(solution)/shard_map/pallas_call | solution.py:796
  101.8 2.3 %all-to-all-done.4 = bf16[32,8,512]{2,1,0:T(8,128)(2,1)S(1)} async-done(((bf16[32,8,512]{2,1,0:T(8,128)(2,1)}), bf16[32,8,512]{2,1,0:T(8,128)(2,1)S(1)}, u32[]{:S(2)}, u32[]{:S(2)}) %all-to-all-start.4) | async-done | bytes 262176 | tf_op jit(solution)/shard_map/all_to_all | solution.py:709
  104.2 3.7 %shard_map.256 = f32[4096,512]{1,0:T(8,128)} custom-call(f32[8,256]{1,0:T(8,128)S(1)} %get-tuple-element.118.row_ref, bf16[256,512]{1,0:T(8,128)(2,1)S(1)} %bitcast.41), custom_call_target="tpu_custom_call" | custom-call | flops 1073741824 | bytes 8388608 | tf_op jit(solution)/shard_map/pallas_call | solution.py:714
  108.6 1.1 shard_map.257
  109.9 1.1 shard_map.258
  (80 shorter events, 9.0 us)
Async XLA Ops:
  2.3 43.8 %copy-start.4 = (f32[512]{0:T(512)S(1)}, f32[512]{0:T(512)}, u32[]{:S(2)}) copy-start(f32[512]{0:T(512)} %param.23) | copy-start | bytes 6148
  2.4 14.6 %collective-permute-start = (bf16[256,512]{1,0:T(8,128)(2,1)}, bf16[256,512]{1,0:T(8,128)(2,1)S(1)}, u32[]{:S(2)}, u32[]{:S(2)}) collective-permute-start(bf16[256,512]{1,0:T(8,128)(2,1)} %og_ref.1), channel_id=1, source_target_pairs={{0,1},{1,0},{2,3},{3,2},{4,5},{5,4},{6,7},{7,6},{8,9},{9,8},{10,11... | collective-permute-start | bytes 786440 | tf_op jit(solution)/shard_map/ppermute | solution.py:573
  51.1 2.9 %collective-permute-start.1 = (bf16[256,1792]{1,0:T(8,128)(2,1)S(1)}, bf16[256,1792]{1,0:T(8,128)(2,1)S(1)}, u32[]{:S(2)}, u32[]{:S(2)}) collective-permute-start(bf16[256,1792]{1,0:T(8,128)(2,1)S(1)} %get-tuple-element.87), channel_id=1, source_target_pairs={{0,1},{1,0},{2,3},{3,2},{4,5},{5,4},{6,7},{7,6},{8,9},{9,8},{10,11... | collective-permute-start | bytes 2752520 | tf_op jit(solution)/shard_map/ppermute | solution.py:573
  54.0 44.7 %copy-start.2 = (s32[4096]{0:T(1024)S(1)}, s32[4096]{0:T(1024)}, u32[]{:S(2)}) copy-start(s32[4096]{0:T(1024)} %param.22) | copy-start | bytes 49156
  55.0 7.2 %collective-permute-start.2 = (bf16[2,16,2688]{2,1,0:T(8,128)(2,1)S(1)}, bf16[2,16,2688]{2,1,0:T(8,128)(2,1)S(1)}, u32[]{:S(2)}, u32[]{:S(2)}) collective-permute-start(bf16[2,16,2688]{2,1,0:T(8,128)(2,1)S(1)} %get-tuple-element.102), channel_id=1, source_target_pairs={{0,2},{2,0},{4,6},{6,4},{8,10},{10,8},{12,14},{14,12},{16,18},{18,... | collective-permute-start | bytes 516104 | tf_op jit(solution)/shard_map/ppermute | solution.py:561
  55.8 10.7 %collective-permute-start.7 = (bf16[2,16,2688]{2,1,0:T(8,128)(2,1)S(1)}, bf16[2,16,2688]{2,1,0:T(8,128)(2,1)S(1)}, u32[]{:S(2)}, u32[]{:S(2)}) collective-permute-start(bf16[2,16,2688]{2,1,0:T(8,128)(2,1)S(1)} %get-tuple-element.111), channel_id=1, source_target_pairs={{0,4},{2,6},{4,0},{6,2},{8,12},{10,14},{12,8},{14,10},{16,20},{18,... | collective-permute-start | bytes 516104 | tf_op jit(solution)/shard_map/ppermute | solution.py:561
  56.5 10.0 %collective-permute-start.8 = (bf16[2,16,2688]{2,1,0:T(8,128)(2,1)S(1)}, bf16[2,16,2688]{2,1,0:T(8,128)(2,1)S(1)}, u32[]{:S(2)}, u32[]{:S(2)}) collective-permute-start(bf16[2,16,2688]{2,1,0:T(8,128)(2,1)S(1)} %get-tuple-element.112), channel_id=1, source_target_pairs={{0,6},{2,4},{4,2},{6,0},{8,14},{10,12},{12,10},{14,8},{16,22},{18,... | collective-permute-start | bytes 516104 | tf_op jit(solution)/shard_map/ppermute | solution.py:561
  58.5 17.8 %all-to-all-start.3 = ((bf16[16,16,512]{2,1,0:T(8,128)(2,1)}), bf16[16,16,512]{2,1,0:T(8,128)(2,1)S(1)}, u32[]{:S(2)}, u32[]{:S(2)}) async-start(bf16[16,16,512]{2,1,0:T(8,128)(2,1)} %bitcast.16), calls=%async_computation.3 | async-start | bytes 524288 | tf_op jit(solution)/shard_map/all_to_all | solution.py:701
  62.2 9.9 %collective-permute-start.3 = (bf16[2,16,2688]{2,1,0:T(8,128)(2,1)S(1)}, bf16[2,16,2688]{2,1,0:T(8,128)(2,1)S(1)}, u32[]{:S(2)}, u32[]{:S(2)}) collective-permute-start(bf16[2,16,2688]{2,1,0:T(8,128)(2,1)S(1)} %get-tuple-element.104), channel_id=1, source_target_pairs={{0,2},{2,0},{4,6},{6,4},{8,10},{10,8},{12,14},{14,12},{16,18},{18,... | collective-permute-start | bytes 516104 | tf_op jit(solution)/shard_map/ppermute | solution.py:561
  64.1 12.1 %collective-permute-start.4 = (bf16[2,16,2688]{2,1,0:T(8,128)(2,1)S(1)}, bf16[2,16,2688]{2,1,0:T(8,128)(2,1)S(1)}, u32[]{:S(2)}, u32[]{:S(2)}) collective-permute-start(bf16[2,16,2688]{2,1,0:T(8,128)(2,1)S(1)} %get-tuple-element.105), channel_id=1, source_target_pairs={{0,4},{2,6},{4,0},{6,2},{8,12},{10,14},{12,8},{14,10},{16,20},{18,... | collective-permute-start | bytes 516104 | tf_op jit(solution)/shard_map/ppermute | solution.py:561
  65.5 10.6 %collective-permute-start.5 = (bf16[2,16,2688]{2,1,0:T(8,128)(2,1)S(1)}, bf16[2,16,2688]{2,1,0:T(8,128)(2,1)S(1)}, u32[]{:S(2)}, u32[]{:S(2)}) collective-permute-start(bf16[2,16,2688]{2,1,0:T(8,128)(2,1)S(1)} %get-tuple-element.106), channel_id=1, source_target_pairs={{0,6},{2,4},{4,2},{6,0},{8,14},{10,12},{12,10},{14,8},{16,22},{18,... | collective-permute-start | bytes 516104 | tf_op jit(solution)/shard_map/ppermute | solution.py:561
  66.6 12.0 %collective-permute-start.9 = (bf16[16,2688]{1,0:T(8,128)(2,1)S(1)}, bf16[16,2688]{1,0:T(8,128)(2,1)S(1)}, u32[]{:S(2)}, u32[]{:S(2)}) collective-permute-start(bf16[16,2688]{1,0:T(8,128)(2,1)S(1)} %get-tuple-element.140), channel_id=1, source_target_pairs={{0,16},{2,18},{4,20},{6,22},{8,24},{10,26},{12,28},{14,30},{16,0},... | collective-permute-start | bytes 258056 | tf_op jit(solution)/shard_map/ppermute | solution.py:561
  68.7 10.0 %collective-permute-start.10 = (bf16[16,2688]{1,0:T(8,128)(2,1)S(1)}, bf16[16,2688]{1,0:T(8,128)(2,1)S(1)}, u32[]{:S(2)}, u32[]{:S(2)}) collective-permute-start(bf16[16,2688]{1,0:T(8,128)(2,1)S(1)} %get-tuple-element.141), channel_id=1, source_target_pairs={{0,24},{2,26},{4,28},{6,30},{8,16},{10,18},{12,20},{14,22},{16,8},... | collective-permute-start | bytes 258056 | tf_op jit(solution)/shard_map/ppermute | solution.py:561
  76.3 4.6 %collective-permute-start.6 = (bf16[16,2688]{1,0:T(8,128)(2,1)S(1)}, bf16[16,2688]{1,0:T(8,128)(2,1)S(1)}, u32[]{:S(2)}, u32[]{:S(2)}) collective-permute-start(bf16[16,2688]{1,0:T(8,128)(2,1)S(1)} %slice_bitcast_fusion.2), channel_id=1, source_target_pairs={{0,8},{2,10},{4,12},{6,14},{8,0},{10,2},{12,4},{14,6},{16,24},{18,... | collective-permute-start | bytes 258056 | tf_op jit(solution)/shard_map/ppermute | solution.py:561
  80.9 4.9 %collective-permute-start.16 = (bf16[16,2688]{1,0:T(8,128)(2,1)S(1)}, bf16[16,2688]{1,0:T(8,128)(2,1)S(1)}, u32[]{:S(2)}, u32[]{:S(2)}) collective-permute-start(bf16[16,2688]{1,0:T(8,128)(2,1)S(1)} %fusion.2), channel_id=1, source_target_pairs={{0,8},{2,10},{4,12},{6,14},{8,0},{10,2},{12,4},{14,6},{16,24},{18,... | collective-permute-start | bytes 258056 | tf_op jit(solution)/shard_map/ppermute | solution.py:561
  82.6 7.1 %collective-permute-start.12 = (bf16[16,2688]{1,0:T(8,128)(2,1)S(1)}, bf16[16,2688]{1,0:T(8,128)(2,1)S(1)}, u32[]{:S(2)}, u32[]{:S(2)}) collective-permute-start(bf16[16,2688]{1,0:T(8,128)(2,1)S(1)} %fusion.2), channel_id=1, source_target_pairs={{0,24},{2,26},{4,28},{6,30},{8,16},{10,18},{12,20},{14,22},{16,8},... | collective-permute-start | bytes 258056 | tf_op jit(solution)/shard_map/ppermute | solution.py:561
  84.2 9.5 %collective-permute-start.11 = (bf16[16,2688]{1,0:T(8,128)(2,1)S(1)}, bf16[16,2688]{1,0:T(8,128)(2,1)S(1)}, u32[]{:S(2)}, u32[]{:S(2)}) collective-permute-start(bf16[16,2688]{1,0:T(8,128)(2,1)S(1)} %fusion.2), channel_id=1, source_target_pairs={{0,16},{2,18},{4,20},{6,22},{8,24},{10,26},{12,28},{14,30},{16,0},... | collective-permute-start | bytes 258056 | tf_op jit(solution)/shard_map/ppermute | solution.py:561
  85.8 8.5 %collective-permute-start.19 = (bf16[2,16,2688]{2,1,0:T(8,128)(2,1)S(1)}, bf16[2,16,2688]{2,1,0:T(8,128)(2,1)S(1)}, u32[]{:S(2)}, u32[]{:S(2)}) collective-permute-start(bf16[2,16,2688]{2,1,0:T(8,128)(2,1)S(1)} %pad_maximum_fusion.1.refs_0_), channel_id=1, source_target_pairs={{0,6},{2,4},{4,2},{6,0},{8,14},{10,12},{12,10},{14,8},{16,22},{18,... | collective-permute-start | bytes 516104 | tf_op jit(solution)/shard_map/ppermute | solution.py:561
  88.1 6.3 %collective-permute-start.18 = (bf16[2,16,2688]{2,1,0:T(8,128)(2,1)S(1)}, bf16[2,16,2688]{2,1,0:T(8,128)(2,1)S(1)}, u32[]{:S(2)}, u32[]{:S(2)}) collective-permute-start(bf16[2,16,2688]{2,1,0:T(8,128)(2,1)S(1)} %pad_maximum_fusion.1.refs_0_), channel_id=1, source_target_pairs={{0,4},{2,6},{4,0},{6,2},{8,12},{10,14},{12,8},{14,10},{16,20},{18,... | collective-permute-start | bytes 516104 | tf_op jit(solution)/shard_map/ppermute | solution.py:561
  88.5 6.4 %collective-permute-start.17 = (bf16[2,16,2688]{2,1,0:T(8,128)(2,1)S(1)}, bf16[2,16,2688]{2,1,0:T(8,128)(2,1)S(1)}, u32[]{:S(2)}, u32[]{:S(2)}) collective-permute-start(bf16[2,16,2688]{2,1,0:T(8,128)(2,1)S(1)} %pad_maximum_fusion.1.refs_0_), channel_id=1, source_target_pairs={{0,2},{2,0},{4,6},{6,4},{8,10},{10,8},{12,14},{14,12},{16,18},{18,... | collective-permute-start | bytes 516104 | tf_op jit(solution)/shard_map/ppermute | solution.py:561
  89.6 14.6 %all-to-all-start.4 = ((bf16[32,8,512]{2,1,0:T(8,128)(2,1)}), bf16[32,8,512]{2,1,0:T(8,128)(2,1)S(1)}, u32[]{:S(2)}, u32[]{:S(2)}) async-start(bf16[32,8,512]{2,1,0:T(8,128)(2,1)} %bitcast.26), calls=%async_computation.4 | async-start | bytes 524288 | tf_op jit(solution)/shard_map/all_to_all | solution.py:709
  93.7 1.5 %collective-permute-start.24 = (bf16[2,16,2688]{2,1,0:T(8,128)(2,1)S(1)}, bf16[2,16,2688]{2,1,0:T(8,128)(2,1)S(1)}, u32[]{:S(2)}, u32[]{:S(2)}) collective-permute-start(bf16[2,16,2688]{2,1,0:T(8,128)(2,1)S(1)} %pad_maximum_fusion.refs_4_), channel_id=1, source_target_pairs={{0,1},{1,0},{2,3},{3,2},{4,5},{5,4},{6,7},{7,6},{8,9},{9,8},{10,11... | collective-permute-start | bytes 516104 | tf_op jit(solution)/shard_map/ppermute | solution.py:573
  93.9 3.8 %collective-permute-start.20 = (bf16[2,16,2688]{2,1,0:T(8,128)(2,1)S(1)}, bf16[2,16,2688]{2,1,0:T(8,128)(2,1)S(1)}, u32[]{:S(2)}, u32[]{:S(2)}) collective-permute-start(bf16[2,16,2688]{2,1,0:T(8,128)(2,1)S(1)} %pad_maximum_fusion.1.refs_0_), channel_id=1, source_target_pairs={{0,1},{1,0},{2,3},{3,2},{4,5},{5,4},{6,7},{7,6},{8,9},{9,8},{10,11... | collective-permute-start | bytes 516104 | tf_op jit(solution)/shard_map/ppermute | solution.py:573
  94.3 4.0 %collective-permute-start.23 = (bf16[2,16,2688]{2,1,0:T(8,128)(2,1)S(1)}, bf16[2,16,2688]{2,1,0:T(8,128)(2,1)S(1)}, u32[]{:S(2)}, u32[]{:S(2)}) collective-permute-start(bf16[2,16,2688]{2,1,0:T(8,128)(2,1)S(1)} %collective-permute-done.19.refs_3_), channel_id=1, source_target_pairs={{0,1},{1,0},{2,3},{3,2},{4,5},{5,4},{6,7},{7,6},{8,9},{9,8},{10,11... | collective-permute-start | bytes 516104 | tf_op jit(solution)/shard_map/ppermute | solution.py:573
  94.4 5.4 %collective-permute-start.22 = (bf16[2,16,2688]{2,1,0:T(8,128)(2,1)S(1)}, bf16[2,16,2688]{2,1,0:T(8,128)(2,1)S(1)}, u32[]{:S(2)}, u32[]{:S(2)}) collective-permute-start(bf16[2,16,2688]{2,1,0:T(8,128)(2,1)S(1)} %collective-permute-done.18.refs_2_), channel_id=1, source_target_pairs={{0,1},{1,0},{2,3},{3,2},{4,5},{5,4},{6,7},{7,6},{8,9},{9,8},{10,11... | collective-permute-start | bytes 516104 | tf_op jit(solution)/shard_map/ppermute | solution.py:573
  94.9 4.9 %collective-permute-start.21 = (bf16[2,16,2688]{2,1,0:T(8,128)(2,1)S(1)}, bf16[2,16,2688]{2,1,0:T(8,128)(2,1)S(1)}, u32[]{:S(2)}, u32[]{:S(2)}) collective-permute-start(bf16[2,16,2688]{2,1,0:T(8,128)(2,1)S(1)} %collective-permute-done.17.refs_1_), channel_id=1, source_target_pairs={{0,1},{1,0},{2,3},{3,2},{4,5},{5,4},{6,7},{7,6},{8,9},{9,8},{10,11... | collective-permute-start | bytes 516104 | tf_op jit(solution)/shard_map/ppermute | solution.py:573
  95.2 12.6 %collective-permute-start.15 = (bf16[2,16,2688]{2,1,0:T(8,128)(2,1)S(1)}, bf16[2,16,2688]{2,1,0:T(8,128)(2,1)S(1)}, u32[]{:S(2)}, u32[]{:S(2)}) collective-permute-start(bf16[2,16,2688]{2,1,0:T(8,128)(2,1)S(1)} %pad_maximum_fusion.refs_4_), channel_id=1, source_target_pairs={{0,6},{2,4},{4,2},{6,0},{8,14},{10,12},{12,10},{14,8},{16,22},{18,... | collective-permute-start | bytes 516104 | tf_op jit(solution)/shard_map/ppermute | solution.py:561
  97.7 10.3 %collective-permute-start.14 = (bf16[2,16,2688]{2,1,0:T(8,128)(2,1)S(1)}, bf16[2,16,2688]{2,1,0:T(8,128)(2,1)S(1)}, u32[]{:S(2)}, u32[]{:S(2)}) collective-permute-start(bf16[2,16,2688]{2,1,0:T(8,128)(2,1)S(1)} %pad_maximum_fusion.refs_4_), channel_id=1, source_target_pairs={{0,4},{2,6},{4,0},{6,2},{8,12},{10,14},{12,8},{14,10},{16,20},{18,... | collective-permute-start | bytes 516104 | tf_op jit(solution)/shard_map/ppermute | solution.py:561
  98.3 9.7 %collective-permute-start.13 = (bf16[2,16,2688]{2,1,0:T(8,128)(2,1)S(1)}, bf16[2,16,2688]{2,1,0:T(8,128)(2,1)S(1)}, u32[]{:S(2)}, u32[]{:S(2)}) collective-permute-start(bf16[2,16,2688]{2,1,0:T(8,128)(2,1)S(1)} %pad_maximum_fusion.refs_4_), channel_id=1, source_target_pairs={{0,2},{2,0},{4,6},{6,4},{8,10},{10,8},{12,14},{14,12},{16,18},{18,... | collective-permute-start | bytes 516104 | tf_op jit(solution)/shard_map/ppermute | solution.py:561
  108.0 1.6 %collective-permute-start.25 = (bf16[2,16,2688]{2,1,0:T(8,128)(2,1)S(1)}, bf16[2,16,2688]{2,1,0:T(8,128)(2,1)S(1)}, u32[]{:S(2)}, u32[]{:S(2)}) collective-permute-start(bf16[2,16,2688]{2,1,0:T(8,128)(2,1)S(1)} %collective-permute-done.13.refs_0_), channel_id=1, source_target_pairs={{0,1},{1,0},{2,3},{3,2},{4,5},{5,4},{6,7},{7,6},{8,9},{9,8},{10,11... | collective-permute-start | bytes 516104 | tf_op jit(solution)/shard_map/ppermute | solution.py:573
  108.0 1.7 %collective-permute-start.26 = (bf16[2,16,2688]{2,1,0:T(8,128)(2,1)S(1)}, bf16[2,16,2688]{2,1,0:T(8,128)(2,1)S(1)}, u32[]{:S(2)}, u32[]{:S(2)}) collective-permute-start(bf16[2,16,2688]{2,1,0:T(8,128)(2,1)S(1)} %collective-permute-done.14.refs_1_), channel_id=1, source_target_pairs={{0,1},{1,0},{2,3},{3,2},{4,5},{5,4},{6,7},{7,6},{8,9},{9,8},{10,11... | collective-permute-start | bytes 516104 | tf_op jit(solution)/shard_map/ppermute | solution.py:573
  108.5 1.4 %collective-permute-start.27 = (bf16[2,16,2688]{2,1,0:T(8,128)(2,1)S(1)}, bf16[2,16,2688]{2,1,0:T(8,128)(2,1)S(1)}, u32[]{:S(2)}, u32[]{:S(2)}) collective-permute-start(bf16[2,16,2688]{2,1,0:T(8,128)(2,1)S(1)} %collective-permute-done.15.refs_2_), channel_id=1, source_target_pairs={{0,1},{1,0},{2,3},{3,2},{4,5},{5,4},{6,7},{7,6},{8,9},{9,8},{10,11... | collective-permute-start | bytes 516104 | tf_op jit(solution)/shard_map/ppermute | solution.py:573
  (13 other events, 464.5 us)

commit v8 on v7

--- a/solution.py
+++ b/solution.py
@@ -420,11 +420,13 @@
     ]
     sums = []
     for g in range(heads):
-        found = jnp.zeros((rows, LANES), F32)
+        total = jnp.zeros((1, LANES), F32)
         for n, (here, index) in enumerate(tables):
-            value = prefix[g * rows : (g + 1) * rows, n * LANES : (n + 1) * LANES]
-            found = found + jnp.where(here, jnp.take_along_axis(value, index, axis=1), 0.0)
-        sums.append(jnp.sum(found, axis=0, keepdims=True))
+            lines = slice(n * LANES, rows)
+            value = prefix[g * rows + n * LANES : (g + 1) * rows, n * LANES : (n + 1) * LANES]
+            found = jnp.where(here[lines], jnp.take_along_axis(value, index[lines], axis=1), 0.0)
+            total = total + jnp.sum(found, axis=0, keepdims=True)
+        sums.append(total)
     sums = jnp.concatenate(sums, axis=0)
     out_ref[at : at + heads, :] = sums
     out_ref[at + heads : at + 2 * heads, 0 : LANES // 2] = sums[:, LANES // 2 :]

time: 112 us -> 111 us (level)
  transfers between devices with their start and end apart: 30 -> 30, of which waited for: 11 -> 10; matrix products, arithmetic and copies ran while one was open for 0% -> 0% of each run, Pallas kernels for 10% -> 10%
where the time goes in v8:
time: 111 us
  blocking collectives  39.3 us (35%)
  starting transfers between devices  32.7 us (29%)
  Pallas kernels  21.3 us (19%)
  waiting for transfers between devices  13.6 us (12%)
  local copies, waits for them, and re-layouts  2.29 us (2%)
  between operations  1.16 us (1%)
    ppermute x18, starting transfers between devices, xor_step(): return lax.ppermute(value, 'dp', [(i, i ^ step) for i in range(size)])  22.8 us
    all_to_all x1, blocking collectives, on_device(): lax.all_to_all(msg.reshape(devices, 1, LANES), BOTH, 0, 0, tiled=True)  14 us
    all_to_all x1, blocking collectives, on_device(): lax.all_to_all(home.reshape(replicas, piece, width), 'dp', 0, 0, tiled=True)  13 us
    all_to_all x1, blocking collectives, on_device(): lax.all_to_all(served.reshape(devices, cap, width), BOTH, 0, 0, tiled=True)  12.3 us
    ppermute x18, waiting for transfers between devices, xor_step(): return lax.ppermute(value, 'dp', [(i, i ^ step) for i in range(size)])  10.6 us
    pallas_call x1, Pallas kernels, on_device(): call(functools.partial(layer_kernel, staged), (shape_of((rows, width), BF...  4.8 us
    all_to_all x1, starting transfers between devices, send_sums(): lax.all_to_all(sums.reshape(devices, cap, width), BOTH, 0, 0, tiled=True)  4.09 us
    pallas_call x1, Pallas kernels, into_table(): call(scatter_kernel, shape_of((rows_dev, width), F32), [VMEM] * 2, 1 << 3...  3.67 us
  transfers between devices with their start and end apart: 30, of which 10 were waited for; matrix products, arithmetic and copies ran while one was open for 0% of the time, Pallas kernels for 10%

profile of v8, /device:TPU:0, one launch (start us, length us, event | category | flops | bytes accessed | tf_op | source)
XLA Modules:
  0.0 110.8 jit_solution(17980450558092621335)
XLA Ops:
  0.6 1.7 %shard_map.247 = s32[32,128]{1,0:T(8,128)} custom-call(s32[8,32]{1,0:T(8,128)} %bitcast.67, s32[1,256]{1,0:T(1,128)} %bitcast.52, s32[1,64]{1,0:T(1,128)} %len_ref.1, s32[1,64]{1,0:T(1,128)} %dest_ref.1, s32[32,128]{1,0:T(8,128)} %bitcast.50), custom_call_target="tpu_custom_call" | custom-call | flops 1048576 | bytes 131072 | tf_op jit(solution)/shard_map/pallas_call | solution.py:618
  3.0 14.0 %all_to_all.25 = s32[32,1,128]{2,1,0:T(1,128)S(1)} all-to-all(s32[32,1,128]{2,1,0:T(1,128)} %bitcast.66), channel_id=1, replica_groups=mesh['dp'=16,'table'=2] {'dp','table'}, dimensions={0} | all-to-all | bytes 32768 | tf_op jit(solution)/shard_map/all_to_all | solution.py:637
  17.0 2.2 %copy-done = bf16[4096,512]{1,0:T(8,128)(2,1)S(1)} copy-done((bf16[4096,512]{1,0:T(8,128)(2,1)S(1)}, bf16[4096,512]{1,0:T(8,128)(2,1)}, u32[]{:S(2)}) %copy-start) | copy-done | bytes 4194328
  19.2 1.4 %shard_map.248 = bf16[256,512]{1,0:T(8,128)(2,1)S(1)} custom-call(s32[32,128]{1,0:T(8,128)S(1)} %bitcast.48, bf16[4096,512]{1,0:T(8,128)(2,1)S(1)} %copy-done), custom_call_target="tpu_custom_call" | custom-call | flops 1073741824 | bytes 5242880 | tf_op jit(solution)/shard_map/pallas_call | solution.py:640
  20.6 12.3 %all_to_all.26 = bf16[32,8,512]{2,1,0:T(8,128)(2,1)S(1)} all-to-all(bf16[32,8,512]{2,1,0:T(8,128)(2,1)S(1)} %bitcast.44), channel_id=1, replica_groups=mesh['dp'=16,'table'=2] {'dp','table'}, dimensions={0} | all-to-all | bytes 524288 | tf_op jit(solution)/shard_map/all_to_all | solution.py:643
  33.2 13.0 %all_to_all.27 = bf16[16,16,512]{2,1,0:T(8,128)(2,1)S(1)} all-to-all(bf16[16,16,512]{2,1,0:T(8,128)(2,1)S(1)} %bitcast.47), channel_id=1, replica_groups=mesh['dp'=16,'table'=2] {'dp'}, dimensions={0} | all-to-all | bytes 524288 | tf_op jit(solution)/shard_map/all_to_all | solution.py:658
  46.3 4.8 %shard_map.250 = (bf16[256,512]{1,0:T(8,128)(2,1)}, bf16[256,512]{1,0:T(8,128)(2,1)S(1)}, bf16[256,512]{1,0:T(8,128)(2,1)S(1)}, bf16[256,512]{1,0:T(8,128)(2,1)S...) custom-call(bf16[256,512]{1,0:T(8,128)(2,1)S(1)} %bitcast.42, ...), custom_call_target="tpu_custom_call" | custom-call | flops 2147483648 | bytes 8388608 | tf_op jit(solution)/shard_map/pallas_call | solution.py:663
  51.1 2.4 %shard_map.251 = (bf16[256,512]{1,0:T(8,128)(2,1)}, f32[256,128]{1,0:T(8,128)S(1)}) custom-call(bf16[256,2048]{1,0:T(8,128)(2,1)S(1)} %get-tuple-element.80.dh_ref, bf16[512,2048]{1,0:T(8,128)(2,1)S(1)} %copy-done.1, bf16[256,512]{1,0:T(8,128)(2,1)S(1)} %bitcast.43, f32[1,512]{1,0:T(1,128)S(1)} %bitcast.56, bf16[256,512]{1,0:T(8,128)(2,1)S(1)} %get-tuple-element.81.go_ref, ...), custom_call_target="tpu_custom_call" | custom-call | flops 536870912 | bytes 4194304 | tf_op jit(solution)/shard_map/pallas_call | solution.py:732
  53.6 0.9 shard_map.252
  56.1 2.0 %collective-permute-start.8 = (bf16[2,16,2688]{2,1,0:T(8,128)(2,1)S(1)}, bf16[2,16,2688]{2,1,0:T(8,128)(2,1)S(1)}, u32[]{:S(2)}, u32[]{:S(2)}) collective-permute-start(bf16[2,16,2688]{2,1,0:T(8,128)(2,1)S(1)} %get-tuple-element.112), channel_id=1, source_target_pairs={{0,6},{2,4},{4,2},{6,0},{8,14},{10,12},{12,10},{14,8},{16,22},{18,... | collective-permute-start | bytes 516104 | tf_op jit(solution)/shard_map/ppermute | solution.py:563
  58.1 3.5 %all-to-all-start.3 = ((bf16[16,16,512]{2,1,0:T(8,128)(2,1)}), bf16[16,16,512]{2,1,0:T(8,128)(2,1)S(1)}, u32[]{:S(2)}, u32[]{:S(2)}) async-start(bf16[16,16,512]{2,1,0:T(8,128)(2,1)} %bitcast.16), calls=%async_computation.3 | async-start | bytes 524288 | tf_op jit(solution)/shard_map/all_to_all | solution.py:703
  61.8 1.9 %collective-permute-start.3 = (bf16[2,16,2688]{2,1,0:T(8,128)(2,1)S(1)}, bf16[2,16,2688]{2,1,0:T(8,128)(2,1)S(1)}, u32[]{:S(2)}, u32[]{:S(2)}) collective-permute-start(bf16[2,16,2688]{2,1,0:T(8,128)(2,1)S(1)} %get-tuple-element.104), channel_id=1, source_target_pairs={{0,2},{2,0},{4,6},{6,4},{8,10},{10,8},{12,14},{14,12},{16,18},{18,... | collective-permute-start | bytes 516104 | tf_op jit(solution)/shard_map/ppermute | solution.py:563
  63.7 1.5 %collective-permute-start.4 = (bf16[2,16,2688]{2,1,0:T(8,128)(2,1)S(1)}, bf16[2,16,2688]{2,1,0:T(8,128)(2,1)S(1)}, u32[]{:S(2)}, u32[]{:S(2)}) collective-permute-start(bf16[2,16,2688]{2,1,0:T(8,128)(2,1)S(1)} %get-tuple-element.105), channel_id=1, source_target_pairs={{0,4},{2,6},{4,0},{6,2},{8,12},{10,14},{12,8},{14,10},{16,20},{18,... | collective-permute-start | bytes 516104 | tf_op jit(solution)/shard_map/ppermute | solution.py:563
  66.2 2.0 %collective-permute-start.9 = (bf16[16,2688]{1,0:T(8,128)(2,1)S(1)}, bf16[16,2688]{1,0:T(8,128)(2,1)S(1)}, u32[]{:S(2)}, u32[]{:S(2)}) collective-permute-start(bf16[16,2688]{1,0:T(8,128)(2,1)S(1)} %get-tuple-element.140), channel_id=1, source_target_pairs={{0,16},{2,18},{4,20},{6,22},{8,24},{10,26},{12,28},{14,30},{16,0},... | collective-permute-start | bytes 258056 | tf_op jit(solution)/shard_map/ppermute | solution.py:563
  68.2 1.5 %collective-permute-start.10 = (bf16[16,2688]{1,0:T(8,128)(2,1)S(1)}, bf16[16,2688]{1,0:T(8,128)(2,1)S(1)}, u32[]{:S(2)}, u32[]{:S(2)}) collective-permute-start(bf16[16,2688]{1,0:T(8,128)(2,1)S(1)} %get-tuple-element.141), channel_id=1, source_target_pairs={{0,24},{2,26},{4,28},{6,30},{8,16},{10,18},{12,20},{14,22},{16,8},... | collective-permute-start | bytes 258056 | tf_op jit(solution)/shard_map/ppermute | solution.py:563
  69.7 2.0 %collective-permute-done.3 = bf16[2,16,2688]{2,1,0:T(8,128)(2,1)S(1)} collective-permute-done((bf16[2,16,2688]{2,1,0:T(8,128)(2,1)S(1)}, bf16[2,16,2688]{2,1,0:T(8,128)(2,1)S(1)}, u32[]{:S(2)}, u32[]{:S(2)}) %collective-permute-start.3) | collective-permute-done | bytes 172064 | tf_op jit(solution)/shard_map/ppermute | solution.py:563
  71.7 4.1 %collective-permute-done.4 = bf16[2,16,2688]{2,1,0:T(8,128)(2,1)S(1)} collective-permute-done((bf16[2,16,2688]{2,1,0:T(8,128)(2,1)S(1)}, bf16[2,16,2688]{2,1,0:T(8,128)(2,1)S(1)}, u32[]{:S(2)}, u32[]{:S(2)}) %collective-permute-start.4) | collective-permute-done | bytes 172064 | tf_op jit(solution)/shard_map/ppermute | solution.py:563
  75.9 1.4 %collective-permute-start.6 = (bf16[16,2688]{1,0:T(8,128)(2,1)S(1)}, bf16[16,2688]{1,0:T(8,128)(2,1)S(1)}, u32[]{:S(2)}, u32[]{:S(2)}) collective-permute-start(bf16[16,2688]{1,0:T(8,128)(2,1)S(1)} %slice_bitcast_fusion.2), channel_id=1, source_target_pairs={{0,8},{2,10},{4,12},{6,14},{8,0},{10,2},{12,4},{14,6},{16,24},{18,... | collective-permute-start | bytes 258056 | tf_op jit(solution)/shard_map/ppermute | solution.py:563
  78.2 2.2 %collective-permute-done.6 = bf16[16,2688]{1,0:T(8,128)(2,1)S(1)} collective-permute-done((bf16[16,2688]{1,0:T(8,128)(2,1)S(1)}, bf16[16,2688]{1,0:T(8,128)(2,1)S(1)}, u32[]{:S(2)}, u32[]{:S(2)}) %collective-permute-start.6) | collective-permute-done | bytes 86048 | tf_op jit(solution)/shard_map/ppermute | solution.py:563
  80.5 1.7 %collective-permute-start.16 = (bf16[16,2688]{1,0:T(8,128)(2,1)S(1)}, bf16[16,2688]{1,0:T(8,128)(2,1)S(1)}, u32[]{:S(2)}, u32[]{:S(2)}) collective-permute-start(bf16[16,2688]{1,0:T(8,128)(2,1)S(1)} %fusion.2), channel_id=1, source_target_pairs={{0,8},{2,10},{4,12},{6,14},{8,0},{10,2},{12,4},{14,6},{16,24},{18,... | collective-permute-start | bytes 258056 | tf_op jit(solution)/shard_map/ppermute | solution.py:563
  82.2 1.6 %collective-permute-start.12 = (bf16[16,2688]{1,0:T(8,128)(2,1)S(1)}, bf16[16,2688]{1,0:T(8,128)(2,1)S(1)}, u32[]{:S(2)}, u32[]{:S(2)}) collective-permute-start(bf16[16,2688]{1,0:T(8,128)(2,1)S(1)} %fusion.2), channel_id=1, source_target_pairs={{0,24},{2,26},{4,28},{6,30},{8,16},{10,18},{12,20},{14,22},{16,8},... | collective-permute-start | bytes 258056 | tf_op jit(solution)/shard_map/ppermute | solution.py:563
  84.0 1.3 %collective-permute-done.16 = bf16[16,2688]{1,0:T(8,128)(2,1)S(1)} collective-permute-done((bf16[16,2688]{1,0:T(8,128)(2,1)S(1)}, bf16[16,2688]{1,0:T(8,128)(2,1)S(1)}, u32[]{:S(2)}, u32[]{:S(2)}) %collective-permute-start.16) | collective-permute-done | bytes 86048 | tf_op jit(solution)/shard_map/ppermute | solution.py:563
  85.3 2.3 %collective-permute-start.19 = (bf16[2,16,2688]{2,1,0:T(8,128)(2,1)S(1)}, bf16[2,16,2688]{2,1,0:T(8,128)(2,1)S(1)}, u32[]{:S(2)}, u32[]{:S(2)}) collective-permute-start(bf16[2,16,2688]{2,1,0:T(8,128)(2,1)S(1)} %pad_maximum_fusion.1.refs_0_), channel_id=1, source_target_pairs={{0,6},{2,4},{4,2},{6,0},{8,14},{10,12},{12,10},{14,8},{16,22},{18,... | collective-permute-start | bytes 516104 | tf_op jit(solution)/shard_map/ppermute | solution.py:563
  88.1 1.1 collective-permute-start.17
  89.2 4.1 %all-to-all-start.4 = ((bf16[32,8,512]{2,1,0:T(8,128)(2,1)}), bf16[32,8,512]{2,1,0:T(8,128)(2,1)S(1)}, u32[]{:S(2)}, u32[]{:S(2)}) async-start(bf16[32,8,512]{2,1,0:T(8,128)(2,1)} %bitcast.26), calls=%async_computation.4 | async-start | bytes 524288 | tf_op jit(solution)/shard_map/all_to_all | solution.py:711
  94.8 2.5 %collective-permute-start.15 = (bf16[2,16,2688]{2,1,0:T(8,128)(2,1)S(1)}, bf16[2,16,2688]{2,1,0:T(8,128)(2,1)S(1)}, u32[]{:S(2)}, u32[]{:S(2)}) collective-permute-start(bf16[2,16,2688]{2,1,0:T(8,128)(2,1)S(1)} %pad_maximum_fusion.refs_4_), channel_id=1, source_target_pairs={{0,6},{2,4},{4,2},{6,0},{8,14},{10,12},{12,10},{14,8},{16,22},{18,... | collective-permute-start | bytes 516104 | tf_op jit(solution)/shard_map/ppermute | solution.py:563
  98.3 1.1 shard_map.255
  99.3 2.0 %shard_map.254 = (f32[512,2048]{1,0:T(8,128)}, f32[512,512]{1,0:T(8,128)}, f32[256,128]{1,0:T(8,128)S(1)}) custom-call(bf16[2,16,2688]{2,1,0:T(8,128)(2,1)S(1)} %pad_maximum_fusion.1.refs_0_, bf16[2,16,2688]{2,1,0:T(8,128)(2,1)S(1)} %collective-permute-done.17.refs_1_, bf16[2,16,2688]{2,1,0:T(8,128)(2,1)S(1)} %collective-permute-done.18.refs_2_, ...), custom_call_target="tpu_custom_call" | custom-call | flops 1048576 | bytes 3145728 | tf_op jit(solution)/shard_map/pallas_call | solution.py:798
  101.4 2.3 %all-to-all-done.4 = bf16[32,8,512]{2,1,0:T(8,128)(2,1)S(1)} async-done(((bf16[32,8,512]{2,1,0:T(8,128)(2,1)}), bf16[32,8,512]{2,1,0:T(8,128)(2,1)S(1)}, u32[]{:S(2)}, u32[]{:S(2)}) %all-to-all-start.4) | async-done | bytes 262176 | tf_op jit(solution)/shard_map/all_to_all | solution.py:711
  103.7 3.7 %shard_map.256 = f32[4096,512]{1,0:T(8,128)} custom-call(f32[8,256]{1,0:T(8,128)S(1)} %get-tuple-element.118.row_ref, bf16[256,512]{1,0:T(8,128)(2,1)S(1)} %bitcast.41), custom_call_target="tpu_custom_call" | custom-call | flops 1073741824 | bytes 8388608 | tf_op jit(solution)/shard_map/pallas_call | solution.py:716
  108.1 1.1 shard_map.257
  109.5 1.1 %shard_map.258 = (f32[512,2048]{1,0:T(8,128)}, f32[512,512]{1,0:T(8,128)}, f32[1,2048]{1,0:T(1,128)}, f32[1,512]{1,0:T(1,128)}, f32[1,512]{1,0:T(1,128)}, /*inde...) custom-call(bf16[2,16,2688]{2,1,0:T(8,128)(2,1)S(1)} %collective-permute-done.2, ...), custom_call_target="tpu_custom_call", output_to_operand_aliasing={{0}: (3, {}), {1}: (4, {})} | custom-call | flops 1048576 | bytes 3145728 | tf_op jit(solution)/shard_map/pallas_call | solution.py:807
  (80 shorter events, 9.0 us)
Async XLA Ops:
  2.3 43.8 %copy-start.4 = (f32[512]{0:T(512)S(1)}, f32[512]{0:T(512)}, u32[]{:S(2)}) copy-start(f32[512]{0:T(512)} %param.23) | copy-start | bytes 6148
  2.4 14.6 %collective-permute-start = (bf16[256,512]{1,0:T(8,128)(2,1)}, bf16[256,512]{1,0:T(8,128)(2,1)S(1)}, u32[]{:S(2)}, u32[]{:S(2)}) collective-permute-start(bf16[256,512]{1,0:T(8,128)(2,1)} %og_ref.1), channel_id=1, source_target_pairs={{0,1},{1,0},{2,3},{3,2},{4,5},{5,4},{6,7},{7,6},{8,9},{9,8},{10,11... | collective-permute-start | bytes 786440 | tf_op jit(solution)/shard_map/ppermute | solution.py:575
  51.1 2.5 %collective-permute-start.1 = (bf16[256,1792]{1,0:T(8,128)(2,1)S(1)}, bf16[256,1792]{1,0:T(8,128)(2,1)S(1)}, u32[]{:S(2)}, u32[]{:S(2)}) collective-permute-start(bf16[256,1792]{1,0:T(8,128)(2,1)S(1)} %get-tuple-element.87), channel_id=1, source_target_pairs={{0,1},{1,0},{2,3},{3,2},{4,5},{5,4},{6,7},{7,6},{8,9},{9,8},{10,11... | collective-permute-start | bytes 2752520 | tf_op jit(solution)/shard_map/ppermute | solution.py:575
  53.6 44.7 %copy-start.2 = (s32[4096]{0:T(1024)S(1)}, s32[4096]{0:T(1024)}, u32[]{:S(2)}) copy-start(s32[4096]{0:T(1024)} %param.22) | copy-start | bytes 49156
  54.6 7.2 %collective-permute-start.2 = (bf16[2,16,2688]{2,1,0:T(8,128)(2,1)S(1)}, bf16[2,16,2688]{2,1,0:T(8,128)(2,1)S(1)}, u32[]{:S(2)}, u32[]{:S(2)}) collective-permute-start(bf16[2,16,2688]{2,1,0:T(8,128)(2,1)S(1)} %get-tuple-element.102), channel_id=1, source_target_pairs={{0,2},{2,0},{4,6},{6,4},{8,10},{10,8},{12,14},{14,12},{16,18},{18,... | collective-permute-start | bytes 516104 | tf_op jit(solution)/shard_map/ppermute | solution.py:563
  55.4 10.7 %collective-permute-start.7 = (bf16[2,16,2688]{2,1,0:T(8,128)(2,1)S(1)}, bf16[2,16,2688]{2,1,0:T(8,128)(2,1)S(1)}, u32[]{:S(2)}, u32[]{:S(2)}) collective-permute-start(bf16[2,16,2688]{2,1,0:T(8,128)(2,1)S(1)} %get-tuple-element.111), channel_id=1, source_target_pairs={{0,4},{2,6},{4,0},{6,2},{8,12},{10,14},{12,8},{14,10},{16,20},{18,... | collective-permute-start | bytes 516104 | tf_op jit(solution)/shard_map/ppermute | solution.py:563
  56.1 10.0 %collective-permute-start.8 = (bf16[2,16,2688]{2,1,0:T(8,128)(2,1)S(1)}, bf16[2,16,2688]{2,1,0:T(8,128)(2,1)S(1)}, u32[]{:S(2)}, u32[]{:S(2)}) collective-permute-start(bf16[2,16,2688]{2,1,0:T(8,128)(2,1)S(1)} %get-tuple-element.112), channel_id=1, source_target_pairs={{0,6},{2,4},{4,2},{6,0},{8,14},{10,12},{12,10},{14,8},{16,22},{18,... | collective-permute-start | bytes 516104 | tf_op jit(solution)/shard_map/ppermute | solution.py:563
  58.1 17.7 %all-to-all-start.3 = ((bf16[16,16,512]{2,1,0:T(8,128)(2,1)}), bf16[16,16,512]{2,1,0:T(8,128)(2,1)S(1)}, u32[]{:S(2)}, u32[]{:S(2)}) async-start(bf16[16,16,512]{2,1,0:T(8,128)(2,1)} %bitcast.16), calls=%async_computation.3 | async-start | bytes 524288 | tf_op jit(solution)/shard_map/all_to_all | solution.py:703
  61.8 9.9 %collective-permute-start.3 = (bf16[2,16,2688]{2,1,0:T(8,128)(2,1)S(1)}, bf16[2,16,2688]{2,1,0:T(8,128)(2,1)S(1)}, u32[]{:S(2)}, u32[]{:S(2)}) collective-permute-start(bf16[2,16,2688]{2,1,0:T(8,128)(2,1)S(1)} %get-tuple-element.104), channel_id=1, source_target_pairs={{0,2},{2,0},{4,6},{6,4},{8,10},{10,8},{12,14},{14,12},{16,18},{18,... | collective-permute-start | bytes 516104 | tf_op jit(solution)/shard_map/ppermute | solution.py:563
  63.7 12.1 %collective-permute-start.4 = (bf16[2,16,2688]{2,1,0:T(8,128)(2,1)S(1)}, bf16[2,16,2688]{2,1,0:T(8,128)(2,1)S(1)}, u32[]{:S(2)}, u32[]{:S(2)}) collective-permute-start(bf16[2,16,2688]{2,1,0:T(8,128)(2,1)S(1)} %get-tuple-element.105), channel_id=1, source_target_pairs={{0,4},{2,6},{4,0},{6,2},{8,12},{10,14},{12,8},{14,10},{16,20},{18,... | collective-permute-start | bytes 516104 | tf_op jit(solution)/shard_map/ppermute | solution.py:563
  65.1 10.6 %collective-permute-start.5 = (bf16[2,16,2688]{2,1,0:T(8,128)(2,1)S(1)}, bf16[2,16,2688]{2,1,0:T(8,128)(2,1)S(1)}, u32[]{:S(2)}, u32[]{:S(2)}) collective-permute-start(bf16[2,16,2688]{2,1,0:T(8,128)(2,1)S(1)} %get-tuple-element.106), channel_id=1, source_target_pairs={{0,6},{2,4},{4,2},{6,0},{8,14},{10,12},{12,10},{14,8},{16,22},{18,... | collective-permute-start | bytes 516104 | tf_op jit(solution)/shard_map/ppermute | solution.py:563
  66.2 12.0 %collective-permute-start.9 = (bf16[16,2688]{1,0:T(8,128)(2,1)S(1)}, bf16[16,2688]{1,0:T(8,128)(2,1)S(1)}, u32[]{:S(2)}, u32[]{:S(2)}) collective-permute-start(bf16[16,2688]{1,0:T(8,128)(2,1)S(1)} %get-tuple-element.140), channel_id=1, source_target_pairs={{0,16},{2,18},{4,20},{6,22},{8,24},{10,26},{12,28},{14,30},{16,0},... | collective-permute-start | bytes 258056 | tf_op jit(solution)/shard_map/ppermute | solution.py:563
  68.2 10.0 %collective-permute-start.10 = (bf16[16,2688]{1,0:T(8,128)(2,1)S(1)}, bf16[16,2688]{1,0:T(8,128)(2,1)S(1)}, u32[]{:S(2)}, u32[]{:S(2)}) collective-permute-start(bf16[16,2688]{1,0:T(8,128)(2,1)S(1)} %get-tuple-element.141), channel_id=1, source_target_pairs={{0,24},{2,26},{4,28},{6,30},{8,16},{10,18},{12,20},{14,22},{16,8},... | collective-permute-start | bytes 258056 | tf_op jit(solution)/shard_map/ppermute | solution.py:563
  75.9 4.6 %collective-permute-start.6 = (bf16[16,2688]{1,0:T(8,128)(2,1)S(1)}, bf16[16,2688]{1,0:T(8,128)(2,1)S(1)}, u32[]{:S(2)}, u32[]{:S(2)}) collective-permute-start(bf16[16,2688]{1,0:T(8,128)(2,1)S(1)} %slice_bitcast_fusion.2), channel_id=1, source_target_pairs={{0,8},{2,10},{4,12},{6,14},{8,0},{10,2},{12,4},{14,6},{16,24},{18,... | collective-permute-start | bytes 258056 | tf_op jit(solution)/shard_map/ppermute | solution.py:563
  80.5 4.9 %collective-permute-start.16 = (bf16[16,2688]{1,0:T(8,128)(2,1)S(1)}, bf16[16,2688]{1,0:T(8,128)(2,1)S(1)}, u32[]{:S(2)}, u32[]{:S(2)}) collective-permute-start(bf16[16,2688]{1,0:T(8,128)(2,1)S(1)} %fusion.2), channel_id=1, source_target_pairs={{0,8},{2,10},{4,12},{6,14},{8,0},{10,2},{12,4},{14,6},{16,24},{18,... | collective-permute-start | bytes 258056 | tf_op jit(solution)/shard_map/ppermute | solution.py:563
  82.2 7.0 %collective-permute-start.12 = (bf16[16,2688]{1,0:T(8,128)(2,1)S(1)}, bf16[16,2688]{1,0:T(8,128)(2,1)S(1)}, u32[]{:S(2)}, u32[]{:S(2)}) collective-permute-start(bf16[16,2688]{1,0:T(8,128)(2,1)S(1)} %fusion.2), channel_id=1, source_target_pairs={{0,24},{2,26},{4,28},{6,30},{8,16},{10,18},{12,20},{14,22},{16,8},... | collective-permute-start | bytes 258056 | tf_op jit(solution)/shard_map/ppermute | solution.py:563
  83.7 9.5 %collective-permute-start.11 = (bf16[16,2688]{1,0:T(8,128)(2,1)S(1)}, bf16[16,2688]{1,0:T(8,128)(2,1)S(1)}, u32[]{:S(2)}, u32[]{:S(2)}) collective-permute-start(bf16[16,2688]{1,0:T(8,128)(2,1)S(1)} %fusion.2), channel_id=1, source_target_pairs={{0,16},{2,18},{4,20},{6,22},{8,24},{10,26},{12,28},{14,30},{16,0},... | collective-permute-start | bytes 258056 | tf_op jit(solution)/shard_map/ppermute | solution.py:563
  85.3 8.5 %collective-permute-start.19 = (bf16[2,16,2688]{2,1,0:T(8,128)(2,1)S(1)}, bf16[2,16,2688]{2,1,0:T(8,128)(2,1)S(1)}, u32[]{:S(2)}, u32[]{:S(2)}) collective-permute-start(bf16[2,16,2688]{2,1,0:T(8,128)(2,1)S(1)} %pad_maximum_fusion.1.refs_0_), channel_id=1, source_target_pairs={{0,6},{2,4},{4,2},{6,0},{8,14},{10,12},{12,10},{14,8},{16,22},{18,... | collective-permute-start | bytes 516104 | tf_op jit(solution)/shard_map/ppermute | solution.py:563
  87.7 6.3 %collective-permute-start.18 = (bf16[2,16,2688]{2,1,0:T(8,128)(2,1)S(1)}, bf16[2,16,2688]{2,1,0:T(8,128)(2,1)S(1)}, u32[]{:S(2)}, u32[]{:S(2)}) collective-permute-start(bf16[2,16,2688]{2,1,0:T(8,128)(2,1)S(1)} %pad_maximum_fusion.1.refs_0_), channel_id=1, source_target_pairs={{0,4},{2,6},{4,0},{6,2},{8,12},{10,14},{12,8},{14,10},{16,20},{18,... | collective-permute-start | bytes 516104 | tf_op jit(solution)/shard_map/ppermute | solution.py:563
  88.1 6.3 %collective-permute-start.17 = (bf16[2,16,2688]{2,1,0:T(8,128)(2,1)S(1)}, bf16[2,16,2688]{2,1,0:T(8,128)(2,1)S(1)}, u32[]{:S(2)}, u32[]{:S(2)}) collective-permute-start(bf16[2,16,2688]{2,1,0:T(8,128)(2,1)S(1)} %pad_maximum_fusion.1.refs_0_), channel_id=1, source_target_pairs={{0,2},{2,0},{4,6},{6,4},{8,10},{10,8},{12,14},{14,12},{16,18},{18,... | collective-permute-start | bytes 516104 | tf_op jit(solution)/shard_map/ppermute | solution.py:563
  89.2 14.6 %all-to-all-start.4 = ((bf16[32,8,512]{2,1,0:T(8,128)(2,1)}), bf16[32,8,512]{2,1,0:T(8,128)(2,1)S(1)}, u32[]{:S(2)}, u32[]{:S(2)}) async-start(bf16[32,8,512]{2,1,0:T(8,128)(2,1)} %bitcast.26), calls=%async_computation.4 | async-start | bytes 524288 | tf_op jit(solution)/shard_map/all_to_all | solution.py:711
  93.3 1.5 %collective-permute-start.24 = (bf16[2,16,2688]{2,1,0:T(8,128)(2,1)S(1)}, bf16[2,16,2688]{2,1,0:T(8,128)(2,1)S(1)}, u32[]{:S(2)}, u32[]{:S(2)}) collective-permute-start(bf16[2,16,2688]{2,1,0:T(8,128)(2,1)S(1)} %pad_maximum_fusion.refs_4_), channel_id=1, source_target_pairs={{0,1},{1,0},{2,3},{3,2},{4,5},{5,4},{6,7},{7,6},{8,9},{9,8},{10,11... | collective-permute-start | bytes 516104 | tf_op jit(solution)/shard_map/ppermute | solution.py:575
  93.4 3.8 %collective-permute-start.20 = (bf16[2,16,2688]{2,1,0:T(8,128)(2,1)S(1)}, bf16[2,16,2688]{2,1,0:T(8,128)(2,1)S(1)}, u32[]{:S(2)}, u32[]{:S(2)}) collective-permute-start(bf16[2,16,2688]{2,1,0:T(8,128)(2,1)S(1)} %pad_maximum_fusion.1.refs_0_), channel_id=1, source_target_pairs={{0,1},{1,0},{2,3},{3,2},{4,5},{5,4},{6,7},{7,6},{8,9},{9,8},{10,11... | collective-permute-start | bytes 516104 | tf_op jit(solution)/shard_map/ppermute | solution.py:575
  93.9 4.0 %collective-permute-start.23 = (bf16[2,16,2688]{2,1,0:T(8,128)(2,1)S(1)}, bf16[2,16,2688]{2,1,0:T(8,128)(2,1)S(1)}, u32[]{:S(2)}, u32[]{:S(2)}) collective-permute-start(bf16[2,16,2688]{2,1,0:T(8,128)(2,1)S(1)} %collective-permute-done.19.refs_3_), channel_id=1, source_target_pairs={{0,1},{1,0},{2,3},{3,2},{4,5},{5,4},{6,7},{7,6},{8,9},{9,8},{10,11... | collective-permute-start | bytes 516104 | tf_op jit(solution)/shard_map/ppermute | solution.py:575
  94.0 5.4 %collective-permute-start.22 = (bf16[2,16,2688]{2,1,0:T(8,128)(2,1)S(1)}, bf16[2,16,2688]{2,1,0:T(8,128)(2,1)S(1)}, u32[]{:S(2)}, u32[]{:S(2)}) collective-permute-start(bf16[2,16,2688]{2,1,0:T(8,128)(2,1)S(1)} %collective-permute-done.18.refs_2_), channel_id=1, source_target_pairs={{0,1},{1,0},{2,3},{3,2},{4,5},{5,4},{6,7},{7,6},{8,9},{9,8},{10,11... | collective-permute-start | bytes 516104 | tf_op jit(solution)/shard_map/ppermute | solution.py:575
  94.4 4.9 %collective-permute-start.21 = (bf16[2,16,2688]{2,1,0:T(8,128)(2,1)S(1)}, bf16[2,16,2688]{2,1,0:T(8,128)(2,1)S(1)}, u32[]{:S(2)}, u32[]{:S(2)}) collective-permute-start(bf16[2,16,2688]{2,1,0:T(8,128)(2,1)S(1)} %collective-permute-done.17.refs_1_), channel_id=1, source_target_pairs={{0,1},{1,0},{2,3},{3,2},{4,5},{5,4},{6,7},{7,6},{8,9},{9,8},{10,11... | collective-permute-start | bytes 516104 | tf_op jit(solution)/shard_map/ppermute | solution.py:575
  94.8 12.6 %collective-permute-start.15 = (bf16[2,16,2688]{2,1,0:T(8,128)(2,1)S(1)}, bf16[2,16,2688]{2,1,0:T(8,128)(2,1)S(1)}, u32[]{:S(2)}, u32[]{:S(2)}) collective-permute-start(bf16[2,16,2688]{2,1,0:T(8,128)(2,1)S(1)} %pad_maximum_fusion.refs_4_), channel_id=1, source_target_pairs={{0,6},{2,4},{4,2},{6,0},{8,14},{10,12},{12,10},{14,8},{16,22},{18,... | collective-permute-start | bytes 516104 | tf_op jit(solution)/shard_map/ppermute | solution.py:563
  97.3 10.3 %collective-permute-start.14 = (bf16[2,16,2688]{2,1,0:T(8,128)(2,1)S(1)}, bf16[2,16,2688]{2,1,0:T(8,128)(2,1)S(1)}, u32[]{:S(2)}, u32[]{:S(2)}) collective-permute-start(bf16[2,16,2688]{2,1,0:T(8,128)(2,1)S(1)} %pad_maximum_fusion.refs_4_), channel_id=1, source_target_pairs={{0,4},{2,6},{4,0},{6,2},{8,12},{10,14},{12,8},{14,10},{16,20},{18,... | collective-permute-start | bytes 516104 | tf_op jit(solution)/shard_map/ppermute | solution.py:563
  97.8 9.7 %collective-permute-start.13 = (bf16[2,16,2688]{2,1,0:T(8,128)(2,1)S(1)}, bf16[2,16,2688]{2,1,0:T(8,128)(2,1)S(1)}, u32[]{:S(2)}, u32[]{:S(2)}) collective-permute-start(bf16[2,16,2688]{2,1,0:T(8,128)(2,1)S(1)} %pad_maximum_fusion.refs_4_), channel_id=1, source_target_pairs={{0,2},{2,0},{4,6},{6,4},{8,10},{10,8},{12,14},{14,12},{16,18},{18,... | collective-permute-start | bytes 516104 | tf_op jit(solution)/shard_map/ppermute | solution.py:563
  107.6 1.6 %collective-permute-start.25 = (bf16[2,16,2688]{2,1,0:T(8,128)(2,1)S(1)}, bf16[2,16,2688]{2,1,0:T(8,128)(2,1)S(1)}, u32[]{:S(2)}, u32[]{:S(2)}) collective-permute-start(bf16[2,16,2688]{2,1,0:T(8,128)(2,1)S(1)} %collective-permute-done.13.refs_0_), channel_id=1, source_target_pairs={{0,1},{1,0},{2,3},{3,2},{4,5},{5,4},{6,7},{7,6},{8,9},{9,8},{10,11... | collective-permute-start | bytes 516104 | tf_op jit(solution)/shard_map/ppermute | solution.py:575
  107.6 1.7 %collective-permute-start.26 = (bf16[2,16,2688]{2,1,0:T(8,128)(2,1)S(1)}, bf16[2,16,2688]{2,1,0:T(8,128)(2,1)S(1)}, u32[]{:S(2)}, u32[]{:S(2)}) collective-permute-start(bf16[2,16,2688]{2,1,0:T(8,128)(2,1)S(1)} %collective-permute-done.14.refs_1_), channel_id=1, source_target_pairs={{0,1},{1,0},{2,3},{3,2},{4,5},{5,4},{6,7},{7,6},{8,9},{9,8},{10,11... | collective-permute-start | bytes 516104 | tf_op jit(solution)/shard_map/ppermute | solution.py:575
  108.1 1.4 %collective-permute-start.27 = (bf16[2,16,2688]{2,1,0:T(8,128)(2,1)S(1)}, bf16[2,16,2688]{2,1,0:T(8,128)(2,1)S(1)}, u32[]{:S(2)}, u32[]{:S(2)}) collective-permute-start(bf16[2,16,2688]{2,1,0:T(8,128)(2,1)S(1)} %collective-permute-done.15.refs_2_), channel_id=1, source_target_pairs={{0,1},{1,0},{2,3},{3,2},{4,5},{5,4},{6,7},{7,6},{8,9},{9,8},{10,11... | collective-permute-start | bytes 516104 | tf_op jit(solution)/shard_map/ppermute | solution.py:575
  (13 other events, 464.5 us)

commit v9 on v8

--- a/solution.py
+++ b/solution.py
@@ -455,8 +455,8 @@
         axis=0,
     )
     go = jnp.concatenate([go_ref[...], got_grad_ref[...]], axis=0)
-    uv_ref[...] = dot_tn(n1, dh)
-    wo_ref[...] = dot_tn(y, go)
+    uv_ref[...] = dot_tn(n1, dh).astype(BF16)
+    wo_ref[...] = dot_tn(y, go).astype(BF16)
     short = half_y // (planes * columns)
     for rel_xy in range(columns):
         for rel_z in range(planes):
@@ -464,9 +464,9 @@
             out = (nears, fars)[rel_z // 2][rel_xy].at[rel_z % 2]
             for part in range(2):
                 at = pl.multiple_of((2 * chunk + part) * short, short)
-                out[:, part * half_cols : (part + 1) * half_cols] = uv_ref[pl.ds(at, short), :].astype(BF16)
+                out[:, part * half_cols : (part + 1) * half_cols] = uv_ref[pl.ds(at, short), :]
             at = pl.multiple_of(chunk * short, short)
-            out[:, 2 * half_cols : 2 * half_cols + width] = wo_ref[pl.ds(at, short), :].astype(BF16)
+            out[:, 2 * half_cols : 2 * half_cols + width] = wo_ref[pl.ds(at, short), :]
             out[:, 2 * half_cols + width :] = small_ref[pl.ds(at, short), :].astype(BF16)
 
 
@@ -746,7 +746,7 @@
             [VMEM] * 7,
             1 << 30,
             6 * mb,
-            scratch=(pltpu.VMEM((width, half_cols), F32), pltpu.VMEM((width // 2, width), F32)),
+            scratch=(pltpu.VMEM((width, half_cols), BF16), pltpu.VMEM((width // 2, width), BF16)),
         )(dh, n1, y, go, got, got_grad, small)
         dx, *pieces = lax.optimization_barrier((dx, *pieces))
         nears, fars = pieces[:columns], pieces[columns:]

time: 111 us -> 111 us (level)
  no operation moved by 1% of the time
where the time goes in v9:
time: 111 us
  blocking collectives  39.3 us (35%)
  starting transfers between devices  32.8 us (30%)
  Pallas kernels  21.3 us (19%)
  waiting for transfers between devices  13.6 us (12%)
  local copies, waits for them, and re-layouts  2.29 us (2%)
  between operations  1.16 us (1%)
    ppermute x18, starting transfers between devices, xor_step(): return lax.ppermute(value, 'dp', [(i, i ^ step) for i in range(size)])  22.8 us
    all_to_all x1, blocking collectives, on_device(): lax.all_to_all(msg.reshape(devices, 1, LANES), BOTH, 0, 0, tiled=True)  14 us
    all_to_all x1, blocking collectives, on_device(): lax.all_to_all(home.reshape(replicas, piece, width), 'dp', 0, 0, tiled=True)  13 us
    all_to_all x1, blocking collectives, on_device(): lax.all_to_all(served.reshape(devices, cap, width), BOTH, 0, 0, tiled=True)  12.3 us
    ppermute x18, waiting for transfers between devices, xor_step(): return lax.ppermute(value, 'dp', [(i, i ^ step) for i in range(size)])  10.6 us
    pallas_call x1, Pallas kernels, on_device(): call(functools.partial(layer_kernel, staged), (shape_of((rows, width), BF...  4.8 us
    all_to_all x1, starting transfers between devices, send_sums(): lax.all_to_all(sums.reshape(devices, cap, width), BOTH, 0, 0, tiled=True)  4.12 us
    pallas_call x1, Pallas kernels, into_table(): call(scatter_kernel, shape_of((rows_dev, width), F32), [VMEM] * 2, 1 << 3...  3.67 us
  transfers between devices with their start and end apart: 30, of which 10 were waited for; matrix products, arithmetic and copies ran while one was open for 0% of the time, Pallas kernels for 10%

profile of v9, /device:TPU:0, one launch (start us, length us, event | category | flops | bytes accessed | tf_op | source)
XLA Modules:
  0.0 110.8 jit_solution(192025101016885463)
XLA Ops:
  0.6 1.7 %shard_map.247 = s32[32,128]{1,0:T(8,128)} custom-call(s32[8,32]{1,0:T(8,128)} %bitcast.67, s32[1,256]{1,0:T(1,128)} %bitcast.52, s32[1,64]{1,0:T(1,128)} %len_ref.1, s32[1,64]{1,0:T(1,128)} %dest_ref.1, s32[32,128]{1,0:T(8,128)} %bitcast.50), custom_call_target="tpu_custom_call" | custom-call | flops 1048576 | bytes 131072 | tf_op jit(solution)/shard_map/pallas_call | solution.py:618
  3.0 14.0 %all_to_all.25 = s32[32,1,128]{2,1,0:T(1,128)S(1)} all-to-all(s32[32,1,128]{2,1,0:T(1,128)} %bitcast.66), channel_id=1, replica_groups=mesh['dp'=16,'table'=2] {'dp','table'}, dimensions={0} | all-to-all | bytes 32768 | tf_op jit(solution)/shard_map/all_to_all | solution.py:637
  17.0 2.2 %copy-done = bf16[4096,512]{1,0:T(8,128)(2,1)S(1)} copy-done((bf16[4096,512]{1,0:T(8,128)(2,1)S(1)}, bf16[4096,512]{1,0:T(8,128)(2,1)}, u32[]{:S(2)}) %copy-start) | copy-done | bytes 4194328
  19.2 1.4 %shard_map.248 = bf16[256,512]{1,0:T(8,128)(2,1)S(1)} custom-call(s32[32,128]{1,0:T(8,128)S(1)} %bitcast.48, bf16[4096,512]{1,0:T(8,128)(2,1)S(1)} %copy-done), custom_call_target="tpu_custom_call" | custom-call | flops 1073741824 | bytes 5242880 | tf_op jit(solution)/shard_map/pallas_call | solution.py:640
  20.6 12.3 %all_to_all.26 = bf16[32,8,512]{2,1,0:T(8,128)(2,1)S(1)} all-to-all(bf16[32,8,512]{2,1,0:T(8,128)(2,1)S(1)} %bitcast.44), channel_id=1, replica_groups=mesh['dp'=16,'table'=2] {'dp','table'}, dimensions={0} | all-to-all | bytes 524288 | tf_op jit(solution)/shard_map/all_to_all | solution.py:643
  33.2 13.0 %all_to_all.27 = bf16[16,16,512]{2,1,0:T(8,128)(2,1)S(1)} all-to-all(bf16[16,16,512]{2,1,0:T(8,128)(2,1)S(1)} %bitcast.47), channel_id=1, replica_groups=mesh['dp'=16,'table'=2] {'dp'}, dimensions={0} | all-to-all | bytes 524288 | tf_op jit(solution)/shard_map/all_to_all | solution.py:658
  46.3 4.8 %shard_map.250 = (bf16[256,512]{1,0:T(8,128)(2,1)}, bf16[256,512]{1,0:T(8,128)(2,1)S(1)}, bf16[256,512]{1,0:T(8,128)(2,1)S(1)}, bf16[256,512]{1,0:T(8,128)(2,1)S...) custom-call(bf16[256,512]{1,0:T(8,128)(2,1)S(1)} %bitcast.42, ...), custom_call_target="tpu_custom_call" | custom-call | flops 2147483648 | bytes 8388608 | tf_op jit(solution)/shard_map/pallas_call | solution.py:663
  51.1 2.4 %shard_map.251 = (bf16[256,512]{1,0:T(8,128)(2,1)}, f32[256,128]{1,0:T(8,128)S(1)}) custom-call(bf16[256,2048]{1,0:T(8,128)(2,1)S(1)} %get-tuple-element.80.dh_ref, bf16[512,2048]{1,0:T(8,128)(2,1)S(1)} %copy-done.1, bf16[256,512]{1,0:T(8,128)(2,1)S(1)} %bitcast.43, f32[1,512]{1,0:T(1,128)S(1)} %bitcast.56, bf16[256,512]{1,0:T(8,128)(2,1)S(1)} %get-tuple-element.81.go_ref, ...), custom_call_target="tpu_custom_call" | custom-call | flops 536870912 | bytes 4194304 | tf_op jit(solution)/shard_map/pallas_call | solution.py:732
  56.1 2.0 %collective-permute-start.8 = (bf16[2,16,2688]{2,1,0:T(8,128)(2,1)S(1)}, bf16[2,16,2688]{2,1,0:T(8,128)(2,1)S(1)}, u32[]{:S(2)}, u32[]{:S(2)}) collective-permute-start(bf16[2,16,2688]{2,1,0:T(8,128)(2,1)S(1)} %get-tuple-element.112), channel_id=1, source_target_pairs={{0,6},{2,4},{4,2},{6,0},{8,14},{10,12},{12,10},{14,8},{16,22},{18,... | collective-permute-start | bytes 516104 | tf_op jit(solution)/shard_map/ppermute | solution.py:563
  58.1 3.6 %all-to-all-start.3 = ((bf16[16,16,512]{2,1,0:T(8,128)(2,1)}), bf16[16,16,512]{2,1,0:T(8,128)(2,1)S(1)}, u32[]{:S(2)}, u32[]{:S(2)}) async-start(bf16[16,16,512]{2,1,0:T(8,128)(2,1)} %bitcast.16), calls=%async_computation.3 | async-start | bytes 524288 | tf_op jit(solution)/shard_map/all_to_all | solution.py:703
  61.8 1.9 %collective-permute-start.3 = (bf16[2,16,2688]{2,1,0:T(8,128)(2,1)S(1)}, bf16[2,16,2688]{2,1,0:T(8,128)(2,1)S(1)}, u32[]{:S(2)}, u32[]{:S(2)}) collective-permute-start(bf16[2,16,2688]{2,1,0:T(8,128)(2,1)S(1)} %get-tuple-element.104), channel_id=1, source_target_pairs={{0,2},{2,0},{4,6},{6,4},{8,10},{10,8},{12,14},{14,12},{16,18},{18,... | collective-permute-start | bytes 516104 | tf_op jit(solution)/shard_map/ppermute | solution.py:563
  63.6 1.5 %collective-permute-start.4 = (bf16[2,16,2688]{2,1,0:T(8,128)(2,1)S(1)}, bf16[2,16,2688]{2,1,0:T(8,128)(2,1)S(1)}, u32[]{:S(2)}, u32[]{:S(2)}) collective-permute-start(bf16[2,16,2688]{2,1,0:T(8,128)(2,1)S(1)} %get-tuple-element.105), channel_id=1, source_target_pairs={{0,4},{2,6},{4,0},{6,2},{8,12},{10,14},{12,8},{14,10},{16,20},{18,... | collective-permute-start | bytes 516104 | tf_op jit(solution)/shard_map/ppermute | solution.py:563
  66.2 2.0 %collective-permute-start.9 = (bf16[16,2688]{1,0:T(8,128)(2,1)S(1)}, bf16[16,2688]{1,0:T(8,128)(2,1)S(1)}, u32[]{:S(2)}, u32[]{:S(2)}) collective-permute-start(bf16[16,2688]{1,0:T(8,128)(2,1)S(1)} %get-tuple-element.140), channel_id=1, source_target_pairs={{0,16},{2,18},{4,20},{6,22},{8,24},{10,26},{12,28},{14,30},{16,0},... | collective-permute-start | bytes 258056 | tf_op jit(solution)/shard_map/ppermute | solution.py:563
  68.2 1.5 %collective-permute-start.10 = (bf16[16,2688]{1,0:T(8,128)(2,1)S(1)}, bf16[16,2688]{1,0:T(8,128)(2,1)S(1)}, u32[]{:S(2)}, u32[]{:S(2)}) collective-permute-start(bf16[16,2688]{1,0:T(8,128)(2,1)S(1)} %get-tuple-element.141), channel_id=1, source_target_pairs={{0,24},{2,26},{4,28},{6,30},{8,16},{10,18},{12,20},{14,22},{16,8},... | collective-permute-start | bytes 258056 | tf_op jit(solution)/shard_map/ppermute | solution.py:563
  69.7 2.0 %collective-permute-done.3 = bf16[2,16,2688]{2,1,0:T(8,128)(2,1)S(1)} collective-permute-done((bf16[2,16,2688]{2,1,0:T(8,128)(2,1)S(1)}, bf16[2,16,2688]{2,1,0:T(8,128)(2,1)S(1)}, u32[]{:S(2)}, u32[]{:S(2)}) %collective-permute-start.3) | collective-permute-done | bytes 172064 | tf_op jit(solution)/shard_map/ppermute | solution.py:563
  71.6 4.1 %collective-permute-done.4 = bf16[2,16,2688]{2,1,0:T(8,128)(2,1)S(1)} collective-permute-done((bf16[2,16,2688]{2,1,0:T(8,128)(2,1)S(1)}, bf16[2,16,2688]{2,1,0:T(8,128)(2,1)S(1)}, u32[]{:S(2)}, u32[]{:S(2)}) %collective-permute-start.4) | collective-permute-done | bytes 172064 | tf_op jit(solution)/shard_map/ppermute | solution.py:563
  75.8 1.4 %collective-permute-start.6 = (bf16[16,2688]{1,0:T(8,128)(2,1)S(1)}, bf16[16,2688]{1,0:T(8,128)(2,1)S(1)}, u32[]{:S(2)}, u32[]{:S(2)}) collective-permute-start(bf16[16,2688]{1,0:T(8,128)(2,1)S(1)} %slice_bitcast_fusion.2), channel_id=1, source_target_pairs={{0,8},{2,10},{4,12},{6,14},{8,0},{10,2},{12,4},{14,6},{16,24},{18,... | collective-permute-start | bytes 258056 | tf_op jit(solution)/shard_map/ppermute | solution.py:563
  77.3 0.9 shard_map.253
  78.2 2.2 %collective-permute-done.6 = bf16[16,2688]{1,0:T(8,128)(2,1)S(1)} collective-permute-done((bf16[16,2688]{1,0:T(8,128)(2,1)S(1)}, bf16[16,2688]{1,0:T(8,128)(2,1)S(1)}, u32[]{:S(2)}, u32[]{:S(2)}) %collective-permute-start.6) | collective-permute-done | bytes 86048 | tf_op jit(solution)/shard_map/ppermute | solution.py:563
  80.4 1.7 %collective-permute-start.16 = (bf16[16,2688]{1,0:T(8,128)(2,1)S(1)}, bf16[16,2688]{1,0:T(8,128)(2,1)S(1)}, u32[]{:S(2)}, u32[]{:S(2)}) collective-permute-start(bf16[16,2688]{1,0:T(8,128)(2,1)S(1)} %fusion.2), channel_id=1, source_target_pairs={{0,8},{2,10},{4,12},{6,14},{8,0},{10,2},{12,4},{14,6},{16,24},{18,... | collective-permute-start | bytes 258056 | tf_op jit(solution)/shard_map/ppermute | solution.py:563
  82.1 1.6 %collective-permute-start.12 = (bf16[16,2688]{1,0:T(8,128)(2,1)S(1)}, bf16[16,2688]{1,0:T(8,128)(2,1)S(1)}, u32[]{:S(2)}, u32[]{:S(2)}) collective-permute-start(bf16[16,2688]{1,0:T(8,128)(2,1)S(1)} %fusion.2), channel_id=1, source_target_pairs={{0,24},{2,26},{4,28},{6,30},{8,16},{10,18},{12,20},{14,22},{16,8},... | collective-permute-start | bytes 258056 | tf_op jit(solution)/shard_map/ppermute | solution.py:563
  84.0 1.3 %collective-permute-done.16 = bf16[16,2688]{1,0:T(8,128)(2,1)S(1)} collective-permute-done((bf16[16,2688]{1,0:T(8,128)(2,1)S(1)}, bf16[16,2688]{1,0:T(8,128)(2,1)S(1)}, u32[]{:S(2)}, u32[]{:S(2)}) %collective-permute-start.16) | collective-permute-done | bytes 86048 | tf_op jit(solution)/shard_map/ppermute | solution.py:563
  85.3 2.3 %collective-permute-start.19 = (bf16[2,16,2688]{2,1,0:T(8,128)(2,1)S(1)}, bf16[2,16,2688]{2,1,0:T(8,128)(2,1)S(1)}, u32[]{:S(2)}, u32[]{:S(2)}) collective-permute-start(bf16[2,16,2688]{2,1,0:T(8,128)(2,1)S(1)} %pad_maximum_fusion.1.refs_0_), channel_id=1, source_target_pairs={{0,6},{2,4},{4,2},{6,0},{8,14},{10,12},{12,10},{14,8},{16,22},{18,... | collective-permute-start | bytes 516104 | tf_op jit(solution)/shard_map/ppermute | solution.py:563
  88.0 1.1 collective-permute-start.17
  89.1 4.1 %all-to-all-start.4 = ((bf16[32,8,512]{2,1,0:T(8,128)(2,1)}), bf16[32,8,512]{2,1,0:T(8,128)(2,1)S(1)}, u32[]{:S(2)}, u32[]{:S(2)}) async-start(bf16[32,8,512]{2,1,0:T(8,128)(2,1)} %bitcast.26), calls=%async_computation.4 | async-start | bytes 524288 | tf_op jit(solution)/shard_map/all_to_all | solution.py:711
  94.8 2.5 %collective-permute-start.15 = (bf16[2,16,2688]{2,1,0:T(8,128)(2,1)S(1)}, bf16[2,16,2688]{2,1,0:T(8,128)(2,1)S(1)}, u32[]{:S(2)}, u32[]{:S(2)}) collective-permute-start(bf16[2,16,2688]{2,1,0:T(8,128)(2,1)S(1)} %pad_maximum_fusion.refs_4_), channel_id=1, source_target_pairs={{0,6},{2,4},{4,2},{6,0},{8,14},{10,12},{12,10},{14,8},{16,22},{18,... | collective-permute-start | bytes 516104 | tf_op jit(solution)/shard_map/ppermute | solution.py:563
  98.3 1.1 shard_map.255
  99.3 2.0 %shard_map.254 = (f32[512,2048]{1,0:T(8,128)}, f32[512,512]{1,0:T(8,128)}, f32[256,128]{1,0:T(8,128)S(1)}) custom-call(bf16[2,16,2688]{2,1,0:T(8,128)(2,1)S(1)} %pad_maximum_fusion.1.refs_0_, bf16[2,16,2688]{2,1,0:T(8,128)(2,1)S(1)} %collective-permute-done.17.refs_1_, bf16[2,16,2688]{2,1,0:T(8,128)(2,1)S(1)} %collective-permute-done.18.refs_2_, ...), custom_call_target="tpu_custom_call" | custom-call | flops 1048576 | bytes 3145728 | tf_op jit(solution)/shard_map/pallas_call | solution.py:798
  101.4 2.3 %all-to-all-done.4 = bf16[32,8,512]{2,1,0:T(8,128)(2,1)S(1)} async-done(((bf16[32,8,512]{2,1,0:T(8,128)(2,1)}), bf16[32,8,512]{2,1,0:T(8,128)(2,1)S(1)}, u32[]{:S(2)}, u32[]{:S(2)}) %all-to-all-start.4) | async-done | bytes 262176 | tf_op jit(solution)/shard_map/all_to_all | solution.py:711
  103.7 3.7 %shard_map.256 = f32[4096,512]{1,0:T(8,128)} custom-call(f32[8,256]{1,0:T(8,128)S(1)} %get-tuple-element.118.row_ref, bf16[256,512]{1,0:T(8,128)(2,1)S(1)} %bitcast.41), custom_call_target="tpu_custom_call" | custom-call | flops 1073741824 | bytes 8388608 | tf_op jit(solution)/shard_map/pallas_call | solution.py:716
  108.1 1.1 shard_map.257
  109.5 1.1 %shard_map.258 = (f32[512,2048]{1,0:T(8,128)}, f32[512,512]{1,0:T(8,128)}, f32[1,2048]{1,0:T(1,128)}, f32[1,512]{1,0:T(1,128)}, f32[1,512]{1,0:T(1,128)}, /*inde...) custom-call(bf16[2,16,2688]{2,1,0:T(8,128)(2,1)S(1)} %collective-permute-done.2, ...), custom_call_target="tpu_custom_call", output_to_operand_aliasing={{0}: (3, {}), {1}: (4, {})} | custom-call | flops 1048576 | bytes 3145728 | tf_op jit(solution)/shard_map/pallas_call | solution.py:807
  (80 shorter events, 9.0 us)
Async XLA Ops:
  2.3 43.8 %copy-start.4 = (f32[512]{0:T(512)S(1)}, f32[512]{0:T(512)}, u32[]{:S(2)}) copy-start(f32[512]{0:T(512)} %param.23) | copy-start | bytes 6148
  2.4 14.6 %collective-permute-start = (bf16[256,512]{1,0:T(8,128)(2,1)}, bf16[256,512]{1,0:T(8,128)(2,1)S(1)}, u32[]{:S(2)}, u32[]{:S(2)}) collective-permute-start(bf16[256,512]{1,0:T(8,128)(2,1)} %og_ref.1), channel_id=1, source_target_pairs={{0,1},{1,0},{2,3},{3,2},{4,5},{5,4},{6,7},{7,6},{8,9},{9,8},{10,11... | collective-permute-start | bytes 786440 | tf_op jit(solution)/shard_map/ppermute | solution.py:575
  51.1 2.5 %collective-permute-start.1 = (bf16[256,1792]{1,0:T(8,128)(2,1)S(1)}, bf16[256,1792]{1,0:T(8,128)(2,1)S(1)}, u32[]{:S(2)}, u32[]{:S(2)}) collective-permute-start(bf16[256,1792]{1,0:T(8,128)(2,1)S(1)} %get-tuple-element.87), channel_id=1, source_target_pairs={{0,1},{1,0},{2,3},{3,2},{4,5},{5,4},{6,7},{7,6},{8,9},{9,8},{10,11... | collective-permute-start | bytes 2752520 | tf_op jit(solution)/shard_map/ppermute | solution.py:575
  53.6 44.7 %copy-start.2 = (s32[4096]{0:T(1024)S(1)}, s32[4096]{0:T(1024)}, u32[]{:S(2)}) copy-start(s32[4096]{0:T(1024)} %param.22) | copy-start | bytes 49156
  54.5 7.2 %collective-permute-start.2 = (bf16[2,16,2688]{2,1,0:T(8,128)(2,1)S(1)}, bf16[2,16,2688]{2,1,0:T(8,128)(2,1)S(1)}, u32[]{:S(2)}, u32[]{:S(2)}) collective-permute-start(bf16[2,16,2688]{2,1,0:T(8,128)(2,1)S(1)} %get-tuple-element.102), channel_id=1, source_target_pairs={{0,2},{2,0},{4,6},{6,4},{8,10},{10,8},{12,14},{14,12},{16,18},{18,... | collective-permute-start | bytes 516104 | tf_op jit(solution)/shard_map/ppermute | solution.py:563
  55.3 10.7 %collective-permute-start.7 = (bf16[2,16,2688]{2,1,0:T(8,128)(2,1)S(1)}, bf16[2,16,2688]{2,1,0:T(8,128)(2,1)S(1)}, u32[]{:S(2)}, u32[]{:S(2)}) collective-permute-start(bf16[2,16,2688]{2,1,0:T(8,128)(2,1)S(1)} %get-tuple-element.111), channel_id=1, source_target_pairs={{0,4},{2,6},{4,0},{6,2},{8,12},{10,14},{12,8},{14,10},{16,20},{18,... | collective-permute-start | bytes 516104 | tf_op jit(solution)/shard_map/ppermute | solution.py:563
  56.1 10.0 %collective-permute-start.8 = (bf16[2,16,2688]{2,1,0:T(8,128)(2,1)S(1)}, bf16[2,16,2688]{2,1,0:T(8,128)(2,1)S(1)}, u32[]{:S(2)}, u32[]{:S(2)}) collective-permute-start(bf16[2,16,2688]{2,1,0:T(8,128)(2,1)S(1)} %get-tuple-element.112), channel_id=1, source_target_pairs={{0,6},{2,4},{4,2},{6,0},{8,14},{10,12},{12,10},{14,8},{16,22},{18,... | collective-permute-start | bytes 516104 | tf_op jit(solution)/shard_map/ppermute | solution.py:563
  58.1 17.7 %all-to-all-start.3 = ((bf16[16,16,512]{2,1,0:T(8,128)(2,1)}), bf16[16,16,512]{2,1,0:T(8,128)(2,1)S(1)}, u32[]{:S(2)}, u32[]{:S(2)}) async-start(bf16[16,16,512]{2,1,0:T(8,128)(2,1)} %bitcast.16), calls=%async_computation.3 | async-start | bytes 524288 | tf_op jit(solution)/shard_map/all_to_all | solution.py:703
  61.8 9.9 %collective-permute-start.3 = (bf16[2,16,2688]{2,1,0:T(8,128)(2,1)S(1)}, bf16[2,16,2688]{2,1,0:T(8,128)(2,1)S(1)}, u32[]{:S(2)}, u32[]{:S(2)}) collective-permute-start(bf16[2,16,2688]{2,1,0:T(8,128)(2,1)S(1)} %get-tuple-element.104), channel_id=1, source_target_pairs={{0,2},{2,0},{4,6},{6,4},{8,10},{10,8},{12,14},{14,12},{16,18},{18,... | collective-permute-start | bytes 516104 | tf_op jit(solution)/shard_map/ppermute | solution.py:563
  63.6 12.1 %collective-permute-start.4 = (bf16[2,16,2688]{2,1,0:T(8,128)(2,1)S(1)}, bf16[2,16,2688]{2,1,0:T(8,128)(2,1)S(1)}, u32[]{:S(2)}, u32[]{:S(2)}) collective-permute-start(bf16[2,16,2688]{2,1,0:T(8,128)(2,1)S(1)} %get-tuple-element.105), channel_id=1, source_target_pairs={{0,4},{2,6},{4,0},{6,2},{8,12},{10,14},{12,8},{14,10},{16,20},{18,... | collective-permute-start | bytes 516104 | tf_op jit(solution)/shard_map/ppermute | solution.py:563
  65.1 10.6 %collective-permute-start.5 = (bf16[2,16,2688]{2,1,0:T(8,128)(2,1)S(1)}, bf16[2,16,2688]{2,1,0:T(8,128)(2,1)S(1)}, u32[]{:S(2)}, u32[]{:S(2)}) collective-permute-start(bf16[2,16,2688]{2,1,0:T(8,128)(2,1)S(1)} %get-tuple-element.106), channel_id=1, source_target_pairs={{0,6},{2,4},{4,2},{6,0},{8,14},{10,12},{12,10},{14,8},{16,22},{18,... | collective-permute-start | bytes 516104 | tf_op jit(solution)/shard_map/ppermute | solution.py:563
  66.2 12.0 %collective-permute-start.9 = (bf16[16,2688]{1,0:T(8,128)(2,1)S(1)}, bf16[16,2688]{1,0:T(8,128)(2,1)S(1)}, u32[]{:S(2)}, u32[]{:S(2)}) collective-permute-start(bf16[16,2688]{1,0:T(8,128)(2,1)S(1)} %get-tuple-element.140), channel_id=1, source_target_pairs={{0,16},{2,18},{4,20},{6,22},{8,24},{10,26},{12,28},{14,30},{16,0},... | collective-permute-start | bytes 258056 | tf_op jit(solution)/shard_map/ppermute | solution.py:563
  68.2 10.0 %collective-permute-start.10 = (bf16[16,2688]{1,0:T(8,128)(2,1)S(1)}, bf16[16,2688]{1,0:T(8,128)(2,1)S(1)}, u32[]{:S(2)}, u32[]{:S(2)}) collective-permute-start(bf16[16,2688]{1,0:T(8,128)(2,1)S(1)} %get-tuple-element.141), channel_id=1, source_target_pairs={{0,24},{2,26},{4,28},{6,30},{8,16},{10,18},{12,20},{14,22},{16,8},... | collective-permute-start | bytes 258056 | tf_op jit(solution)/shard_map/ppermute | solution.py:563
  75.8 4.6 %collective-permute-start.6 = (bf16[16,2688]{1,0:T(8,128)(2,1)S(1)}, bf16[16,2688]{1,0:T(8,128)(2,1)S(1)}, u32[]{:S(2)}, u32[]{:S(2)}) collective-permute-start(bf16[16,2688]{1,0:T(8,128)(2,1)S(1)} %slice_bitcast_fusion.2), channel_id=1, source_target_pairs={{0,8},{2,10},{4,12},{6,14},{8,0},{10,2},{12,4},{14,6},{16,24},{18,... | collective-permute-start | bytes 258056 | tf_op jit(solution)/shard_map/ppermute | solution.py:563
  80.4 4.9 %collective-permute-start.16 = (bf16[16,2688]{1,0:T(8,128)(2,1)S(1)}, bf16[16,2688]{1,0:T(8,128)(2,1)S(1)}, u32[]{:S(2)}, u32[]{:S(2)}) collective-permute-start(bf16[16,2688]{1,0:T(8,128)(2,1)S(1)} %fusion.2), channel_id=1, source_target_pairs={{0,8},{2,10},{4,12},{6,14},{8,0},{10,2},{12,4},{14,6},{16,24},{18,... | collective-permute-start | bytes 258056 | tf_op jit(solution)/shard_map/ppermute | solution.py:563
  82.1 7.0 %collective-permute-start.12 = (bf16[16,2688]{1,0:T(8,128)(2,1)S(1)}, bf16[16,2688]{1,0:T(8,128)(2,1)S(1)}, u32[]{:S(2)}, u32[]{:S(2)}) collective-permute-start(bf16[16,2688]{1,0:T(8,128)(2,1)S(1)} %fusion.2), channel_id=1, source_target_pairs={{0,24},{2,26},{4,28},{6,30},{8,16},{10,18},{12,20},{14,22},{16,8},... | collective-permute-start | bytes 258056 | tf_op jit(solution)/shard_map/ppermute | solution.py:563
  83.7 9.6 %collective-permute-start.11 = (bf16[16,2688]{1,0:T(8,128)(2,1)S(1)}, bf16[16,2688]{1,0:T(8,128)(2,1)S(1)}, u32[]{:S(2)}, u32[]{:S(2)}) collective-permute-start(bf16[16,2688]{1,0:T(8,128)(2,1)S(1)} %fusion.2), channel_id=1, source_target_pairs={{0,16},{2,18},{4,20},{6,22},{8,24},{10,26},{12,28},{14,30},{16,0},... | collective-permute-start | bytes 258056 | tf_op jit(solution)/shard_map/ppermute | solution.py:563
  85.3 8.6 %collective-permute-start.19 = (bf16[2,16,2688]{2,1,0:T(8,128)(2,1)S(1)}, bf16[2,16,2688]{2,1,0:T(8,128)(2,1)S(1)}, u32[]{:S(2)}, u32[]{:S(2)}) collective-permute-start(bf16[2,16,2688]{2,1,0:T(8,128)(2,1)S(1)} %pad_maximum_fusion.1.refs_0_), channel_id=1, source_target_pairs={{0,6},{2,4},{4,2},{6,0},{8,14},{10,12},{12,10},{14,8},{16,22},{18,... | collective-permute-start | bytes 516104 | tf_op jit(solution)/shard_map/ppermute | solution.py:563
  87.6 6.3 %collective-permute-start.18 = (bf16[2,16,2688]{2,1,0:T(8,128)(2,1)S(1)}, bf16[2,16,2688]{2,1,0:T(8,128)(2,1)S(1)}, u32[]{:S(2)}, u32[]{:S(2)}) collective-permute-start(bf16[2,16,2688]{2,1,0:T(8,128)(2,1)S(1)} %pad_maximum_fusion.1.refs_0_), channel_id=1, source_target_pairs={{0,4},{2,6},{4,0},{6,2},{8,12},{10,14},{12,8},{14,10},{16,20},{18,... | collective-permute-start | bytes 516104 | tf_op jit(solution)/shard_map/ppermute | solution.py:563
  88.0 6.3 %collective-permute-start.17 = (bf16[2,16,2688]{2,1,0:T(8,128)(2,1)S(1)}, bf16[2,16,2688]{2,1,0:T(8,128)(2,1)S(1)}, u32[]{:S(2)}, u32[]{:S(2)}) collective-permute-start(bf16[2,16,2688]{2,1,0:T(8,128)(2,1)S(1)} %pad_maximum_fusion.1.refs_0_), channel_id=1, source_target_pairs={{0,2},{2,0},{4,6},{6,4},{8,10},{10,8},{12,14},{14,12},{16,18},{18,... | collective-permute-start | bytes 516104 | tf_op jit(solution)/shard_map/ppermute | solution.py:563
  89.1 14.6 %all-to-all-start.4 = ((bf16[32,8,512]{2,1,0:T(8,128)(2,1)}), bf16[32,8,512]{2,1,0:T(8,128)(2,1)S(1)}, u32[]{:S(2)}, u32[]{:S(2)}) async-start(bf16[32,8,512]{2,1,0:T(8,128)(2,1)} %bitcast.26), calls=%async_computation.4 | async-start | bytes 524288 | tf_op jit(solution)/shard_map/all_to_all | solution.py:711
  93.3 1.5 %collective-permute-start.24 = (bf16[2,16,2688]{2,1,0:T(8,128)(2,1)S(1)}, bf16[2,16,2688]{2,1,0:T(8,128)(2,1)S(1)}, u32[]{:S(2)}, u32[]{:S(2)}) collective-permute-start(bf16[2,16,2688]{2,1,0:T(8,128)(2,1)S(1)} %pad_maximum_fusion.refs_4_), channel_id=1, source_target_pairs={{0,1},{1,0},{2,3},{3,2},{4,5},{5,4},{6,7},{7,6},{8,9},{9,8},{10,11... | collective-permute-start | bytes 516104 | tf_op jit(solution)/shard_map/ppermute | solution.py:575
  93.4 3.8 %collective-permute-start.20 = (bf16[2,16,2688]{2,1,0:T(8,128)(2,1)S(1)}, bf16[2,16,2688]{2,1,0:T(8,128)(2,1)S(1)}, u32[]{:S(2)}, u32[]{:S(2)}) collective-permute-start(bf16[2,16,2688]{2,1,0:T(8,128)(2,1)S(1)} %pad_maximum_fusion.1.refs_0_), channel_id=1, source_target_pairs={{0,1},{1,0},{2,3},{3,2},{4,5},{5,4},{6,7},{7,6},{8,9},{9,8},{10,11... | collective-permute-start | bytes 516104 | tf_op jit(solution)/shard_map/ppermute | solution.py:575
  93.9 4.0 %collective-permute-start.23 = (bf16[2,16,2688]{2,1,0:T(8,128)(2,1)S(1)}, bf16[2,16,2688]{2,1,0:T(8,128)(2,1)S(1)}, u32[]{:S(2)}, u32[]{:S(2)}) collective-permute-start(bf16[2,16,2688]{2,1,0:T(8,128)(2,1)S(1)} %collective-permute-done.19.refs_3_), channel_id=1, source_target_pairs={{0,1},{1,0},{2,3},{3,2},{4,5},{5,4},{6,7},{7,6},{8,9},{9,8},{10,11... | collective-permute-start | bytes 516104 | tf_op jit(solution)/shard_map/ppermute | solution.py:575
  94.0 5.4 %collective-permute-start.22 = (bf16[2,16,2688]{2,1,0:T(8,128)(2,1)S(1)}, bf16[2,16,2688]{2,1,0:T(8,128)(2,1)S(1)}, u32[]{:S(2)}, u32[]{:S(2)}) collective-permute-start(bf16[2,16,2688]{2,1,0:T(8,128)(2,1)S(1)} %collective-permute-done.18.refs_2_), channel_id=1, source_target_pairs={{0,1},{1,0},{2,3},{3,2},{4,5},{5,4},{6,7},{7,6},{8,9},{9,8},{10,11... | collective-permute-start | bytes 516104 | tf_op jit(solution)/shard_map/ppermute | solution.py:575
  94.4 4.9 %collective-permute-start.21 = (bf16[2,16,2688]{2,1,0:T(8,128)(2,1)S(1)}, bf16[2,16,2688]{2,1,0:T(8,128)(2,1)S(1)}, u32[]{:S(2)}, u32[]{:S(2)}) collective-permute-start(bf16[2,16,2688]{2,1,0:T(8,128)(2,1)S(1)} %collective-permute-done.17.refs_1_), channel_id=1, source_target_pairs={{0,1},{1,0},{2,3},{3,2},{4,5},{5,4},{6,7},{7,6},{8,9},{9,8},{10,11... | collective-permute-start | bytes 516104 | tf_op jit(solution)/shard_map/ppermute | solution.py:575
  94.8 12.6 %collective-permute-start.15 = (bf16[2,16,2688]{2,1,0:T(8,128)(2,1)S(1)}, bf16[2,16,2688]{2,1,0:T(8,128)(2,1)S(1)}, u32[]{:S(2)}, u32[]{:S(2)}) collective-permute-start(bf16[2,16,2688]{2,1,0:T(8,128)(2,1)S(1)} %pad_maximum_fusion.refs_4_), channel_id=1, source_target_pairs={{0,6},{2,4},{4,2},{6,0},{8,14},{10,12},{12,10},{14,8},{16,22},{18,... | collective-permute-start | bytes 516104 | tf_op jit(solution)/shard_map/ppermute | solution.py:563
  97.3 10.3 %collective-permute-start.14 = (bf16[2,16,2688]{2,1,0:T(8,128)(2,1)S(1)}, bf16[2,16,2688]{2,1,0:T(8,128)(2,1)S(1)}, u32[]{:S(2)}, u32[]{:S(2)}) collective-permute-start(bf16[2,16,2688]{2,1,0:T(8,128)(2,1)S(1)} %pad_maximum_fusion.refs_4_), channel_id=1, source_target_pairs={{0,4},{2,6},{4,0},{6,2},{8,12},{10,14},{12,8},{14,10},{16,20},{18,... | collective-permute-start | bytes 516104 | tf_op jit(solution)/shard_map/ppermute | solution.py:563
  97.8 9.7 %collective-permute-start.13 = (bf16[2,16,2688]{2,1,0:T(8,128)(2,1)S(1)}, bf16[2,16,2688]{2,1,0:T(8,128)(2,1)S(1)}, u32[]{:S(2)}, u32[]{:S(2)}) collective-permute-start(bf16[2,16,2688]{2,1,0:T(8,128)(2,1)S(1)} %pad_maximum_fusion.refs_4_), channel_id=1, source_target_pairs={{0,2},{2,0},{4,6},{6,4},{8,10},{10,8},{12,14},{14,12},{16,18},{18,... | collective-permute-start | bytes 516104 | tf_op jit(solution)/shard_map/ppermute | solution.py:563
  107.6 1.6 %collective-permute-start.25 = (bf16[2,16,2688]{2,1,0:T(8,128)(2,1)S(1)}, bf16[2,16,2688]{2,1,0:T(8,128)(2,1)S(1)}, u32[]{:S(2)}, u32[]{:S(2)}) collective-permute-start(bf16[2,16,2688]{2,1,0:T(8,128)(2,1)S(1)} %collective-permute-done.13.refs_0_), channel_id=1, source_target_pairs={{0,1},{1,0},{2,3},{3,2},{4,5},{5,4},{6,7},{7,6},{8,9},{9,8},{10,11... | collective-permute-start | bytes 516104 | tf_op jit(solution)/shard_map/ppermute | solution.py:575
  107.6 1.7 %collective-permute-start.26 = (bf16[2,16,2688]{2,1,0:T(8,128)(2,1)S(1)}, bf16[2,16,2688]{2,1,0:T(8,128)(2,1)S(1)}, u32[]{:S(2)}, u32[]{:S(2)}) collective-permute-start(bf16[2,16,2688]{2,1,0:T(8,128)(2,1)S(1)} %collective-permute-done.14.refs_1_), channel_id=1, source_target_pairs={{0,1},{1,0},{2,3},{3,2},{4,5},{5,4},{6,7},{7,6},{8,9},{9,8},{10,11... | collective-permute-start | bytes 516104 | tf_op jit(solution)/shard_map/ppermute | solution.py:575
  108.1 1.4 %collective-permute-start.27 = (bf16[2,16,2688]{2,1,0:T(8,128)(2,1)S(1)}, bf16[2,16,2688]{2,1,0:T(8,128)(2,1)S(1)}, u32[]{:S(2)}, u32[]{:S(2)}) collective-permute-start(bf16[2,16,2688]{2,1,0:T(8,128)(2,1)S(1)} %collective-permute-done.15.refs_2_), channel_id=1, source_target_pairs={{0,1},{1,0},{2,3},{3,2},{4,5},{5,4},{6,7},{7,6},{8,9},{9,8},{10,11... | collective-permute-start | bytes 516104 | tf_op jit(solution)/shard_map/ppermute | solution.py:575
  (13 other events, 464.5 us)
